TPU v7x, 32 devices: a whole 2x2x4 slice. The times are simulated.
32 devices in a mesh: row: 4 (over z), col: 8 (over y, x, core).
Axes of the slice: x: 2, y: 2, z: 4, core: 2. Of those that a mesh axis runs over, the one named last changes fastest.
Arguments:
- tokens: bfloat16 [768, 14336], P('col', 'row'), may hold values from -6 to 6
- weight_in: bfloat16 [14336, 14336], P('row', 'col'), may hold values from -0.046875 to 0.046875
- bias_hidden: float32 [14336], P('col'), may hold values from -3 to 3
- weight_out: bfloat16 [14336, 14336], P('col', 'row'), may hold values from -0.046875 to 0.046875
- out_grad: bfloat16 [768, 14336], P('col', 'row'), may hold values from -0.75 to 0.75
Outputs:
- grad_tokens: bfloat16 [768, 14336], P('col', 'row')
- grad_weight_in: float32 [14336, 14336], P('row', 'col')
- grad_bias: float32 [14336], P('col')
- grad_weight_out: float32 [14336, 14336], P('col', 'row')
All inputs are finite; a program needn't handle non-finite values.
Results may differ from a plain program's by a relative error of at most 0.007.
Values may be sent and summed in bfloat16 or wider, within the bound.
No kernel may reach another device: no remote copies, remote signals or barrier semaphores. Data moves between devices by JAX's collectives and lax.ppermute only.
A program may use at most 192 MiB of HBM per device.

v0:
```python
import jax
import jax.numpy as jnp
from jax import lax
from jax.sharding import PartitionSpec as P

GELU_SCALE = 0.7978845608
GELU_CUBIC = 0.044715


def gelu_parts(values):
    inner = GELU_SCALE * (values + GELU_CUBIC * values * values * values)
    tangent = jnp.tanh(inner)
    result = 0.5 * values * (1.0 + tangent)
    slope = 0.5 * (1.0 + tangent) + 0.5 * values * (1.0 - tangent * tangent) * GELU_SCALE * (
        1.0 + 3.0 * GELU_CUBIC * values * values
    )
    return (result, slope)


def contract_rows(left, right):
    return lax.dot_general(
        left, right, (((0,), (0,)), ((), ())), preferred_element_type=jnp.float32
    )


def contract_cols(left, right):
    return lax.dot_general(
        left, right, (((1,), (1,)), ((), ())), preferred_element_type=jnp.float32
    )


def local(tokens, weight_in, bias_hidden, weight_out, out_grad):
    tok_all, grad_all = (
        lax.all_gather(tokens, "col", axis=0, tiled=True),
        lax.all_gather(out_grad, "col", axis=0, tiled=True),
    )
    pre_part = jnp.dot(tok_all, weight_in, preferred_element_type=jnp.float32)
    act_part = contract_cols(grad_all, weight_out)
    pre_mine, act_mine = (
        lax.psum_scatter(pre_part, "row", scatter_dimension=0, tiled=True),
        lax.psum_scatter(act_part, "row", scatter_dimension=0, tiled=True),
    )
    result, slope = gelu_parts(pre_mine + bias_hidden)
    act_local = result.astype(jnp.bfloat16)
    pre_grad_local = (act_mine * slope).astype(jnp.bfloat16)
    bias_local = jnp.sum(pre_grad_local, axis=0, dtype=jnp.float32)
    act_all, pre_grad_all = (
        lax.all_gather(act_local, "row", axis=0, tiled=True),
        lax.all_gather(pre_grad_local, "row", axis=0, tiled=True),
    )
    grad_bias = lax.psum(bias_local, "row")
    grad_weight_out = contract_rows(act_all, grad_all)
    grad_weight_in = contract_rows(tok_all, pre_grad_all)
    grad_tokens = lax.psum_scatter(
        contract_cols(pre_grad_all, weight_in), "col", scatter_dimension=0, tiled=True
    ).astype(jnp.bfloat16)
    return (grad_tokens, grad_weight_in, grad_bias, grad_weight_out)


def solution(mesh):
    placed = (P("col", "row"), P("row", "col"), P("col"), P("col", "row"), P("col", "row"))
    return jax.shard_map(
        local,
        mesh=mesh,
        in_specs=placed,
        out_specs=(P("col", "row"), P("row", "col"), P("col"), P("col", "row")),
        check_vma=False,
    )
```

profile of v0, /device:TPU:0, one launch (start us, length us, event | category | flops | bytes accessed | tf_op | source)
XLA Modules:
  0.0 515.9 jit_solution(8817194882196787144)
XLA Ops:
  7.2 0.0 all-gather.5.cloned.1.call-start
  7.2 0.7 all-gather.5.cloned.1.call-update
  7.9 0.0 all-gather.7.cloned.1.call-start
  7.9 0.7 all-gather.7.cloned.1.call-update
  8.6 0.0 reduce-scatter.4.cloned.1.call-start
  8.7 46.1 %all-gather.5.cloned.1.call-done = bf16[768,3584]{1,0:T(8,128)(2,1)} async-done(((bf16[96,3584]{1,0:T(8,128)(2,1)}), bf16[768,3584]{1,0:T(8,128)(2,1)}) %all-gather.5.cloned.1.call-update) | async-done | bytes 5505040 | tf_op jit(solution)/shard_map/all_gather | solution.py:35
  54.8 16.4 %fusion.8 = f32[768,1792]{1,0:T(8,128)} fusion(bf16[768,3584]{1,0:T(8,128)(2,1)} %all-gather.5.cloned.1.call-done, bf16[1792,3584]{1,0:T(8,128)(2,1)} %param.8), kind=kOutput, calls=%fused_computation.12 | convolution fusion | flops 9865003008 | bytes 23855104 | tf_op jit(solution)/shard_map/dot_general | solution.py:27
  71.3 0.0 reduce-scatter.4.cloned.1.call-update
  71.3 0.0 reduce-scatter.6.cloned.1.call-start
  71.4 27.6 %all-gather.7.cloned.1.call-done = bf16[768,3584]{1,0:T(8,128)(2,1)} async-done(((bf16[96,3584]{1,0:T(8,128)(2,1)}), bf16[768,3584]{1,0:T(8,128)(2,1)}) %all-gather.7.cloned.1.call-update) | async-done | bytes 5505040 | tf_op jit(solution)/shard_map/all_gather | solution.py:34
  99.0 16.4 %fusion.9 = f32[768,1792]{1,0:T(8,128)} fusion(bf16[768,3584]{1,0:T(8,128)(2,1)} %all-gather.7.cloned.1.call-done, bf16[3584,1792]{1,0:T(8,128)(2,1)} %param.6), kind=kOutput, calls=%fused_computation.13 | convolution fusion | flops 9865003008 | bytes 23855104 | tf_op jit(solution)/shard_map/dot_general | solution.py:37
  115.4 0.0 copy-start
  115.4 0.0 reduce-scatter.6.cloned.1.call-update
  115.4 0.0 all-gather.9.cloned.1.call-start
  115.4 84.4 %reduce-scatter.4.cloned.1.call-done = f32[192,1792]{1,0:T(8,128)} async-done(((f32[768,1792]{1,0:T(8,128)}), f32[192,1792]{1,0:T(8,128)}) %reduce-scatter.4.cloned.1.call-update) | async-done | bytes 1376272 | tf_op jit(solution)/shard_map/reduce_scatter | solution.py:41
  199.9 101.3 %reduce-scatter.6.cloned.1.call-done = f32[192,1792]{1,0:T(8,128)} async-done(((f32[768,1792]{1,0:T(8,128)}), f32[192,1792]{1,0:T(8,128)}) %reduce-scatter.6.cloned.1.call-update) | async-done | bytes 1376272 | tf_op jit(solution)/shard_map/reduce_scatter | solution.py:40
  301.2 0.0 copy-done
  301.2 3.9 convert_reduce_fusion
  305.1 0.0 all-gather.9.cloned.1.call-update
  305.1 0.0 all-gather.11.cloned.1.call-start
  305.1 0.5 all-gather.11.cloned.1.call-update
  305.7 0.0 reduce-scatter.8.cloned.1.call-start
  305.7 57.0 %all-gather.9.cloned.1.call-done = bf16[768,1792]{1,0:T(8,128)(2,1)} async-done(((bf16[192,1792]{1,0:T(8,128)(2,1)}), bf16[768,1792]{1,0:T(8,128)(2,1)}) %all-gather.9.cloned.1.call-update) | async-done | bytes 2752528 | tf_op jit(solution)/shard_map/all_gather | solution.py:49
  362.8 16.5 %fusion.10 = f32[768,3584]{1,0:T(8,128)} fusion(bf16[768,1792]{1,0:T(8,128)(2,1)} %all-gather.9.cloned.1.call-done, bf16[3584,1792]{1,0:T(8,128)(2,1)} %param.6), kind=kOutput, calls=%fused_computation.14 | convolution fusion | flops 9865003008 | bytes 26607616 | tf_op jit(solution)/shard_map/dot_general | solution.py:27
  379.3 0.0 copy-start.1
  379.3 0.0 reduce-scatter.8.cloned.1.call-update
  379.3 10.9 %psum.7 = f32[1792]{0:T(1024)} all-reduce(f32[1792]{0:T(1024)S(1)} %get-tuple-element.8), channel_id=1, replica_groups=mesh['row'=4,'col'=8] {'row'}, use_global_device_ids=true, to_apply=%region_4.0 | all-reduce | flops 1792 | bytes 14336 | tf_op jit(solution)/shard_map/psum | solution.py:51
  390.2 0.0 copy-done.1
  390.2 17.9 %convolution_bitcast_fusion = f32[3584,1792]{0,1:T(8,128)} fusion(bf16[768,1792]{1,0:T(8,128)(2,1)S(1)} %copy-done.1, bf16[768,3584]{1,0:T(8,128)(2,1)} %all-gather.7.cloned.1.call-done), kind=kOutput, calls=%fused_computation | convolution fusion | flops 9865003008 | bytes 33947648 | tf_op jit(solution)/shard_map/dot_general | solution.py:21
  408.1 28.1 %copy.9 = f32[3584,1792]{1,0:T(8,128)} copy(f32[3584,1792]{0,1:T(8,128)} %convolution_bitcast_fusion) | data formatting | bytes 51380224
  436.2 0.0 all-gather.11.cloned.1.call-done
  436.2 19.2 %fusion.11 = f32[1792,3584]{1,0:T(8,128)} fusion(bf16[768,1792]{1,0:T(8,128)(2,1)} %all-gather.11.cloned.1.call-done, bf16[768,3584]{1,0:T(8,128)(2,1)} %all-gather.5.cloned.1.call-done), kind=kOutput, calls=%fused_computation.15 | convolution fusion | flops 9865003008 | bytes 33947648 | tf_op jit(solution)/shard_map/dot_general | solution.py:21
  455.4 51.4 %reduce-scatter.8.cloned.1.call-done = f32[96,3584]{1,0:T(8,128)} async-done(((f32[768,3584]{1,0:T(8,128)}), f32[96,3584]{1,0:T(8,128)}) %reduce-scatter.8.cloned.1.call-update) | async-done | bytes 1376272 | tf_op jit(solution)/shard_map/reduce_scatter | solution.py:54
  506.8 2.3 convert_element_type.13
Async XLA Ops:
  7.2 47.7 %all-gather.5.cloned.1.call-start = ((), (), s32[]{:S(2)}) async-start(), calls=%async_computation.3 | async-start | bytes 6193152 | tf_op jit(solution)/shard_map/all_gather | solution.py:35
  7.9 91.1 %all-gather.7.cloned.1.call-start = ((), (), s32[]{:S(2)}) async-start(), calls=%async_computation.5 | async-start | bytes 6193152 | tf_op jit(solution)/shard_map/all_gather | solution.py:34
  8.6 191.2 %reduce-scatter.4.cloned.1.call-start = ((), (), s32[]{:S(2)}) async-start(), calls=%async_computation.4 | async-start | bytes 6881280 | tf_op jit(solution)/shard_map/reduce_scatter | solution.py:41
  71.3 229.9 %reduce-scatter.6.cloned.1.call-start = ((), (), s32[]{:S(2)}) async-start(), calls=%async_computation.6 | async-start | bytes 6881280 | tf_op jit(solution)/shard_map/reduce_scatter | solution.py:40
  115.4 185.8 %copy-start = (f32[1792]{0:T(1024)S(1)}, f32[1792]{0:T(1024)}, u32[]{:S(2)}) copy-start(f32[1792]{0:T(1024)} %param.7) | copy-start | bytes 21508
  115.4 247.4 %all-gather.9.cloned.1.call-start = ((), (), s32[]{:S(2)}) async-start(), calls=%async_computation.7 | async-start | bytes 3440640 | tf_op jit(solution)/shard_map/all_gather | solution.py:49
  305.1 131.2 %all-gather.11.cloned.1.call-start = ((), (), s32[]{:S(2)}) async-start(), calls=%async_computation.9 | async-start | bytes 3440640 | tf_op jit(solution)/shard_map/all_gather | solution.py:48
  305.7 201.1 %reduce-scatter.8.cloned.1.call-start = ((), (), s32[]{:S(2)}) async-start(), calls=%async_computation.8 | async-start | bytes 12386304 | tf_op jit(solution)/shard_map/reduce_scatter | solution.py:54
  379.3 10.9 %copy-start.1 = (bf16[768,1792]{1,0:T(8,128)(2,1)S(1)}, bf16[768,1792]{1,0:T(8,128)(2,1)}, u32[]{:S(2)}) copy-start(bf16[768,1792]{1,0:T(8,128)(2,1)} %all-gather.9.cloned.1.call-done) | copy-start | bytes 8257540
Sparse Core Ops, SparseCore 0:
  9.9 44.9 all-gather.4
  56.7 42.2 all-gather.6
  101.9 97.9 reduce-scatter.3
  202.6 98.5 reduce-scatter.5
  305.2 57.5 all-gather.8
  364.2 56.2 all-gather.10
  424.0 82.7 reduce-scatter.7
where the time goes:
time: 517 us; the launch traced here: 516 us
  waiting for transfers between devices  370 us (72%)
  matrix products  86.5 us (17%)
  local copies, waits for them, and re-layouts  28.1 us (5%)
  between operations  14.1 us (3%)
  blocking collectives  10.9 us (2%)
  other arithmetic  6.14 us (1%)
    reduce_scatter x1, waiting for transfers between devices, local(): lax.psum_scatter(pre_part, 'row', scatter_dimension=0, tiled=True)  101 us
    reduce_scatter x1, waiting for transfers between devices, local(): lax.psum_scatter(act_part, 'row', scatter_dimension=0, tiled=True)  84.4 us
    all_gather x1, waiting for transfers between devices, local(): lax.all_gather(pre_grad_local, 'row', axis=0, tiled=True)  57 us
    reduce_scatter x1, waiting for transfers between devices, local(): lax.psum_scatter(contract_cols(pre_grad_all, weight_in), 'col', scatter_d...  51.4 us
    all_gather x1, waiting for transfers between devices, local(): lax.all_gather(out_grad, 'col', axis=0, tiled=True)  46.1 us
    dot_general x2, matrix products, contract_rows(): lax.dot_general(left, right, (((0,), (0,)), ((), ())), preferred_element_...  37.1 us
    dot_general x2, matrix products, contract_cols(): lax.dot_general(left, right, (((1,), (1,)), ((), ())), preferred_element_...  33 us
    unnamed x5, local copies, waits for them, and re-layouts  28.1 us
  transfers between devices with their start and end apart: 7, of which 6 were waited for; matrix products, arithmetic and copies ran while one was open for 22% of the time, Pallas kernels for 0%

commit v1 on v0

v1 whole, which is shorter than its diff:
```python
import functools

import jax
import jax.numpy as jnp
from jax import lax
from jax.experimental import pallas as pl
from jax.experimental.pallas import tpu as pltpu
from jax.sharding import PartitionSpec as P

GELU_SCALE = 0.7978845608
GELU_CUBIC = 0.044715
F32, BF16 = jnp.float32, jnp.bfloat16
VMEM_LIMIT = 48 * 1024 * 1024
GROUPS, CHUNKS, TILE = 2, 7, 512


def dot(left, right, dims):
    return lax.dot_general(left, right, ((dims[:1], dims[1:]), ((), ())), preferred_element_type=F32)


def call(kernel, flops, moved, **kwargs):
    return pl.pallas_call(
        kernel,
        compiler_params=pltpu.CompilerParams(vmem_limit_bytes=VMEM_LIMIT),
        cost_estimate=pl.CostEstimate(flops=flops, bytes_accessed=moved, transcendentals=0),
        **kwargs,
    )


def partials(tok, out_grad, weight_in, weight_out, first, count):
    rows, depth = tok.shape
    width = weight_in.shape[1] // CHUNKS

    def kernel(tok_ref, grad_ref, win_ref, wout_ref, *outs):
        pre = dot(tok_ref[...], win_ref[...], (1, 0)).astype(BF16)
        act = dot(grad_ref[...], wout_ref[...], (1, 1)).astype(BF16)
        for at, out in enumerate(outs):

            @pl.when(pl.program_id(0) == at)
            def _():
                out[0] = pre
                out[1] = act

    whole = pl.BlockSpec((rows, depth), lambda i: (0, 0), pipeline_mode=pl.Buffered(1))
    return call(
        kernel,
        4 * rows * depth * width * count,
        4 * depth * (rows + width * count) + 4 * rows * width * count,
        grid=(count,),
        in_specs=[
            whole,
            whole,
            pl.BlockSpec((depth, width), lambda i: (0, first + i)),
            pl.BlockSpec((width, depth), lambda i: (first + i, 0)),
        ],
        out_specs=[pl.BlockSpec((2, rows, width), lambda i: (0, 0, 0), pipeline_mode=pl.Buffered(1))] * count,
        out_shape=[jax.ShapeDtypeStruct((2, rows, width), BF16)] * count,
    )(tok, out_grad, weight_in, weight_out)


def gelu_parts(values):
    inner = GELU_SCALE * (values + GELU_CUBIC * values * values * values)
    tangent = jnp.tanh(inner)
    result = 0.5 * values * (1.0 + tangent)
    slope = 0.5 * (1.0 + tangent) + 0.5 * values * (1.0 - tangent * tangent) * GELU_SCALE * (
        1.0 + 3.0 * GELU_CUBIC * values * values
    )
    return (result, slope)


def activate(terms, bias, at):
    _, rows, width = terms[0].shape

    def kernel(bias_ref, *refs):
        ins, (act_ref, grad_ref, sum_ref) = refs[:-3], refs[-3:]
        pre, act = (functools.reduce(jnp.add, [ref[half].astype(F32) for ref in ins]) for half in range(2))
        result, slope = gelu_parts(pre + bias_ref[...])
        act_ref[...] = result.astype(BF16)
        grad = (act * slope).astype(BF16)
        grad_ref[...] = grad
        sum_ref[...] = jnp.sum(grad.astype(F32), axis=0, keepdims=True)

    return call(
        kernel,
        40 * rows * width,
        4 * rows * width * (len(terms) + 1),
        grid=(1,),
        in_specs=[pl.BlockSpec((1, width), lambda i: (0, at))]
        + [pl.BlockSpec((2, rows, width), lambda i: (0, 0, 0))] * len(terms),
        out_specs=[pl.BlockSpec((rows, width), lambda i: (0, 0))] * 2 + [pl.BlockSpec((1, width), lambda i: (0, 0))],
        out_shape=[jax.ShapeDtypeStruct((rows, width), BF16)] * 2 + [jax.ShapeDtypeStruct((1, width), F32)],
    )(bias, *terms)


def add_bf16(left, right):
    return (left.astype(F32) + right.astype(F32)).astype(BF16)


def outer(lefts, rights, into, shape, first, count, chunk_rows):
    rows, depth = lefts[0].shape
    width = rights[0][0].shape[1]
    tile = TILE if depth % TILE == 0 else depth
    groups = len(lefts)

    def kernel(*refs):
        wide, thin, out = refs[:groups], refs[groups : groups + groups * count], refs[-1]
        for i in range(count):
            total = None
            for group in range(groups):
                chunk = thin[group * count + i][...]
                pair = (chunk, wide[group][...]) if chunk_rows else (wide[group][...], chunk)
                term = dot(*pair, (0, 0))
                total = term if total is None else total + term
            if chunk_rows:
                out[i * width : (i + 1) * width, :] = total
            else:
                out[:, i * width : (i + 1) * width] = total

    at = first // count
    block = (count * width, tile) if chunk_rows else (tile, count * width)
    place = (lambda j: (at, j)) if chunk_rows else (lambda j: (j, at))
    operands = list(lefts) + [chunk for group in rights for chunk in group]
    specs = [pl.BlockSpec((rows, tile), lambda j: (0, j))] * groups
    specs += [pl.BlockSpec((rows, width), lambda j: (0, 0))] * (groups * count)
    aliases = {}
    if into is not None:
        aliases = {len(operands): 0}
        operands.append(into)
        specs.append(pl.BlockSpec(memory_space=pl.ANY))
    return call(
        kernel,
        2 * groups * rows * depth * width * count,
        2 * groups * rows * depth + 4 * depth * width * count,
        grid=(depth // tile,),
        in_specs=specs,
        out_specs=pl.BlockSpec(block, place),
        out_shape=jax.ShapeDtypeStruct(shape, F32),
        input_output_aliases=aliases,
    )(*operands)


def back(grads, weight_in, first, base, last):
    rows, width = grads[0].shape
    depth = weight_in.shape[0]
    tile = TILE if depth % TILE == 0 else depth
    count = len(grads)

    def kernel(*refs):
        parts, weights = refs[:count], refs[count : 2 * count]
        total = None if base is None else refs[2 * count][...]
        for part, weight in zip(parts, weights):
            term = dot(part[...], weight[...], (1, 1))
            total = term if total is None else total + term
        if last:
            refs[-2][...] = total[: rows // 2].astype(BF16)
            refs[-1][...] = total[rows // 2 :].astype(BF16)
        else:
            refs[-1][...] = total

    specs = [pl.BlockSpec((rows, width), lambda j: (0, 0))] * count
    specs += [pl.BlockSpec((tile, width), lambda j, at=first + i: (j, at)) for i in range(count)]
    operands = list(grads) + [weight_in] * count
    if base is not None:
        specs.append(pl.BlockSpec((rows, tile), lambda j: (0, j)))
        operands.append(base)
    out_rows, kind = (rows // 2, BF16) if last else (rows, F32)
    outs = 2 if last else 1
    result = call(
        kernel,
        2 * rows * depth * width * count,
        2 * depth * width * count + 4 * rows * depth,
        grid=(depth // tile,),
        in_specs=specs,
        out_specs=[pl.BlockSpec((out_rows, tile), lambda j: (0, j))] * outs,
        out_shape=[jax.ShapeDtypeStruct((out_rows, depth), kind)] * outs,
    )(*operands)
    return result if last else result[0]


def swap(value, bit, size):
    return lax.ppermute(value, "col", [(i, i ^ bit) for i in range(size)])


def gather(block, bits, size):
    held = {0: block}
    for bit in bits:
        keys = list(held)
        for key in keys:
            held[key ^ bit] = swap(held[key], bit, size)
    return jnp.concatenate([held[key] for key in sorted(held)], axis=0)


def scatter(total, bits, size):
    held = dict(total)
    for bit in bits:
        sent = {key: swap(held[key], bit, size) for key in held if key & bit}
        held = {key: held[key].astype(F32) + sent[key ^ bit].astype(F32) for key in held if not key & bit}
        held = {key: value.astype(BF16) for key, value in held.items()}
    return held[0]


def gate(value, after):
    return lax.optimization_barrier((value, after))[0]


def local(rows_of, cols_of, tokens, weight_in, bias_hidden, weight_out, out_grad):
    mine, depth = tokens.shape
    hidden = bias_hidden.shape[0]
    part = mine // GROUPS
    bias = bias_hidden.reshape(1, hidden)
    chip_bits = [1 << i for i in range(1, cols_of.bit_length() - 1)]
    steps = rows_of - 1

    def send(value, step):
        pairs = [(step - 1, step), (rows_of - step, rows_of - step - 1)]
        return lax.ppermute(value, "row", pairs)

    def collect(group):
        rows = slice(group * part, (group + 1) * part)
        tok = gather(tokens[rows], chip_bits, cols_of)
        grad = gather(out_grad[rows], chip_bits[::-1], cols_of)
        return tuple(jnp.concatenate([x, swap(x, 1, cols_of)], axis=0) for x in (tok, grad))

    tok, grad = zip(*[collect(group) for group in range(GROUPS)])
    own = []
    for group in range(GROUPS):
        args = (tok[group], grad[group], weight_in, weight_out)
        for first, count in ((0, 1), (1, 2), (3, 4)):
            own += partials(*args, first, count)

    total = len(own)
    got = [[None] * steps for _ in range(total)]
    act, pre_grad, sums = [None] * total, [None] * total, [None] * total
    grad_weight_in = grad_weight_out = None
    base, grad_tokens = None, [None] * GROUPS
    got[0][0] = send(own[0], 1)
    for slot in range(total + steps - 1):
        if slot + 1 < total:
            value = own[slot + 1]
            if slot > 0:
                value = gate(value, got[slot - 1][0])
            got[slot + 1][0] = send(value, 1)
        for step in range(2, steps + 1):
            at = slot - step + 2
            if 0 <= at < total:
                got[at][step - 1] = send(add_bf16(got[at][step - 2], own[at]), step)
        at = slot - steps + 1
        if at < 0:
            continue
        group, chunk = divmod(at, CHUNKS)
        act[at], pre_grad[at], sums[at] = activate([own[at]] + got[at], bias, chunk)
        if chunk == CHUNKS - 2:
            base = back(pre_grad[group * CHUNKS : at + 1], weight_in, 0, None, False)
        if chunk == CHUNKS - 1:
            keep, other = back([pre_grad[at]], weight_in, chunk, base, True)
            pair = add_bf16(keep, swap(other, 1, cols_of))
            half = depth // 2
            pieces = []
            for side, bits in enumerate((chip_bits, chip_bits[::-1])):
                blocks = {
                    2 * key: pair[key * part : (key + 1) * part, side * half : (side + 1) * half]
                    for key in range(cols_of // 2)
                }
                pieces.append(scatter(blocks, bits, cols_of))
            grad_tokens[group] = jnp.concatenate(pieces, axis=1)
        if group == GROUPS - 1 and (chunk % 2 or chunk == CHUNKS - 1):
            count = 2 if chunk % 2 else 1
            first = chunk + 1 - count
            pick = lambda values: [
                [values[g * CHUNKS + first + i] for i in range(count)] for g in range(GROUPS)
            ]
            grad_weight_out = outer(grad, pick(act), grad_weight_out, (hidden, depth), first, count, True)
            grad_weight_in = outer(tok, pick(pre_grad), grad_weight_in, (depth, hidden), first, count, False)

    sums = jnp.concatenate(
        [functools.reduce(jnp.add, sums[chunk::CHUNKS]) for chunk in range(CHUNKS)], axis=1
    ).reshape(hidden)
    for bit in [1 << i for i in range(rows_of.bit_length() - 1)]:
        sums = sums + lax.ppermute(sums, "row", [(i, i ^ bit) for i in range(rows_of)])
    grad_bias = sums * (1.0 / rows_of)
    return (jnp.concatenate(grad_tokens, axis=0), grad_weight_in, grad_bias, grad_weight_out)


def solution(mesh):
    placed = (P("col", "row"), P("row", "col"), P("col"), P("col", "row"), P("col", "row"))
    return jax.shard_map(
        functools.partial(local, mesh.shape["row"], mesh.shape["col"]),
        mesh=mesh,
        in_specs=placed,
        out_specs=(P("col", "row"), P("row", "col"), P("col"), P("col", "row")),
        check_vma=False,
    )
```

time: 517 us -> 398 us (0.77)
  waiting for transfers between devices: 370 us -> 85.3 us
  Pallas kernels: 0 us -> 153 us
  starting transfers between devices: 0.28 us -> 128 us
  matrix products: 86.5 us -> 0 us
  local copies, waits for them, and re-layouts: 28.1 us -> 9.57 us
  between operations: 14.1 us -> 2 us
  other arithmetic: 6.14 us -> 18 us
  blocking collectives: 10.9 us -> 0 us
    reduce_scatter x3 -> x0, waiting for transfers between devices: 237 us -> none  [the longest x1 101 us: local(): lax.psum_scatter(pre_part, 'row', scatter_dimension=0, tiled=True)]
    pallas_call x0 -> x32, Pallas kernels: none -> 153 us  [the longest x8 65.2 us: outer(): call(kernel, 2 * groups * rows * depth * width * count, 2 * groups * rows...]
    all_gather x4 -> x0, waiting for transfers between devices: 131 us -> none  [the longest x1 57 us: local(): lax.all_gather(pre_grad_local, 'row', axis=0, tiled=True)]
    ppermute x0 -> x74, starting transfers between devices: none -> 128 us  [the longest x42 86.6 us: send(): return lax.ppermute(value, 'row', pairs)]
    dot_general x5 -> x0, matrix products: 86.5 us -> none  [the longest x2 37.1 us: contract_rows(): lax.dot_general(left, right, (((0,), (0,)), ((), ())), preferred_element_...]
    ppermute x0 -> x74, waiting for transfers between devices: none -> 85.3 us  [the longest x30 55.2 us: swap(): return lax.ppermute(value, 'col', [(i, i ^ bit) for i in range(size)])]
    unnamed x5 -> x100, local copies, waits for them, and re-layouts: 28.1 us -> 4.07 us
    convert_element_type x1 -> x36, other arithmetic: 2.25 us -> 14.9 us  [the longest x30 14.5 us: add_bf16(): return (left.astype(F32) + right.astype(F32)).astype(BF16)]
  transfers between devices with their start and end apart: 7 -> 74, of which waited for: 6 -> 23; matrix products, arithmetic and copies ran while one was open for 22% -> 5% of each run, Pallas kernels for 0% -> 39%
where the time goes in v1:
time: 398 us; the launch traced here: 395 us
  Pallas kernels  153 us (38%)
  starting transfers between devices  128 us (32%)
  waiting for transfers between devices  85.3 us (21%)
  other arithmetic  18 us (5%)
  local copies, waits for them, and re-layouts  9.57 us (2%)
    ppermute x42, starting transfers between devices, send(): return lax.ppermute(value, 'row', pairs)  86.6 us
    pallas_call x8, Pallas kernels, outer(): call(kernel, 2 * groups * rows * depth * width * count, 2 * groups * rows...  65.2 us
    ppermute x30, waiting for transfers between devices, swap(): return lax.ppermute(value, 'col', [(i, i ^ bit) for i in range(size)])  55.2 us
    pallas_call x6, Pallas kernels, partials(): call(kernel, 4 * rows * depth * width * count, 4 * depth * (rows + width...  42.9 us
    pallas_call x4, Pallas kernels, back(): call(kernel, 2 * rows * depth * width * count, 2 * depth * width * count...  36.1 us
    ppermute x42, waiting for transfers between devices, send(): return lax.ppermute(value, 'row', pairs)  30 us
    ppermute x30, starting transfers between devices, swap(): return lax.ppermute(value, 'col', [(i, i ^ bit) for i in range(size)])  29.3 us
    convert_element_type x30, other arithmetic, add_bf16(): return (left.astype(F32) + right.astype(F32)).astype(BF16)  14.5 us
  transfers between devices with their start and end apart: 74, of which 23 were waited for; matrix products, arithmetic and copies ran while one was open for 5% of the time, Pallas kernels for 39%

profile of v1, /device:TPU:0, one launch (start us, length us, event | category | flops | bytes accessed | tf_op | source)
XLA Modules:
  0.0 395.5 jit_solution(16555363607498970188)
XLA Ops:
  1.8 3.0 collective-permute-start.1
  10.2 5.7 %collective-permute-done = bf16[48,3584]{1,0:T(8,128)(2,1)S(1)} collective-permute-done((bf16[48,3584]{1,0:T(8,128)(2,1)S(1)}, bf16[48,3584]{1,0:T(8,128)(2,1)S(1)}, u32[]{:S(2)}, u32[]{:S(2)}) %collective-permute-start) | collective-permute-done | bytes 344096 | tf_op jit(solution)/shard_map/ppermute | solution.py:181
  17.4 5.9 %collective-permute-done.36 = bf16[48,3584]{1,0:T(8,128)(2,1)S(1)} collective-permute-done((bf16[48,3584]{1,0:T(8,128)(2,1)S(1)}, bf16[48,3584]{1,0:T(8,128)(2,1)S(1)}, u32[]{:S(2)}, u32[]{:S(2)}) %collective-permute-start.36) | collective-permute-done | bytes 344096 | tf_op jit(solution)/shard_map/ppermute | solution.py:181
  23.3 5.8 %collective-permute-done.4 = bf16[48,3584]{1,0:T(8,128)(2,1)S(1)} collective-permute-done((bf16[48,3584]{1,0:T(8,128)(2,1)S(1)}, bf16[48,3584]{1,0:T(8,128)(2,1)S(1)}, u32[]{:S(2)}, u32[]{:S(2)}) %collective-permute-start.4) | collective-permute-done | bytes 344096 | tf_op jit(solution)/shard_map/ppermute | solution.py:181
  31.3 6.5 %collective-permute-done.40 = bf16[48,3584]{1,0:T(8,128)(2,1)S(1)} collective-permute-done((bf16[48,3584]{1,0:T(8,128)(2,1)S(1)}, bf16[48,3584]{1,0:T(8,128)(2,1)S(1)}, u32[]{:S(2)}, u32[]{:S(2)}) %collective-permute-start.40) | collective-permute-done | bytes 344096 | tf_op jit(solution)/shard_map/ppermute | solution.py:181
  40.7 9.1 %collective-permute-done.38 = bf16[48,3584]{1,0:T(8,128)(2,1)S(1)} collective-permute-done((bf16[48,3584]{1,0:T(8,128)(2,1)S(1)}, bf16[48,3584]{1,0:T(8,128)(2,1)S(1)}, u32[]{:S(2)}, u32[]{:S(2)}) %collective-permute-start.38) | collective-permute-done | bytes 344096 | tf_op jit(solution)/shard_map/ppermute | solution.py:181
  50.6 3.0 collective-permute-done.42
  55.7 4.2 %collective-permute-done.7 = bf16[192,3584]{1,0:T(8,128)(2,1)S(1)} collective-permute-done((bf16[192,3584]{1,0:T(8,128)(2,1)S(1)}, bf16[192,3584]{1,0:T(8,128)(2,1)S(1)}, u32[]{:S(2)}, u32[]{:S(2)}) %collective-permute-start.7) | collective-permute-done | bytes 1376288 | tf_op jit(solution)/shard_map/ppermute | solution.py:181
  60.0 4.7 %shard_map.86.refs_0_ = bf16[2,384,256]{2,1,0:T(8,128)(2,1)S(1)} custom-call(bf16[384,3584]{1,0:T(8,128)(2,1)S(1)} %constant_dynamic-update-slice_fusion.tok_ref.refs_0_, bf16[384,3584]{1,0:T(8,128)(2,1)S(1)} %constant_dynamic-update-slice_fusion.5.grad_ref.refs_0_, bf16[3584,1792]{1,0:T(8,128)(2,1)} %refs_1_.3, bf16[1792,3584]{1,0:T(8,128)(2,1)} %wout_ref.11), custom_call_target="tpu_custom_call" | custom-call | flops 1409286144 | bytes 9568256 | tf_op jit(solution)/shard_map/pallas_call | solution.py:45
  64.7 3.0 collective-permute-start.8
  67.7 6.2 %shard_map.85 = (bf16[2,384,256]{2,1,0:T(8,128)(2,1)S(1)}, bf16[2,384,256]{2,1,0:T(8,128)(2,1)S(1)}) custom-call(bf16[384,3584]{1,0:T(8,128)(2,1)S(1)} %constant_dynamic-update-slice_fusion.tok_ref.refs_0_, bf16[384,3584]{1,0:T(8,128)(2,1)} %copy-done.7, bf16[3584,1792]{1,0:T(8,128)(2,1)} %refs_1_.3, bf16[1792,3584]{1,0:T(8,128)(2,1)} %wout_ref.11), custom_call_target="tpu_custom_call" | custom-call | flops 2818572288 | bytes 13631488 | tf_op jit(solution)/shard_map/pallas_call | solution.py:45
  76.7 11.1 %shard_map.84 = (bf16[2,384,256]{2,1,0:T(8,128)(2,1)S(1)}, bf16[2,384,256]{2,1,0:T(8,128)(2,1)S(1)}, bf16[2,384,256]{2,1,0:T(8,128)(2,1)S(1)}, bf16[2,384,256]{2,1,0:T(8,128)(2,1)S(1)}) custom-call(bf16[384,3584]{1,0:T(8,128)(2,1)S(1)} %constant_dynamic-update-slice_fusion.tok_ref.refs_0_, bf16[384,3584]{1,0:T(8,128)(2,1)} %copy-done.7, ...), custom_call_target="tpu_custom_call" | custom-call | flops 5637144576 | bytes 21757952 | tf_op jit(solution)/shard_map/pallas_call | solution.py:45
  90.8 10.1 %shard_map.96 = (bf16[2,384,256]{2,1,0:T(8,128)(2,1)S(1)}, bf16[2,384,256]{2,1,0:T(8,128)(2,1)S(1)}, bf16[2,384,256]{2,1,0:T(8,128)(2,1)S(1)}, bf16[2,384,256]{2,1,0:T(8,128)(2,1)S(1)}) custom-call(bf16[384,3584]{1,0:T(8,128)(2,1)S(1)} %constant_dynamic-update-slice_fusion.10.tok_ref.refs_1_, bf16[384,3584]{1,0:T(8,128)(2,1)} %copy-done, ...), custom_call_target="tpu_custom_call" | custom-call | flops 5637144576 | bytes 21757952 | tf_op jit(solution)/shard_map/pallas_call | solution.py:45
  101.9 7.1 %shard_map.97 = (bf16[2,384,256]{2,1,0:T(8,128)(2,1)S(1)}, bf16[2,384,256]{2,1,0:T(8,128)(2,1)S(1)}) custom-call(bf16[384,3584]{1,0:T(8,128)(2,1)S(1)} %constant_dynamic-update-slice_fusion.10.tok_ref.refs_1_, bf16[384,3584]{1,0:T(8,128)(2,1)} %copy-done, bf16[3584,1792]{1,0:T(8,128)(2,1)} %refs_1_.3, bf16[1792,3584]{1,0:T(8,128)(2,1)} %wout_ref.11), custom_call_target="tpu_custom_call" | custom-call | flops 2818572288 | bytes 13631488 | tf_op jit(solution)/shard_map/pallas_call | solution.py:45
  109.0 3.8 shard_map.98.refs_0_
  112.8 3.3 collective-permute-start.9
  117.0 3.0 collective-permute-start.21
  121.4 4.3 %collective-permute-done.9.refs_1_ = bf16[2,384,256]{2,1,0:T(8,128)(2,1)S(1)} collective-permute-done((bf16[2,384,256]{2,1,0:T(8,128)(2,1)S(1)}, bf16[2,384,256]{2,1,0:T(8,128)(2,1)S(1)}, u32[]{:S(2)}, u32[]{:S(2)}) %collective-permute-start.9) | collective-permute-done | bytes 393248 | tf_op jit(solution)/shard_map/ppermute | solution.py:216
  128.7 4.2 %collective-permute-done.21.refs_1_ = bf16[2,384,256]{2,1,0:T(8,128)(2,1)S(1)} collective-permute-done((bf16[2,384,256]{2,1,0:T(8,128)(2,1)S(1)}, bf16[2,384,256]{2,1,0:T(8,128)(2,1)S(1)}, u32[]{:S(2)}, u32[]{:S(2)}) %collective-permute-start.21) | collective-permute-done | bytes 393248 | tf_op jit(solution)/shard_map/ppermute | solution.py:216
  132.9 4.5 %collective-permute-start.26 = (bf16[2,384,256]{2,1,0:T(8,128)(2,1)S(1)}, bf16[2,384,256]{2,1,0:T(8,128)(2,1)S(1)}, u32[]{:S(2)}, u32[]{:S(2)}) collective-permute-start(bf16[2,384,256]{2,1,0:T(8,128)(2,1)S(1)} %get-tuple-element.90.refs_0_), channel_id=1, source_target_pairs={{0,8},{24,16},{1,9},{25,17},{2,10},{26,18},{3,11},{27,19},{4,12},{... | collective-permute-start | bytes 1179656 | tf_op jit(solution)/shard_map/ppermute | solution.py:216
  138.3 3.0 collective-permute-start.10
  141.4 5.6 %collective-permute-done.26.refs_1_ = bf16[2,384,256]{2,1,0:T(8,128)(2,1)S(1)} collective-permute-done((bf16[2,384,256]{2,1,0:T(8,128)(2,1)S(1)}, bf16[2,384,256]{2,1,0:T(8,128)(2,1)S(1)}, u32[]{:S(2)}, u32[]{:S(2)}) %collective-permute-start.26) | collective-permute-done | bytes 393248 | tf_op jit(solution)/shard_map/ppermute | solution.py:216
  149.9 3.5 collective-permute-done.10.refs_1_
  154.7 4.8 %collective-permute-start.44 = (bf16[2,384,256]{2,1,0:T(8,128)(2,1)S(1)}, bf16[2,384,256]{2,1,0:T(8,128)(2,1)S(1)}, u32[]{:S(2)}, u32[]{:S(2)}) collective-permute-start(bf16[2,384,256]{2,1,0:T(8,128)(2,1)S(1)} %shard_map.98.refs_0_), channel_id=1, source_target_pairs={{0,8},{24,16},{1,9},{25,17},{2,10},{26,18},{3,11},{27,19},{4,12},{... | collective-permute-start | bytes 1179656 | tf_op jit(solution)/shard_map/ppermute | solution.py:216
  161.4 3.0 collective-permute-start.11
  164.4 4.4 %collective-permute-done.44.refs_1_ = bf16[2,384,256]{2,1,0:T(8,128)(2,1)S(1)} collective-permute-done((bf16[2,384,256]{2,1,0:T(8,128)(2,1)S(1)}, bf16[2,384,256]{2,1,0:T(8,128)(2,1)S(1)}, u32[]{:S(2)}, u32[]{:S(2)}) %collective-permute-start.44) | collective-permute-done | bytes 393248 | tf_op jit(solution)/shard_map/ppermute | solution.py:216
  170.9 3.2 collective-permute-done.11.refs_1_
  174.8 6.1 %collective-permute-start.45 = (bf16[2,384,256]{2,1,0:T(8,128)(2,1)S(1)}, bf16[2,384,256]{2,1,0:T(8,128)(2,1)S(1)}, u32[]{:S(2)}, u32[]{:S(2)}) collective-permute-start(bf16[2,384,256]{2,1,0:T(8,128)(2,1)S(1)} %get-tuple-element.98.refs_0_), channel_id=1, source_target_pairs={{0,8},{24,16},{1,9},{25,17},{2,10},{26,18},{3,11},{27,19},{4,12},{... | collective-permute-start | bytes 1179656 | tf_op jit(solution)/shard_map/ppermute | solution.py:216
  185.6 7.4 %collective-permute-start.52 = (bf16[2,384,256]{2,1,0:T(8,128)(2,1)S(1)}, bf16[2,384,256]{2,1,0:T(8,128)(2,1)S(1)}, u32[]{:S(2)}, u32[]{:S(2)}) collective-permute-start(bf16[2,384,256]{2,1,0:T(8,128)(2,1)S(1)} %get-tuple-element.104.refs_0_), channel_id=1, source_target_pairs={{0,8},{24,16},{1,9},{25,17},{2,10},{26,18},{3,11},{27,19},{4,12},{... | collective-permute-start | bytes 1179656 | tf_op jit(solution)/shard_map/ppermute | solution.py:216
  201.6 7.6 %collective-permute-start.57 = (bf16[2,384,256]{2,1,0:T(8,128)(2,1)S(1)}, bf16[2,384,256]{2,1,0:T(8,128)(2,1)S(1)}, u32[]{:S(2)}, u32[]{:S(2)}) collective-permute-start(bf16[2,384,256]{2,1,0:T(8,128)(2,1)S(1)} %get-tuple-element.108.refs_0_), channel_id=1, source_target_pairs={{0,8},{24,16},{1,9},{25,17},{2,10},{26,18},{3,11},{27,19},{4,12},{... | collective-permute-start | bytes 1179656 | tf_op jit(solution)/shard_map/ppermute | solution.py:216
  209.8 10.7 %shard_map.94.refs_2_ = f32[384,3584]{1,0:T(8,128)} custom-call(bf16[384,256]{1,0:T(8,128)(2,1)S(1)} %get-tuple-element.81.refs_0_.refs_2_, bf16[384,256]{1,0:T(8,128)(2,1)S(1)} %get-tuple-element.83.refs_1_.refs_3_, bf16[384,256]{1,0:T(8,128)(2,1)S(1)} %get-tuple-element.84.refs_2_, bf16[384,256]{1,0:T(8,128)(2,1)S(1)} %get-tuple-element.87.refs_3_, ...), custom_call_target="tpu_custom_call" | custom-call | flops 4227858432 | bytes 16515072 | tf_op jit(solution)/shard_map/pallas_call | solution.py:168
  227.9 6.2 %collective-permute-start.62 = (bf16[2,384,256]{2,1,0:T(8,128)(2,1)S(1)}, bf16[2,384,256]{2,1,0:T(8,128)(2,1)S(1)}, u32[]{:S(2)}, u32[]{:S(2)}) collective-permute-start(bf16[2,384,256]{2,1,0:T(8,128)(2,1)S(1)} %get-tuple-element.112.refs_0_), channel_id=1, source_target_pairs={{0,8},{24,16},{1,9},{25,17},{2,10},{26,18},{3,11},{27,19},{4,12},{... | collective-permute-start | bytes 1179656 | tf_op jit(solution)/shard_map/ppermute | solution.py:216
  235.9 7.4 %shard_map.95 = (bf16[192,3584]{1,0:T(8,128)(2,1)S(1)}, bf16[192,3584]{1,0:T(8,128)(2,1)}) custom-call(bf16[384,256]{1,0:T(8,128)(2,1)S(1)} %get-tuple-element.80.refs_0_.refs_2_, bf16[3584,1792]{1,0:T(8,128)(2,1)} %refs_1_.3, f32[384,3584]{1,0:T(8,128)} %shard_map.94.refs_2_), custom_call_target="tpu_custom_call" | custom-call | flops 704643072 | bytes 7340032 | tf_op jit(solution)/shard_map/pallas_call | solution.py:168
  243.3 4.1 %collective-permute-start.47 = (bf16[2,384,256]{2,1,0:T(8,128)(2,1)S(1)}, bf16[2,384,256]{2,1,0:T(8,128)(2,1)S(1)}, u32[]{:S(2)}, u32[]{:S(2)}) collective-permute-start(bf16[2,384,256]{2,1,0:T(8,128)(2,1)S(1)} %get-tuple-element.100.refs_0_), channel_id=1, source_target_pairs={{0,8},{24,16},{1,9},{25,17},{2,10},{26,18},{3,11},{27,19},{4,12},{... | collective-permute-start | bytes 1179656 | tf_op jit(solution)/shard_map/ppermute | solution.py:216
  251.1 9.2 %shard_map.108.refs_6_ = f32[3584,1792]{1,0:T(8,128)} custom-call(bf16[384,3584]{1,0:T(8,128)(2,1)S(1)} %constant_dynamic-update-slice_fusion.tok_ref.refs_0_, bf16[384,3584]{1,0:T(8,128)(2,1)} %copy-done.3, bf16[384,256]{1,0:T(8,128)(2,1)S(1)} %get-tuple-element.81.refs_0_.refs_2_, bf16[384,256]{1,0:T(8,128)(2,1)S(1)} %get-tuple-element.83.refs_1_.refs_3_, ...), custom_call_target="tpu_custom_call" | custom-call | flops 2818572288 | bytes 12845056 | tf_op jit(solution)/shard_map/pallas_call | solution.py:130
  262.5 9.0 %shard_map.112.refs_6_ = f32[1792,3584]{1,0:T(8,128)} custom-call(bf16[384,3584]{1,0:T(8,128)(2,1)S(1)} %copy-done.8, bf16[384,3584]{1,0:T(8,128)(2,1)} %copy-done, bf16[384,256]{1,0:T(8,128)(2,1)S(1)} %get-tuple-element.140.refs_2_, bf16[384,256]{1,0:T(8,128)(2,1)S(1)} %get-tuple-element.141.refs_3_, bf16[384,256]{1,0:T(8,128)(2,1)S(1)} %get-tuple-element.142.refs_4_, ...), custom_call_target="tpu_custom_call" | custom-call | flops 2818572288 | bytes 12845056 | tf_op jit(solution)/shard_map/pallas_call | solution.py:130
  277.5 9.2 %shard_map.109.refs_6_ = f32[3584,1792]{1,0:T(8,128)} custom-call(bf16[384,3584]{1,0:T(8,128)(2,1)S(1)} %constant_dynamic-update-slice_fusion.tok_ref.refs_0_, bf16[384,3584]{1,0:T(8,128)(2,1)} %copy-done.3, bf16[384,256]{1,0:T(8,128)(2,1)S(1)} %get-tuple-element.84.refs_2_, bf16[384,256]{1,0:T(8,128)(2,1)S(1)} %copy-done.22, ...), custom_call_target="tpu_custom_call", output_to_operand_aliasing={{}: (6, {})} | custom-call | flops 2818572288 | bytes 12845056 | tf_op jit(solution)/shard_map/pallas_call | solution.py:130
  286.6 8.9 %shard_map.113.refs_6_ = f32[1792,3584]{1,0:T(8,128)} custom-call(bf16[384,3584]{1,0:T(8,128)(2,1)S(1)} %copy-done.8, bf16[384,3584]{1,0:T(8,128)(2,1)} %copy-done, bf16[384,256]{1,0:T(8,128)(2,1)S(1)} %copy-done.34, bf16[384,256]{1,0:T(8,128)(2,1)S(1)} %copy-done.36, ...), custom_call_target="tpu_custom_call", output_to_operand_aliasing={{}: (6, {})} | custom-call | flops 2818572288 | bytes 12845056 | tf_op jit(solution)/shard_map/pallas_call | solution.py:130
  301.2 11.0 %collective-permute-start.72 = (f32[1792]{0:T(1024)S(1)}, f32[1792]{0:T(1024)S(1)}, u32[]{:S(2)}, u32[]{:S(2)}) collective-permute-start(f32[1792]{0:T(1024)S(1)} %reduce), channel_id=1, source_target_pairs={{0,8},{8,0},{16,24},{24,16},{1,9},{9,1},{17,25},{25,17},{2,10},{10... | collective-permute-start | bytes 21512 | tf_op jit(solution)/shard_map/ppermute | solution.py:279
  312.2 10.6 %shard_map.106.refs_2_ = f32[384,3584]{1,0:T(8,128)} custom-call(bf16[384,256]{1,0:T(8,128)(2,1)S(1)} %copy-done.26, bf16[384,256]{1,0:T(8,128)(2,1)S(1)} %copy-done.28, bf16[384,256]{1,0:T(8,128)(2,1)S(1)} %get-tuple-element.106.refs_2_.refs_4_, bf16[384,256]{1,0:T(8,128)(2,1)S(1)} %get-tuple-element.109.refs_3_.refs_5_, ...), custom_call_target="tpu_custom_call" | custom-call | flops 4227858432 | bytes 16515072 | tf_op jit(solution)/shard_map/pallas_call | solution.py:168
  322.8 7.4 %shard_map.107 = (bf16[192,3584]{1,0:T(8,128)(2,1)S(1)}, bf16[192,3584]{1,0:T(8,128)(2,1)}) custom-call(bf16[384,256]{1,0:T(8,128)(2,1)S(1)} %get-tuple-element.101.refs_0_.refs_3_, bf16[3584,1792]{1,0:T(8,128)(2,1)} %refs_1_.3, f32[384,3584]{1,0:T(8,128)} %shard_map.106.refs_2_), custom_call_target="tpu_custom_call" | custom-call | flops 704643072 | bytes 7340032 | tf_op jit(solution)/shard_map/pallas_call | solution.py:168
  330.4 9.2 %shard_map.110.refs_4_ = f32[3584,1792]{1,0:T(8,128)} custom-call(bf16[384,3584]{1,0:T(8,128)(2,1)S(1)} %copy-done.6, bf16[384,3584]{1,0:T(8,128)(2,1)} %copy-done.3, bf16[384,256]{1,0:T(8,128)(2,1)S(1)} %copy-done.20, bf16[384,256]{1,0:T(8,128)(2,1)S(1)} %get-tuple-element.91.refs_5_.refs_3_, ...), custom_call_target="tpu_custom_call", output_to_operand_aliasing={{}: (6, {})} | custom-call | flops 2818572288 | bytes 12845056 | tf_op jit(solution)/shard_map/pallas_call | solution.py:130
  339.6 9.1 %shard_map.114.refs_4_ = f32[1792,3584]{1,0:T(8,128)} custom-call(bf16[384,3584]{1,0:T(8,128)(2,1)S(1)} %copy-done.9, bf16[384,3584]{1,0:T(8,128)(2,1)} %copy-done, bf16[384,256]{1,0:T(8,128)(2,1)S(1)} %copy-done.32, bf16[384,256]{1,0:T(8,128)(2,1)S(1)} %copy-done.30, ...), custom_call_target="tpu_custom_call", output_to_operand_aliasing={{}: (6, {})} | custom-call | flops 2818572288 | bytes 12845056 | tf_op jit(solution)/shard_map/pallas_call | solution.py:130
  348.8 5.3 %shard_map.111 = f32[3584,1792]{1,0:T(8,128)} custom-call(bf16[384,3584]{1,0:T(8,128)(2,1)S(1)} %copy-done.6, bf16[384,3584]{1,0:T(8,128)(2,1)S(1)} %copy-done.4, bf16[384,256]{1,0:T(8,128)(2,1)S(1)} %copy-done.24, bf16[384,256]{1,0:T(8,128)(2,1)S(1)} %get-tuple-element.101.refs_0_.refs_3_, ...), custom_call_target="tpu_custom_call", output_to_operand_aliasing={{}: (4, {})} | custom-call | flops 1409286144 | bytes 9175040 | tf_op jit(solution)/shard_map/pallas_call | solution.py:130
  355.2 5.2 %shard_map.115 = f32[1792,3584]{1,0:T(8,128)} custom-call(bf16[384,3584]{1,0:T(8,128)(2,1)S(1)} %copy-done.10, bf16[384,3584]{1,0:T(8,128)(2,1)S(1)} %copy-done.2, bf16[384,256]{1,0:T(8,128)(2,1)S(1)} %copy-done.38, bf16[384,256]{1,0:T(8,128)(2,1)S(1)} %copy-done.40, f32[1792,3584]{1,0:T(8,128)} %shard_map.114.refs_4_), custom_call_target="tpu_custom_call", output_to_operand_aliasing={{}: (4, {})} | custom-call | flops 1409286144 | bytes 9175040 | tf_op jit(solution)/shard_map/pallas_call | solution.py:130
  370.2 3.6 collective-permute-done.31
  385.5 3.4 collective-permute-done.68
  390.8 3.7 collective-permute-done.71
  (292 shorter events, 103.4 us)
Async XLA Ops:
  1.8 38.0 %collective-permute-start.1 = (bf16[48,3584]{1,0:T(8,128)(2,1)S(1)}, bf16[48,3584]{1,0:T(8,128)(2,1)S(1)}, u32[]{:S(2)}, u32[]{:S(2)}) collective-permute-start(bf16[48,3584]{1,0:T(8,128)(2,1)S(1)} %get-tuple-element.160), channel_id=1, source_target_pairs={{0,4},{1,5},{2,6},{3,7},{4,0},{5,1},{6,2},{7,3},{8,12},{9,13},{10,... | collective-permute-start | bytes 1032200 | tf_op jit(solution)/shard_map/ppermute | solution.py:181
  6.4 34.3 %collective-permute-start.37 = (bf16[48,3584]{1,0:T(8,128)(2,1)S(1)}, bf16[48,3584]{1,0:T(8,128)(2,1)S(1)}, u32[]{:S(2)}, u32[]{:S(2)}) collective-permute-start(bf16[48,3584]{1,0:T(8,128)(2,1)S(1)} %get-tuple-element.163), channel_id=1, source_target_pairs={{0,4},{1,5},{2,6},{3,7},{4,0},{5,1},{6,2},{7,3},{8,12},{9,13},{10,... | collective-permute-start | bytes 1032200 | tf_op jit(solution)/shard_map/ppermute | solution.py:181
  6.9 16.4 %collective-permute-start.36 = (bf16[48,3584]{1,0:T(8,128)(2,1)S(1)}, bf16[48,3584]{1,0:T(8,128)(2,1)S(1)}, u32[]{:S(2)}, u32[]{:S(2)}) collective-permute-start(bf16[48,3584]{1,0:T(8,128)(2,1)S(1)} %get-tuple-element.163), channel_id=1, source_target_pairs={{0,2},{1,3},{2,0},{3,1},{4,6},{5,7},{6,4},{7,5},{8,10},{9,11},{10,... | collective-permute-start | bytes 1032200 | tf_op jit(solution)/shard_map/ppermute | solution.py:181
  8.1 22.5 %collective-permute-start.5 = (bf16[48,3584]{1,0:T(8,128)(2,1)S(1)}, bf16[48,3584]{1,0:T(8,128)(2,1)S(1)}, u32[]{:S(2)}, u32[]{:S(2)}) collective-permute-start(bf16[48,3584]{1,0:T(8,128)(2,1)S(1)} %get-tuple-element.156), channel_id=1, source_target_pairs={{0,4},{1,5},{2,6},{3,7},{4,0},{5,1},{6,2},{7,3},{8,12},{9,13},{10,... | collective-permute-start | bytes 1032200 | tf_op jit(solution)/shard_map/ppermute | solution.py:181
  15.9 13.3 %collective-permute-start.4 = (bf16[48,3584]{1,0:T(8,128)(2,1)S(1)}, bf16[48,3584]{1,0:T(8,128)(2,1)S(1)}, u32[]{:S(2)}, u32[]{:S(2)}) collective-permute-start(bf16[48,3584]{1,0:T(8,128)(2,1)S(1)} %get-tuple-element.156), channel_id=1, source_target_pairs={{0,2},{1,3},{2,0},{3,1},{4,6},{5,7},{6,4},{7,5},{8,10},{9,11},{10,... | collective-permute-start | bytes 1032200 | tf_op jit(solution)/shard_map/ppermute | solution.py:181
  23.2 15.2 %collective-permute-start.41 = (bf16[48,3584]{1,0:T(8,128)(2,1)S(1)}, bf16[48,3584]{1,0:T(8,128)(2,1)S(1)}, u32[]{:S(2)}, u32[]{:S(2)}) collective-permute-start(bf16[48,3584]{1,0:T(8,128)(2,1)S(1)} %get-tuple-element.159), channel_id=1, source_target_pairs={{0,4},{1,5},{2,6},{3,7},{4,0},{5,1},{6,2},{7,3},{8,12},{9,13},{10,... | collective-permute-start | bytes 1032200 | tf_op jit(solution)/shard_map/ppermute | solution.py:181
  30.7 19.3 %collective-permute-start.2 = (bf16[48,3584]{1,0:T(8,128)(2,1)S(1)}, bf16[48,3584]{1,0:T(8,128)(2,1)S(1)}, u32[]{:S(2)}, u32[]{:S(2)}) collective-permute-start(bf16[48,3584]{1,0:T(8,128)(2,1)S(1)} %collective-permute-done), channel_id=1, source_target_pairs={{0,4},{1,5},{2,6},{3,7},{4,0},{5,1},{6,2},{7,3},{8,12},{9,13},{10,... | collective-permute-start | bytes 1032200 | tf_op jit(solution)/shard_map/ppermute | solution.py:181
  38.5 16.3 %collective-permute-start.6 = (bf16[48,3584]{1,0:T(8,128)(2,1)S(1)}, bf16[48,3584]{1,0:T(8,128)(2,1)S(1)}, u32[]{:S(2)}, u32[]{:S(2)}) collective-permute-start(bf16[48,3584]{1,0:T(8,128)(2,1)S(1)} %collective-permute-done.5), channel_id=1, source_target_pairs={{0,2},{1,3},{2,0},{3,1},{4,6},{5,7},{6,4},{7,5},{8,10},{9,11},{10,... | collective-permute-start | bytes 1032200 | tf_op jit(solution)/shard_map/ppermute | solution.py:181
  39.9 13.7 %collective-permute-start.42 = (bf16[48,3584]{1,0:T(8,128)(2,1)S(1)}, bf16[48,3584]{1,0:T(8,128)(2,1)S(1)}, u32[]{:S(2)}, u32[]{:S(2)}) collective-permute-start(bf16[48,3584]{1,0:T(8,128)(2,1)S(1)} %collective-permute-done.41), channel_id=1, source_target_pairs={{0,2},{1,3},{2,0},{3,1},{4,6},{5,7},{6,4},{7,5},{8,10},{9,11},{10,... | collective-permute-start | bytes 1032200 | tf_op jit(solution)/shard_map/ppermute | solution.py:181
  49.9 25.4 %collective-permute-start.39 = (bf16[192,3584]{1,0:T(8,128)(2,1)S(1)}, bf16[192,3584]{1,0:T(8,128)(2,1)}, u32[]{:S(2)}, u32[]{:S(2)}) collective-permute-start(bf16[192,3584]{1,0:T(8,128)(2,1)S(1)} %pad_maximum_fusion.2), channel_id=1, source_target_pairs={{0,1},{1,0},{2,3},{3,2},{4,5},{5,4},{6,7},{7,6},{8,9},{9,8},{10,11... | collective-permute-start | bytes 4128776 | tf_op jit(solution)/shard_map/ppermute | solution.py:181
  54.8 33.0 %collective-permute-start.43 = (bf16[192,3584]{1,0:T(8,128)(2,1)}, bf16[192,3584]{1,0:T(8,128)(2,1)}, u32[]{:S(2)}, u32[]{:S(2)}) collective-permute-start(bf16[192,3584]{1,0:T(8,128)(2,1)} %pad_maximum_fusion.3), channel_id=1, source_target_pairs={{0,1},{1,0},{2,3},{3,2},{4,5},{5,4},{6,7},{7,6},{8,9},{9,8},{10,11... | collective-permute-start | bytes 4128776 | tf_op jit(solution)/shard_map/ppermute | solution.py:181
  64.7 36.2 %collective-permute-start.8 = (bf16[2,384,256]{2,1,0:T(8,128)(2,1)S(1)}, bf16[2,384,256]{2,1,0:T(8,128)(2,1)S(1)}, u32[]{:S(2)}, u32[]{:S(2)}) collective-permute-start(bf16[2,384,256]{2,1,0:T(8,128)(2,1)S(1)} %shard_map.86.refs_0_), channel_id=1, source_target_pairs={{0,8},{24,16},{1,9},{25,17},{2,10},{26,18},{3,11},{27,19},{4,12},{... | collective-permute-start | bytes 1179656 | tf_op jit(solution)/shard_map/ppermute | solution.py:216
  73.9 42.2 %collective-permute-start.16 = (bf16[2,384,256]{2,1,0:T(8,128)(2,1)S(1)}, bf16[2,384,256]{2,1,0:T(8,128)(2,1)S(1)}, u32[]{:S(2)}, u32[]{:S(2)}) collective-permute-start(bf16[2,384,256]{2,1,0:T(8,128)(2,1)S(1)} %get-tuple-element.82.refs_0_), channel_id=1, source_target_pairs={{0,8},{24,16},{1,9},{25,17},{2,10},{26,18},{3,11},{27,19},{4,12},{... | collective-permute-start | bytes 1179656 | tf_op jit(solution)/shard_map/ppermute | solution.py:216
  101.0 18.9 %collective-permute-start.14 = (bf16[2,384,256]{2,1,0:T(8,128)(2,1)S(1)}, bf16[2,384,256]{2,1,0:T(8,128)(2,1)S(1)}, u32[]{:S(2)}, u32[]{:S(2)}) collective-permute-start(bf16[2,384,256]{2,1,0:T(8,128)(2,1)S(1)} %fusion.2), channel_id=1, source_target_pairs={{8,16},{16,8},{9,17},{17,9},{10,18},{18,10},{11,19},{19,11},{12,20... | collective-permute-start | bytes 1179656 | tf_op jit(solution)/shard_map/ppermute | solution.py:216
  117.0 16.0 %collective-permute-start.21 = (bf16[2,384,256]{2,1,0:T(8,128)(2,1)S(1)}, bf16[2,384,256]{2,1,0:T(8,128)(2,1)S(1)}, u32[]{:S(2)}, u32[]{:S(2)}) collective-permute-start(bf16[2,384,256]{2,1,0:T(8,128)(2,1)S(1)} %get-tuple-element.86.refs_0_), channel_id=1, source_target_pairs={{0,8},{24,16},{1,9},{25,17},{2,10},{26,18},{3,11},{27,19},{4,12},{... | collective-permute-start | bytes 1179656 | tf_op jit(solution)/shard_map/ppermute | solution.py:216
  120.1 34.6 %collective-permute-start.15 = (bf16[2,384,256]{2,1,0:T(8,128)(2,1)S(1)}, bf16[2,384,256]{2,1,0:T(8,128)(2,1)S(1)}, u32[]{:S(2)}, u32[]{:S(2)}) collective-permute-start(bf16[2,384,256]{2,1,0:T(8,128)(2,1)S(1)} %fusion.3), channel_id=1, source_target_pairs={{16,24},{8,0},{17,25},{9,1},{18,26},{10,2},{19,27},{11,3},{20,28},... | collective-permute-start | bytes 1179656 | tf_op jit(solution)/shard_map/ppermute | solution.py:216
  127.4 32.7 %collective-permute-start.18 = (bf16[2,384,256]{2,1,0:T(8,128)(2,1)}, bf16[2,384,256]{2,1,0:T(8,128)(2,1)S(1)}, u32[]{:S(2)}, u32[]{:S(2)}) collective-permute-start(bf16[2,384,256]{2,1,0:T(8,128)(2,1)} %fusion.5), channel_id=1, source_target_pairs={{16,24},{8,0},{17,25},{9,1},{18,26},{10,2},{19,27},{11,3},{20,28},... | collective-permute-start | bytes 1179656 | tf_op jit(solution)/shard_map/ppermute | solution.py:216
  132.9 14.1 %collective-permute-start.26 = (bf16[2,384,256]{2,1,0:T(8,128)(2,1)S(1)}, bf16[2,384,256]{2,1,0:T(8,128)(2,1)S(1)}, u32[]{:S(2)}, u32[]{:S(2)}) collective-permute-start(bf16[2,384,256]{2,1,0:T(8,128)(2,1)S(1)} %get-tuple-element.90.refs_0_), channel_id=1, source_target_pairs={{0,8},{24,16},{1,9},{25,17},{2,10},{26,18},{3,11},{27,19},{4,12},{... | collective-permute-start | bytes 1179656 | tf_op jit(solution)/shard_map/ppermute | solution.py:216
  138.3 15.1 %collective-permute-start.10 = (bf16[2,384,256]{2,1,0:T(8,128)(2,1)S(1)}, bf16[2,384,256]{2,1,0:T(8,128)(2,1)S(1)}, u32[]{:S(2)}, u32[]{:S(2)}) collective-permute-start(bf16[2,384,256]{2,1,0:T(8,128)(2,1)S(1)} %get-tuple-element.78.refs_0_), channel_id=1, source_target_pairs={{0,8},{24,16},{1,9},{25,17},{2,10},{26,18},{3,11},{27,19},{4,12},{... | collective-permute-start | bytes 1179656 | tf_op jit(solution)/shard_map/ppermute | solution.py:216
  147.0 34.7 %collective-permute-start.20 = (bf16[2,384,256]{2,1,0:T(8,128)(2,1)S(1)}, bf16[2,384,256]{2,1,0:T(8,128)(2,1)S(1)}, u32[]{:S(2)}, u32[]{:S(2)}) collective-permute-start(bf16[2,384,256]{2,1,0:T(8,128)(2,1)S(1)} %fusion.7), channel_id=1, source_target_pairs={{16,24},{8,0},{17,25},{9,1},{18,26},{10,2},{19,27},{11,3},{20,28},... | collective-permute-start | bytes 1179656 | tf_op jit(solution)/shard_map/ppermute | solution.py:216
  153.4 30.3 %collective-permute-start.23 = (bf16[2,384,256]{2,1,0:T(8,128)(2,1)S(1)}, bf16[2,384,256]{2,1,0:T(8,128)(2,1)S(1)}, u32[]{:S(2)}, u32[]{:S(2)}) collective-permute-start(bf16[2,384,256]{2,1,0:T(8,128)(2,1)S(1)} %fusion.9), channel_id=1, source_target_pairs={{16,24},{8,0},{17,25},{9,1},{18,26},{10,2},{19,27},{11,3},{20,28},... | collective-permute-start | bytes 1179656 | tf_op jit(solution)/shard_map/ppermute | solution.py:216
  154.7 14.1 %collective-permute-start.44 = (bf16[2,384,256]{2,1,0:T(8,128)(2,1)S(1)}, bf16[2,384,256]{2,1,0:T(8,128)(2,1)S(1)}, u32[]{:S(2)}, u32[]{:S(2)}) collective-permute-start(bf16[2,384,256]{2,1,0:T(8,128)(2,1)S(1)} %shard_map.98.refs_0_), channel_id=1, source_target_pairs={{0,8},{24,16},{1,9},{25,17},{2,10},{26,18},{3,11},{27,19},{4,12},{... | collective-permute-start | bytes 1179656 | tf_op jit(solution)/shard_map/ppermute | solution.py:216
  160.1 14.7 %collective-permute-start.24 = (bf16[2,384,256]{2,1,0:T(8,128)(2,1)S(1)}, bf16[2,384,256]{2,1,0:T(8,128)(2,1)S(1)}, u32[]{:S(2)}, u32[]{:S(2)}) collective-permute-start(bf16[2,384,256]{2,1,0:T(8,128)(2,1)S(1)} %fusion.10), channel_id=1, source_target_pairs={{8,16},{16,8},{9,17},{17,9},{10,18},{18,10},{11,19},{19,11},{12,20... | collective-permute-start | bytes 1179656 | tf_op jit(solution)/shard_map/ppermute | solution.py:216
  168.8 31.6 %collective-permute-start.28 = (bf16[2,384,256]{2,1,0:T(8,128)(2,1)S(1)}, bf16[2,384,256]{2,1,0:T(8,128)(2,1)S(1)}, u32[]{:S(2)}, u32[]{:S(2)}) collective-permute-start(bf16[2,384,256]{2,1,0:T(8,128)(2,1)S(1)} %fusion.13), channel_id=1, source_target_pairs={{16,24},{8,0},{17,25},{9,1},{18,26},{10,2},{19,27},{11,3},{20,28},... | collective-permute-start | bytes 1179656 | tf_op jit(solution)/shard_map/ppermute | solution.py:216
  174.8 19.0 %collective-permute-start.45 = (bf16[2,384,256]{2,1,0:T(8,128)(2,1)S(1)}, bf16[2,384,256]{2,1,0:T(8,128)(2,1)S(1)}, u32[]{:S(2)}, u32[]{:S(2)}) collective-permute-start(bf16[2,384,256]{2,1,0:T(8,128)(2,1)S(1)} %get-tuple-element.98.refs_0_), channel_id=1, source_target_pairs={{0,8},{24,16},{1,9},{25,17},{2,10},{26,18},{3,11},{27,19},{4,12},{... | collective-permute-start | bytes 1179656 | tf_op jit(solution)/shard_map/ppermute | solution.py:216
  181.7 19.9 %collective-permute-start.25 = (bf16[2,384,256]{2,1,0:T(8,128)(2,1)}, bf16[2,384,256]{2,1,0:T(8,128)(2,1)S(1)}, u32[]{:S(2)}, u32[]{:S(2)}) collective-permute-start(bf16[2,384,256]{2,1,0:T(8,128)(2,1)} %fusion.11), channel_id=1, source_target_pairs={{16,24},{8,0},{17,25},{9,1},{18,26},{10,2},{19,27},{11,3},{20,28},... | collective-permute-start | bytes 1179656 | tf_op jit(solution)/shard_map/ppermute | solution.py:216
  193.8 34.0 %collective-permute-start.51 = (bf16[2,384,256]{2,1,0:T(8,128)(2,1)}, bf16[2,384,256]{2,1,0:T(8,128)(2,1)S(1)}, u32[]{:S(2)}, u32[]{:S(2)}) collective-permute-start(bf16[2,384,256]{2,1,0:T(8,128)(2,1)} %fusion.17), channel_id=1, source_target_pairs={{16,24},{8,0},{17,25},{9,1},{18,26},{10,2},{19,27},{11,3},{20,28},... | collective-permute-start | bytes 1179656 | tf_op jit(solution)/shard_map/ppermute | solution.py:216
  196.0 24.5 %collective-permute-start.55 = (bf16[2,384,256]{2,1,0:T(8,128)(2,1)}, bf16[2,384,256]{2,1,0:T(8,128)(2,1)S(1)}, u32[]{:S(2)}, u32[]{:S(2)}) collective-permute-start(bf16[2,384,256]{2,1,0:T(8,128)(2,1)} %fusion.20), channel_id=1, source_target_pairs={{8,16},{16,8},{9,17},{17,9},{10,18},{18,10},{11,19},{19,11},{12,20... | collective-permute-start | bytes 1179656 | tf_op jit(solution)/shard_map/ppermute | solution.py:216
  198.2 36.4 %collective-permute-start.13 = (bf16[2,384,256]{2,1,0:T(8,128)(2,1)S(1)}, bf16[2,384,256]{2,1,0:T(8,128)(2,1)S(1)}, u32[]{:S(2)}, u32[]{:S(2)}) collective-permute-start(bf16[2,384,256]{2,1,0:T(8,128)(2,1)S(1)} %fusion.1), channel_id=1, source_target_pairs={{16,24},{8,0},{17,25},{9,1},{18,26},{10,2},{19,27},{11,3},{20,28},... | collective-permute-start | bytes 1179656 | tf_op jit(solution)/shard_map/ppermute | solution.py:216
  200.4 22.3 %collective-permute-start.53 = (bf16[2,384,256]{2,1,0:T(8,128)(2,1)}, bf16[2,384,256]{2,1,0:T(8,128)(2,1)S(1)}, u32[]{:S(2)}, u32[]{:S(2)}) collective-permute-start(bf16[2,384,256]{2,1,0:T(8,128)(2,1)} %fusion.18), channel_id=1, source_target_pairs={{8,16},{16,8},{9,17},{17,9},{10,18},{18,10},{11,19},{19,11},{12,20... | collective-permute-start | bytes 1179656 | tf_op jit(solution)/shard_map/ppermute | solution.py:216
  201.6 23.3 %collective-permute-start.57 = (bf16[2,384,256]{2,1,0:T(8,128)(2,1)S(1)}, bf16[2,384,256]{2,1,0:T(8,128)(2,1)S(1)}, u32[]{:S(2)}, u32[]{:S(2)}) collective-permute-start(bf16[2,384,256]{2,1,0:T(8,128)(2,1)S(1)} %get-tuple-element.108.refs_0_), channel_id=1, source_target_pairs={{0,8},{24,16},{1,9},{25,17},{2,10},{26,18},{3,11},{27,19},{4,12},{... | collective-permute-start | bytes 1179656 | tf_op jit(solution)/shard_map/ppermute | solution.py:216
  222.7 48.7 %collective-permute-start.56 = (bf16[2,384,256]{2,1,0:T(8,128)(2,1)}, bf16[2,384,256]{2,1,0:T(8,128)(2,1)}, u32[]{:S(2)}, u32[]{:S(2)}) collective-permute-start(bf16[2,384,256]{2,1,0:T(8,128)(2,1)} %fusion.21), channel_id=1, source_target_pairs={{16,24},{8,0},{17,25},{9,1},{18,26},{10,2},{19,27},{11,3},{20,28},... | collective-permute-start | bytes 1179656 | tf_op jit(solution)/shard_map/ppermute | solution.py:216
  224.9 18.5 %collective-permute-start.54 = (bf16[2,384,256]{2,1,0:T(8,128)(2,1)}, bf16[2,384,256]{2,1,0:T(8,128)(2,1)S(1)}, u32[]{:S(2)}, u32[]{:S(2)}) collective-permute-start(bf16[2,384,256]{2,1,0:T(8,128)(2,1)} %fusion.19), channel_id=1, source_target_pairs={{16,24},{8,0},{17,25},{9,1},{18,26},{10,2},{19,27},{11,3},{20,28},... | collective-permute-start | bytes 1179656 | tf_op jit(solution)/shard_map/ppermute | solution.py:216
  227.1 20.9 %collective-permute-start.58 = (bf16[2,384,256]{2,1,0:T(8,128)(2,1)S(1)}, bf16[2,384,256]{2,1,0:T(8,128)(2,1)S(1)}, u32[]{:S(2)}, u32[]{:S(2)}) collective-permute-start(bf16[2,384,256]{2,1,0:T(8,128)(2,1)S(1)} %fusion.22), channel_id=1, source_target_pairs={{8,16},{16,8},{9,17},{17,9},{10,18},{18,10},{11,19},{19,11},{12,20... | collective-permute-start | bytes 1179656 | tf_op jit(solution)/shard_map/ppermute | solution.py:216
  227.9 20.3 %collective-permute-start.62 = (bf16[2,384,256]{2,1,0:T(8,128)(2,1)S(1)}, bf16[2,384,256]{2,1,0:T(8,128)(2,1)S(1)}, u32[]{:S(2)}, u32[]{:S(2)}) collective-permute-start(bf16[2,384,256]{2,1,0:T(8,128)(2,1)S(1)} %get-tuple-element.112.refs_0_), channel_id=1, source_target_pairs={{0,8},{24,16},{1,9},{25,17},{2,10},{26,18},{3,11},{27,19},{4,12},{... | collective-permute-start | bytes 1179656 | tf_op jit(solution)/shard_map/ppermute | solution.py:216
  234.7 15.7 %collective-permute-start.60 = (bf16[2,384,256]{2,1,0:T(8,128)(2,1)S(1)}, bf16[2,384,256]{2,1,0:T(8,128)(2,1)S(1)}, u32[]{:S(2)}, u32[]{:S(2)}) collective-permute-start(bf16[2,384,256]{2,1,0:T(8,128)(2,1)S(1)} %fusion.24), channel_id=1, source_target_pairs={{8,16},{16,8},{9,17},{17,9},{10,18},{18,10},{11,19},{19,11},{12,20... | collective-permute-start | bytes 1179656 | tf_op jit(solution)/shard_map/ppermute | solution.py:216
  243.3 17.0 %collective-permute-start.47 = (bf16[2,384,256]{2,1,0:T(8,128)(2,1)S(1)}, bf16[2,384,256]{2,1,0:T(8,128)(2,1)S(1)}, u32[]{:S(2)}, u32[]{:S(2)}) collective-permute-start(bf16[2,384,256]{2,1,0:T(8,128)(2,1)S(1)} %get-tuple-element.100.refs_0_), channel_id=1, source_target_pairs={{0,8},{24,16},{1,9},{25,17},{2,10},{26,18},{3,11},{27,19},{4,12},{... | collective-permute-start | bytes 1179656 | tf_op jit(solution)/shard_map/ppermute | solution.py:216
  248.0 113.0 %collective-permute-start.29 = (bf16[192,3584]{1,0:T(8,128)(2,1)}, bf16[192,3584]{1,0:T(8,128)(2,1)}, u32[]{:S(2)}, u32[]{:S(2)}) collective-permute-start(bf16[192,3584]{1,0:T(8,128)(2,1)} %get-tuple-element.93), channel_id=1, source_target_pairs={{0,1},{1,0},{2,3},{3,2},{4,5},{5,4},{6,7},{7,6},{8,9},{9,8},{10,11... | collective-permute-start | bytes 4128776 | tf_op jit(solution)/shard_map/ppermute | solution.py:181
  248.2 28.7 %collective-permute-start.59 = (bf16[2,384,256]{2,1,0:T(8,128)(2,1)S(1)}, bf16[2,384,256]{2,1,0:T(8,128)(2,1)S(1)}, u32[]{:S(2)}, u32[]{:S(2)}) collective-permute-start(bf16[2,384,256]{2,1,0:T(8,128)(2,1)S(1)} %fusion.23), channel_id=1, source_target_pairs={{16,24},{8,0},{17,25},{9,1},{18,26},{10,2},{19,27},{11,3},{20,28},... | collective-permute-start | bytes 1179656 | tf_op jit(solution)/shard_map/ppermute | solution.py:216
  250.3 23.7 %collective-permute-start.63 = (bf16[2,384,256]{2,1,0:T(8,128)(2,1)}, bf16[2,384,256]{2,1,0:T(8,128)(2,1)S(1)}, u32[]{:S(2)}, u32[]{:S(2)}) collective-permute-start(bf16[2,384,256]{2,1,0:T(8,128)(2,1)} %fusion.26), channel_id=1, source_target_pairs={{8,16},{16,8},{9,17},{17,9},{10,18},{18,10},{11,19},{19,11},{12,20... | collective-permute-start | bytes 1179656 | tf_op jit(solution)/shard_map/ppermute | solution.py:216
  260.3 35.2 %collective-permute-start.61 = (bf16[2,384,256]{2,1,0:T(8,128)(2,1)S(1)}, bf16[2,384,256]{2,1,0:T(8,128)(2,1)S(1)}, u32[]{:S(2)}, u32[]{:S(2)}) collective-permute-start(bf16[2,384,256]{2,1,0:T(8,128)(2,1)S(1)} %fusion.25), channel_id=1, source_target_pairs={{16,24},{8,0},{17,25},{9,1},{18,26},{10,2},{19,27},{11,3},{20,28},... | collective-permute-start | bytes 1179656 | tf_op jit(solution)/shard_map/ppermute | solution.py:216
  274.2 22.0 %collective-permute-start.64 = (bf16[2,384,256]{2,1,0:T(8,128)(2,1)S(1)}, bf16[2,384,256]{2,1,0:T(8,128)(2,1)S(1)}, u32[]{:S(2)}, u32[]{:S(2)}) collective-permute-start(bf16[2,384,256]{2,1,0:T(8,128)(2,1)S(1)} %fusion.27), channel_id=1, source_target_pairs={{16,24},{8,0},{17,25},{9,1},{18,26},{10,2},{19,27},{11,3},{20,28},... | collective-permute-start | bytes 1179656 | tf_op jit(solution)/shard_map/ppermute | solution.py:216
  275.6 24.4 %collective-permute-start.49 = (bf16[2,384,256]{2,1,0:T(8,128)(2,1)S(1)}, bf16[2,384,256]{2,1,0:T(8,128)(2,1)S(1)}, u32[]{:S(2)}, u32[]{:S(2)}) collective-permute-start(bf16[2,384,256]{2,1,0:T(8,128)(2,1)S(1)} %fusion.15), channel_id=1, source_target_pairs={{16,24},{8,0},{17,25},{9,1},{18,26},{10,2},{19,27},{11,3},{20,28},... | collective-permute-start | bytes 1179656 | tf_op jit(solution)/shard_map/ppermute | solution.py:216
  301.2 52.9 %collective-permute-start.72 = (f32[1792]{0:T(1024)S(1)}, f32[1792]{0:T(1024)S(1)}, u32[]{:S(2)}, u32[]{:S(2)}) collective-permute-start(f32[1792]{0:T(1024)S(1)} %reduce), channel_id=1, source_target_pairs={{0,8},{8,0},{16,24},{24,16},{1,9},{9,1},{17,25},{25,17},{2,10},{10... | collective-permute-start | bytes 21512 | tf_op jit(solution)/shard_map/ppermute | solution.py:279
  330.3 36.7 %collective-permute-start.65 = (bf16[192,3584]{1,0:T(8,128)(2,1)}, bf16[192,3584]{1,0:T(8,128)(2,1)}, u32[]{:S(2)}, u32[]{:S(2)}) collective-permute-start(bf16[192,3584]{1,0:T(8,128)(2,1)} %get-tuple-element.115), channel_id=1, source_target_pairs={{0,1},{1,0},{2,3},{3,2},{4,5},{5,4},{6,7},{7,6},{8,9},{9,8},{10,11... | collective-permute-start | bytes 4128776 | tf_op jit(solution)/shard_map/ppermute | solution.py:181
  362.9 15.3 %collective-permute-start.30 = (bf16[48,1792]{1,0:T(8,128)(2,1)S(1)}, bf16[48,1792]{1,0:T(8,128)(2,1)S(1)}, u32[]{:S(2)}, u32[]{:S(2)}) collective-permute-start(bf16[48,1792]{1,0:T(8,128)(2,1)S(1)} %get-tuple-element.146), channel_id=1, source_target_pairs={{0,2},{1,3},{2,0},{3,1},{4,6},{5,7},{6,4},{7,5},{8,10},{9,11},{10,... | collective-permute-start | bytes 516104 | tf_op jit(solution)/shard_map/ppermute | solution.py:181
  364.4 15.3 %collective-permute-start.34 = (bf16[48,1792]{1,0:T(8,128)(2,1)S(1)}, bf16[48,1792]{1,0:T(8,128)(2,1)S(1)}, u32[]{:S(2)}, u32[]{:S(2)}) collective-permute-start(bf16[48,1792]{1,0:T(8,128)(2,1)S(1)} %get-tuple-element.147), channel_id=1, source_target_pairs={{0,4},{1,5},{2,6},{3,7},{4,0},{5,1},{6,2},{7,3},{8,12},{9,13},{10,... | collective-permute-start | bytes 516104 | tf_op jit(solution)/shard_map/ppermute | solution.py:181
  365.9 24.1 %collective-permute-start.33 = (bf16[48,1792]{1,0:T(8,128)(2,1)S(1)}, bf16[48,1792]{1,0:T(8,128)(2,1)S(1)}, u32[]{:S(2)}, u32[]{:S(2)}) collective-permute-start(bf16[48,1792]{1,0:T(8,128)(2,1)S(1)} %get-tuple-element.148), channel_id=1, source_target_pairs={{0,4},{1,5},{2,6},{3,7},{4,0},{5,1},{6,2},{7,3},{8,12},{9,13},{10,... | collective-permute-start | bytes 516104 | tf_op jit(solution)/shard_map/ppermute | solution.py:181
  (70 other events, 1039.8 us)

commit v2 on v0

v2 whole, which is shorter than its diff:
```python
import functools

import jax
import jax.numpy as jnp
from jax import lax
from jax.experimental import pallas as pl
from jax.experimental.pallas import tpu as pltpu
from jax.sharding import PartitionSpec as P

GELU_SCALE = 0.7978845608
GELU_CUBIC = 0.044715
F32, BF16 = jnp.float32, jnp.bfloat16
VMEM_LIMIT = 24 * 1024 * 1024
HALVES, UNITS, SPLIT, TILE = 2, 7, (4, 3), 512


def dot(left, right, dims):
    return lax.dot_general(left, right, ((dims[:1], dims[1:]), ((), ())), preferred_element_type=F32)


def call(kernel, flops, moved, **kwargs):
    return pl.pallas_call(
        kernel,
        compiler_params=pltpu.CompilerParams(vmem_limit_bytes=VMEM_LIMIT),
        cost_estimate=pl.CostEstimate(flops=flops, bytes_accessed=moved, transcendentals=0),
        **kwargs,
    )


def pick_tile(size):
    return TILE if size % TILE == 0 else size


def partial_sums(rows, weight, first, count, transposed):
    tokens, depth = rows.shape
    hidden = weight.shape[0 if transposed else 1]
    width = hidden // UNITS

    def kernel(rows_ref, weight_ref, out_ref):
        out_ref[...] = dot(rows_ref[...], weight_ref[...], (1, 1) if transposed else (1, 0)).astype(BF16)

    if transposed:
        weight_spec = pl.BlockSpec((width, depth), lambda i: (first + i, 0))
    else:
        weight_spec = pl.BlockSpec((depth, width), lambda i: (0, first + i))
    return call(
        kernel,
        2 * tokens * depth * width * count,
        2 * (tokens * depth + depth * width * count + tokens * width * count),
        grid=(count,),
        in_specs=[
            pl.BlockSpec((tokens, depth), lambda i: (0, 0), pipeline_mode=pl.Buffered(1)),
            weight_spec,
        ],
        out_specs=pl.BlockSpec((tokens, width), lambda i: (0, i)),
        out_shape=jax.ShapeDtypeStruct((tokens, width * count), BF16),
    )(rows, weight)


def activate(terms, bias, first, count):
    rows, columns = terms[0].shape
    width = columns // count

    def kernel(bias_ref, *refs):
        ins, (act_ref, slope_ref) = refs[:-2], refs[-2:]
        pre = functools.reduce(jnp.add, [ref[...].astype(F32) for ref in ins]) + bias_ref[...]
        tangent = jnp.tanh(GELU_SCALE * (pre + GELU_CUBIC * pre * pre * pre))
        act_ref[...] = (0.5 * pre * (1.0 + tangent)).astype(BF16)
        slope_ref[...] = 0.5 * (1.0 + tangent) + 0.5 * pre * (1.0 - tangent * tangent) * GELU_SCALE * (
            1.0 + 3.0 * GELU_CUBIC * pre * pre
        )

    block = pl.BlockSpec((rows, width), lambda i: (0, i))
    return call(
        kernel,
        30 * rows * columns,
        rows * columns * (2 * len(terms) + 6),
        grid=(count,),
        in_specs=[pl.BlockSpec((1, width), lambda i: (0, first + i))] + [block] * len(terms),
        out_specs=[block] * 2,
        out_shape=[jax.ShapeDtypeStruct((rows, columns), kind) for kind in (BF16, F32)],
    )(bias, *terms)


def differentiate(terms, slope, count):
    rows, columns = slope.shape
    width = columns // count

    def kernel(slope_ref, *refs):
        ins, (grad_ref, sum_ref) = refs[:-2], refs[-2:]
        grad = functools.reduce(jnp.add, [ref[...].astype(F32) for ref in ins]) * slope_ref[...]
        grad = grad.astype(BF16)
        grad_ref[...] = grad
        sum_ref[...] = jnp.sum(grad.astype(F32), axis=0, keepdims=True)

    block = pl.BlockSpec((rows, width), lambda i: (0, i))
    return call(
        kernel,
        8 * rows * columns,
        rows * columns * (2 * len(terms) + 6),
        grid=(count,),
        in_specs=[block] * (1 + len(terms)),
        out_specs=[block, pl.BlockSpec((1, width), lambda i: (0, i))],
        out_shape=[
            jax.ShapeDtypeStruct((rows, columns), BF16),
            jax.ShapeDtypeStruct((1, columns), F32),
        ],
    )(slope, *terms)


def add_bf16(left, right):
    return (left.astype(F32) + right.astype(F32)).astype(BF16)


def weight_out_grad(acts, grads, into, hidden, first, count):
    rows, depth = grads[0].shape
    width = hidden // UNITS
    tile = pick_tile(depth)

    def kernel(*refs):
        acts, grads, out = refs[:HALVES], refs[HALVES : 2 * HALVES], refs[-1]
        turned = [act[...].T for act in acts]
        for at in range(0, depth, tile):
            terms = [dot(act, grad[:, at : at + tile], (1, 0)) for act, grad in zip(turned, grads)]
            out[:, at : at + tile] = functools.reduce(jnp.add, terms)

    operands = [*acts, *grads]
    specs = [pl.BlockSpec((rows, width), lambda i: (0, i))] * HALVES
    specs += [pl.BlockSpec((rows, depth), lambda i: (0, 0), pipeline_mode=pl.Buffered(1))] * HALVES
    aliases = {}
    if into is not None:
        aliases = {len(operands): 0}
        operands.append(into)
        specs.append(pl.BlockSpec(memory_space=pl.ANY))
    return call(
        kernel,
        2 * HALVES * rows * depth * width * count,
        2 * HALVES * rows * depth + 4 * depth * width * count,
        grid=(count,),
        in_specs=specs,
        out_specs=pl.BlockSpec((width, depth), lambda i: (first + i, 0)),
        out_shape=jax.ShapeDtypeStruct((hidden, depth), F32),
        input_output_aliases=aliases,
    )(*operands)


def weight_in_grad(toks, grads):
    rows, depth = toks[0].shape
    hidden = sum(piece.shape[1] for piece in grads[0])
    pieces = len(grads[0])
    tile = pick_tile(depth)

    def kernel(*refs):
        toks, parts, out = refs[:HALVES], refs[HALVES:-1], refs[-1]
        turned = [tok[...].T for tok in toks]
        at = 0
        for piece in range(pieces):
            width = parts[piece].shape[1]
            terms = [dot(turned[half], parts[half * pieces + piece][...], (1, 0)) for half in range(HALVES)]
            out[:, at : at + width] = functools.reduce(jnp.add, terms)
            at += width

    flat = [piece for half in grads for piece in half]
    return call(
        kernel,
        2 * HALVES * rows * depth * hidden,
        2 * HALVES * rows * (depth + hidden) + 4 * depth * hidden,
        grid=(depth // tile,),
        in_specs=[pl.BlockSpec((rows, tile), lambda j: (0, j))] * HALVES
        + [pl.BlockSpec(piece.shape, lambda j: (0, 0), pipeline_mode=pl.Buffered(1)) for piece in flat],
        out_specs=pl.BlockSpec((tile, hidden), lambda j: (j, 0)),
        out_shape=jax.ShapeDtypeStruct((depth, hidden), F32),
    )(*toks, *flat)


def token_grad(grads, weight_in):
    rows = grads[0].shape[0]
    depth, hidden = weight_in.shape
    tile = pick_tile(depth)

    def kernel(*refs):
        parts, weight, out = refs[:-2], refs[-2], refs[-1]
        at, terms = 0, []
        for part in parts:
            width = part.shape[1]
            terms.append(dot(part[...], weight[:, at : at + width], (1, 1)))
            at += width
        out[...] = functools.reduce(jnp.add, terms).astype(BF16)

    return call(
        kernel,
        2 * rows * depth * hidden,
        2 * (rows * depth + depth * hidden + rows * hidden),
        grid=(depth // tile,),
        in_specs=[pl.BlockSpec(grad.shape, lambda j: (0, 0), pipeline_mode=pl.Buffered(1)) for grad in grads]
        + [pl.BlockSpec((tile, hidden), lambda j: (j, 0))],
        out_specs=pl.BlockSpec((rows, tile), lambda j: (0, j)),
        out_shape=jax.ShapeDtypeStruct((rows, depth), BF16),
    )(*grads, weight_in)


def after(value, *deps):
    return lax.optimization_barrier((value, *deps))[0]


def local(rows_of, tokens, weight_in, bias_hidden, weight_out, out_grad):
    mine, depth = tokens.shape
    hidden = bias_hidden.shape[0]
    part = mine // HALVES
    bias = bias_hidden.reshape(1, hidden)
    steps = rows_of - 1
    starts = [sum(SPLIT[:i]) for i in range(len(SPLIT))]
    cuts = len(SPLIT)
    parts = 2 * HALVES
    total = parts * cuts

    def send(value, step):
        pairs = [(step - 1, step), (rows_of - step, rows_of - step - 1)]
        return lax.ppermute(value, "row", pairs)

    gathered = []
    for source in (tokens, out_grad):
        for half in range(HALVES):
            block = source[half * part : (half + 1) * part]
            if gathered:
                block = after(block, gathered[-1])
            gathered.append(lax.all_gather(block, "col", axis=0, tiled=True))
    toks, grads = gathered[:HALVES], gathered[HALVES:]

    chain = []

    def link(value):
        return after(value, chain[-1]) if chain else value

    own = [None] * total
    got = [[None] * steps for _ in range(total)]
    act, slope, pre_grad, sums = ([[None] * cuts for _ in range(HALVES)] for _ in range(4))
    held = {}

    def compute_own(at):
        where, cut = divmod(at, cuts)
        weight = weight_in if where < HALVES else weight_out
        own[at] = partial_sums(link(gathered[where]), weight, starts[cut], SPLIT[cut], where >= HALVES)
        chain.append(own[at])

    def forward(at, step):
        payload = add_bf16(got[at][step - 2], link(own[at]))
        chain.append(payload)
        got[at][step - 1] = send(payload, step)

    def finish(at):
        where, cut = divmod(at, cuts)
        half = where % HALVES
        terms = [link(own[at])] + got[at]
        if where < HALVES:
            act[half][cut], slope[half][cut] = activate(terms, bias, starts[cut], SPLIT[cut])
            chain.append(act[half][cut])
        else:
            pre_grad[half][cut], sums[half][cut] = differentiate(terms, slope[half][cut], SPLIT[cut])
            chain.append(pre_grad[half][cut])

    def out_rows(cut):
        acts = [link(act[half][cut]) for half in range(HALVES)]
        held["out"] = weight_out_grad(acts, grads, held.get("out"), hidden, starts[cut], SPLIT[cut])
        chain.append(held["out"])

    def tokens_of(half):
        part_sum = token_grad([link(piece) for piece in pre_grad[half]], weight_in)
        chain.append(part_sum)
        held[half] = lax.psum_scatter(part_sum, "col", scatter_dimension=0, tiled=True)

    def has(values):
        return all(value is not None for value in values)

    later = [(functools.partial(compute_own, at), lambda: True) for at in range(2, total)]
    later += [(functools.partial(tokens_of, 0), lambda: has(pre_grad[0]))]
    for cut in range(cuts):
        later.insert(-1 if cut == 0 else len(later), (functools.partial(out_rows, cut), lambda cut=cut: has(a[cut] for a in act)))
    compute_own(0)
    got[0][0] = send(own[0], 1)
    compute_own(1)
    for slot in range(total + steps - 1):
        if slot + 1 < total:
            got[slot + 1][0] = send(link(own[slot + 1]), 1)
        for step in range(2, steps + 1):
            if 0 <= slot - step + 2 < total:
                forward(slot - step + 2, step)
        if slot >= steps - 1:
            finish(slot - steps + 1)
        if later and later[0][1]():
            later.pop(0)[0]()
    for work, _ in later:
        work()
    for half in range(1, HALVES):
        tokens_of(half)
    grad_weight_in = weight_in_grad(toks, [[link(piece) for piece in half] for half in pre_grad])
    grad_weight_out = held["out"]
    grad_tokens = [held[half] for half in range(HALVES)]
    sums = jnp.concatenate(
        [functools.reduce(jnp.add, [sums[half][cut] for half in range(HALVES)]) for cut in range(cuts)], axis=1
    ).reshape(hidden)
    for bit in [1 << i for i in range(rows_of.bit_length() - 1)]:
        sums = sums + lax.ppermute(sums, "row", [(i, i ^ bit) for i in range(rows_of)])
    grad_bias = sums * (1.0 / rows_of)
    return (jnp.concatenate(grad_tokens, axis=0), grad_weight_in, grad_bias, grad_weight_out)


def solution(mesh):
    placed = (P("col", "row"), P("row", "col"), P("col"), P("col", "row"), P("col", "row"))
    return jax.shard_map(
        functools.partial(local, mesh.shape["row"]),
        mesh=mesh,
        in_specs=placed,
        out_specs=(P("col", "row"), P("row", "col"), P("col"), P("col", "row")),
        check_vma=False,
    )
```

time: 517 us -> 389 us (0.75)
  waiting for transfers between devices: 370 us -> 156 us
  Pallas kernels: 0 us -> 92.8 us
  matrix products: 86.5 us -> 0 us
  starting transfers between devices: 0.28 us -> 64.3 us
  local copies, waits for them, and re-layouts: 28.1 us -> 43.8 us
  blocking collectives: 10.9 us -> 0 us
  other arithmetic: 6.14 us -> 14.3 us
    reduce_scatter x3 -> x2, waiting for transfers between devices: 237 us -> 18 us  [tokens_of(): lax.psum_scatter(part_sum, 'col', scatter_dimension=0, tiled=True)]
    pallas_call x0 -> x21, Pallas kernels: none -> 92.8 us  [the longest x8 28 us: partial_sums(): call(kernel, 2 * tokens * depth * width * count, 2 * (tokens * depth + de...]
    dot_general x5 -> x0, matrix products: 86.5 us -> none  [the longest x2 37.1 us: contract_rows(): lax.dot_general(left, right, (((0,), (0,)), ((), ())), preferred_element_...]
    ppermute x0 -> x26, starting transfers between devices: none -> 64 us  [the longest x24 63.7 us: send(): return lax.ppermute(value, 'row', pairs)]
    ppermute x0 -> x26, waiting for transfers between devices: none -> 38.6 us  [the longest x24 34.9 us: send(): return lax.ppermute(value, 'row', pairs)]
    all_gather x4, waiting for transfers between devices: 131 us -> 99.8 us  [local(): gathered.append(lax.all_gather(block, 'col', axis=0, tiled=True))]
    unnamed x5 -> x180, local copies, waits for them, and re-layouts: 28.1 us -> 40.8 us
    psum x1 -> x0, blocking collectives: 10.9 us -> none  [local(): grad_bias = lax.psum(bias_local, 'row')]
  transfers between devices with their start and end apart: 7 -> 32, of which waited for: 6 -> 9; matrix products, arithmetic and copies ran while one was open for 22% -> 3% of each run, Pallas kernels for 0% -> 22%
where the time goes in v2:
time: 389 us; the launch traced here: 387 us
  waiting for transfers between devices  156 us (40%)
  Pallas kernels  92.8 us (24%)
  starting transfers between devices  64.3 us (17%)
  local copies, waits for them, and re-layouts  43.8 us (11%)
  between operations  15.5 us (4%)
  other arithmetic  14.3 us (4%)
    all_gather x4, waiting for transfers between devices, local(): gathered.append(lax.all_gather(block, 'col', axis=0, tiled=True))  99.8 us
    ppermute x24, starting transfers between devices, send(): return lax.ppermute(value, 'row', pairs)  63.7 us
    unnamed x180, local copies, waits for them, and re-layouts  40.8 us
    ppermute x24, waiting for transfers between devices, send(): return lax.ppermute(value, 'row', pairs)  34.9 us
    pallas_call x8, Pallas kernels, partial_sums(): call(kernel, 2 * tokens * depth * width * count, 2 * (tokens * depth + de...  28 us
    pallas_call x2, Pallas kernels, weight_out_grad(): call(kernel, 2 * HALVES * rows * depth * width * count, 2 * HALVES * rows...  18.7 us
    reduce_scatter x2, waiting for transfers between devices, tokens_of(): lax.psum_scatter(part_sum, 'col', scatter_dimension=0, tiled=True)  18 us
    pallas_call x1, Pallas kernels, weight_in_grad(): call(kernel, 2 * HALVES * rows * depth * hidden, 2 * HALVES * rows * (dep...  17 us
  transfers between devices with their start and end apart: 32, of which 9 were waited for; matrix products, arithmetic and copies ran while one was open for 3% of the time, Pallas kernels for 22%

profile of v2, /device:TPU:0, one launch (start us, length us, event | category | flops | bytes accessed | tf_op | source)
XLA Modules:
  0.0 387.2 jit_solution(16319118869915415684)
XLA Ops:
  7.2 2.0 fusion.1
  9.3 34.5 %all-gather.5.cloned.1.call-done.rows_ref.refs_0_ = bf16[384,3584]{1,0:T(8,128)(2,1)} async-done(((bf16[48,3584]{1,0:T(8,128)(2,1)}), bf16[384,3584]{1,0:T(8,128)(2,1)}) %all-gather.5.cloned.1.call-update) | async-done | bytes 2752528 | tf_op jit(solution)/shard_map/all_gather | solution.py:227
  44.8 32.2 %all-gather.7.cloned.1.call-done.rows_ref.refs_1_ = bf16[384,3584]{1,0:T(8,128)(2,1)} async-done(((bf16[48,3584]{1,0:T(8,128)(2,1)}), bf16[384,3584]{1,0:T(8,128)(2,1)}) %all-gather.7.cloned.1.call-update) | async-done | bytes 2752528 | tf_op jit(solution)/shard_map/all_gather | solution.py:227
  77.1 33.1 %all-gather.9.cloned.1.call-done.rows_ref.refs_2_ = bf16[384,3584]{1,0:T(8,128)(2,1)} async-done(((bf16[48,3584]{1,0:T(8,128)(2,1)}), bf16[384,3584]{1,0:T(8,128)(2,1)}) %all-gather.9.cloned.1.call-update) | async-done | bytes 2752528 | tf_op jit(solution)/shard_map/all_gather | solution.py:227
  110.3 4.6 %copy-done.1 = bf16[3584,1792]{1,0:T(8,128)(2,1)S(1)} copy-done((bf16[3584,1792]{1,0:T(8,128)(2,1)S(1)}, bf16[3584,1792]{1,0:T(8,128)(2,1)}, u32[]{:S(2)}) %copy-start.1) | copy-done | bytes 12845080
  114.9 1.8 copy-done.15
  116.7 4.1 %shard_map.84.refs_0_ = bf16[384,1024]{1,0:T(8,128)(2,1)S(1)} custom-call(bf16[384,3584]{1,0:T(8,128)(2,1)S(1)} %copy-done.15, bf16[3584,1792]{1,0:T(8,128)(2,1)S(1)} %copy-done.1), custom_call_target="tpu_custom_call" | custom-call | flops 2818572288 | bytes 10878976 | tf_op jit(solution)/shard_map/pallas_call | solution.py:46
  120.8 3.7 collective-permute-start.1
  124.6 3.1 shard_map.85.refs_0_
  129.0 13.4 %collective-permute-done.1.refs_1_ = bf16[384,1024]{1,0:T(8,128)(2,1)S(1)} collective-permute-done((bf16[384,1024]{1,0:T(8,128)(2,1)S(1)}, bf16[384,1024]{1,0:T(8,128)(2,1)S(1)}, u32[]{:S(2)}, u32[]{:S(2)}) %collective-permute-start.1) | collective-permute-done | bytes 786464 | tf_op jit(solution)/shard_map/ppermute | solution.py:219
  144.0 1.8 copy-done.17
  145.8 4.1 %shard_map.86.refs_0_ = bf16[384,1024]{1,0:T(8,128)(2,1)S(1)} custom-call(bf16[384,3584]{1,0:T(8,128)(2,1)S(1)} %copy-done.17, bf16[3584,1792]{1,0:T(8,128)(2,1)S(1)} %bitcast.5), custom_call_target="tpu_custom_call" | custom-call | flops 2818572288 | bytes 10878976 | tf_op jit(solution)/shard_map/pallas_call | solution.py:46
  149.9 7.1 %collective-permute-start.3 = (bf16[384,1024]{1,0:T(8,128)(2,1)S(1)}, bf16[384,1024]{1,0:T(8,128)(2,1)S(1)}, u32[]{:S(2)}, u32[]{:S(2)}) collective-permute-start(bf16[384,1024]{1,0:T(8,128)(2,1)S(1)} %shard_map.86.refs_0_), channel_id=1, source_target_pairs={{0,8},{24,16},{1,9},{25,17},{2,10},{26,18},{3,11},{27,19},{4,12},{... | collective-permute-start | bytes 2359304 | tf_op jit(solution)/shard_map/ppermute | solution.py:219
  159.8 4.6 %copy-done.2 = bf16[3584,1792]{1,0:T(8,128)(2,1)S(1)} copy-done((bf16[3584,1792]{1,0:T(8,128)(2,1)S(1)}, bf16[3584,1792]{1,0:T(8,128)(2,1)}, u32[]{:S(2)}) %copy-start.2) | copy-done | bytes 12845080
  164.4 3.1 shard_map.87.refs_0_
  167.6 12.3 %collective-permute-start.7 = (bf16[384,768]{1,0:T(8,128)(2,1)S(1)}, bf16[384,768]{1,0:T(8,128)(2,1)S(1)}, u32[]{:S(2)}, u32[]{:S(2)}) collective-permute-start(bf16[384,768]{1,0:T(8,128)(2,1)S(1)} %shard_map.87.refs_0_), channel_id=1, source_target_pairs={{0,8},{24,16},{1,9},{25,17},{2,10},{26,18},{3,11},{27,19},{4,12},{... | collective-permute-start | bytes 1769480 | tf_op jit(solution)/shard_map/ppermute | solution.py:219
  181.0 1.6 collective-permute-start.8
  182.6 2.3 collective-permute-done.5.refs_3_
  184.9 2.2 shard_map.88
  188.0 3.7 shard_map.89.refs_0_
  191.8 2.4 collective-permute-start.11
  196.9 1.5 shard_map.90
  199.4 3.4 shard_map.91.refs_0_
  202.8 7.1 %collective-permute-start.9 = (bf16[384,768]{1,0:T(8,128)(2,1)}, bf16[384,768]{1,0:T(8,128)(2,1)}, u32[]{:S(2)}, u32[]{:S(2)}) collective-permute-start(bf16[384,768]{1,0:T(8,128)(2,1)} %shard_map.91.refs_0_), channel_id=1, source_target_pairs={{0,8},{24,16},{1,9},{25,17},{2,10},{26,18},{3,11},{27,19},{4,12},{... | collective-permute-start | bytes 1769480 | tf_op jit(solution)/shard_map/ppermute | solution.py:219
  211.1 1.6 collective-permute-start.15
  215.1 2.2 shard_map.92
  219.4 4.6 %copy-done = bf16[1792,3584]{1,0:T(8,128)(2,1)S(1)} copy-done((bf16[1792,3584]{1,0:T(8,128)(2,1)S(1)}, bf16[1792,3584]{1,0:T(8,128)(2,1)}, u32[]{:S(2)}) %copy-start) | copy-done | bytes 12845080
  224.0 1.8 copy-done.4
  225.8 3.7 shard_map.93.refs_0_
  229.6 7.0 %collective-permute-start.14 = (bf16[384,1024]{1,0:T(8,128)(2,1)S(1)}, bf16[384,1024]{1,0:T(8,128)(2,1)S(1)}, u32[]{:S(2)}, u32[]{:S(2)}) collective-permute-start(bf16[384,1024]{1,0:T(8,128)(2,1)S(1)} %shard_map.93.refs_0_), channel_id=1, source_target_pairs={{0,8},{24,16},{1,9},{25,17},{2,10},{26,18},{3,11},{27,19},{4,12},{... | collective-permute-start | bytes 2359304 | tf_op jit(solution)/shard_map/ppermute | solution.py:219
  241.9 2.8 shard_map.94
  244.8 2.8 shard_map.95.refs_0_
  247.6 4.9 %collective-permute-start.19 = (bf16[384,768]{1,0:T(8,128)(2,1)S(1)}, bf16[384,768]{1,0:T(8,128)(2,1)S(1)}, u32[]{:S(2)}, u32[]{:S(2)}) collective-permute-start(bf16[384,768]{1,0:T(8,128)(2,1)S(1)} %shard_map.95.refs_0_), channel_id=1, source_target_pairs={{0,8},{24,16},{1,9},{25,17},{2,10},{26,18},{3,11},{27,19},{4,12},{... | collective-permute-start | bytes 1769480 | tf_op jit(solution)/shard_map/ppermute | solution.py:219
  256.3 3.5 collective-permute-done.17.refs_3_
  259.7 2.8 shard_map.96
  262.6 10.5 %shard_map.97.refs_4_ = f32[1792,3584]{1,0:T(8,128)} custom-call(bf16[384,1024]{1,0:T(8,128)(2,1)S(1)} %copy-done.53, bf16[384,1024]{1,0:T(8,128)(2,1)S(1)} %copy-done.55, bf16[384,3584]{1,0:T(8,128)(2,1)S(1)} %copy-done.3, bf16[384,3584]{1,0:T(8,128)(2,1)S(1)} %copy-done.4), custom_call_target="tpu_custom_call" | custom-call | flops 5637144576 | bytes 20185088 | tf_op jit(solution)/shard_map/pallas_call | solution.py:135
  275.9 2.5 shard_map.98
  278.4 6.5 %shard_map.99 = bf16[384,3584]{1,0:T(8,128)(2,1)S(1)} custom-call(bf16[384,1024]{1,0:T(8,128)(2,1)S(1)} %get-tuple-element.134.refs_0_.refs_2_, bf16[384,768]{1,0:T(8,128)(2,1)S(1)} %get-tuple-element.135.refs_1_.refs_3_, bf16[3584,1792]{1,0:T(8,128)(2,1)S(1)} %bitcast.7), custom_call_target="tpu_custom_call" | custom-call | flops 4932501504 | bytes 16973824 | tf_op jit(solution)/shard_map/pallas_call | solution.py:190
  284.9 1.6 copy-done.34
  292.1 15.7 %collective-permute-done.22.refs_3_ = bf16[384,1024]{1,0:T(8,128)(2,1)S(1)} collective-permute-done((bf16[384,1024]{1,0:T(8,128)(2,1)}, bf16[384,1024]{1,0:T(8,128)(2,1)S(1)}, u32[]{:S(2)}, u32[]{:S(2)}) %collective-permute-start.22) | collective-permute-done | bytes 786464 | tf_op jit(solution)/shard_map/ppermute | solution.py:219
  314.3 8.2 %shard_map.101 = f32[1792,3584]{1,0:T(8,128)} custom-call(bf16[384,768]{1,0:T(8,128)(2,1)S(1)} %copy-done.57, bf16[384,768]{1,0:T(8,128)(2,1)S(1)} %copy-done.59, bf16[384,3584]{1,0:T(8,128)(2,1)S(1)} %copy-done.3, bf16[384,3584]{1,0:T(8,128)(2,1)S(1)} %copy-done.5, f32[1792,3584]{1,0:T(8,128)} %shard_map.97.refs_4_), custom_call_target="tpu_custom_call", output_to_operand_aliasing={{}: (4, {})} | custom-call | flops 4227858432 | bytes 16515072 | tf_op jit(solution)/shard_map/pallas_call | solution.py:135
  323.4 6.5 %shard_map.103 = bf16[384,3584]{1,0:T(8,128)(2,1)S(1)} custom-call(bf16[384,1024]{1,0:T(8,128)(2,1)S(1)} %get-tuple-element.136.refs_0_.refs_4_, bf16[384,768]{1,0:T(8,128)(2,1)S(1)} %get-tuple-element.137.refs_1_.refs_5_, bf16[3584,1792]{1,0:T(8,128)(2,1)S(1)} %bitcast.9), custom_call_target="tpu_custom_call" | custom-call | flops 4932501504 | bytes 16973824 | tf_op jit(solution)/shard_map/pallas_call | solution.py:190
  330.0 1.6 copy-done.35
  332.6 3.6 collective-permute-done.24
  336.5 1.8 copy-done.19
  342.8 17.0 %shard_map.104 = f32[3584,1792]{1,0:T(8,128)} custom-call(bf16[384,3584]{1,0:T(8,128)(2,1)S(1)} %copy-done.16, bf16[384,3584]{1,0:T(8,128)(2,1)S(1)} %copy-done.19, bf16[384,1024]{1,0:T(8,128)(2,1)S(1)} %copy-done.61, bf16[384,768]{1,0:T(8,128)(2,1)S(1)} %copy-done.65, bf16[384,1024]{1,0:T(8,128)(2,1)S(1)} %copy-done.63, bf16[384,768]{1,0:T(8,128)(2,1)S(1)} %copy-done.67), custom_call_target="tpu_custom_call" | custom-call | flops 9865003008 | bytes 33947648 | tf_op jit(solution)/shard_map/pallas_call | solution.py:164
  360.4 18.0 %reduce-scatter.5.cloned.1.call-done = bf16[48,3584]{1,0:T(8,128)(2,1)} async-done(((bf16[384,3584]{1,0:T(8,128)(2,1)}), bf16[48,3584]{1,0:T(8,128)(2,1)}) %reduce-scatter.5.cloned.1.call-update) | async-done | bytes 344080 | tf_op jit(solution)/shard_map/reduce_scatter | solution.py:270
  378.4 2.0 pad_maximum_fusion
  (253 shorter events, 48.7 us)
Async XLA Ops:
  7.2 36.8 %copy-start.68 = (bf16[96,3584]{1,0:T(8,128)(2,1)S(1)}, bf16[96,3584]{1,0:T(8,128)(2,1)}, u32[]{:S(2)}) copy-start(bf16[96,3584]{1,0:T(8,128)(2,1)} %param.9) | copy-start | bytes 2064388
  7.2 36.7 %all-gather.5.cloned.1.call-start = ((), (), s32[]{:S(2)}) async-start(), calls=%async_computation.2 | async-start | bytes 3096576 | tf_op jit(solution)/shard_map/all_gather | solution.py:227
  9.3 67.7 %all-gather.7.cloned.1.call-start = ((), (), s32[]{:S(2)}) async-start(), calls=%async_computation.3 | async-start | bytes 3096576 | tf_op jit(solution)/shard_map/all_gather | solution.py:227
  43.9 66.3 %all-gather.9.cloned.1.call-start = ((), (), s32[]{:S(2)}) async-start(), calls=%async_computation.4 | async-start | bytes 3096576 | tf_op jit(solution)/shard_map/all_gather | solution.py:227
  77.0 142.3 %all-gather.11.cloned.1.call-start = ((), (), s32[]{:S(2)}) async-start(), calls=%async_computation.5 | async-start | bytes 3096576 | tf_op jit(solution)/shard_map/all_gather | solution.py:227
  110.2 250.2 %reduce-scatter.3.cloned.1.call-start = ((), (), s32[]{:S(2)}) async-start(), calls=%async_computation.6 | async-start | bytes 3096576 | tf_op jit(solution)/shard_map/reduce_scatter | solution.py:270
  116.7 27.3 %slice-start.8 = ((s8[12845056]{0:T(1024)(128)(4,1)}), s8[4194304]{0:T(1024)(128)(4,1)S(1)}, s32[]{:S(2)}) async-start(s8[12845056]{0:T(1024)(128)(4,1)} %bitcast.4), calls=%async_computation.16 | async-start | bytes 8388608
  116.7 27.3 %slice-start.9 = ((s8[12845056]{0:T(1024)(128)(4,1)}), s8[4194304]{0:T(1024)(128)(4,1)S(1)}, s32[]{:S(2)}) async-start(s8[12845056]{0:T(1024)(128)(4,1)} %bitcast.4), calls=%async_computation.17 | async-start | bytes 8388608
  120.8 37.3 %copy-start.13 = (bf16[384,1024]{1,0:T(8,128)(2,1)}, bf16[384,1024]{1,0:T(8,128)(2,1)S(1)}, u32[]{:S(2)}) copy-start(bf16[384,1024]{1,0:T(8,128)(2,1)S(1)} %shard_map.84.refs_0_) | copy-start | bytes 2359300
  120.8 23.2 %slice-start.10 = ((s8[12845056]{0:T(1024)(128)(4,1)}), s8[4194304]{0:T(1024)(128)(4,1)S(1)}, s32[]{:S(2)}) async-start(s8[12845056]{0:T(1024)(128)(4,1)} %bitcast.4), calls=%async_computation.18 | async-start | bytes 8388608
  120.8 23.2 %slice-start.11 = ((s8[12845056]{0:T(1024)(128)(4,1)}), s8[262144]{0:T(1024)(128)(4,1)S(1)}, s32[]{:S(2)}) async-start(s8[12845056]{0:T(1024)(128)(4,1)} %bitcast.4), calls=%async_computation.19 | async-start | bytes 524288
  120.8 21.5 %collective-permute-start.1 = (bf16[384,1024]{1,0:T(8,128)(2,1)S(1)}, bf16[384,1024]{1,0:T(8,128)(2,1)S(1)}, u32[]{:S(2)}, u32[]{:S(2)}) collective-permute-start(bf16[384,1024]{1,0:T(8,128)(2,1)S(1)} %shard_map.84.refs_0_), channel_id=1, source_target_pairs={{0,8},{24,16},{1,9},{25,17},{2,10},{26,18},{3,11},{27,19},{4,12},{... | collective-permute-start | bytes 2359304 | tf_op jit(solution)/shard_map/ppermute | solution.py:219
  127.6 29.4 %collective-permute-start = (bf16[384,768]{1,0:T(8,128)(2,1)S(1)}, bf16[384,768]{1,0:T(8,128)(2,1)S(1)}, u32[]{:S(2)}, u32[]{:S(2)}) collective-permute-start(bf16[384,768]{1,0:T(8,128)(2,1)S(1)} %shard_map.85.refs_0_), channel_id=1, source_target_pairs={{0,8},{24,16},{1,9},{25,17},{2,10},{26,18},{3,11},{27,19},{4,12},{... | collective-permute-start | bytes 1769480 | tf_op jit(solution)/shard_map/ppermute | solution.py:219
  143.3 14.8 %collective-permute-start.4 = (bf16[384,1024]{1,0:T(8,128)(2,1)S(1)}, bf16[384,1024]{1,0:T(8,128)(2,1)S(1)}, u32[]{:S(2)}, u32[]{:S(2)}) collective-permute-start(bf16[384,1024]{1,0:T(8,128)(2,1)S(1)} %add_convert_fusion.7), channel_id=1, source_target_pairs={{8,16},{16,8},{9,17},{17,9},{10,18},{18,10},{11,19},{19,11},{12,20... | collective-permute-start | bytes 2359304 | tf_op jit(solution)/shard_map/ppermute | solution.py:219
  145.8 42.2 %slice-start = ((s8[12845056]{0:T(1024)(128)(4,1)}), s8[4194304]{0:T(1024)(128)(4,1)S(1)}, s32[]{:S(2)}) async-start(s8[12845056]{0:T(1024)(128)(4,1)} %bitcast), calls=%async_computation.8 | async-start | bytes 8388608
  145.8 42.2 %slice-start.1 = ((s8[12845056]{0:T(1024)(128)(4,1)}), s8[4194304]{0:T(1024)(128)(4,1)S(1)}, s32[]{:S(2)}) async-start(s8[12845056]{0:T(1024)(128)(4,1)} %bitcast), calls=%async_computation.9 | async-start | bytes 8388608
  149.9 45.3 %copy-start.11 = (bf16[384,1024]{1,0:T(8,128)(2,1)}, bf16[384,1024]{1,0:T(8,128)(2,1)S(1)}, u32[]{:S(2)}) copy-start(bf16[384,1024]{1,0:T(8,128)(2,1)S(1)} %shard_map.86.refs_0_) | copy-start | bytes 2359300
  149.9 29.9 %collective-permute-start.3 = (bf16[384,1024]{1,0:T(8,128)(2,1)S(1)}, bf16[384,1024]{1,0:T(8,128)(2,1)S(1)}, u32[]{:S(2)}, u32[]{:S(2)}) collective-permute-start(bf16[384,1024]{1,0:T(8,128)(2,1)S(1)} %shard_map.86.refs_0_), channel_id=1, source_target_pairs={{0,8},{24,16},{1,9},{25,17},{2,10},{26,18},{3,11},{27,19},{4,12},{... | collective-permute-start | bytes 2359304 | tf_op jit(solution)/shard_map/ppermute | solution.py:219
  157.2 23.6 %collective-permute-start.2 = (bf16[384,768]{1,0:T(8,128)(2,1)S(1)}, bf16[384,768]{1,0:T(8,128)(2,1)S(1)}, u32[]{:S(2)}, u32[]{:S(2)}) collective-permute-start(bf16[384,768]{1,0:T(8,128)(2,1)S(1)} %add_convert_fusion.15), channel_id=1, source_target_pairs={{8,16},{16,8},{9,17},{17,9},{10,18},{18,10},{11,19},{19,11},{12,20... | collective-permute-start | bytes 1769480 | tf_op jit(solution)/shard_map/ppermute | solution.py:219
  158.4 26.4 %collective-permute-start.5 = (bf16[384,1024]{1,0:T(8,128)(2,1)S(1)}, bf16[384,1024]{1,0:T(8,128)(2,1)S(1)}, u32[]{:S(2)}, u32[]{:S(2)}) collective-permute-start(bf16[384,1024]{1,0:T(8,128)(2,1)S(1)} %add_convert_fusion.6), channel_id=1, source_target_pairs={{16,24},{8,0},{17,25},{9,1},{18,26},{10,2},{19,27},{11,3},{20,28},... | collective-permute-start | bytes 2359304 | tf_op jit(solution)/shard_map/ppermute | solution.py:219
  164.4 23.6 %slice-start.2 = ((s8[12845056]{0:T(1024)(128)(4,1)}), s8[4194304]{0:T(1024)(128)(4,1)S(1)}, s32[]{:S(2)}) async-start(s8[12845056]{0:T(1024)(128)(4,1)} %bitcast), calls=%async_computation.10 | async-start | bytes 8388608
  164.4 23.6 %slice-start.3 = ((s8[12845056]{0:T(1024)(128)(4,1)}), s8[262144]{0:T(1024)(128)(4,1)S(1)}, s32[]{:S(2)}) async-start(s8[12845056]{0:T(1024)(128)(4,1)} %bitcast), calls=%async_computation.11 | async-start | bytes 524288
  167.5 45.2 %copy-start.20 = (bf16[384,768]{1,0:T(8,128)(2,1)}, bf16[384,768]{1,0:T(8,128)(2,1)S(1)}, u32[]{:S(2)}) copy-start(bf16[384,768]{1,0:T(8,128)(2,1)S(1)} %shard_map.87.refs_0_) | copy-start | bytes 1769476
  167.6 26.6 %collective-permute-start.7 = (bf16[384,768]{1,0:T(8,128)(2,1)S(1)}, bf16[384,768]{1,0:T(8,128)(2,1)S(1)}, u32[]{:S(2)}, u32[]{:S(2)}) collective-permute-start(bf16[384,768]{1,0:T(8,128)(2,1)S(1)} %shard_map.87.refs_0_), channel_id=1, source_target_pairs={{0,8},{24,16},{1,9},{25,17},{2,10},{26,18},{3,11},{27,19},{4,12},{... | collective-permute-start | bytes 1769480 | tf_op jit(solution)/shard_map/ppermute | solution.py:219
  180.1 15.1 %collective-permute-start.6 = (bf16[384,1024]{1,0:T(8,128)(2,1)S(1)}, bf16[384,1024]{1,0:T(8,128)(2,1)S(1)}, u32[]{:S(2)}, u32[]{:S(2)}) collective-permute-start(bf16[384,1024]{1,0:T(8,128)(2,1)S(1)} %add_convert_fusion.5), channel_id=1, source_target_pairs={{8,16},{16,8},{9,17},{17,9},{10,18},{18,10},{11,19},{19,11},{12,20... | collective-permute-start | bytes 2359304 | tf_op jit(solution)/shard_map/ppermute | solution.py:219
  181.0 15.8 %collective-permute-start.8 = (bf16[384,768]{1,0:T(8,128)(2,1)S(1)}, bf16[384,768]{1,0:T(8,128)(2,1)S(1)}, u32[]{:S(2)}, u32[]{:S(2)}) collective-permute-start(bf16[384,768]{1,0:T(8,128)(2,1)S(1)} %add_convert_fusion.14), channel_id=1, source_target_pairs={{16,24},{8,0},{17,25},{9,1},{18,26},{10,2},{19,27},{11,3},{20,28},... | collective-permute-start | bytes 1769480 | tf_op jit(solution)/shard_map/ppermute | solution.py:219
  191.8 18.1 %collective-permute-start.11 = (bf16[384,1024]{1,0:T(8,128)(2,1)S(1)}, bf16[384,1024]{1,0:T(8,128)(2,1)S(1)}, u32[]{:S(2)}, u32[]{:S(2)}) collective-permute-start(bf16[384,1024]{1,0:T(8,128)(2,1)S(1)} %shard_map.89.refs_0_), channel_id=1, source_target_pairs={{0,8},{24,16},{1,9},{25,17},{2,10},{26,18},{3,11},{27,19},{4,12},{... | collective-permute-start | bytes 2359304 | tf_op jit(solution)/shard_map/ppermute | solution.py:219
  194.4 18.4 %collective-permute-start.10 = (bf16[384,768]{1,0:T(8,128)(2,1)S(1)}, bf16[384,768]{1,0:T(8,128)(2,1)S(1)}, u32[]{:S(2)}, u32[]{:S(2)}) collective-permute-start(bf16[384,768]{1,0:T(8,128)(2,1)S(1)} %add_convert_fusion.13), channel_id=1, source_target_pairs={{8,16},{16,8},{9,17},{17,9},{10,18},{18,10},{11,19},{19,11},{12,20... | collective-permute-start | bytes 1769480 | tf_op jit(solution)/shard_map/ppermute | solution.py:219
  195.5 19.5 %collective-permute-start.12 = (bf16[384,1024]{1,0:T(8,128)(2,1)S(1)}, bf16[384,1024]{1,0:T(8,128)(2,1)S(1)}, u32[]{:S(2)}, u32[]{:S(2)}) collective-permute-start(bf16[384,1024]{1,0:T(8,128)(2,1)S(1)} %add_convert_fusion.4), channel_id=1, source_target_pairs={{16,24},{8,0},{17,25},{9,1},{18,26},{10,2},{19,27},{11,3},{20,28},... | collective-permute-start | bytes 2359304 | tf_op jit(solution)/shard_map/ppermute | solution.py:219
  202.8 33.8 %collective-permute-start.9 = (bf16[384,768]{1,0:T(8,128)(2,1)}, bf16[384,768]{1,0:T(8,128)(2,1)}, u32[]{:S(2)}, u32[]{:S(2)}) collective-permute-start(bf16[384,768]{1,0:T(8,128)(2,1)} %shard_map.91.refs_0_), channel_id=1, source_target_pairs={{0,8},{24,16},{1,9},{25,17},{2,10},{26,18},{3,11},{27,19},{4,12},{... | collective-permute-start | bytes 1769480 | tf_op jit(solution)/shard_map/ppermute | solution.py:219
  211.1 27.7 %collective-permute-start.15 = (bf16[384,1024]{1,0:T(8,128)(2,1)}, bf16[384,1024]{1,0:T(8,128)(2,1)}, u32[]{:S(2)}, u32[]{:S(2)}) collective-permute-start(bf16[384,1024]{1,0:T(8,128)(2,1)} %add_convert_fusion.3), channel_id=1, source_target_pairs={{8,16},{16,8},{9,17},{17,9},{10,18},{18,10},{11,19},{19,11},{12,20... | collective-permute-start | bytes 2359304 | tf_op jit(solution)/shard_map/ppermute | solution.py:219
  213.8 28.1 %collective-permute-start.16 = (bf16[384,768]{1,0:T(8,128)(2,1)}, bf16[384,768]{1,0:T(8,128)(2,1)}, u32[]{:S(2)}, u32[]{:S(2)}) collective-permute-start(bf16[384,768]{1,0:T(8,128)(2,1)} %add_convert_fusion.12), channel_id=1, source_target_pairs={{16,24},{8,0},{17,25},{9,1},{18,26},{10,2},{19,27},{11,3},{20,28},... | collective-permute-start | bytes 1769480 | tf_op jit(solution)/shard_map/ppermute | solution.py:219
  215.1 29.6 %slice-start.4 = ((s8[12845056]{0:T(1024)(128)(4,1)}), s8[262144]{0:T(1024)(128)(4,1)S(1)}, s32[]{:S(2)}) async-start(s8[12845056]{0:T(1024)(128)(4,1)} %bitcast.2), calls=%async_computation.12 | async-start | bytes 524288
  229.6 23.0 %copy-start.8 = (bf16[384,1024]{1,0:T(8,128)(2,1)}, bf16[384,1024]{1,0:T(8,128)(2,1)S(1)}, u32[]{:S(2)}) copy-start(bf16[384,1024]{1,0:T(8,128)(2,1)S(1)} %shard_map.93.refs_0_) | copy-start | bytes 2359300
  229.6 22.9 %collective-permute-start.14 = (bf16[384,1024]{1,0:T(8,128)(2,1)S(1)}, bf16[384,1024]{1,0:T(8,128)(2,1)S(1)}, u32[]{:S(2)}, u32[]{:S(2)}) collective-permute-start(bf16[384,1024]{1,0:T(8,128)(2,1)S(1)} %shard_map.93.refs_0_), channel_id=1, source_target_pairs={{0,8},{24,16},{1,9},{25,17},{2,10},{26,18},{3,11},{27,19},{4,12},{... | collective-permute-start | bytes 2359304 | tf_op jit(solution)/shard_map/ppermute | solution.py:219
  238.1 14.8 %collective-permute-start.13 = (bf16[384,768]{1,0:T(8,128)(2,1)S(1)}, bf16[384,768]{1,0:T(8,128)(2,1)S(1)}, u32[]{:S(2)}, u32[]{:S(2)}) collective-permute-start(bf16[384,768]{1,0:T(8,128)(2,1)S(1)} %add_convert_fusion.11), channel_id=1, source_target_pairs={{8,16},{16,8},{9,17},{17,9},{10,18},{18,10},{11,19},{19,11},{12,20... | collective-permute-start | bytes 1769480 | tf_op jit(solution)/shard_map/ppermute | solution.py:219
  240.4 19.4 %collective-permute-start.17 = (bf16[384,1024]{1,0:T(8,128)(2,1)S(1)}, bf16[384,1024]{1,0:T(8,128)(2,1)S(1)}, u32[]{:S(2)}, u32[]{:S(2)}) collective-permute-start(bf16[384,1024]{1,0:T(8,128)(2,1)S(1)} %add_convert_fusion.2), channel_id=1, source_target_pairs={{16,24},{8,0},{17,25},{9,1},{18,26},{10,2},{19,27},{11,3},{20,28},... | collective-permute-start | bytes 2359304 | tf_op jit(solution)/shard_map/ppermute | solution.py:219
  247.6 25.5 %copy-start.22 = (bf16[384,768]{1,0:T(8,128)(2,1)}, bf16[384,768]{1,0:T(8,128)(2,1)S(1)}, u32[]{:S(2)}) copy-start(bf16[384,768]{1,0:T(8,128)(2,1)S(1)} %shard_map.95.refs_0_) | copy-start | bytes 1769476
  247.6 25.5 %collective-permute-start.19 = (bf16[384,768]{1,0:T(8,128)(2,1)S(1)}, bf16[384,768]{1,0:T(8,128)(2,1)S(1)}, u32[]{:S(2)}, u32[]{:S(2)}) collective-permute-start(bf16[384,768]{1,0:T(8,128)(2,1)S(1)} %shard_map.95.refs_0_), channel_id=1, source_target_pairs={{0,8},{24,16},{1,9},{25,17},{2,10},{26,18},{3,11},{27,19},{4,12},{... | collective-permute-start | bytes 1769480 | tf_op jit(solution)/shard_map/ppermute | solution.py:219
  254.2 21.6 %collective-permute-start.20 = (bf16[384,768]{1,0:T(8,128)(2,1)S(1)}, bf16[384,768]{1,0:T(8,128)(2,1)S(1)}, u32[]{:S(2)}, u32[]{:S(2)}) collective-permute-start(bf16[384,768]{1,0:T(8,128)(2,1)S(1)} %add_convert_fusion.10), channel_id=1, source_target_pairs={{16,24},{8,0},{17,25},{9,1},{18,26},{10,2},{19,27},{11,3},{20,28},... | collective-permute-start | bytes 1769480 | tf_op jit(solution)/shard_map/ppermute | solution.py:219
  255.5 18.6 %collective-permute-start.18 = (bf16[384,1024]{1,0:T(8,128)(2,1)S(1)}, bf16[384,1024]{1,0:T(8,128)(2,1)S(1)}, u32[]{:S(2)}, u32[]{:S(2)}) collective-permute-start(bf16[384,1024]{1,0:T(8,128)(2,1)S(1)} %add_convert_fusion.1), channel_id=1, source_target_pairs={{8,16},{16,8},{9,17},{17,9},{10,18},{18,10},{11,19},{19,11},{12,20... | collective-permute-start | bytes 2359304 | tf_op jit(solution)/shard_map/ppermute | solution.py:219
  287.4 91.0 %reduce-scatter.5.cloned.1.call-start = ((), (), s32[]{:S(2)}) async-start(), calls=%async_computation.7 | async-start | bytes 3096576 | tf_op jit(solution)/shard_map/reduce_scatter | solution.py:270
  287.4 20.4 %copy-start.10 = (bf16[384,1024]{1,0:T(8,128)(2,1)S(1)}, bf16[384,1024]{1,0:T(8,128)(2,1)}, u32[]{:S(2)}) copy-start(bf16[384,1024]{1,0:T(8,128)(2,1)} %copy-done.8) | copy-start | bytes 2359300
  287.5 2.1 collective-permute-start.21
  288.3 19.5 %collective-permute-start.22 = (bf16[384,1024]{1,0:T(8,128)(2,1)}, bf16[384,1024]{1,0:T(8,128)(2,1)S(1)}, u32[]{:S(2)}, u32[]{:S(2)}) collective-permute-start(bf16[384,1024]{1,0:T(8,128)(2,1)} %add_convert_fusion), channel_id=1, source_target_pairs={{16,24},{8,0},{17,25},{9,1},{18,26},{10,2},{19,27},{11,3},{20,28},... | collective-permute-start | bytes 2359304 | tf_op jit(solution)/shard_map/ppermute | solution.py:219
  290.8 31.7 %collective-permute-start.23 = (bf16[384,768]{1,0:T(8,128)(2,1)S(1)}, bf16[384,768]{1,0:T(8,128)(2,1)S(1)}, u32[]{:S(2)}, u32[]{:S(2)}) collective-permute-start(bf16[384,768]{1,0:T(8,128)(2,1)S(1)} %add_convert_fusion.8), channel_id=1, source_target_pairs={{16,24},{8,0},{17,25},{9,1},{18,26},{10,2},{19,27},{11,3},{20,28},... | collective-permute-start | bytes 1769480 | tf_op jit(solution)/shard_map/ppermute | solution.py:219
  332.5 3.7 collective-permute-start.24
  336.2 23.6 %collective-permute-start.25 = (f32[1792]{0:T(1024)S(1)}, f32[1792]{0:T(1024)S(1)}, u32[]{:S(2)}, u32[]{:S(2)}) collective-permute-start(f32[1792]{0:T(1024)S(1)} %add.82), channel_id=1, source_target_pairs={{0,16},{8,24},{16,0},{24,8},{1,17},{9,25},{17,1},{25,9},{2,18},{10... | collective-permute-start | bytes 21512 | tf_op jit(solution)/shard_map/ppermute | solution.py:303
  (74 other events, 478.2 us)
Sparse Core Ops, SparseCore 0:
  10.5 33.3 all-gather.4
  46.3 30.6 all-gather.6
  79.5 30.6 all-gather.8
  111.9 30.6 all-gather.10
  287.5 42.8 reduce-scatter.2
  334.0 44.2 reduce-scatter.4

commit v3 on v0

v3 whole, which is shorter than its diff:
```python
import functools

import jax
import jax.numpy as jnp
from jax import lax
from jax.experimental import pallas as pl
from jax.experimental.pallas import tpu as pltpu
from jax.sharding import PartitionSpec as P

GELU_SCALE = 0.7978845608
GELU_CUBIC = 0.044715
F32, BF16 = jnp.float32, jnp.bfloat16
VMEM_LIMIT = 48 * 1024 * 1024
UNITS = 7


def dot(left, right, dims):
    return lax.dot_general(left, right, ((dims[:1], dims[1:]), ((), ())), preferred_element_type=F32)


def call(kernel, flops, moved, place, operands, grid, in_specs, out_specs, out_shape, into=(), outs=()):
    scalars = 1
    aliases = {}
    in_specs, operands = list(in_specs), list(operands)
    for array, out in zip(into, outs):
        if array is not None:
            aliases[scalars + len(operands)] = out
            operands.append(array)
            in_specs.append(pl.BlockSpec(memory_space=pl.ANY))
    return pl.pallas_call(
        kernel,
        grid_spec=pltpu.PrefetchScalarGridSpec(
            num_scalar_prefetch=scalars, grid=grid, in_specs=in_specs, out_specs=out_specs
        ),
        out_shape=out_shape,
        input_output_aliases=aliases,
        compiler_params=pltpu.CompilerParams(vmem_limit_bytes=VMEM_LIMIT),
        cost_estimate=pl.CostEstimate(flops=flops, bytes_accessed=moved, transcendentals=0),
    )(place, *operands)


def whole(shape):
    return pl.BlockSpec(shape, lambda i, s: (0,) * len(shape), pipeline_mode=pl.Buffered(1))


def chip_block(rows, columns, key, tiled=False):
    return pl.BlockSpec((rows, columns), lambda i, s: (s[0] ^ key, i if tiled else 0))


def pick_tile(size):
    return size // UNITS


def weight_units(weight, transposed):
    if transposed:
        return pl.BlockSpec((weight.shape[0] // UNITS, weight.shape[1]), lambda i, s: (i, 0))
    return pl.BlockSpec((weight.shape[0], weight.shape[1] // UNITS), lambda i, s: (0, i))


def own_partial(place, mine, other, weight, transposed):
    rows, depth = mine.shape
    hidden = weight.shape[0 if transposed else 1]
    dims = (1, 1) if transposed else (1, 0)

    def kernel(s, mine_ref, other_ref, weight_ref, out):
        out[pl.ds(pl.multiple_of(s[1] * rows, rows), rows), :] = dot(mine_ref[...], weight_ref[...], dims).astype(BF16)
        out[pl.ds(pl.multiple_of((1 - s[1]) * rows, rows), rows), :] = dot(
            other_ref[...], weight_ref[...], dims
        ).astype(BF16)

    return call(
        kernel,
        4 * rows * depth * hidden,
        4 * rows * (depth + hidden) + 2 * depth * hidden,
        place,
        [mine, other, weight],
        (UNITS,),
        [whole((rows, depth))] * 2 + [weight_units(weight, transposed)],
        pl.BlockSpec((2 * rows, hidden // UNITS), lambda i, s: (0, i)),
        jax.ShapeDtypeStruct((2 * rows, hidden), BF16),
    )


def partials(place, gathered, weight, transposed, keys, rows):
    depth = gathered.shape[1]
    hidden = weight.shape[0 if transposed else 1]
    dims = (1, 1) if transposed else (1, 0)
    count = len(keys)

    def kernel(s, *refs):
        weight_ref = refs[count]
        for tokens, out in zip(refs[:count], refs[count + 1 :]):
            out[...] = dot(tokens[...], weight_ref[...], dims).astype(BF16)

    return call(
        kernel,
        2 * count * rows * depth * hidden,
        2 * count * rows * (depth + hidden) + 2 * depth * hidden,
        place,
        [gathered] * count + [weight],
        (UNITS,),
        [chip_block(rows, depth, key) for key in keys] + [weight_units(weight, transposed)],
        [pl.BlockSpec((rows, hidden // UNITS), lambda i, s: (0, i))] * count,
        [jax.ShapeDtypeStruct((rows, hidden), BF16)] * count,
    )


def activate(place, terms, bias, key, into, tokens):
    rows, hidden = terms[0].shape
    width = hidden // UNITS

    def kernel(s, bias_ref, *refs):
        ins, (act_ref, slope_ref) = refs[: len(terms)], refs[-2:]
        pre = functools.reduce(jnp.add, [ref[...].astype(F32) for ref in ins]) + bias_ref[...]
        tangent = jnp.tanh(GELU_SCALE * (pre + GELU_CUBIC * pre * pre * pre))
        act_ref[...] = (0.5 * pre * (1.0 + tangent)).astype(BF16)
        slope_ref[...] = 0.5 * (1.0 + tangent) + 0.5 * pre * (1.0 - tangent * tangent) * GELU_SCALE * (
            1.0 + 3.0 * GELU_CUBIC * pre * pre
        )

    block = pl.BlockSpec((rows, width), lambda i, s: (0, i))
    return call(
        kernel,
        30 * rows * hidden,
        rows * hidden * (2 * len(terms) + 6),
        place,
        [bias, *terms],
        (UNITS,),
        [pl.BlockSpec((1, width), lambda i, s: (0, i))] + [block] * len(terms),
        [chip_block(rows, width, key, True), block],
        [jax.ShapeDtypeStruct((tokens, hidden), BF16), jax.ShapeDtypeStruct((rows, hidden), F32)],
        [into],
        [0],
    )


def differentiate(place, terms, slope, key, into, tokens):
    rows, hidden = slope.shape
    width = hidden // UNITS

    def kernel(s, slope_ref, *refs):
        ins, (grad_ref, sum_ref) = refs[: len(terms)], refs[-2:]
        grad = functools.reduce(jnp.add, [ref[...].astype(F32) for ref in ins]) * slope_ref[...]
        grad = grad.astype(BF16)
        grad_ref[...] = grad
        sum_ref[...] = jnp.sum(grad.astype(F32), axis=0, keepdims=True)

    block = pl.BlockSpec((rows, width), lambda i, s: (0, i))
    return call(
        kernel,
        8 * rows * hidden,
        rows * hidden * (2 * len(terms) + 6),
        place,
        [slope, *terms],
        (UNITS,),
        [block] * (1 + len(terms)),
        [chip_block(rows, width, key, True), pl.BlockSpec((1, width), lambda i, s: (0, i))],
        [jax.ShapeDtypeStruct((tokens, hidden), BF16), jax.ShapeDtypeStruct((1, hidden), F32)],
        [into],
        [0],
    )


def add_bf16(left, right):
    return (left.astype(F32) + right.astype(F32)).astype(BF16)


def weight_out_grad(place, act, grad, into, first, count):
    tokens, depth = grad.shape
    hidden = act.shape[1]
    width = hidden // UNITS
    tile = pick_tile(depth)

    def kernel(s, act_ref, grad_ref, *refs):
        turned = act_ref[...].T
        for at in range(0, depth, tile):
            refs[-1][:, at : at + tile] = dot(turned, grad_ref[:, at : at + tile], (1, 0))

    return call(
        kernel,
        2 * tokens * depth * width * count,
        2 * tokens * depth + 4 * depth * width * count,
        place,
        [act, grad],
        (count,),
        [pl.BlockSpec((tokens, width), lambda i, s: (0, first + i)), whole((tokens, depth))],
        pl.BlockSpec((width, depth), lambda i, s: (first + i, 0)),
        jax.ShapeDtypeStruct((hidden, depth), F32),
        [into],
        [0],
    )


def weight_in_grad(place, tok, grad, into, first, count):
    tokens, depth = tok.shape
    hidden = grad.shape[1]
    tile = pick_tile(depth)
    width = hidden // UNITS

    def kernel(s, tok_ref, grad_ref, *refs):
        turned = tok_ref[...].T
        for at in range(0, hidden, width):
            refs[-1][:, at : at + width] = dot(turned, grad_ref[:, at : at + width], (1, 0))

    return call(
        kernel,
        2 * tokens * tile * count * hidden,
        2 * tokens * (tile * count + hidden) + 4 * tile * count * hidden,
        place,
        [tok, grad],
        (count,),
        [pl.BlockSpec((tokens, tile), lambda j, s: (0, first + j)), whole((tokens, hidden))],
        pl.BlockSpec((tile, hidden), lambda j, s: (first + j, 0)),
        jax.ShapeDtypeStruct((depth, hidden), F32),
        [into],
        [0],
    )


def token_grad(place, grad, weight_in, keys, rows, first, count):
    depth, hidden = weight_in.shape
    tile = pick_tile(depth)
    half = rows // 2
    number = len(keys)

    def kernel(s, *refs):
        weight_ref = refs[number]
        for at in range(number):
            total = dot(refs[at][...], weight_ref[...], (1, 1)).astype(BF16)
            low = s[1] == 0
            refs[number + 1 + 2 * at][...] = jnp.where(low, total[:half], total[half:])
            refs[number + 2 + 2 * at][...] = jnp.where(low, total[half:], total[:half])

    outs = call(
        kernel,
        2 * number * rows * tile * count * hidden,
        2 * (number * rows * (tile * count + hidden) + tile * count * hidden),
        place,
        [grad] * number + [weight_in],
        (count,),
        [chip_block(rows, hidden, key) for key in keys] + [pl.BlockSpec((tile, hidden), lambda j, s: (first + j, 0))],
        [pl.BlockSpec((half, tile), lambda j, s: (0, j))] * (2 * number),
        [jax.ShapeDtypeStruct((half, tile * count), BF16)] * (2 * number),
    )
    return [tuple(outs[2 * at : 2 * at + 2]) for at in range(number)]


def after(value, *deps):
    return lax.optimization_barrier((value, *deps))[0]


def local(rows_of, cols_of, tokens, weight_in, bias_hidden, weight_out, out_grad):
    mine, depth = tokens.shape
    hidden = bias_hidden.shape[0]
    rows, everyone = 2 * mine, cols_of * mine
    bias = bias_hidden.reshape(1, hidden)
    steps = rows_of - 1
    me = lax.axis_index("col")
    place = jnp.stack([me // 2, me % 2]).astype(jnp.int32)
    others = sorted(range(1, cols_of // 2), key=lambda key: (-key.bit_count(), key))
    chunks = [("pre", 0), ("act", 0)] + [(kind, key) for kind in ("pre", "act") for key in others]
    total = len(chunks)

    def send(value, step):
        pairs = [(step - 1, step), (rows_of - step, rows_of - step - 1)]
        return lax.ppermute(value, "row", pairs)

    def swap(value, bits):
        return lax.ppermute(value, "col", [(i, i ^ bits) for i in range(cols_of)])

    chain = []

    def link(value):
        return after(value, chain[-1]) if chain else value

    own = {}
    got = {chunk: [None] * steps for chunk in chunks}
    held = {}
    slopes, sums, arrived = {}, {}, []

    def compute_own(kind, keys):
        source, weight = (tokens, weight_in) if kind == "pre" else (out_grad, weight_out)
        if keys == [0]:
            outs = [own_partial(place, link(source), held["pair", kind], weight, kind == "act")]
        else:
            outs = partials(place, link(held[kind]), weight, kind == "act", keys, rows)
        chain.append(outs[0])
        for key, out in zip(keys, outs):
            own[kind, key] = out

    def first_send(at):
        got[chunks[at]][0] = send(link(own[chunks[at]]), 1)

    def forward(at, step):
        payload = add_bf16(got[chunks[at]][step - 2], link(own[chunks[at]]))
        chain.append(payload)
        got[chunks[at]][step - 1] = send(payload, step)

    def finish(at):
        kind, key = chunks[at]
        terms = [link(own[kind, key])] + got[kind, key]
        if kind == "pre":
            held["activations"], slopes[key] = activate(place, terms, bias, key, held.get("activations"), everyone)
            chain.append(held["activations"])
        else:
            held["grads"], sums[key] = differentiate(place, terms, slopes[key], key, held.get("grads"), everyone)
            chain.append(held["grads"])

    def out_rows(first, count):
        held["out"] = weight_out_grad(
            place, link(held["activations"]), held["act"], held.get("out"), first, count
        )
        chain.append(held["out"])

    def in_rows(first, count):
        held["in"] = weight_in_grad(place, held["pre"], link(held["grads"]), held.get("in"), first, count)
        chain.append(held["in"])

    def tokens_of(keys, first=0, count=UNITS):
        parts = token_grad(place, link(held["grads"]), weight_in, keys, rows, first, count)
        chain.append(parts[0][0])
        return [(key, keep, swap(give, 1)) for key, (keep, give) in zip(keys, parts)]

    def deliver(parts):
        results = []
        for key, keep, given in parts:
            pair = add_bf16(link(keep), given)
            chain.append(pair)
            results.append(swap(pair, 2 * key) if key else pair)
        return results

    held["pair", "pre"], held["pair", "act"] = swap(tokens, 1), swap(out_grad, 1)
    held["pre"] = lax.all_gather(tokens, "col", axis=0, tiled=True)
    compute_own("pre", [0])
    first_send(0)
    compute_own("act", [0])
    first_send(1)
    early = None
    last = others[-1]
    for slot in range(total + steps - 1):
        if 3 <= slot + 1 < total:
            first_send(slot + 1)
        for step in range(2, steps + 1):
            if 0 <= slot - step + 2 < total:
                forward(slot - step + 2, step)
        if slot >= steps - 1:
            finish(slot - steps + 1)
        if slot == 1:
            compute_own("pre", others[:1])
            held["act"] = lax.all_gather(link(out_grad), "col", axis=0, tiled=True)
            first_send(2)
            compute_own("pre", others[1:])
        if slot == len(others):
            compute_own("act", others[:1])
        if slot == len(others) + 1:
            compute_own("act", others[1:])
        if slot == total + steps - 6:
            early = tokens_of([0])
        if slot == total + steps - 5:
            out_rows(0, 3)
            arrived += deliver(early)
        if slot == total + steps - 4:
            out_rows(3, 2)
        if slot == total + steps - 3:
            out_rows(5, UNITS - 5)
            early = tokens_of(others[:-1])
    arrived += deliver(early)
    front = UNITS // 2
    parts = [tokens_of([last], 0, front), tokens_of([last], front, UNITS - front)]
    in_rows(0, 1)
    sides = [deliver(parts[0])[0]]
    in_rows(1, 1)
    sides.append(deliver(parts[1])[0])
    in_rows(2, UNITS - 2)
    arrived.append(jnp.concatenate(sides, axis=1))
    grad_tokens = functools.reduce(jnp.add, [part.astype(F32) for part in arrived]).astype(BF16)

    sums = functools.reduce(jnp.add, [sums[key] for key in sorted(sums)]).reshape(hidden)
    for bit in [1 << i for i in range(rows_of.bit_length() - 1)]:
        sums = sums + lax.ppermute(sums, "row", [(i, i ^ bit) for i in range(rows_of)])
    grad_bias = sums * (1.0 / rows_of)
    return (grad_tokens, held["in"], grad_bias, held["out"])


def solution(mesh):
    placed = (P("col", "row"), P("row", "col"), P("col"), P("col", "row"), P("col", "row"))
    return jax.shard_map(
        functools.partial(local, mesh.shape["row"], mesh.shape["col"]),
        mesh=mesh,
        in_specs=placed,
        out_specs=(P("col", "row"), P("row", "col"), P("col"), P("col", "row")),
        check_vma=False,
    )
```

time: 517 us -> 322 us (0.62)
  waiting for transfers between devices: 370 us -> 30.7 us
  Pallas kernels: 0 us -> 181 us
  matrix products: 86.5 us -> 0 us
  starting transfers between devices: 0.28 us -> 72.1 us
  local copies, waits for them, and re-layouts: 28.1 us -> 10.5 us
  blocking collectives: 10.9 us -> 0 us
    reduce_scatter x3 -> x0, waiting for transfers between devices: 237 us -> none  [the longest x1 101 us: local(): lax.psum_scatter(pre_part, 'row', scatter_dimension=0, tiled=True)]
    pallas_call x0 -> x24, Pallas kernels: none -> 181 us  [call(): pl.pallas_call(kernel, grid_spec=pltpu.PrefetchScalarGridSpec(num_scalar_...]
    all_gather x4 -> x2, waiting for transfers between devices: 131 us -> 0.01 us  [the longest x1 0.01 us: local(): held['pre'] = lax.all_gather(tokens, 'col', axis=0, tiled=True)]
    dot_general x5 -> x0, matrix products: 86.5 us -> none  [the longest x2 37.1 us: contract_rows(): lax.dot_general(left, right, (((0,), (0,)), ((), ())), preferred_element_...]
    ppermute x0 -> x37, starting transfers between devices: none -> 72 us  [the longest x24 62.9 us: send(): return lax.ppermute(value, 'row', pairs)]
    ppermute x0 -> x37, waiting for transfers between devices: none -> 30 us  [the longest x24 28.1 us: send(): return lax.ppermute(value, 'row', pairs)]
    unnamed x5 -> x60, local copies, waits for them, and re-layouts: 28.1 us -> 10.5 us
    psum x1 -> x0, blocking collectives: 10.9 us -> none  [local(): grad_bias = lax.psum(bias_local, 'row')]
  transfers between devices with their start and end apart: 7 -> 39, of which waited for: 6 -> 5; matrix products, arithmetic and copies ran while one was open for 22% -> 3% of each run, Pallas kernels for 0% -> 54%
where the time goes in v3:
time: 322 us; the launch traced here: 320 us
  Pallas kernels  181 us (56%)
  starting transfers between devices  72.1 us (22%)
  waiting for transfers between devices  30.7 us (10%)
  between operations  14.8 us (5%)
  other arithmetic  11 us (3%)
  local copies, waits for them, and re-layouts  10.5 us (3%)
    pallas_call x24, Pallas kernels, call(): pl.pallas_call(kernel, grid_spec=pltpu.PrefetchScalarGridSpec(num_scalar_...  181 us
    ppermute x24, starting transfers between devices, send(): return lax.ppermute(value, 'row', pairs)  62.9 us
    ppermute x24, waiting for transfers between devices, send(): return lax.ppermute(value, 'row', pairs)  28.1 us
    unnamed x60, local copies, waits for them, and re-layouts  10.5 us
    convert_element_type x21, other arithmetic, add_bf16(): return (left.astype(F32) + right.astype(F32)).astype(BF16)  9.14 us
    ppermute x11, starting transfers between devices, swap(): return lax.ppermute(value, 'col', [(i, i ^ bits) for i in range(cols_of)])  7.19 us
  transfers between devices with their start and end apart: 39, of which 5 were waited for; matrix products, arithmetic and copies ran while one was open for 3% of the time, Pallas kernels for 54%

profile of v3, /device:TPU:0, one launch (start us, length us, event | category | flops | bytes accessed | tf_op | source)
XLA Modules:
  0.0 319.7 jit_solution(9208529016503978650)
XLA Ops:
  8.6 1.8 collective-permute-done.other_ref
  11.5 9.8 %shard_map.84.refs_0_ = bf16[192,1792]{1,0:T(8,128)(2,1)S(1)} custom-call(s32[2]{0:T(128)S(1)} %pad_add_fusion.s, bf16[96,3584]{1,0:T(8,128)(2,1)S(1)} %copy-done.7, bf16[96,3584]{1,0:T(8,128)(2,1)S(1)} %collective-permute-done.other_ref, bf16[3584,1792]{1,0:T(8,128)(2,1)} %refs_1_.9), custom_call_target="tpu_custom_call" | custom-call | flops 2466250752 | bytes 14909440 | tf_op jit(solution)/shard_map/pallas_call | solution.py:30
  21.4 4.8 %collective-permute-start.3 = (bf16[192,1792]{1,0:T(8,128)(2,1)S(1)}, bf16[192,1792]{1,0:T(8,128)(2,1)S(1)}, u32[]{:S(2)}, u32[]{:S(2)}) collective-permute-start(bf16[192,1792]{1,0:T(8,128)(2,1)S(1)} %shard_map.84.refs_0_), channel_id=1, source_target_pairs={{0,8},{24,16},{1,9},{25,17},{2,10},{26,18},{3,11},{27,19},{4,12},{... | collective-permute-start | bytes 2064392 | tf_op jit(solution)/shard_map/ppermute | solution.py:266
  26.2 11.9 %shard_map.85.refs_0_ = bf16[192,1792]{1,0:T(8,128)(2,1)S(1)} custom-call(s32[2]{0:T(128)S(1)} %pad_add_fusion.s, bf16[96,3584]{1,0:T(8,128)(2,1)S(1)} %copy-done.8, bf16[96,3584]{1,0:T(8,128)(2,1)S(1)} %collective-permute-done.1.other_ref, bf16[1792,3584]{1,0:T(8,128)(2,1)} %refs_2_.4), custom_call_target="tpu_custom_call" | custom-call | flops 2466250752 | bytes 14909440 | tf_op jit(solution)/shard_map/pallas_call | solution.py:30
  38.1 1.3 collective-permute-start.2
  39.5 2.5 collective-permute-done.3.refs_1_
  42.9 13.0 %collective-permute-done.2.refs_1_ = bf16[192,1792]{1,0:T(8,128)(2,1)S(1)} collective-permute-done((bf16[192,1792]{1,0:T(8,128)(2,1)S(1)}, bf16[192,1792]{1,0:T(8,128)(2,1)S(1)}, u32[]{:S(2)}, u32[]{:S(2)}) %collective-permute-start.2) | collective-permute-done | bytes 688160 | tf_op jit(solution)/shard_map/ppermute | solution.py:266
  58.9 2.6 copy-done.3
  61.5 8.8 %shard_map.86.refs_0_ = bf16[192,1792]{1,0:T(8,128)(2,1)S(1)} custom-call(s32[2]{0:T(128)S(1)} %pad_add_fusion.s, bf16[768,3584]{1,0:T(8,128)(2,1)S(1)} %copy-done.3, bf16[3584,1792]{1,0:T(8,128)(2,1)} %refs_1_.9), custom_call_target="tpu_custom_call" | custom-call | flops 2466250752 | bytes 14909440 | tf_op jit(solution)/shard_map/pallas_call | solution.py:30
  70.4 7.4 %collective-permute-start.6 = (bf16[192,1792]{1,0:T(8,128)(2,1)S(1)}, bf16[192,1792]{1,0:T(8,128)(2,1)S(1)}, u32[]{:S(2)}, u32[]{:S(2)}) collective-permute-start(bf16[192,1792]{1,0:T(8,128)(2,1)S(1)} %shard_map.86.refs_0_), channel_id=1, source_target_pairs={{0,8},{24,16},{1,9},{25,17},{2,10},{26,18},{3,11},{27,19},{4,12},{... | collective-permute-start | bytes 2064392 | tf_op jit(solution)/shard_map/ppermute | solution.py:266
  78.5 1.3 collective-permute-start.7
  79.8 11.5 %shard_map.87 = (bf16[192,1792]{1,0:T(8,128)(2,1)S(1)}, bf16[192,1792]{1,0:T(8,128)(2,1)S(1)}) custom-call(s32[2]{0:T(128)S(1)} %pad_add_fusion.s, bf16[768,3584]{1,0:T(8,128)(2,1)} %all-gather.3.cloned.1.call-done.refs_0_.refs_1_.tok_ref, bf16[768,3584]{1,0:T(8,128)(2,1)} %all-gather.3.cloned.1.call-done.refs_0_.refs_1_.tok_ref, bf16[3584,1792]{1,0:T(8,128)(2,1)} %refs_1_.9), custom_call_target="tpu_custom_call" | custom-call | flops 4932501504 | bytes 16973824 | tf_op jit(solution)/shard_map/pallas_call | solution.py:30
  91.3 4.6 %collective-permute-start.9 = (bf16[192,1792]{1,0:T(8,128)(2,1)S(1)}, bf16[192,1792]{1,0:T(8,128)(2,1)S(1)}, u32[]{:S(2)}, u32[]{:S(2)}) collective-permute-start(bf16[192,1792]{1,0:T(8,128)(2,1)S(1)} %get-tuple-element.120.refs_0_), channel_id=1, source_target_pairs={{0,8},{24,16},{1,9},{25,17},{2,10},{26,18},{3,11},{27,19},{4,12},{... | collective-permute-start | bytes 2064392 | tf_op jit(solution)/shard_map/ppermute | solution.py:266
  98.6 3.8 %shard_map.88 = (bf16[768,1792]{1,0:T(8,128)(2,1)}, f32[192,1792]{1,0:T(8,128)S(1)}) custom-call(s32[2]{0:T(128)S(1)} %pad_add_fusion.s, f32[1,1792]{1,0:T(1,128)S(1)} %reshape.14.bias_ref, bf16[192,1792]{1,0:T(8,128)(2,1)S(1)} %shard_map.84.refs_0_, bf16[192,1792]{1,0:T(8,128)(2,1)S(1)} %copy-done.16, bf16[192,1792]{1,0:T(8,128)(2,1)S(1)} %copy-done.18, ...), custom_call_target="tpu_custom_call" | custom-call | flops 10321920 | bytes 4816896 | tf_op jit(solution)/shard_map/pallas_call | solution.py:30
  102.3 5.3 %collective-permute-done.9.refs_1_ = bf16[192,1792]{1,0:T(8,128)(2,1)S(1)} collective-permute-done((bf16[192,1792]{1,0:T(8,128)(2,1)S(1)}, bf16[192,1792]{1,0:T(8,128)(2,1)S(1)}, u32[]{:S(2)}, u32[]{:S(2)}) %collective-permute-start.9) | collective-permute-done | bytes 688160 | tf_op jit(solution)/shard_map/ppermute | solution.py:266
  108.7 1.7 collective-permute-start.14
  110.4 6.3 %collective-permute-start.11 = (bf16[192,1792]{1,0:T(8,128)(2,1)S(1)}, bf16[192,1792]{1,0:T(8,128)(2,1)S(1)}, u32[]{:S(2)}, u32[]{:S(2)}) collective-permute-start(bf16[192,1792]{1,0:T(8,128)(2,1)S(1)} %get-tuple-element.127.refs_0_), channel_id=1, source_target_pairs={{0,8},{24,16},{1,9},{25,17},{2,10},{26,18},{3,11},{27,19},{4,12},{... | collective-permute-start | bytes 2064392 | tf_op jit(solution)/shard_map/ppermute | solution.py:266
  119.2 3.7 %shard_map.89 = (bf16[768,1792]{1,0:T(8,128)(2,1)}, f32[1,1792]{1,0:T(1,128)S(1)}) custom-call(s32[2]{0:T(128)S(1)} %pad_add_fusion.s, f32[192,1792]{1,0:T(8,128)S(1)} %get-tuple-element.100.slope_ref, bf16[192,1792]{1,0:T(8,128)(2,1)S(1)} %shard_map.85.refs_0_, bf16[192,1792]{1,0:T(8,128)(2,1)S(1)} %copy-done.20, ...), custom_call_target="tpu_custom_call" | custom-call | flops 2752512 | bytes 4816896 | tf_op jit(solution)/shard_map/pallas_call | solution.py:30
  122.9 2.6 copy-done.4
  125.4 9.7 %shard_map.90.refs_0_ = bf16[192,1792]{1,0:T(8,128)(2,1)S(1)} custom-call(s32[2]{0:T(128)S(1)} %pad_add_fusion.s, bf16[768,3584]{1,0:T(8,128)(2,1)S(1)} %copy-done.4, bf16[1792,3584]{1,0:T(8,128)(2,1)} %refs_2_.4), custom_call_target="tpu_custom_call" | custom-call | flops 2466250752 | bytes 14909440 | tf_op jit(solution)/shard_map/pallas_call | solution.py:30
  135.1 5.4 %collective-permute-start.13 = (bf16[192,1792]{1,0:T(8,128)(2,1)S(1)}, bf16[192,1792]{1,0:T(8,128)(2,1)S(1)}, u32[]{:S(2)}, u32[]{:S(2)}) collective-permute-start(bf16[192,1792]{1,0:T(8,128)(2,1)S(1)} %shard_map.90.refs_0_), channel_id=1, source_target_pairs={{0,8},{24,16},{1,9},{25,17},{2,10},{26,18},{3,11},{27,19},{4,12},{... | collective-permute-start | bytes 2064392 | tf_op jit(solution)/shard_map/ppermute | solution.py:266
  140.7 1.4 add_convert_fusion.11
  144.1 5.7 %shard_map.91 = (bf16[768,1792]{1,0:T(8,128)(2,1)}, f32[192,1792]{1,0:T(8,128)S(1)}) custom-call(s32[2]{0:T(128)S(1)} %pad_add_fusion.s, f32[1,1792]{1,0:T(1,128)S(1)} %reshape.14.bias_ref, bf16[192,1792]{1,0:T(8,128)(2,1)S(1)} %shard_map.86.refs_0_, bf16[192,1792]{1,0:T(8,128)(2,1)S(1)} %copy-done.12, ...), custom_call_target="tpu_custom_call", output_to_operand_aliasing={{0}: (6, {})} | custom-call | flops 10321920 | bytes 4816896 | tf_op jit(solution)/shard_map/pallas_call | solution.py:30
  149.8 12.9 %shard_map.92 = (bf16[192,1792]{1,0:T(8,128)(2,1)S(1)}, bf16[192,1792]{1,0:T(8,128)(2,1)S(1)}) custom-call(s32[2]{0:T(128)S(1)} %pad_add_fusion.s, bf16[768,3584]{1,0:T(8,128)(2,1)} %all-gather.5.cloned.1.call-done.refs_0_.refs_1_.grad_ref, bf16[768,3584]{1,0:T(8,128)(2,1)} %all-gather.5.cloned.1.call-done.refs_0_.refs_1_.grad_ref, bf16[1792,3584]{1,0:T(8,128)(2,1)} %refs_2_.4), custom_call_target="tpu_custom_call" | custom-call | flops 4932501504 | bytes 16973824 | tf_op jit(solution)/shard_map/pallas_call | solution.py:30
  162.7 6.4 %collective-permute-start.18 = (bf16[192,1792]{1,0:T(8,128)(2,1)S(1)}, bf16[192,1792]{1,0:T(8,128)(2,1)S(1)}, u32[]{:S(2)}, u32[]{:S(2)}) collective-permute-start(bf16[192,1792]{1,0:T(8,128)(2,1)S(1)} %get-tuple-element.142.refs_0_), channel_id=1, source_target_pairs={{0,8},{24,16},{1,9},{25,17},{2,10},{26,18},{3,11},{27,19},{4,12},{... | collective-permute-start | bytes 2064392 | tf_op jit(solution)/shard_map/ppermute | solution.py:266
  170.2 1.4 collective-permute-start.19
  172.4 5.9 %shard_map.93 = (bf16[768,1792]{1,0:T(8,128)(2,1)}, f32[192,1792]{1,0:T(8,128)S(1)}) custom-call(s32[2]{0:T(128)S(1)} %pad_add_fusion.s, f32[1,1792]{1,0:T(1,128)S(1)} %reshape.14.bias_ref, bf16[192,1792]{1,0:T(8,128)(2,1)S(1)} %get-tuple-element.120.refs_0_, bf16[192,1792]{1,0:T(8,128)(2,1)S(1)} %copy-done.10, ...), custom_call_target="tpu_custom_call", output_to_operand_aliasing={{0}: (6, {})} | custom-call | flops 10321920 | bytes 4816896 | tf_op jit(solution)/shard_map/pallas_call | solution.py:30
  179.4 9.7 %shard_map.94 = (bf16[96,3584]{1,0:T(8,128)(2,1)S(1)}, bf16[96,3584]{1,0:T(8,128)(2,1)S(1)}) custom-call(s32[2]{0:T(128)S(1)} %pad_add_fusion.s, bf16[768,1792]{1,0:T(8,128)(2,1)S(1)} %copy-done, bf16[3584,1792]{1,0:T(8,128)(2,1)} %refs_1_.9), custom_call_target="tpu_custom_call" | custom-call | flops 2466250752 | bytes 14909440 | tf_op jit(solution)/shard_map/pallas_call | solution.py:30
  190.1 9.1 %collective-permute-start.21 = (bf16[192,1792]{1,0:T(8,128)(2,1)S(1)}, bf16[192,1792]{1,0:T(8,128)(2,1)S(1)}, u32[]{:S(2)}, u32[]{:S(2)}) collective-permute-start(bf16[192,1792]{1,0:T(8,128)(2,1)S(1)} %get-tuple-element.148.refs_0_), channel_id=1, source_target_pairs={{0,8},{24,16},{1,9},{25,17},{2,10},{26,18},{3,11},{27,19},{4,12},{... | collective-permute-start | bytes 2064392 | tf_op jit(solution)/shard_map/ppermute | solution.py:266
  200.7 3.8 %shard_map.95 = (bf16[768,1792]{1,0:T(8,128)(2,1)}, f32[192,1792]{1,0:T(8,128)S(1)}) custom-call(s32[2]{0:T(128)S(1)} %pad_add_fusion.s, f32[1,1792]{1,0:T(1,128)S(1)} %reshape.14.bias_ref, bf16[192,1792]{1,0:T(8,128)(2,1)S(1)} %get-tuple-element.127.refs_0_, bf16[192,1792]{1,0:T(8,128)(2,1)S(1)} %collective-permute-done.11.refs_1_, ...), custom_call_target="tpu_custom_call", output_to_operand_aliasing={{0}: (6, {})} | custom-call | flops 10321920 | bytes 4816896 | tf_op jit(solution)/shard_map/pallas_call | solution.py:30
  204.5 2.3 copy-done.5
  206.8 10.1 %shard_map.96.refs_0_ = f32[1792,3584]{1,0:T(8,128)} custom-call(s32[2]{0:T(128)S(1)} %pad_add_fusion.s, bf16[768,1792]{1,0:T(8,128)(2,1)S(1)} %copy-done.5, bf16[768,3584]{1,0:T(8,128)(2,1)} %all-gather.5.cloned.1.call-done.refs_0_.refs_1_.grad_ref), custom_call_target="tpu_custom_call" | custom-call | flops 4227858432 | bytes 16515072 | tf_op jit(solution)/shard_map/pallas_call | solution.py:30
  219.7 3.7 %shard_map.97 = (bf16[768,1792]{1,0:T(8,128)(2,1)}, f32[1,1792]{1,0:T(1,128)S(1)}) custom-call(s32[2]{0:T(128)S(1)} %pad_add_fusion.s, f32[192,1792]{1,0:T(8,128)S(1)} %copy-done.24, bf16[192,1792]{1,0:T(8,128)(2,1)S(1)} %shard_map.90.refs_0_, bf16[192,1792]{1,0:T(8,128)(2,1)S(1)} %collective-permute-done.13.refs_1_, ...), custom_call_target="tpu_custom_call", output_to_operand_aliasing={{0}: (6, {})} | custom-call | flops 2752512 | bytes 4816896 | tf_op jit(solution)/shard_map/pallas_call | solution.py:30
  223.5 8.2 %shard_map.98.refs_0_ = f32[1792,3584]{1,0:T(8,128)} custom-call(s32[2]{0:T(128)S(1)} %pad_add_fusion.s, bf16[768,1792]{1,0:T(8,128)(2,1)S(1)} %copy-done.6, bf16[768,3584]{1,0:T(8,128)(2,1)} %all-gather.5.cloned.1.call-done.refs_0_.refs_1_.grad_ref, f32[1792,3584]{1,0:T(8,128)} %shard_map.96.refs_0_), custom_call_target="tpu_custom_call", output_to_operand_aliasing={{}: (3, {})} | custom-call | flops 2818572288 | bytes 12845056 | tf_op jit(solution)/shard_map/pallas_call | solution.py:30
  231.9 1.4 collective-permute-start.26
  233.3 7.3 %collective-permute-done.25.refs_3_ = bf16[192,1792]{1,0:T(8,128)(2,1)S(1)} collective-permute-done((bf16[192,1792]{1,0:T(8,128)(2,1)S(1)}, bf16[192,1792]{1,0:T(8,128)(2,1)S(1)}, u32[]{:S(2)}, u32[]{:S(2)}) %collective-permute-start.25) | collective-permute-done | bytes 688160 | tf_op jit(solution)/shard_map/ppermute | solution.py:266
  240.6 3.7 %shard_map.99 = (bf16[768,1792]{1,0:T(8,128)(2,1)}, f32[1,1792]{1,0:T(1,128)S(1)}) custom-call(s32[2]{0:T(128)S(1)} %pad_add_fusion.s, f32[192,1792]{1,0:T(8,128)S(1)} %copy-done.26, bf16[192,1792]{1,0:T(8,128)(2,1)S(1)} %get-tuple-element.142.refs_0_, bf16[192,1792]{1,0:T(8,128)(2,1)S(1)} %collective-permute-done.18.refs_1_, ...), custom_call_target="tpu_custom_call", output_to_operand_aliasing={{0}: (6, {})} | custom-call | flops 2752512 | bytes 4816896 | tf_op jit(solution)/shard_map/pallas_call | solution.py:30
  244.3 8.5 %shard_map.100 = f32[1792,3584]{1,0:T(8,128)} custom-call(s32[2]{0:T(128)S(1)} %pad_add_fusion.s, bf16[768,1792]{1,0:T(8,128)(2,1)S(1)} %copy-done.6, bf16[768,3584]{1,0:T(8,128)(2,1)} %all-gather.5.cloned.1.call-done.refs_0_.refs_1_.grad_ref, f32[1792,3584]{1,0:T(8,128)} %shard_map.98.refs_0_), custom_call_target="tpu_custom_call", output_to_operand_aliasing={{}: (3, {})} | custom-call | flops 2818572288 | bytes 12845056 | tf_op jit(solution)/shard_map/pallas_call | solution.py:30
  252.8 12.1 %shard_map.101 = (bf16[96,3584]{1,0:T(8,128)(2,1)S(1)}, bf16[96,3584]{1,0:T(8,128)(2,1)S(1)}, bf16[96,3584]{1,0:T(8,128)(2,1)S(1)}, bf16[96,3584]{1,0:T(8,128)(2,1)S(1)}) custom-call(s32[2]{0:T(128)S(1)} %pad_add_fusion.s, bf16[768,1792]{1,0:T(8,128)(2,1)S(1)} %copy-done.1, bf16[768,1792]{1,0:T(8,128)(2,1)S(1)} %copy-done.1, bf16[3584,1792]{1,0:T(8,128)(2,1)} %refs_1_.9), custom_call_target="tpu_custom_call" | custom-call | flops 4932501504 | bytes 16973824 | tf_op jit(solution)/shard_map/pallas_call | solution.py:30
  265.4 3.7 %shard_map.102 = (bf16[768,1792]{1,0:T(8,128)(2,1)}, f32[1,1792]{1,0:T(1,128)S(1)}) custom-call(s32[2]{0:T(128)S(1)} %pad_add_fusion.s, f32[192,1792]{1,0:T(8,128)S(1)} %copy-done.28, bf16[192,1792]{1,0:T(8,128)(2,1)S(1)} %get-tuple-element.148.refs_0_, bf16[192,1792]{1,0:T(8,128)(2,1)S(1)} %collective-permute-done.21.refs_1_, ...), custom_call_target="tpu_custom_call", output_to_operand_aliasing={{0}: (6, {})} | custom-call | flops 2752512 | bytes 4816896 | tf_op jit(solution)/shard_map/pallas_call | solution.py:30
  269.2 2.6 collective-permute-start.28
  272.9 5.1 %shard_map.103 = (bf16[96,1536]{1,0:T(8,128)(2,1)S(1)}, bf16[96,1536]{1,0:T(8,128)(2,1)S(1)}) custom-call(s32[2]{0:T(128)S(1)} %pad_add_fusion.s, bf16[768,1792]{1,0:T(8,128)(2,1)S(1)} %copy-done.2, bf16[3584,1792]{1,0:T(8,128)(2,1)} %refs_1_.9), custom_call_target="tpu_custom_call" | custom-call | flops 1056964608 | bytes 6782976 | tf_op jit(solution)/shard_map/pallas_call | solution.py:30
  278.1 6.0 %shard_map.104 = (bf16[96,2048]{1,0:T(8,128)(2,1)S(1)}, bf16[96,2048]{1,0:T(8,128)(2,1)S(1)}) custom-call(s32[2]{0:T(128)S(1)} %pad_add_fusion.s, bf16[768,1792]{1,0:T(8,128)(2,1)S(1)} %copy-done.2, bf16[3584,1792]{1,0:T(8,128)(2,1)} %refs_1_.9), custom_call_target="tpu_custom_call" | custom-call | flops 1409286144 | bytes 8814592 | tf_op jit(solution)/shard_map/pallas_call | solution.py:30
  284.7 1.6 collective-permute-start.36
  286.3 5.2 %shard_map.105.refs_0_ = f32[3584,1792]{1,0:T(8,128)} custom-call(s32[2]{0:T(128)S(1)} %pad_add_fusion.s, bf16[768,3584]{1,0:T(8,128)(2,1)} %all-gather.3.cloned.1.call-done.refs_0_.refs_1_.tok_ref, bf16[768,1792]{1,0:T(8,128)(2,1)S(1)} %copy-done.2), custom_call_target="tpu_custom_call" | custom-call | flops 1409286144 | bytes 7208960 | tf_op jit(solution)/shard_map/pallas_call | solution.py:30
  292.8 5.2 %shard_map.106.refs_0_ = f32[3584,1792]{1,0:T(8,128)} custom-call(s32[2]{0:T(128)S(1)} %pad_add_fusion.s, bf16[768,3584]{1,0:T(8,128)(2,1)} %all-gather.3.cloned.1.call-done.refs_0_.refs_1_.tok_ref, bf16[768,1792]{1,0:T(8,128)(2,1)S(1)} %copy-done.2, f32[3584,1792]{1,0:T(8,128)} %shard_map.105.refs_0_), custom_call_target="tpu_custom_call", output_to_operand_aliasing={{}: (3, {})} | custom-call | flops 1409286144 | bytes 7208960 | tf_op jit(solution)/shard_map/pallas_call | solution.py:30
  298.1 1.5 collective-permute-start.34
  299.6 12.1 %shard_map.107 = f32[3584,1792]{1,0:T(8,128)} custom-call(s32[2]{0:T(128)S(1)} %pad_add_fusion.s, bf16[768,3584]{1,0:T(8,128)(2,1)} %all-gather.3.cloned.1.call-done.refs_0_.refs_1_.tok_ref, bf16[768,1792]{1,0:T(8,128)(2,1)S(1)} %copy-done.2, f32[3584,1792]{1,0:T(8,128)} %shard_map.106.refs_0_), custom_call_target="tpu_custom_call", output_to_operand_aliasing={{}: (3, {})} | custom-call | flops 7046430720 | bytes 25034752 | tf_op jit(solution)/shard_map/pallas_call | solution.py:30
  (143 shorter events, 28.9 us)
Async XLA Ops:
  7.2 51.8 %all-gather.3.cloned.1.call-start = ((), (), s32[]{:S(2)}) async-start(), calls=%async_computation | async-start | bytes 6193152 | tf_op jit(solution)/shard_map/all_gather | solution.py:333
  7.9 115.0 %all-gather.5.cloned.1.call-start = ((), (), s32[]{:S(2)}) async-start(), calls=%async_computation.1 | async-start | bytes 6193152 | tf_op jit(solution)/shard_map/all_gather | solution.py:350
  7.9 2.5 collective-permute-start
  8.5 17.7 %collective-permute-start.1 = (bf16[96,3584]{1,0:T(8,128)(2,1)}, bf16[96,3584]{1,0:T(8,128)(2,1)S(1)}, u32[]{:S(2)}, u32[]{:S(2)}) collective-permute-start(bf16[96,3584]{1,0:T(8,128)(2,1)} %mine_ref.2), channel_id=1, source_target_pairs={{0,1},{1,0},{2,3},{3,2},{4,5},{5,4},{6,7},{7,6},{8,9},{9,8},{10,11... | collective-permute-start | bytes 2064392 | tf_op jit(solution)/shard_map/ppermute | solution.py:269
  11.5 14.7 %copy-start.8 = (bf16[96,3584]{1,0:T(8,128)(2,1)S(1)}, bf16[96,3584]{1,0:T(8,128)(2,1)}, u32[]{:S(2)}) copy-start(bf16[96,3584]{1,0:T(8,128)(2,1)} %mine_ref.2) | copy-start | bytes 2064388
  21.4 20.6 %collective-permute-start.3 = (bf16[192,1792]{1,0:T(8,128)(2,1)S(1)}, bf16[192,1792]{1,0:T(8,128)(2,1)S(1)}, u32[]{:S(2)}, u32[]{:S(2)}) collective-permute-start(bf16[192,1792]{1,0:T(8,128)(2,1)S(1)} %shard_map.84.refs_0_), channel_id=1, source_target_pairs={{0,8},{24,16},{1,9},{25,17},{2,10},{26,18},{3,11},{27,19},{4,12},{... | collective-permute-start | bytes 2064392 | tf_op jit(solution)/shard_map/ppermute | solution.py:266
  38.1 17.7 %collective-permute-start.2 = (bf16[192,1792]{1,0:T(8,128)(2,1)S(1)}, bf16[192,1792]{1,0:T(8,128)(2,1)S(1)}, u32[]{:S(2)}, u32[]{:S(2)}) collective-permute-start(bf16[192,1792]{1,0:T(8,128)(2,1)S(1)} %shard_map.85.refs_0_), channel_id=1, source_target_pairs={{0,8},{24,16},{1,9},{25,17},{2,10},{26,18},{3,11},{27,19},{4,12},{... | collective-permute-start | bytes 2064392 | tf_op jit(solution)/shard_map/ppermute | solution.py:266
  41.9 15.1 %copy-start.15 = (bf16[192,1792]{1,0:T(8,128)(2,1)}, bf16[192,1792]{1,0:T(8,128)(2,1)S(1)}, u32[]{:S(2)}) copy-start(bf16[192,1792]{1,0:T(8,128)(2,1)S(1)} %collective-permute-done.3.refs_1_) | copy-start | bytes 2064388
  42.1 14.9 %collective-permute-start.5 = (bf16[192,1792]{1,0:T(8,128)(2,1)S(1)}, bf16[192,1792]{1,0:T(8,128)(2,1)S(1)}, u32[]{:S(2)}, u32[]{:S(2)}) collective-permute-start(bf16[192,1792]{1,0:T(8,128)(2,1)S(1)} %add_convert_fusion.19), channel_id=1, source_target_pairs={{8,16},{16,8},{9,17},{17,9},{10,18},{18,10},{11,19},{19,11},{12,20... | collective-permute-start | bytes 2064392 | tf_op jit(solution)/shard_map/ppermute | solution.py:266
  61.5 16.2 %copy-start.29 = (f32[1792]{0:T(1024)S(1)}, f32[1792]{0:T(1024)}, u32[]{:S(2)}) copy-start(f32[1792]{0:T(1024)} %param.7) | copy-start | bytes 21508
  70.4 25.6 %collective-permute-start.6 = (bf16[192,1792]{1,0:T(8,128)(2,1)S(1)}, bf16[192,1792]{1,0:T(8,128)(2,1)S(1)}, u32[]{:S(2)}, u32[]{:S(2)}) collective-permute-start(bf16[192,1792]{1,0:T(8,128)(2,1)S(1)} %shard_map.86.refs_0_), channel_id=1, source_target_pairs={{0,8},{24,16},{1,9},{25,17},{2,10},{26,18},{3,11},{27,19},{4,12},{... | collective-permute-start | bytes 2064392 | tf_op jit(solution)/shard_map/ppermute | solution.py:266
  77.8 19.3 %collective-permute-start.4 = (bf16[192,1792]{1,0:T(8,128)(2,1)}, bf16[192,1792]{1,0:T(8,128)(2,1)S(1)}, u32[]{:S(2)}, u32[]{:S(2)}) collective-permute-start(bf16[192,1792]{1,0:T(8,128)(2,1)} %add_convert_fusion.18), channel_id=1, source_target_pairs={{8,16},{16,8},{9,17},{17,9},{10,18},{18,10},{11,19},{19,11},{12,20... | collective-permute-start | bytes 2064392 | tf_op jit(solution)/shard_map/ppermute | solution.py:266
  78.5 20.1 %collective-permute-start.7 = (bf16[192,1792]{1,0:T(8,128)(2,1)}, bf16[192,1792]{1,0:T(8,128)(2,1)S(1)}, u32[]{:S(2)}, u32[]{:S(2)}) collective-permute-start(bf16[192,1792]{1,0:T(8,128)(2,1)} %add_convert_fusion.17), channel_id=1, source_target_pairs={{16,24},{8,0},{17,25},{9,1},{18,26},{10,2},{19,27},{11,3},{20,28},... | collective-permute-start | bytes 2064392 | tf_op jit(solution)/shard_map/ppermute | solution.py:266
  91.3 16.3 %collective-permute-start.9 = (bf16[192,1792]{1,0:T(8,128)(2,1)S(1)}, bf16[192,1792]{1,0:T(8,128)(2,1)S(1)}, u32[]{:S(2)}, u32[]{:S(2)}) collective-permute-start(bf16[192,1792]{1,0:T(8,128)(2,1)S(1)} %get-tuple-element.120.refs_0_), channel_id=1, source_target_pairs={{0,8},{24,16},{1,9},{25,17},{2,10},{26,18},{3,11},{27,19},{4,12},{... | collective-permute-start | bytes 2064392 | tf_op jit(solution)/shard_map/ppermute | solution.py:266
  96.2 20.5 %collective-permute-start.8 = (bf16[192,1792]{1,0:T(8,128)(2,1)S(1)}, bf16[192,1792]{1,0:T(8,128)(2,1)S(1)}, u32[]{:S(2)}, u32[]{:S(2)}) collective-permute-start(bf16[192,1792]{1,0:T(8,128)(2,1)S(1)} %add_convert_fusion.16), channel_id=1, source_target_pairs={{8,16},{16,8},{9,17},{17,9},{10,18},{18,10},{11,19},{19,11},{12,20... | collective-permute-start | bytes 2064392 | tf_op jit(solution)/shard_map/ppermute | solution.py:266
  97.2 21.9 %collective-permute-start.10 = (bf16[192,1792]{1,0:T(8,128)(2,1)S(1)}, bf16[192,1792]{1,0:T(8,128)(2,1)S(1)}, u32[]{:S(2)}, u32[]{:S(2)}) collective-permute-start(bf16[192,1792]{1,0:T(8,128)(2,1)S(1)} %add_convert_fusion.15), channel_id=1, source_target_pairs={{16,24},{8,0},{17,25},{9,1},{18,26},{10,2},{19,27},{11,3},{20,28},... | collective-permute-start | bytes 2064392 | tf_op jit(solution)/shard_map/ppermute | solution.py:266
  107.7 10.2 %copy-start.9 = (bf16[192,1792]{1,0:T(8,128)(2,1)}, bf16[192,1792]{1,0:T(8,128)(2,1)S(1)}, u32[]{:S(2)}) copy-start(bf16[192,1792]{1,0:T(8,128)(2,1)S(1)} %collective-permute-done.9.refs_1_) | copy-start | bytes 2064388
  108.7 10.4 %copy-start.20 = (bf16[192,1792]{1,0:T(8,128)(2,1)S(1)}, bf16[192,1792]{1,0:T(8,128)(2,1)}, u32[]{:S(2)}) copy-start(bf16[192,1792]{1,0:T(8,128)(2,1)} %copy-done.19) | copy-start | bytes 2064388
  108.7 32.0 %collective-permute-start.14 = (bf16[192,1792]{1,0:T(8,128)(2,1)}, bf16[192,1792]{1,0:T(8,128)(2,1)}, u32[]{:S(2)}, u32[]{:S(2)}) collective-permute-start(bf16[192,1792]{1,0:T(8,128)(2,1)} %add_convert_fusion.14), channel_id=1, source_target_pairs={{8,16},{16,8},{9,17},{17,9},{10,18},{18,10},{11,19},{19,11},{12,20... | collective-permute-start | bytes 2064392 | tf_op jit(solution)/shard_map/ppermute | solution.py:266
  110.4 30.1 %collective-permute-start.11 = (bf16[192,1792]{1,0:T(8,128)(2,1)S(1)}, bf16[192,1792]{1,0:T(8,128)(2,1)S(1)}, u32[]{:S(2)}, u32[]{:S(2)}) collective-permute-start(bf16[192,1792]{1,0:T(8,128)(2,1)S(1)} %get-tuple-element.127.refs_0_), channel_id=1, source_target_pairs={{0,8},{24,16},{1,9},{25,17},{2,10},{26,18},{3,11},{27,19},{4,12},{... | collective-permute-start | bytes 2064392 | tf_op jit(solution)/shard_map/ppermute | solution.py:266
  117.9 26.2 %collective-permute-start.15 = (bf16[192,1792]{1,0:T(8,128)(2,1)}, bf16[192,1792]{1,0:T(8,128)(2,1)}, u32[]{:S(2)}, u32[]{:S(2)}) collective-permute-start(bf16[192,1792]{1,0:T(8,128)(2,1)} %add_convert_fusion.13), channel_id=1, source_target_pairs={{16,24},{8,0},{17,25},{9,1},{18,26},{10,2},{19,27},{11,3},{20,28},... | collective-permute-start | bytes 2064392 | tf_op jit(solution)/shard_map/ppermute | solution.py:266
  135.1 34.0 %collective-permute-start.13 = (bf16[192,1792]{1,0:T(8,128)(2,1)S(1)}, bf16[192,1792]{1,0:T(8,128)(2,1)S(1)}, u32[]{:S(2)}, u32[]{:S(2)}) collective-permute-start(bf16[192,1792]{1,0:T(8,128)(2,1)S(1)} %shard_map.90.refs_0_), channel_id=1, source_target_pairs={{0,8},{24,16},{1,9},{25,17},{2,10},{26,18},{3,11},{27,19},{4,12},{... | collective-permute-start | bytes 2064392 | tf_op jit(solution)/shard_map/ppermute | solution.py:266
  142.1 30.3 %collective-permute-start.16 = (bf16[192,1792]{1,0:T(8,128)(2,1)S(1)}, bf16[192,1792]{1,0:T(8,128)(2,1)S(1)}, u32[]{:S(2)}, u32[]{:S(2)}) collective-permute-start(bf16[192,1792]{1,0:T(8,128)(2,1)S(1)} %add_convert_fusion.11), channel_id=1, source_target_pairs={{16,24},{8,0},{17,25},{9,1},{18,26},{10,2},{19,27},{11,3},{20,28},... | collective-permute-start | bytes 2064392 | tf_op jit(solution)/shard_map/ppermute | solution.py:266
  143.4 26.7 %collective-permute-start.12 = (bf16[192,1792]{1,0:T(8,128)(2,1)S(1)}, bf16[192,1792]{1,0:T(8,128)(2,1)S(1)}, u32[]{:S(2)}, u32[]{:S(2)}) collective-permute-start(bf16[192,1792]{1,0:T(8,128)(2,1)S(1)} %add_convert_fusion.12), channel_id=1, source_target_pairs={{8,16},{16,8},{9,17},{17,9},{10,18},{18,10},{11,19},{19,11},{12,20... | collective-permute-start | bytes 2064392 | tf_op jit(solution)/shard_map/ppermute | solution.py:266
  149.8 12.9 %copy-start.23 = (f32[192,1792]{1,0:T(8,128)}, f32[192,1792]{1,0:T(8,128)S(1)}, u32[]{:S(2)}) copy-start(f32[192,1792]{1,0:T(8,128)S(1)} %get-tuple-element.136.slope_ref) | copy-start | bytes 4128772
  162.7 26.4 %collective-permute-start.18 = (bf16[192,1792]{1,0:T(8,128)(2,1)S(1)}, bf16[192,1792]{1,0:T(8,128)(2,1)S(1)}, u32[]{:S(2)}, u32[]{:S(2)}) collective-permute-start(bf16[192,1792]{1,0:T(8,128)(2,1)S(1)} %get-tuple-element.142.refs_0_), channel_id=1, source_target_pairs={{0,8},{24,16},{1,9},{25,17},{2,10},{26,18},{3,11},{27,19},{4,12},{... | collective-permute-start | bytes 2064392 | tf_op jit(solution)/shard_map/ppermute | solution.py:266
  170.2 30.5 %collective-permute-start.19 = (bf16[192,1792]{1,0:T(8,128)(2,1)S(1)}, bf16[192,1792]{1,0:T(8,128)(2,1)S(1)}, u32[]{:S(2)}, u32[]{:S(2)}) collective-permute-start(bf16[192,1792]{1,0:T(8,128)(2,1)S(1)} %add_convert_fusion.9), channel_id=1, source_target_pairs={{16,24},{8,0},{17,25},{9,1},{18,26},{10,2},{19,27},{11,3},{20,28},... | collective-permute-start | bytes 2064392 | tf_op jit(solution)/shard_map/ppermute | solution.py:266
  171.7 27.5 %collective-permute-start.17 = (bf16[192,1792]{1,0:T(8,128)(2,1)}, bf16[192,1792]{1,0:T(8,128)(2,1)S(1)}, u32[]{:S(2)}, u32[]{:S(2)}) collective-permute-start(bf16[192,1792]{1,0:T(8,128)(2,1)} %add_convert_fusion.10), channel_id=1, source_target_pairs={{8,16},{16,8},{9,17},{17,9},{10,18},{18,10},{11,19},{19,11},{12,20... | collective-permute-start | bytes 2064392 | tf_op jit(solution)/shard_map/ppermute | solution.py:266
  189.3 28.9 %collective-permute-start.23 = (bf16[192,1792]{1,0:T(8,128)(2,1)S(1)}, bf16[192,1792]{1,0:T(8,128)(2,1)S(1)}, u32[]{:S(2)}, u32[]{:S(2)}) collective-permute-start(bf16[192,1792]{1,0:T(8,128)(2,1)S(1)} %add_convert_fusion.8), channel_id=1, source_target_pairs={{8,16},{16,8},{9,17},{17,9},{10,18},{18,10},{11,19},{19,11},{12,20... | collective-permute-start | bytes 2064392 | tf_op jit(solution)/shard_map/ppermute | solution.py:266
  190.1 27.0 %collective-permute-start.21 = (bf16[192,1792]{1,0:T(8,128)(2,1)S(1)}, bf16[192,1792]{1,0:T(8,128)(2,1)S(1)}, u32[]{:S(2)}, u32[]{:S(2)}) collective-permute-start(bf16[192,1792]{1,0:T(8,128)(2,1)S(1)} %get-tuple-element.148.refs_0_), channel_id=1, source_target_pairs={{0,8},{24,16},{1,9},{25,17},{2,10},{26,18},{3,11},{27,19},{4,12},{... | collective-permute-start | bytes 2064392 | tf_op jit(solution)/shard_map/ppermute | solution.py:266
  199.1 17.7 %collective-permute-start.20 = (bf16[96,3584]{1,0:T(8,128)(2,1)S(1)}, bf16[96,3584]{1,0:T(8,128)(2,1)S(1)}, u32[]{:S(2)}, u32[]{:S(2)}) collective-permute-start(bf16[96,3584]{1,0:T(8,128)(2,1)S(1)} %get-tuple-element.131), channel_id=1, source_target_pairs={{0,1},{1,0},{2,3},{3,2},{4,5},{5,4},{6,7},{7,6},{8,9},{9,8},{10,11... | collective-permute-start | bytes 2064392 | tf_op jit(solution)/shard_map/ppermute | solution.py:269
  199.4 20.3 %collective-permute-start.24 = (bf16[192,1792]{1,0:T(8,128)(2,1)S(1)}, bf16[192,1792]{1,0:T(8,128)(2,1)S(1)}, u32[]{:S(2)}, u32[]{:S(2)}) collective-permute-start(bf16[192,1792]{1,0:T(8,128)(2,1)S(1)} %add_convert_fusion.7), channel_id=1, source_target_pairs={{16,24},{8,0},{17,25},{9,1},{18,26},{10,2},{19,27},{11,3},{20,28},... | collective-permute-start | bytes 2064392 | tf_op jit(solution)/shard_map/ppermute | solution.py:266
  204.5 12.3 %copy-start.27 = (f32[192,1792]{1,0:T(8,128)}, f32[192,1792]{1,0:T(8,128)S(1)}, u32[]{:S(2)}) copy-start(f32[192,1792]{1,0:T(8,128)S(1)} %get-tuple-element.147.slope_ref) | copy-start | bytes 4128772
  217.2 14.5 %collective-permute-start.22 = (bf16[192,1792]{1,0:T(8,128)(2,1)S(1)}, bf16[192,1792]{1,0:T(8,128)(2,1)S(1)}, u32[]{:S(2)}, u32[]{:S(2)}) collective-permute-start(bf16[192,1792]{1,0:T(8,128)(2,1)S(1)} %add_convert_fusion.5), channel_id=1, source_target_pairs={{8,16},{16,8},{9,17},{17,9},{10,18},{18,10},{11,19},{19,11},{12,20... | collective-permute-start | bytes 2064392 | tf_op jit(solution)/shard_map/ppermute | solution.py:266
  218.4 22.2 %collective-permute-start.25 = (bf16[192,1792]{1,0:T(8,128)(2,1)S(1)}, bf16[192,1792]{1,0:T(8,128)(2,1)S(1)}, u32[]{:S(2)}, u32[]{:S(2)}) collective-permute-start(bf16[192,1792]{1,0:T(8,128)(2,1)S(1)} %add_convert_fusion.4), channel_id=1, source_target_pairs={{16,24},{8,0},{17,25},{9,1},{18,26},{10,2},{19,27},{11,3},{20,28},... | collective-permute-start | bytes 2064392 | tf_op jit(solution)/shard_map/ppermute | solution.py:266
  231.7 8.9 %copy-start.26 = (f32[192,1792]{1,0:T(8,128)S(1)}, f32[192,1792]{1,0:T(8,128)}, u32[]{:S(2)}) copy-start(f32[192,1792]{1,0:T(8,128)} %copy-done.25) | copy-start | bytes 4128772
  231.9 33.5 %collective-permute-start.26 = (bf16[192,1792]{1,0:T(8,128)(2,1)S(1)}, bf16[192,1792]{1,0:T(8,128)(2,1)S(1)}, u32[]{:S(2)}, u32[]{:S(2)}) collective-permute-start(bf16[192,1792]{1,0:T(8,128)(2,1)S(1)} %add_convert_fusion.3), channel_id=1, source_target_pairs={{16,24},{8,0},{17,25},{9,1},{18,26},{10,2},{19,27},{11,3},{20,28},... | collective-permute-start | bytes 2064392 | tf_op jit(solution)/shard_map/ppermute | solution.py:266
  252.8 12.6 %copy-start.28 = (f32[192,1792]{1,0:T(8,128)S(1)}, f32[192,1792]{1,0:T(8,128)}, u32[]{:S(2)}) copy-start(f32[192,1792]{1,0:T(8,128)} %copy-done.27) | copy-start | bytes 4128772
  264.8 4.3 %collective-permute-start.27 = (bf16[96,3584]{1,0:T(8,128)(2,1)S(1)}, bf16[96,3584]{1,0:T(8,128)(2,1)S(1)}, u32[]{:S(2)}, u32[]{:S(2)}) collective-permute-start(bf16[96,3584]{1,0:T(8,128)(2,1)S(1)} %get-tuple-element.151), channel_id=1, source_target_pairs={{0,1},{1,0},{2,3},{3,2},{4,5},{5,4},{6,7},{7,6},{8,9},{9,8},{10,11... | collective-permute-start | bytes 2064392 | tf_op jit(solution)/shard_map/ppermute | solution.py:269
  264.9 6.9 %collective-permute-start.29 = (bf16[96,3584]{1,0:T(8,128)(2,1)S(1)}, bf16[96,3584]{1,0:T(8,128)(2,1)S(1)}, u32[]{:S(2)}, u32[]{:S(2)}) collective-permute-start(bf16[96,3584]{1,0:T(8,128)(2,1)S(1)} %get-tuple-element.154), channel_id=1, source_target_pairs={{0,1},{1,0},{2,3},{3,2},{4,5},{5,4},{6,7},{7,6},{8,9},{9,8},{10,11... | collective-permute-start | bytes 2064392 | tf_op jit(solution)/shard_map/ppermute | solution.py:269
  269.2 42.4 %collective-permute-start.28 = (bf16[96,3584]{1,0:T(8,128)(2,1)S(1)}, bf16[96,3584]{1,0:T(8,128)(2,1)S(1)}, u32[]{:S(2)}, u32[]{:S(2)}) collective-permute-start(bf16[96,3584]{1,0:T(8,128)(2,1)S(1)} %add_convert_fusion.2), channel_id=1, source_target_pairs={{0,6},{1,7},{2,4},{3,5},{4,2},{5,3},{6,0},{7,1},{8,14},{9,15},{10,... | collective-permute-start | bytes 2064392 | tf_op jit(solution)/shard_map/ppermute | solution.py:269
  272.0 39.7 %collective-permute-start.30 = (bf16[96,3584]{1,0:T(8,128)(2,1)S(1)}, bf16[96,3584]{1,0:T(8,128)(2,1)S(1)}, u32[]{:S(2)}, u32[]{:S(2)}) collective-permute-start(bf16[96,3584]{1,0:T(8,128)(2,1)S(1)} %add_convert_fusion.1), channel_id=1, source_target_pairs={{0,2},{1,3},{2,0},{3,1},{4,6},{5,7},{6,4},{7,5},{8,10},{9,11},{10,... | collective-permute-start | bytes 2064392 | tf_op jit(solution)/shard_map/ppermute | solution.py:269
  272.6 12.1 %collective-permute-start.35 = (f32[1792]{0:T(1024)S(1)}, f32[1792]{0:T(1024)S(1)}, u32[]{:S(2)}, u32[]{:S(2)}) collective-permute-start(f32[1792]{0:T(1024)S(1)} %add_reduce_fusion), channel_id=1, source_target_pairs={{0,8},{8,0},{16,24},{24,16},{1,9},{9,1},{17,25},{25,17},{2,10},{10... | collective-permute-start | bytes 21512 | tf_op jit(solution)/shard_map/ppermute | solution.py:380
  278.0 14.1 %collective-permute-start.31 = (bf16[96,1536]{1,0:T(8,128)(2,1)S(1)}, bf16[96,1536]{1,0:T(8,128)(2,1)S(1)}, u32[]{:S(2)}, u32[]{:S(2)}) collective-permute-start(bf16[96,1536]{1,0:T(8,128)(2,1)S(1)} %get-tuple-element.161), channel_id=1, source_target_pairs={{0,1},{1,0},{2,3},{3,2},{4,5},{5,4},{6,7},{7,6},{8,9},{9,8},{10,11... | collective-permute-start | bytes 884744 | tf_op jit(solution)/shard_map/ppermute | solution.py:269
  284.1 13.9 %collective-permute-start.33 = (bf16[96,2048]{1,0:T(8,128)(2,1)S(1)}, bf16[96,2048]{1,0:T(8,128)(2,1)S(1)}, u32[]{:S(2)}, u32[]{:S(2)}) collective-permute-start(bf16[96,2048]{1,0:T(8,128)(2,1)S(1)} %get-tuple-element.164), channel_id=1, source_target_pairs={{0,1},{1,0},{2,3},{3,2},{4,5},{5,4},{6,7},{7,6},{8,9},{9,8},{10,11... | collective-permute-start | bytes 1179656 | tf_op jit(solution)/shard_map/ppermute | solution.py:269
  284.7 6.8 %collective-permute-start.36 = (f32[1792]{0:T(1024)S(1)}, f32[1792]{0:T(1024)S(1)}, u32[]{:S(2)}, u32[]{:S(2)}) collective-permute-start(f32[1792]{0:T(1024)S(1)} %add.120), channel_id=1, source_target_pairs={{0,16},{8,24},{16,0},{24,8},{1,17},{9,25},{17,1},{25,9},{2,18},{10... | collective-permute-start | bytes 21512 | tf_op jit(solution)/shard_map/ppermute | solution.py:380
  292.1 19.5 %collective-permute-start.32 = (bf16[96,1536]{1,0:T(8,128)(2,1)S(1)}, bf16[96,1536]{1,0:T(8,128)(2,1)S(1)}, u32[]{:S(2)}, u32[]{:S(2)}) collective-permute-start(bf16[96,1536]{1,0:T(8,128)(2,1)S(1)} %add_convert_fusion.21), channel_id=1, source_target_pairs={{0,4},{1,5},{2,6},{3,7},{4,0},{5,1},{6,2},{7,3},{8,12},{9,13},{10,... | collective-permute-start | bytes 884744 | tf_op jit(solution)/shard_map/ppermute | solution.py:269
  298.1 13.6 %collective-permute-start.34 = (bf16[96,2048]{1,0:T(8,128)(2,1)S(1)}, bf16[96,2048]{1,0:T(8,128)(2,1)S(1)}, u32[]{:S(2)}, u32[]{:S(2)}) collective-permute-start(bf16[96,2048]{1,0:T(8,128)(2,1)S(1)} %add_convert_fusion.20), channel_id=1, source_target_pairs={{0,4},{1,5},{2,6},{3,7},{4,0},{5,1},{6,2},{7,3},{8,12},{9,13},{10,... | collective-permute-start | bytes 1179656 | tf_op jit(solution)/shard_map/ppermute | solution.py:269
  (21 other events, 62.5 us)
Sparse Core Ops, SparseCore 0:
  9.9 44.9 all-gather.2
  70.5 46.3 all-gather.4

commit v4 on v3

v4 whole, which is shorter than its diff:
```python
import functools

import jax
import jax.numpy as jnp
from jax import lax
from jax.experimental import pallas as pl
from jax.experimental.pallas import tpu as pltpu
from jax.sharding import PartitionSpec as P

GELU_SCALE = 0.7978845608
GELU_CUBIC = 0.044715
F32, BF16 = jnp.float32, jnp.bfloat16
VMEM_LIMIT = 48 * 1024 * 1024
UNITS, AHEAD = 7, 3


def dot(left, right, dims):
    return lax.dot_general(left, right, ((dims[:1], dims[1:]), ((), ())), preferred_element_type=F32)


def call(kernel, flops, moved, place, operands, grid, in_specs, out_specs, out_shape, into=(), outs=(), scratch=()):
    scalars = 1
    aliases = {}
    in_specs, operands = list(in_specs), list(operands)
    for array, out in zip(into, outs):
        if array is not None:
            aliases[scalars + len(operands)] = out
            operands.append(array)
            in_specs.append(pl.BlockSpec(memory_space=pl.ANY))
    return pl.pallas_call(
        kernel,
        grid_spec=pltpu.PrefetchScalarGridSpec(
            num_scalar_prefetch=scalars,
            grid=grid,
            in_specs=in_specs,
            out_specs=out_specs,
            scratch_shapes=list(scratch),
        ),
        out_shape=out_shape,
        input_output_aliases=aliases,
        compiler_params=pltpu.CompilerParams(vmem_limit_bytes=VMEM_LIMIT),
        cost_estimate=pl.CostEstimate(flops=flops, bytes_accessed=moved, transcendentals=0),
    )(place, *operands)


def whole(shape):
    return pl.BlockSpec(shape, lambda i, s: (0,) * len(shape), pipeline_mode=pl.Buffered(1))


def chip_block(rows, columns, key):
    return pl.BlockSpec((rows, columns), lambda i, s: (s[0] ^ key, 0))


def streamed(place, blocks, weight, pieces, dims, flops, write, out_shape):
    axis, first, last = pieces
    size = weight.shape[axis] // UNITS
    count = last - first
    arrays = []
    for block in blocks:
        for array, _, _ in block:
            if not any(array is other for other in arrays):
                arrays.append(array)
    rows, depth = sum(part[2] for part in blocks[0]), blocks[0][0][0].shape[1]
    parts = sum(len(block) for block in blocks)
    shape = (size, weight.shape[1]) if axis == 0 else (weight.shape[0], size)

    def kernel(s, *refs):
        sources, weight_ref = refs[: len(arrays)], refs[len(arrays)]
        outs, (block_ref, piece_ref, block_sem, piece_sem) = refs[len(arrays) + 1 : -4], refs[-4:]

        def piece(at):
            where = pl.ds(pl.multiple_of((first + at) * size, size), size)
            source = weight_ref.at[where, :] if axis == 0 else weight_ref.at[:, where]
            return pltpu.make_async_copy(source, piece_ref.at[at], piece_sem.at[at])

        copies = []
        for at, block in enumerate(blocks):
            for array, start, length, into in block_rows(s, block):
                source = next(ref for ref, other in zip(sources, arrays) if other is array)
                copies.append(
                    pltpu.make_async_copy(
                        source.at[pl.ds(pl.multiple_of(start, 16), length), :],
                        block_ref.at[at, pl.ds(pl.multiple_of(into, 16), length), :],
                        block_sem.at[len(copies)],
                    )
                )
        piece(0).start()
        for copy in copies:
            copy.start()
        for at in range(1, min(AHEAD, count)):
            piece(at).start()
        for copy in copies:
            copy.wait()

        def step(at, carry):
            piece(at).wait()

            @pl.when(at + AHEAD < count)
            def _():
                piece(at + AHEAD).start()

            for block in range(len(blocks)):
                write(s, block, at, dot(block_ref[block], piece_ref[at], dims), outs)
            return carry

        lax.fori_loop(0, count, step, 0)

    def block_rows(s, block):
        into = 0
        for array, start, length in block:
            yield array, start(s), length, (into if len(block) == 1 else start_of(s, into // length) * length)
            into += length

    def start_of(s, at):
        return s[1] if at == 0 else 1 - s[1]

    moved = 2 * (len(blocks) * rows * depth + shape[0] * shape[1] * count)
    anywhere = pl.BlockSpec(memory_space=pl.ANY)
    return call(
        kernel,
        flops,
        moved,
        place,
        [*arrays, weight],
        (1,),
        [anywhere] * (len(arrays) + 1),
        [whole(out.shape) for out in out_shape],
        out_shape,
        scratch=[
            pltpu.VMEM((len(blocks), rows, depth), BF16),
            pltpu.VMEM((count, *shape), BF16),
            pltpu.SemaphoreType.DMA((parts,)),
            pltpu.SemaphoreType.DMA((count,)),
        ],
    )


def columns_of(at, size):
    return pl.ds(pl.multiple_of(at * size, size), size)


def partials(place, blocks, weight, transposed):
    hidden = weight.shape[0 if transposed else 1]
    rows = sum(part[2] for part in blocks[0])
    width = hidden // UNITS

    def write(s, block, at, product, outs):
        outs[block][:, columns_of(at, width)] = product.astype(BF16)

    return streamed(
        place,
        blocks,
        weight,
        (0 if transposed else 1, 0, UNITS),
        (1, 1) if transposed else (1, 0),
        2 * len(blocks) * rows * weight.size,
        write,
        [jax.ShapeDtypeStruct((rows, hidden), BF16)] * len(blocks),
    )


def token_grad(place, grad, weight_in, keys, rows, first, last):
    depth, hidden = weight_in.shape
    tile = depth // UNITS
    half = rows // 2

    def write(s, block, at, product, outs):
        product = product.astype(BF16)
        low = s[1] == 0
        place_of = (slice(block * half, (block + 1) * half), columns_of(at, tile))
        outs[0][place_of] = jnp.where(low, product[:half], product[half:])
        outs[1][place_of] = jnp.where(low, product[half:], product[:half])

    return streamed(
        place,
        [[(grad, lambda s, key=key: (s[0] ^ key) * rows, rows)] for key in keys],
        weight_in,
        (0, first, last),
        (1, 1),
        2 * len(keys) * rows * tile * (last - first) * hidden,
        write,
        [jax.ShapeDtypeStruct((len(keys) * half, tile * (last - first)), BF16)] * 2,
    )


def activate(place, terms, bias, key, into, tokens):
    rows, hidden = terms[0].shape

    def kernel(s, bias_ref, *refs):
        ins, (act_ref, slope_ref) = refs[: len(terms)], refs[-2:]
        pre = functools.reduce(jnp.add, [ref[...].astype(F32) for ref in ins]) + bias_ref[...]
        tangent = jnp.tanh(GELU_SCALE * (pre + GELU_CUBIC * pre * pre * pre))
        act_ref[...] = (0.5 * pre * (1.0 + tangent)).astype(BF16)
        slope_ref[...] = 0.5 * (1.0 + tangent) + 0.5 * pre * (1.0 - tangent * tangent) * GELU_SCALE * (
            1.0 + 3.0 * GELU_CUBIC * pre * pre
        )

    block = pl.BlockSpec((rows, hidden), lambda i, s: (0, 0))
    return call(
        kernel,
        30 * rows * hidden,
        rows * hidden * (2 * len(terms) + 6),
        place,
        [bias, *terms],
        (1,),
        [pl.BlockSpec((1, hidden), lambda i, s: (0, 0))] + [block] * len(terms),
        [chip_block(rows, hidden, key), block],
        [jax.ShapeDtypeStruct((tokens, hidden), BF16), jax.ShapeDtypeStruct((rows, hidden), F32)],
        [into],
        [0],
    )


def differentiate(place, terms, slope, key, into, tokens):
    rows, hidden = slope.shape

    def kernel(s, slope_ref, *refs):
        ins, (grad_ref, sum_ref) = refs[: len(terms)], refs[-2:]
        grad = functools.reduce(jnp.add, [ref[...].astype(F32) for ref in ins]) * slope_ref[...]
        grad = grad.astype(BF16)
        grad_ref[...] = grad
        sum_ref[...] = jnp.sum(grad.astype(F32), axis=0, keepdims=True)

    block = pl.BlockSpec((rows, hidden), lambda i, s: (0, 0))
    return call(
        kernel,
        8 * rows * hidden,
        rows * hidden * (2 * len(terms) + 6),
        place,
        [slope, *terms],
        (1,),
        [block] * (1 + len(terms)),
        [chip_block(rows, hidden, key), pl.BlockSpec((1, hidden), lambda i, s: (0, 0))],
        [jax.ShapeDtypeStruct((tokens, hidden), BF16), jax.ShapeDtypeStruct((1, hidden), F32)],
        [into],
        [0],
    )


def add_bf16(left, right):
    return (left.astype(F32) + right.astype(F32)).astype(BF16)


def weight_out_grad(place, act, grad, into, first, count):
    tokens, depth = grad.shape
    hidden = act.shape[1]
    tile, width = depth // UNITS, hidden // UNITS

    def kernel(s, act_ref, grad_ref, *refs):
        out, turned = refs[-2:]

        @pl.when(pl.program_id(0) == 0)
        def _():
            for at in range(0, hidden, width):
                turned[at : at + width, :] = act_ref[:, at : at + width].T

        for at in range(0, hidden, hidden // 2):
            out[at : at + hidden // 2, :] = dot(turned[at : at + hidden // 2, :], grad_ref[...], (1, 0))

    return call(
        kernel,
        2 * tokens * tile * count * hidden,
        2 * tokens * (tile * count + hidden) + 4 * tile * count * hidden,
        place,
        [act, grad],
        (count,),
        [whole((tokens, hidden)), pl.BlockSpec((tokens, tile), lambda j, s: (0, first + j))],
        pl.BlockSpec((hidden, tile), lambda j, s: (0, first + j)),
        jax.ShapeDtypeStruct((hidden, depth), F32),
        [into],
        [0],
        [pltpu.VMEM((hidden, tokens), BF16)],
    )


def weight_in_grad(place, tok, grad, into, first, count):
    tokens, depth = tok.shape
    hidden = grad.shape[1]
    tile, width = depth // UNITS, hidden // 2

    def kernel(s, tok_ref, grad_ref, *refs):
        turned = tok_ref[...].T
        for at in range(0, hidden, width):
            refs[-1][:, at : at + width] = dot(turned, grad_ref[:, at : at + width], (1, 0))

    return call(
        kernel,
        2 * tokens * tile * count * hidden,
        2 * tokens * (tile * count + hidden) + 4 * tile * count * hidden,
        place,
        [tok, grad],
        (count,),
        [pl.BlockSpec((tokens, tile), lambda j, s: (0, first + j)), whole((tokens, hidden))],
        pl.BlockSpec((tile, hidden), lambda j, s: (first + j, 0)),
        jax.ShapeDtypeStruct((depth, hidden), F32),
        [into],
        [0],
    )


def after(value, *deps):
    return lax.optimization_barrier((value, *deps))[0]


def local(rows_of, cols_of, tokens, weight_in, bias_hidden, weight_out, out_grad):
    mine, depth = tokens.shape
    hidden = bias_hidden.shape[0]
    rows, everyone = 2 * mine, cols_of * mine
    bias = bias_hidden.reshape(1, hidden)
    steps = rows_of - 1
    me = lax.axis_index("col")
    place = jnp.stack([me // 2, me % 2]).astype(jnp.int32)
    others = sorted(range(1, cols_of // 2), key=lambda key: (-key.bit_count(), key))
    chunks = [("pre", 0), ("act", 0)] + [(kind, key) for kind in ("pre", "act") for key in others]
    total = len(chunks)

    def send(value, step):
        pairs = [(step - 1, step), (rows_of - step, rows_of - step - 1)]
        return lax.ppermute(value, "row", pairs)

    def swap(value, bits):
        return lax.ppermute(value, "col", [(i, i ^ bits) for i in range(cols_of)])

    chain = []

    def link(value):
        return after(value, chain[-1]) if chain else value

    own, ahead = {}, {}
    got = {chunk: [None] * steps for chunk in chunks}
    held = {}
    slopes, sums, arrived = {}, {}, []

    def compute_own(kind, keys):
        source, weight = (tokens, weight_in) if kind == "pre" else (out_grad, weight_out)
        if keys == [0]:
            first = lambda s: 0
            blocks = [[(link(source), first, mine), (held["pair", kind], first, mine)]]
        else:
            gathered = link(held[kind])
            blocks = [[(gathered, lambda s, key=key: (s[0] ^ key) * rows, rows)] for key in keys]
        outs = partials(place, blocks, weight, kind == "act")
        chain.append(outs[0])
        for key, out in zip(keys, outs):
            own[kind, key] = out

    def first_send(at):
        got[chunks[at]][0] = send(link(own[chunks[at]]), 1)

    def forward(at, step):
        chunk = chunks[at]
        payload = add_bf16(got[chunk][step - 2], link(own[chunk]))
        chain.append(payload)
        ahead.setdefault(chunk, payload)
        got[chunk][step - 1] = send(payload, step)

    def finish(at):
        kind, key = chunk = chunks[at]
        terms = [link(ahead[chunk])] + got[chunk][1:]
        if kind == "pre":
            held["activations"], slopes[key] = activate(place, terms, bias, key, held.get("activations"), everyone)
            chain.append(held["activations"])
        else:
            held["grads"], sums[key] = differentiate(place, terms, slopes[key], key, held.get("grads"), everyone)
            chain.append(held["grads"])

    def out_columns(first, count):
        held["out"] = weight_out_grad(
            place, link(held["activations"]), held["act"], held.get("out"), first, count
        )
        chain.append(held["out"])

    def in_rows(first, count):
        held["in"] = weight_in_grad(place, held["pre"], link(held["grads"]), held.get("in"), first, count)
        chain.append(held["in"])

    def tokens_of(keys, first, last):
        keep, give = token_grad(place, link(held["grads"]), weight_in, keys, rows, first, last)
        chain.append(keep)
        return keys, keep, swap(give, 1)

    def deliver(parts):
        keys, keep, given = parts
        results = []
        for at, key in enumerate(keys):
            block = slice(at * mine, (at + 1) * mine)
            pair = add_bf16(link(keep)[block], given[block])
            results.append(swap(pair, 2 * key) if key else pair)
        chain.append(pair)
        return results

    held["pair", "pre"], held["pair", "act"] = swap(tokens, 1), swap(out_grad, 1)
    held["pre"] = lax.all_gather(tokens, "col", axis=0, tiled=True)
    held["act"] = lax.all_gather(after(out_grad, held["pair", "pre"]), "col", axis=0, tiled=True)
    compute_own("pre", [0])
    first_send(0)
    compute_own("act", [0])
    first_send(1)
    end = total + steps - 1
    for slot in range(end):
        if 3 <= slot + 1 < total:
            first_send(slot + 1)
        late = slot == 2
        order = range(steps, 1, -1) if late else range(2, steps + 1)
        if late and slot >= steps - 1:
            finish(slot - steps + 1)
        for step in order:
            if 0 <= slot - step + 2 < total:
                forward(slot - step + 2, step)
        if slot == 1:
            compute_own("pre", others)
            first_send(2)
        if not late and slot >= steps - 1:
            finish(slot - steps + 1)
        if slot == len(others):
            compute_own("act", others)
        if slot == end - 4:
            out_columns(0, 4)
        if slot == end - 3:
            early = tokens_of([0] + others[:-2], 0, UNITS)
        if slot == end - 2:
            out_columns(4, UNITS - 4)
    arrived += deliver(early)
    front = UNITS // 2
    parts = [tokens_of(others[-2:], 0, front), tokens_of(others[-2:], front, UNITS)]
    sides = [deliver(parts[0])]
    in_rows(0, 2)
    sides.append(deliver(parts[1]))
    in_rows(2, UNITS - 2)
    arrived += [jnp.concatenate(halves, axis=1) for halves in zip(*sides)]
    grad_tokens = functools.reduce(jnp.add, [part.astype(F32) for part in arrived]).astype(BF16)

    sums = functools.reduce(jnp.add, [sums[key] for key in sorted(sums)]).reshape(hidden)
    for bit in [1 << i for i in range(rows_of.bit_length() - 1)]:
        sums = sums + lax.ppermute(sums, "row", [(i, i ^ bit) for i in range(rows_of)])
    grad_bias = sums * (1.0 / rows_of)
    return (grad_tokens, held["in"], grad_bias, held["out"])


def solution(mesh):
    placed = (P("col", "row"), P("row", "col"), P("col"), P("col", "row"), P("col", "row"))
    return jax.shard_map(
        functools.partial(local, mesh.shape["row"], mesh.shape["col"]),
        mesh=mesh,
        in_specs=placed,
        out_specs=(P("col", "row"), P("row", "col"), P("col"), P("col", "row")),
        check_vma=False,
    )
```

time: 322 us -> 302 us (0.938)
  waiting for transfers between devices: 30.7 us -> 88.7 us
  Pallas kernels: 181 us -> 124 us
  local copies, waits for them, and re-layouts: 10.5 us -> 0.4 us
  starting transfers between devices: 72.1 us -> 62.7 us
    pallas_call x24 -> x19, Pallas kernels: 181 us -> 124 us  [call(): pl.pallas_call(kernel, grid_spec=pltpu.PrefetchScalarGridSpec(num_scalar_...]
    ppermute x24, waiting for transfers between devices: 28.1 us -> 75.4 us  [send(): return lax.ppermute(value, 'row', pairs)]
    unnamed x60 -> x42, local copies, waits for them, and re-layouts: 10.5 us -> 0.4 us
    ppermute x24, starting transfers between devices: 62.9 us -> 53.6 us  [send(): return lax.ppermute(value, 'row', pairs)]
    ppermute x11 -> x10, waiting for transfers between devices: 1.85 us -> 8.9 us  [swap(): return lax.ppermute(value, 'col', [(i, i ^ bits) for i in range(cols_of)])]
    ppermute x2, waiting for transfers between devices: 0.01 us -> 3.64 us  [local(): lax.ppermute(sums, 'row', [(i, i ^ bit) for i in range(rows_of)])]
    convert_element_type x21 -> x19, other arithmetic: 9.14 us -> 8.63 us  [add_bf16(): return (left.astype(F32) + right.astype(F32)).astype(BF16)]
    ppermute x11 -> x10, starting transfers between devices: 7.19 us -> 7.59 us  [swap(): return lax.ppermute(value, 'col', [(i, i ^ bits) for i in range(cols_of)])]
  transfers between devices with their start and end apart: 39 -> 38, of which waited for: 5 -> 13; matrix products, arithmetic and copies ran while one was open for 3% -> 3% of each run, Pallas kernels for 54% -> 39%
where the time goes in v4:
time: 302 us; the launch traced here: 301 us
  Pallas kernels  124 us (41%)
  waiting for transfers between devices  88.7 us (29%)
  starting transfers between devices  62.7 us (21%)
  between operations  14.8 us (5%)
  other arithmetic  10.6 us (4%)
    pallas_call x19, Pallas kernels, call(): pl.pallas_call(kernel, grid_spec=pltpu.PrefetchScalarGridSpec(num_scalar_...  124 us
    ppermute x24, waiting for transfers between devices, send(): return lax.ppermute(value, 'row', pairs)  75.4 us
    ppermute x24, starting transfers between devices, send(): return lax.ppermute(value, 'row', pairs)  53.6 us
    ppermute x10, waiting for transfers between devices, swap(): return lax.ppermute(value, 'col', [(i, i ^ bits) for i in range(cols_of)])  8.9 us
    convert_element_type x19, other arithmetic, add_bf16(): return (left.astype(F32) + right.astype(F32)).astype(BF16)  8.63 us
    ppermute x10, starting transfers between devices, swap(): return lax.ppermute(value, 'col', [(i, i ^ bits) for i in range(cols_of)])  7.59 us
  transfers between devices with their start and end apart: 38, of which 13 were waited for; matrix products, arithmetic and copies ran while one was open for 3% of the time, Pallas kernels for 39%

profile of v4, /device:TPU:0, one launch (start us, length us, event | category | flops | bytes accessed | tf_op | source)
XLA Modules:
  0.0 301.2 jit_solution(106589136564426147)
XLA Ops:
  8.5 2.0 collective-permute-done.refs_1_
  11.0 6.3 %shard_map.84 = bf16[192,1792]{1,0:T(8,128)(2,1)S(1)} custom-call(s32[2]{0:T(128)S(1)} %pad_add_fusion.s, bf16[96,3584]{1,0:T(8,128)(2,1)S(1)} %copy-done.2, bf16[96,3584]{1,0:T(8,128)(2,1)S(1)} %collective-permute-done.refs_1_, bf16[3584,1792]{1,0:T(8,128)(2,1)} %refs_1_.9), custom_call_target="tpu_custom_call" | custom-call | flops 2466250752 | bytes 14221312 | tf_op jit(solution)/shard_map/pallas_call | solution.py:30
  17.3 4.7 %collective-permute-start.1 = (bf16[192,1792]{1,0:T(8,128)(2,1)S(1)}, bf16[192,1792]{1,0:T(8,128)(2,1)S(1)}, u32[]{:S(2)}, u32[]{:S(2)}) collective-permute-start(bf16[192,1792]{1,0:T(8,128)(2,1)S(1)} %shard_map.84), channel_id=1, source_target_pairs={{0,8},{24,16},{1,9},{25,17},{2,10},{26,18},{3,11},{27,19},{4,12},{... | collective-permute-start | bytes 2064392 | tf_op jit(solution)/shard_map/ppermute | solution.py:319
  22.0 7.3 %shard_map.85 = bf16[192,1792]{1,0:T(8,128)(2,1)S(1)} custom-call(s32[2]{0:T(128)S(1)} %pad_add_fusion.s, bf16[96,3584]{1,0:T(8,128)(2,1)S(1)} %copy-done.3, bf16[96,3584]{1,0:T(8,128)(2,1)S(1)} %collective-permute-done.2.refs_1_, bf16[1792,3584]{1,0:T(8,128)(2,1)} %refs_1_.6), custom_call_target="tpu_custom_call" | custom-call | flops 2466250752 | bytes 14221312 | tf_op jit(solution)/shard_map/pallas_call | solution.py:30
  29.3 1.5 collective-permute-start.4
  30.8 6.9 %collective-permute-done.1 = bf16[192,1792]{1,0:T(8,128)(2,1)S(1)} collective-permute-done((bf16[192,1792]{1,0:T(8,128)(2,1)S(1)}, bf16[192,1792]{1,0:T(8,128)(2,1)S(1)}, u32[]{:S(2)}, u32[]{:S(2)}) %collective-permute-start.1) | collective-permute-done | bytes 688160 | tf_op jit(solution)/shard_map/ppermute | solution.py:319
  38.5 13.3 %collective-permute-done.4 = bf16[192,1792]{1,0:T(8,128)(2,1)S(1)} collective-permute-done((bf16[192,1792]{1,0:T(8,128)(2,1)S(1)}, bf16[192,1792]{1,0:T(8,128)(2,1)S(1)}, u32[]{:S(2)}, u32[]{:S(2)}) %collective-permute-start.4) | collective-permute-done | bytes 688160 | tf_op jit(solution)/shard_map/ppermute | solution.py:319
  53.8 1.4 collective-permute-start.7
  55.2 13.4 %shard_map.86 = (bf16[192,1792]{1,0:T(8,128)(2,1)S(1)}, bf16[192,1792]{1,0:T(8,128)(2,1)S(1)}, bf16[192,1792]{1,0:T(8,128)(2,1)}) custom-call(s32[2]{0:T(128)S(1)} %pad_add_fusion.s, bf16[768,3584]{1,0:T(8,128)(2,1)} %all-gather.3.cloned.1.call-done.refs_0_.tok_ref, bf16[3584,1792]{1,0:T(8,128)(2,1)} %refs_1_.9), custom_call_target="tpu_custom_call" | custom-call | flops 7398752256 | bytes 16973824 | tf_op jit(solution)/shard_map/pallas_call | solution.py:30
  68.7 8.8 %collective-permute-start.5 = (bf16[192,1792]{1,0:T(8,128)(2,1)S(1)}, bf16[192,1792]{1,0:T(8,128)(2,1)S(1)}, u32[]{:S(2)}, u32[]{:S(2)}) collective-permute-start(bf16[192,1792]{1,0:T(8,128)(2,1)S(1)} %get-tuple-element.98), channel_id=1, source_target_pairs={{0,8},{24,16},{1,9},{25,17},{2,10},{26,18},{3,11},{27,19},{4,12},{... | collective-permute-start | bytes 2064392 | tf_op jit(solution)/shard_map/ppermute | solution.py:319
  77.5 2.9 shard_map.87
  80.4 1.3 collective-permute-start.8
  81.9 11.4 %collective-permute-done.5 = bf16[192,1792]{1,0:T(8,128)(2,1)S(1)} collective-permute-done((bf16[192,1792]{1,0:T(8,128)(2,1)S(1)}, bf16[192,1792]{1,0:T(8,128)(2,1)S(1)}, u32[]{:S(2)}, u32[]{:S(2)}) %collective-permute-start.5) | collective-permute-done | bytes 688160 | tf_op jit(solution)/shard_map/ppermute | solution.py:319
  94.2 1.3 collective-permute-start.12
  95.5 10.2 %collective-permute-done.8 = bf16[192,1792]{1,0:T(8,128)(2,1)S(1)} collective-permute-done((bf16[192,1792]{1,0:T(8,128)(2,1)S(1)}, bf16[192,1792]{1,0:T(8,128)(2,1)S(1)}, u32[]{:S(2)}, u32[]{:S(2)}) %collective-permute-start.8) | collective-permute-done | bytes 688160 | tf_op jit(solution)/shard_map/ppermute | solution.py:319
  105.9 1.7 collective-permute-start.9
  107.5 6.5 %collective-permute-start.10 = (bf16[192,1792]{1,0:T(8,128)(2,1)}, bf16[192,1792]{1,0:T(8,128)(2,1)}, u32[]{:S(2)}, u32[]{:S(2)}) collective-permute-start(bf16[192,1792]{1,0:T(8,128)(2,1)} %get-tuple-element.112), channel_id=1, source_target_pairs={{0,8},{24,16},{1,9},{25,17},{2,10},{26,18},{3,11},{27,19},{4,12},{... | collective-permute-start | bytes 2064392 | tf_op jit(solution)/shard_map/ppermute | solution.py:319
  115.1 1.3 collective-permute-start.13
  117.5 17.3 %shard_map.89 = (bf16[192,1792]{1,0:T(8,128)(2,1)S(1)}, bf16[192,1792]{1,0:T(8,128)(2,1)S(1)}, bf16[192,1792]{1,0:T(8,128)(2,1)S(1)}) custom-call(s32[2]{0:T(128)S(1)} %pad_add_fusion.s, bf16[768,3584]{1,0:T(8,128)(2,1)} %all-gather.5.cloned.1.call-done.refs_0_.grad_ref, bf16[1792,3584]{1,0:T(8,128)(2,1)} %refs_1_.6), custom_call_target="tpu_custom_call" | custom-call | flops 7398752256 | bytes 16973824 | tf_op jit(solution)/shard_map/pallas_call | solution.py:30
  134.8 5.4 %collective-permute-start.14 = (bf16[192,1792]{1,0:T(8,128)(2,1)S(1)}, bf16[192,1792]{1,0:T(8,128)(2,1)S(1)}, u32[]{:S(2)}, u32[]{:S(2)}) collective-permute-start(bf16[192,1792]{1,0:T(8,128)(2,1)S(1)} %get-tuple-element.118), channel_id=1, source_target_pairs={{0,8},{24,16},{1,9},{25,17},{2,10},{26,18},{3,11},{27,19},{4,12},{... | collective-permute-start | bytes 2064392 | tf_op jit(solution)/shard_map/ppermute | solution.py:319
  140.3 1.6 add_convert_fusion.11.refs_0_
  142.8 1.3 add_convert_fusion.10
  144.1 1.3 collective-permute-start.17
  145.4 2.9 shard_map.90
  148.3 4.6 %collective-permute-start.15 = (bf16[192,1792]{1,0:T(8,128)(2,1)S(1)}, bf16[192,1792]{1,0:T(8,128)(2,1)S(1)}, u32[]{:S(2)}, u32[]{:S(2)}) collective-permute-start(bf16[192,1792]{1,0:T(8,128)(2,1)S(1)} %get-tuple-element.123), channel_id=1, source_target_pairs={{0,8},{24,16},{1,9},{25,17},{2,10},{26,18},{3,11},{27,19},{4,12},{... | collective-permute-start | bytes 2064392 | tf_op jit(solution)/shard_map/ppermute | solution.py:319
  156.1 1.5 collective-permute-start.21
  157.6 4.3 %collective-permute-done.17.refs_2_ = bf16[192,1792]{1,0:T(8,128)(2,1)S(1)} collective-permute-done((bf16[192,1792]{1,0:T(8,128)(2,1)S(1)}, bf16[192,1792]{1,0:T(8,128)(2,1)S(1)}, u32[]{:S(2)}, u32[]{:S(2)}) %collective-permute-start.17) | collective-permute-done | bytes 688160 | tf_op jit(solution)/shard_map/ppermute | solution.py:319
  161.9 2.9 shard_map.91
  164.8 3.1 %collective-permute-start.19 = (bf16[192,1792]{1,0:T(8,128)(2,1)S(1)}, bf16[192,1792]{1,0:T(8,128)(2,1)S(1)}, u32[]{:S(2)}, u32[]{:S(2)}) collective-permute-start(bf16[192,1792]{1,0:T(8,128)(2,1)S(1)} %get-tuple-element.130), channel_id=1, source_target_pairs={{0,8},{24,16},{1,9},{25,17},{2,10},{26,18},{3,11},{27,19},{4,12},{... | collective-permute-start | bytes 2064392 | tf_op jit(solution)/shard_map/ppermute | solution.py:319
  169.8 1.3 collective-permute-start.22
  171.1 5.1 %collective-permute-done.21.refs_2_ = bf16[192,1792]{1,0:T(8,128)(2,1)S(1)} collective-permute-done((bf16[192,1792]{1,0:T(8,128)(2,1)S(1)}, bf16[192,1792]{1,0:T(8,128)(2,1)S(1)}, u32[]{:S(2)}, u32[]{:S(2)}) %collective-permute-start.21) | collective-permute-done | bytes 688160 | tf_op jit(solution)/shard_map/ppermute | solution.py:319
  176.2 1.8 shard_map.92
  177.9 11.0 %shard_map.93.refs_0_ = f32[1792,3584]{1,0:T(8,128)} custom-call(s32[2]{0:T(128)S(1)} %pad_add_fusion.s, bf16[768,1792]{1,0:T(8,128)(2,1)S(1)} %get-tuple-element.133.act_ref, bf16[768,3584]{1,0:T(8,128)(2,1)} %all-gather.5.cloned.1.call-done.refs_0_.grad_ref), custom_call_target="tpu_custom_call" | custom-call | flops 5637144576 | bytes 20578304 | tf_op jit(solution)/shard_map/pallas_call | solution.py:30
  191.5 11.5 %shard_map.95 = (bf16[192,3584]{1,0:T(8,128)(2,1)S(1)}, bf16[192,3584]{1,0:T(8,128)(2,1)S(1)}) custom-call(s32[2]{0:T(128)S(1)} %pad_add_fusion.s, bf16[768,1792]{1,0:T(8,128)(2,1)S(1)} %get-tuple-element.126.refs_0_.refs_3_, bf16[3584,1792]{1,0:T(8,128)(2,1)} %refs_1_.9), custom_call_target="tpu_custom_call" | custom-call | flops 4932501504 | bytes 14221312 | tf_op jit(solution)/shard_map/pallas_call | solution.py:30
  203.1 1.4 collective-permute-start.24
  204.7 1.5 collective-permute-start.25
  206.2 18.2 %collective-permute-done.24.refs_2_ = bf16[192,1792]{1,0:T(8,128)(2,1)S(1)} collective-permute-done((bf16[192,1792]{1,0:T(8,128)(2,1)S(1)}, bf16[192,1792]{1,0:T(8,128)(2,1)S(1)}, u32[]{:S(2)}, u32[]{:S(2)}) %collective-permute-start.24) | collective-permute-done | bytes 688160 | tf_op jit(solution)/shard_map/ppermute | solution.py:319
  225.4 9.3 %shard_map.97 = f32[1792,3584]{1,0:T(8,128)} custom-call(s32[2]{0:T(128)S(1)} %pad_add_fusion.s, bf16[768,1792]{1,0:T(8,128)(2,1)S(1)} %get-tuple-element.133.act_ref, bf16[768,3584]{1,0:T(8,128)(2,1)} %all-gather.5.cloned.1.call-done.refs_0_.grad_ref, f32[1792,3584]{1,0:T(8,128)} %shard_map.93.refs_0_), custom_call_target="tpu_custom_call", output_to_operand_aliasing={{}: (3, {})} | custom-call | flops 4227858432 | bytes 16121856 | tf_op jit(solution)/shard_map/pallas_call | solution.py:30
  234.7 4.1 %collective-permute-done.25.refs_2_ = bf16[192,1792]{1,0:T(8,128)(2,1)S(1)} collective-permute-done((bf16[192,1792]{1,0:T(8,128)(2,1)S(1)}, bf16[192,1792]{1,0:T(8,128)(2,1)S(1)}, u32[]{:S(2)}, u32[]{:S(2)}) %collective-permute-start.25) | collective-permute-done | bytes 688160 | tf_op jit(solution)/shard_map/ppermute | solution.py:319
  240.0 6.1 %shard_map.99 = (bf16[192,1536]{1,0:T(8,128)(2,1)S(1)}, bf16[192,1536]{1,0:T(8,128)(2,1)S(1)}) custom-call(s32[2]{0:T(128)S(1)} %pad_add_fusion.s, bf16[768,1792]{1,0:T(8,128)(2,1)S(1)} %get-tuple-element.147.refs_0_.grad_ref, bf16[3584,1792]{1,0:T(8,128)(2,1)} %refs_1_.9), custom_call_target="tpu_custom_call" | custom-call | flops 2113929216 | bytes 6881280 | tf_op jit(solution)/shard_map/pallas_call | solution.py:30
  246.3 3.6 %collective-permute-done.34 = f32[1792]{0:T(1024)S(1)} collective-permute-done((f32[1792]{0:T(1024)S(1)}, f32[1792]{0:T(1024)S(1)}, u32[]{:S(2)}, u32[]{:S(2)}) %collective-permute-start.34) | collective-permute-done | bytes 7200 | tf_op jit(solution)/shard_map/ppermute | solution.py:435
  249.9 1.3 collective-permute-start.35
  251.3 7.5 %shard_map.100 = (bf16[192,2048]{1,0:T(8,128)(2,1)S(1)}, bf16[192,2048]{1,0:T(8,128)(2,1)S(1)}) custom-call(s32[2]{0:T(128)S(1)} %pad_add_fusion.s, bf16[768,1792]{1,0:T(8,128)(2,1)S(1)} %get-tuple-element.147.refs_0_.grad_ref, bf16[3584,1792]{1,0:T(8,128)(2,1)} %refs_1_.9), custom_call_target="tpu_custom_call" | custom-call | flops 2818572288 | bytes 8716288 | tf_op jit(solution)/shard_map/pallas_call | solution.py:30
  259.4 2.2 collective-permute-start.27
  262.6 7.2 %shard_map.101.refs_0_ = f32[3584,1792]{1,0:T(8,128)} custom-call(s32[2]{0:T(128)S(1)} %pad_add_fusion.s, bf16[768,3584]{1,0:T(8,128)(2,1)} %all-gather.3.cloned.1.call-done.refs_0_.tok_ref, bf16[768,1792]{1,0:T(8,128)(2,1)S(1)} %get-tuple-element.147.refs_0_.grad_ref), custom_call_target="tpu_custom_call" | custom-call | flops 2818572288 | bytes 11665408 | tf_op jit(solution)/shard_map/pallas_call | solution.py:30
  270.6 1.6 collective-permute-start.33
  273.4 12.7 %shard_map.102 = f32[3584,1792]{1,0:T(8,128)} custom-call(s32[2]{0:T(128)S(1)} %pad_add_fusion.s, bf16[768,3584]{1,0:T(8,128)(2,1)} %all-gather.3.cloned.1.call-done.refs_0_.tok_ref, bf16[768,1792]{1,0:T(8,128)(2,1)S(1)} %get-tuple-element.147.refs_0_.grad_ref, f32[3584,1792]{1,0:T(8,128)} %shard_map.101.refs_0_), custom_call_target="tpu_custom_call", output_to_operand_aliasing={{}: (3, {})} | custom-call | flops 7046430720 | bytes 25034752 | tf_op jit(solution)/shard_map/pallas_call | solution.py:30
  286.1 6.9 %collective-permute-done.31 = bf16[96,2048]{1,0:T(8,128)(2,1)S(1)} collective-permute-done((bf16[96,2048]{1,0:T(8,128)(2,1)S(1)}, bf16[96,2048]{1,0:T(8,128)(2,1)S(1)}, u32[]{:S(2)}, u32[]{:S(2)}) %collective-permute-start.31) | collective-permute-done | bytes 393248 | tf_op jit(solution)/shard_map/ppermute | solution.py:322
  (116 shorter events, 23.8 us)
Async XLA Ops:
  7.2 48.0 %all-gather.3.cloned.1.call-start = ((), (), s32[]{:S(2)}) async-start(), calls=%async_computation | async-start | bytes 6193152 | tf_op jit(solution)/shard_map/all_gather | solution.py:393
  7.9 109.5 %all-gather.5.cloned.1.call-start = ((), (), s32[]{:S(2)}) async-start(), calls=%async_computation.1 | async-start | bytes 6193152 | tf_op jit(solution)/shard_map/all_gather | solution.py:394
  8.0 2.5 collective-permute-start
  10.5 11.5 %collective-permute-start.2 = (bf16[96,3584]{1,0:T(8,128)(2,1)S(1)}, bf16[96,3584]{1,0:T(8,128)(2,1)S(1)}, u32[]{:S(2)}, u32[]{:S(2)}) collective-permute-start(bf16[96,3584]{1,0:T(8,128)(2,1)S(1)} %copy-done.3), channel_id=1, source_target_pairs={{0,1},{1,0},{2,3},{3,2},{4,5},{5,4},{6,7},{7,6},{8,9},{9,8},{10,11... | collective-permute-start | bytes 2064392 | tf_op jit(solution)/shard_map/ppermute | solution.py:322
  17.3 20.4 %collective-permute-start.1 = (bf16[192,1792]{1,0:T(8,128)(2,1)S(1)}, bf16[192,1792]{1,0:T(8,128)(2,1)S(1)}, u32[]{:S(2)}, u32[]{:S(2)}) collective-permute-start(bf16[192,1792]{1,0:T(8,128)(2,1)S(1)} %shard_map.84), channel_id=1, source_target_pairs={{0,8},{24,16},{1,9},{25,17},{2,10},{26,18},{3,11},{27,19},{4,12},{... | collective-permute-start | bytes 2064392 | tf_op jit(solution)/shard_map/ppermute | solution.py:319
  29.3 22.6 %collective-permute-start.4 = (bf16[192,1792]{1,0:T(8,128)(2,1)S(1)}, bf16[192,1792]{1,0:T(8,128)(2,1)S(1)}, u32[]{:S(2)}, u32[]{:S(2)}) collective-permute-start(bf16[192,1792]{1,0:T(8,128)(2,1)S(1)} %shard_map.85), channel_id=1, source_target_pairs={{0,8},{24,16},{1,9},{25,17},{2,10},{26,18},{3,11},{27,19},{4,12},{... | collective-permute-start | bytes 2064392 | tf_op jit(solution)/shard_map/ppermute | solution.py:319
  37.8 14.9 %collective-permute-start.3 = (bf16[192,1792]{1,0:T(8,128)(2,1)S(1)}, bf16[192,1792]{1,0:T(8,128)(2,1)S(1)}, u32[]{:S(2)}, u32[]{:S(2)}) collective-permute-start(bf16[192,1792]{1,0:T(8,128)(2,1)S(1)} %add_convert_fusion.18.refs_0_), channel_id=1, source_target_pairs={{8,16},{16,8},{9,17},{17,9},{10,18},{18,10},{11,19},{19,11},{12,20... | collective-permute-start | bytes 2064392 | tf_op jit(solution)/shard_map/ppermute | solution.py:319
  52.0 16.7 %copy-start.10 = (bf16[192,1792]{1,0:T(8,128)(2,1)}, bf16[192,1792]{1,0:T(8,128)(2,1)S(1)}, u32[]{:S(2)}) copy-start(bf16[192,1792]{1,0:T(8,128)(2,1)S(1)} %add_convert_fusion.17.refs_0_) | copy-start | bytes 2064388
  52.0 29.7 %collective-permute-start.6 = (bf16[192,1792]{1,0:T(8,128)(2,1)S(1)}, bf16[192,1792]{1,0:T(8,128)(2,1)S(1)}, u32[]{:S(2)}, u32[]{:S(2)}) collective-permute-start(bf16[192,1792]{1,0:T(8,128)(2,1)S(1)} %add_convert_fusion.17.refs_0_), channel_id=1, source_target_pairs={{8,16},{16,8},{9,17},{17,9},{10,18},{18,10},{11,19},{19,11},{12,20... | collective-permute-start | bytes 2064392 | tf_op jit(solution)/shard_map/ppermute | solution.py:319
  53.8 23.7 %copy-start.20 = (f32[1792]{0:T(1024)S(1)}, f32[1792]{0:T(1024)}, u32[]{:S(2)}) copy-start(f32[1792]{0:T(1024)} %param.7) | copy-start | bytes 21508
  53.8 23.7 %collective-permute-start.7 = (bf16[192,1792]{1,0:T(8,128)(2,1)}, bf16[192,1792]{1,0:T(8,128)(2,1)}, u32[]{:S(2)}, u32[]{:S(2)}) collective-permute-start(bf16[192,1792]{1,0:T(8,128)(2,1)} %add_convert_fusion.16), channel_id=1, source_target_pairs={{16,24},{8,0},{17,25},{9,1},{18,26},{10,2},{19,27},{11,3},{20,28},... | collective-permute-start | bytes 2064392 | tf_op jit(solution)/shard_map/ppermute | solution.py:319
  68.7 37.0 %copy-start.8 = (bf16[192,1792]{1,0:T(8,128)(2,1)}, bf16[192,1792]{1,0:T(8,128)(2,1)S(1)}, u32[]{:S(2)}) copy-start(bf16[192,1792]{1,0:T(8,128)(2,1)S(1)} %get-tuple-element.104) | copy-start | bytes 2064388
  68.7 24.6 %collective-permute-start.5 = (bf16[192,1792]{1,0:T(8,128)(2,1)S(1)}, bf16[192,1792]{1,0:T(8,128)(2,1)S(1)}, u32[]{:S(2)}, u32[]{:S(2)}) collective-permute-start(bf16[192,1792]{1,0:T(8,128)(2,1)S(1)} %get-tuple-element.98), channel_id=1, source_target_pairs={{0,8},{24,16},{1,9},{25,17},{2,10},{26,18},{3,11},{27,19},{4,12},{... | collective-permute-start | bytes 2064392 | tf_op jit(solution)/shard_map/ppermute | solution.py:319
  80.4 13.1 %copy-start = (bf16[768,1792]{1,0:T(8,128)(2,1)}, bf16[768,1792]{1,0:T(8,128)(2,1)S(1)}, u32[]{:S(2)}) copy-start(bf16[768,1792]{1,0:T(8,128)(2,1)S(1)} %get-tuple-element.88.refs_3_) | copy-start | bytes 8257540
  80.4 25.3 %collective-permute-start.8 = (bf16[192,1792]{1,0:T(8,128)(2,1)S(1)}, bf16[192,1792]{1,0:T(8,128)(2,1)S(1)}, u32[]{:S(2)}, u32[]{:S(2)}) collective-permute-start(bf16[192,1792]{1,0:T(8,128)(2,1)S(1)} %get-tuple-element.104), channel_id=1, source_target_pairs={{0,8},{24,16},{1,9},{25,17},{2,10},{26,18},{3,11},{27,19},{4,12},{... | collective-permute-start | bytes 2064392 | tf_op jit(solution)/shard_map/ppermute | solution.py:319
  81.7 11.7 %copy-start.12 = (bf16[192,1792]{1,0:T(8,128)(2,1)}, bf16[192,1792]{1,0:T(8,128)(2,1)S(1)}, u32[]{:S(2)}) copy-start(bf16[192,1792]{1,0:T(8,128)(2,1)S(1)} %collective-permute-done.6.refs_1_) | copy-start | bytes 2064388
  93.5 21.6 %copy-start.4 = (bf16[192,1792]{1,0:T(8,128)(2,1)}, bf16[192,1792]{1,0:T(8,128)(2,1)S(1)}, u32[]{:S(2)}) copy-start(bf16[192,1792]{1,0:T(8,128)(2,1)S(1)} %add_convert_fusion.14.refs_0_) | copy-start | bytes 2064388
  93.5 20.5 %collective-permute-start.11 = (bf16[192,1792]{1,0:T(8,128)(2,1)S(1)}, bf16[192,1792]{1,0:T(8,128)(2,1)S(1)}, u32[]{:S(2)}, u32[]{:S(2)}) collective-permute-start(bf16[192,1792]{1,0:T(8,128)(2,1)S(1)} %add_convert_fusion.14.refs_0_), channel_id=1, source_target_pairs={{8,16},{16,8},{9,17},{17,9},{10,18},{18,10},{11,19},{19,11},{12,20... | collective-permute-start | bytes 2064392 | tf_op jit(solution)/shard_map/ppermute | solution.py:319
  94.2 22.2 %collective-permute-start.12 = (bf16[192,1792]{1,0:T(8,128)(2,1)S(1)}, bf16[192,1792]{1,0:T(8,128)(2,1)S(1)}, u32[]{:S(2)}, u32[]{:S(2)}) collective-permute-start(bf16[192,1792]{1,0:T(8,128)(2,1)S(1)} %add_convert_fusion.15), channel_id=1, source_target_pairs={{16,24},{8,0},{17,25},{9,1},{18,26},{10,2},{19,27},{11,3},{20,28},... | collective-permute-start | bytes 2064392 | tf_op jit(solution)/shard_map/ppermute | solution.py:319
  105.9 36.9 %collective-permute-start.9 = (bf16[192,1792]{1,0:T(8,128)(2,1)S(1)}, bf16[192,1792]{1,0:T(8,128)(2,1)}, u32[]{:S(2)}, u32[]{:S(2)}) collective-permute-start(bf16[192,1792]{1,0:T(8,128)(2,1)S(1)} %add_convert_fusion.13.refs_0_), channel_id=1, source_target_pairs={{8,16},{16,8},{9,17},{17,9},{10,18},{18,10},{11,19},{19,11},{12,20... | collective-permute-start | bytes 2064392 | tf_op jit(solution)/shard_map/ppermute | solution.py:319
  107.5 32.7 %collective-permute-start.10 = (bf16[192,1792]{1,0:T(8,128)(2,1)}, bf16[192,1792]{1,0:T(8,128)(2,1)}, u32[]{:S(2)}, u32[]{:S(2)}) collective-permute-start(bf16[192,1792]{1,0:T(8,128)(2,1)} %get-tuple-element.112), channel_id=1, source_target_pairs={{0,8},{24,16},{1,9},{25,17},{2,10},{26,18},{3,11},{27,19},{4,12},{... | collective-permute-start | bytes 2064392 | tf_op jit(solution)/shard_map/ppermute | solution.py:319
  115.1 30.3 %collective-permute-start.13 = (bf16[192,1792]{1,0:T(8,128)(2,1)}, bf16[192,1792]{1,0:T(8,128)(2,1)}, u32[]{:S(2)}, u32[]{:S(2)}) collective-permute-start(bf16[192,1792]{1,0:T(8,128)(2,1)} %add_convert_fusion.12), channel_id=1, source_target_pairs={{16,24},{8,0},{17,25},{9,1},{18,26},{10,2},{19,27},{11,3},{20,28},... | collective-permute-start | bytes 2064392 | tf_op jit(solution)/shard_map/ppermute | solution.py:319
  117.5 25.3 %copy-start.9 = (bf16[192,1792]{1,0:T(8,128)(2,1)S(1)}, bf16[192,1792]{1,0:T(8,128)(2,1)}, u32[]{:S(2)}) copy-start(bf16[192,1792]{1,0:T(8,128)(2,1)} %copy-done.8) | copy-start | bytes 2064388
  134.8 19.1 %collective-permute-start.14 = (bf16[192,1792]{1,0:T(8,128)(2,1)S(1)}, bf16[192,1792]{1,0:T(8,128)(2,1)S(1)}, u32[]{:S(2)}, u32[]{:S(2)}) collective-permute-start(bf16[192,1792]{1,0:T(8,128)(2,1)S(1)} %get-tuple-element.118), channel_id=1, source_target_pairs={{0,8},{24,16},{1,9},{25,17},{2,10},{26,18},{3,11},{27,19},{4,12},{... | collective-permute-start | bytes 2064392 | tf_op jit(solution)/shard_map/ppermute | solution.py:319
  141.9 12.9 %collective-permute-start.16 = (bf16[192,1792]{1,0:T(8,128)(2,1)S(1)}, bf16[192,1792]{1,0:T(8,128)(2,1)S(1)}, u32[]{:S(2)}, u32[]{:S(2)}) collective-permute-start(bf16[192,1792]{1,0:T(8,128)(2,1)S(1)} %add_convert_fusion.11.refs_0_), channel_id=1, source_target_pairs={{8,16},{16,8},{9,17},{17,9},{10,18},{18,10},{11,19},{19,11},{12,20... | collective-permute-start | bytes 2064392 | tf_op jit(solution)/shard_map/ppermute | solution.py:319
  144.1 17.9 %collective-permute-start.17 = (bf16[192,1792]{1,0:T(8,128)(2,1)S(1)}, bf16[192,1792]{1,0:T(8,128)(2,1)S(1)}, u32[]{:S(2)}, u32[]{:S(2)}) collective-permute-start(bf16[192,1792]{1,0:T(8,128)(2,1)S(1)} %add_convert_fusion.10), channel_id=1, source_target_pairs={{16,24},{8,0},{17,25},{9,1},{18,26},{10,2},{19,27},{11,3},{20,28},... | collective-permute-start | bytes 2064392 | tf_op jit(solution)/shard_map/ppermute | solution.py:319
  148.3 20.4 %collective-permute-start.15 = (bf16[192,1792]{1,0:T(8,128)(2,1)S(1)}, bf16[192,1792]{1,0:T(8,128)(2,1)S(1)}, u32[]{:S(2)}, u32[]{:S(2)}) collective-permute-start(bf16[192,1792]{1,0:T(8,128)(2,1)S(1)} %get-tuple-element.123), channel_id=1, source_target_pairs={{0,8},{24,16},{1,9},{25,17},{2,10},{26,18},{3,11},{27,19},{4,12},{... | collective-permute-start | bytes 2064392 | tf_op jit(solution)/shard_map/ppermute | solution.py:319
  154.1 15.5 %collective-permute-start.20 = (bf16[192,1792]{1,0:T(8,128)(2,1)S(1)}, bf16[192,1792]{1,0:T(8,128)(2,1)S(1)}, u32[]{:S(2)}, u32[]{:S(2)}) collective-permute-start(bf16[192,1792]{1,0:T(8,128)(2,1)S(1)} %add_convert_fusion.9.refs_0_), channel_id=1, source_target_pairs={{8,16},{16,8},{9,17},{17,9},{10,18},{18,10},{11,19},{19,11},{12,20... | collective-permute-start | bytes 2064392 | tf_op jit(solution)/shard_map/ppermute | solution.py:319
  156.1 20.1 %collective-permute-start.21 = (bf16[192,1792]{1,0:T(8,128)(2,1)S(1)}, bf16[192,1792]{1,0:T(8,128)(2,1)S(1)}, u32[]{:S(2)}, u32[]{:S(2)}) collective-permute-start(bf16[192,1792]{1,0:T(8,128)(2,1)S(1)} %add_convert_fusion.8), channel_id=1, source_target_pairs={{16,24},{8,0},{17,25},{9,1},{18,26},{10,2},{19,27},{11,3},{20,28},... | collective-permute-start | bytes 2064392 | tf_op jit(solution)/shard_map/ppermute | solution.py:319
  164.8 24.2 %collective-permute-start.19 = (bf16[192,1792]{1,0:T(8,128)(2,1)S(1)}, bf16[192,1792]{1,0:T(8,128)(2,1)S(1)}, u32[]{:S(2)}, u32[]{:S(2)}) collective-permute-start(bf16[192,1792]{1,0:T(8,128)(2,1)S(1)} %get-tuple-element.130), channel_id=1, source_target_pairs={{0,8},{24,16},{1,9},{25,17},{2,10},{26,18},{3,11},{27,19},{4,12},{... | collective-permute-start | bytes 2064392 | tf_op jit(solution)/shard_map/ppermute | solution.py:319
  168.9 21.1 %collective-permute-start.18 = (bf16[192,1792]{1,0:T(8,128)(2,1)S(1)}, bf16[192,1792]{1,0:T(8,128)(2,1)S(1)}, u32[]{:S(2)}, u32[]{:S(2)}) collective-permute-start(bf16[192,1792]{1,0:T(8,128)(2,1)S(1)} %add_convert_fusion.7.refs_0_), channel_id=1, source_target_pairs={{8,16},{16,8},{9,17},{17,9},{10,18},{18,10},{11,19},{19,11},{12,20... | collective-permute-start | bytes 2064392 | tf_op jit(solution)/shard_map/ppermute | solution.py:319
  169.8 20.4 %collective-permute-start.22 = (bf16[192,1792]{1,0:T(8,128)(2,1)S(1)}, bf16[192,1792]{1,0:T(8,128)(2,1)S(1)}, u32[]{:S(2)}, u32[]{:S(2)}) collective-permute-start(bf16[192,1792]{1,0:T(8,128)(2,1)S(1)} %add_convert_fusion.6), channel_id=1, source_target_pairs={{16,24},{8,0},{17,25},{9,1},{18,26},{10,2},{19,27},{11,3},{20,28},... | collective-permute-start | bytes 2064392 | tf_op jit(solution)/shard_map/ppermute | solution.py:319
  177.9 11.0 %copy-start.18 = (f32[192,1792]{1,0:T(8,128)}, f32[192,1792]{1,0:T(8,128)S(1)}, u32[]{:S(2)}) copy-start(f32[192,1792]{1,0:T(8,128)S(1)} %get-tuple-element.128.slope_ref) | copy-start | bytes 4128772
  189.2 15.4 %collective-permute-start.23 = (bf16[192,1792]{1,0:T(8,128)(2,1)S(1)}, bf16[192,1792]{1,0:T(8,128)(2,1)S(1)}, u32[]{:S(2)}, u32[]{:S(2)}) collective-permute-start(bf16[192,1792]{1,0:T(8,128)(2,1)S(1)} %add_convert_fusion.5.refs_0_), channel_id=1, source_target_pairs={{8,16},{16,8},{9,17},{17,9},{10,18},{18,10},{11,19},{19,11},{12,20... | collective-permute-start | bytes 2064392 | tf_op jit(solution)/shard_map/ppermute | solution.py:319
  203.0 21.4 %copy-start.17 = (f32[192,1792]{1,0:T(8,128)S(1)}, f32[192,1792]{1,0:T(8,128)}, u32[]{:S(2)}) copy-start(f32[192,1792]{1,0:T(8,128)} %copy-done.16) | copy-start | bytes 4128772
  203.0 36.8 %collective-permute-start.26 = (bf16[192,3584]{1,0:T(8,128)(2,1)S(1)}, bf16[192,3584]{1,0:T(8,128)(2,1)S(1)}, u32[]{:S(2)}, u32[]{:S(2)}) collective-permute-start(bf16[192,3584]{1,0:T(8,128)(2,1)S(1)} %get-tuple-element.137), channel_id=1, source_target_pairs={{0,1},{1,0},{2,3},{3,2},{4,5},{5,4},{6,7},{7,6},{8,9},{9,8},{10,11... | collective-permute-start | bytes 4128776 | tf_op jit(solution)/shard_map/ppermute | solution.py:322
  203.1 21.3 %collective-permute-start.24 = (bf16[192,1792]{1,0:T(8,128)(2,1)S(1)}, bf16[192,1792]{1,0:T(8,128)(2,1)S(1)}, u32[]{:S(2)}, u32[]{:S(2)}) collective-permute-start(bf16[192,1792]{1,0:T(8,128)(2,1)S(1)} %add_convert_fusion.4), channel_id=1, source_target_pairs={{16,24},{8,0},{17,25},{9,1},{18,26},{10,2},{19,27},{11,3},{20,28},... | collective-permute-start | bytes 2064392 | tf_op jit(solution)/shard_map/ppermute | solution.py:319
  204.7 34.1 %collective-permute-start.25 = (bf16[192,1792]{1,0:T(8,128)(2,1)S(1)}, bf16[192,1792]{1,0:T(8,128)(2,1)S(1)}, u32[]{:S(2)}, u32[]{:S(2)}) collective-permute-start(bf16[192,1792]{1,0:T(8,128)(2,1)S(1)} %add_convert_fusion.3), channel_id=1, source_target_pairs={{16,24},{8,0},{17,25},{9,1},{18,26},{10,2},{19,27},{11,3},{20,28},... | collective-permute-start | bytes 2064392 | tf_op jit(solution)/shard_map/ppermute | solution.py:319
  225.4 13.4 %copy-start.19 = (f32[192,1792]{1,0:T(8,128)S(1)}, f32[192,1792]{1,0:T(8,128)}, u32[]{:S(2)}) copy-start(f32[192,1792]{1,0:T(8,128)} %copy-done.18) | copy-start | bytes 4128772
  246.1 15.6 %collective-permute-start.28 = (bf16[192,1536]{1,0:T(8,128)(2,1)S(1)}, bf16[192,1536]{1,0:T(8,128)(2,1)S(1)}, u32[]{:S(2)}, u32[]{:S(2)}) collective-permute-start(bf16[192,1536]{1,0:T(8,128)(2,1)S(1)} %get-tuple-element.143), channel_id=1, source_target_pairs={{0,1},{1,0},{2,3},{3,2},{4,5},{5,4},{6,7},{7,6},{8,9},{9,8},{10,11... | collective-permute-start | bytes 1769480 | tf_op jit(solution)/shard_map/ppermute | solution.py:322
  246.2 3.7 %collective-permute-start.34 = (f32[1792]{0:T(1024)S(1)}, f32[1792]{0:T(1024)S(1)}, u32[]{:S(2)}, u32[]{:S(2)}) collective-permute-start(f32[1792]{0:T(1024)S(1)} %add_reduce_fusion), channel_id=1, source_target_pairs={{0,8},{8,0},{16,24},{24,16},{1,9},{9,1},{17,25},{25,17},{2,10},{10... | collective-permute-start | bytes 21512 | tf_op jit(solution)/shard_map/ppermute | solution.py:435
  249.9 8.9 %collective-permute-start.35 = (f32[1792]{0:T(1024)S(1)}, f32[1792]{0:T(1024)S(1)}, u32[]{:S(2)}, u32[]{:S(2)}) collective-permute-start(f32[1792]{0:T(1024)S(1)} %add.124), channel_id=1, source_target_pairs={{0,16},{8,24},{16,0},{24,8},{1,17},{9,25},{17,1},{25,9},{2,18},{10... | collective-permute-start | bytes 21512 | tf_op jit(solution)/shard_map/ppermute | solution.py:435
  258.8 11.6 %collective-permute-start.30 = (bf16[192,2048]{1,0:T(8,128)(2,1)S(1)}, bf16[192,2048]{1,0:T(8,128)(2,1)S(1)}, u32[]{:S(2)}, u32[]{:S(2)}) collective-permute-start(bf16[192,2048]{1,0:T(8,128)(2,1)S(1)} %get-tuple-element.146), channel_id=1, source_target_pairs={{0,1},{1,0},{2,3},{3,2},{4,5},{5,4},{6,7},{7,6},{8,9},{9,8},{10,11... | collective-permute-start | bytes 2359304 | tf_op jit(solution)/shard_map/ppermute | solution.py:322
  259.4 26.7 %collective-permute-start.27 = (bf16[96,3584]{1,0:T(8,128)(2,1)S(1)}, bf16[96,3584]{1,0:T(8,128)(2,1)S(1)}, u32[]{:S(2)}, u32[]{:S(2)}) collective-permute-start(bf16[96,3584]{1,0:T(8,128)(2,1)S(1)} %add_convert_fusion.1), channel_id=1, source_target_pairs={{0,6},{1,7},{2,4},{3,5},{4,2},{5,3},{6,0},{7,1},{8,14},{9,15},{10,... | collective-permute-start | bytes 2064392 | tf_op jit(solution)/shard_map/ppermute | solution.py:322
  261.8 24.3 %collective-permute-start.32 = (bf16[96,1536]{1,0:T(8,128)(2,1)S(1)}, bf16[96,1536]{1,0:T(8,128)(2,1)S(1)}, u32[]{:S(2)}, u32[]{:S(2)}) collective-permute-start(bf16[96,1536]{1,0:T(8,128)(2,1)S(1)} %get-tuple-element.155), channel_id=1, source_target_pairs={{0,4},{1,5},{2,6},{3,7},{4,0},{5,1},{6,2},{7,3},{8,12},{9,13},{10,... | collective-permute-start | bytes 884744 | tf_op jit(solution)/shard_map/ppermute | solution.py:322
  269.8 16.3 %collective-permute-start.29 = (bf16[96,1536]{1,0:T(8,128)(2,1)S(1)}, bf16[96,1536]{1,0:T(8,128)(2,1)S(1)}, u32[]{:S(2)}, u32[]{:S(2)}) collective-permute-start(bf16[96,1536]{1,0:T(8,128)(2,1)S(1)} %get-tuple-element.154), channel_id=1, source_target_pairs={{0,2},{1,3},{2,0},{3,1},{4,6},{5,7},{6,4},{7,5},{8,10},{9,11},{10,... | collective-permute-start | bytes 884744 | tf_op jit(solution)/shard_map/ppermute | solution.py:322
  270.6 22.5 %collective-permute-start.33 = (bf16[96,2048]{1,0:T(8,128)(2,1)S(1)}, bf16[96,2048]{1,0:T(8,128)(2,1)S(1)}, u32[]{:S(2)}, u32[]{:S(2)}) collective-permute-start(bf16[96,2048]{1,0:T(8,128)(2,1)S(1)} %get-tuple-element.152), channel_id=1, source_target_pairs={{0,4},{1,5},{2,6},{3,7},{4,0},{5,1},{6,2},{7,3},{8,12},{9,13},{10,... | collective-permute-start | bytes 1179656 | tf_op jit(solution)/shard_map/ppermute | solution.py:322
  272.2 20.9 %collective-permute-start.31 = (bf16[96,2048]{1,0:T(8,128)(2,1)S(1)}, bf16[96,2048]{1,0:T(8,128)(2,1)S(1)}, u32[]{:S(2)}, u32[]{:S(2)}) collective-permute-start(bf16[96,2048]{1,0:T(8,128)(2,1)S(1)} %get-tuple-element.153), channel_id=1, source_target_pairs={{0,2},{1,3},{2,0},{3,1},{4,6},{5,7},{6,4},{7,5},{8,10},{9,11},{10,... | collective-permute-start | bytes 1179656 | tf_op jit(solution)/shard_map/ppermute | solution.py:322
  (11 other events, 57.1 us)
Sparse Core Ops, SparseCore 0:
  9.9 44.9 all-gather.2
  56.7 42.2 all-gather.4

commit v5 on v4

--- a/solution.py
+++ b/solution.py
@@ -10,7 +10,7 @@
 GELU_SCALE = 0.7978845608
 GELU_CUBIC = 0.044715
 F32, BF16 = jnp.float32, jnp.bfloat16
-VMEM_LIMIT = 48 * 1024 * 1024
+MIB = 1024 * 1024
 UNITS, AHEAD = 7, 3
 
 
@@ -18,7 +18,7 @@
     return lax.dot_general(left, right, ((dims[:1], dims[1:]), ((), ())), preferred_element_type=F32)
 
 
-def call(kernel, flops, moved, place, operands, grid, in_specs, out_specs, out_shape, into=(), outs=(), scratch=()):
+def call(kernel, flops, moved, place, operands, grid, in_specs, out_specs, out_shape, into=(), outs=(), scratch=(), vmem=48):
     scalars = 1
     aliases = {}
     in_specs, operands = list(in_specs), list(operands)
@@ -38,7 +38,7 @@
         ),
         out_shape=out_shape,
         input_output_aliases=aliases,
-        compiler_params=pltpu.CompilerParams(vmem_limit_bytes=VMEM_LIMIT),
+        compiler_params=pltpu.CompilerParams(vmem_limit_bytes=vmem * MIB),
         cost_estimate=pl.CostEstimate(flops=flops, bytes_accessed=moved, transcendentals=0),
     )(place, *operands)
 
@@ -51,7 +51,7 @@
     return pl.BlockSpec((rows, columns), lambda i, s: (s[0] ^ key, 0))
 
 
-def streamed(place, blocks, weight, pieces, dims, flops, write, out_shape):
+def streamed(place, blocks, weight, pieces, dims, flops, write, out_shape, vmem=48):
     axis, first, last = pieces
     size = weight.shape[axis] // UNITS
     count = last - first
@@ -60,7 +60,7 @@
         for array, _, _ in block:
             if not any(array is other for other in arrays):
                 arrays.append(array)
-    rows, depth = sum(part[2] for part in blocks[0]), blocks[0][0][0].shape[1]
+    total, depth = sum(part[2] for block in blocks for part in block), blocks[0][0][0].shape[1]
     parts = sum(len(block) for block in blocks)
     shape = (size, weight.shape[1]) if axis == 0 else (weight.shape[0], size)
 
@@ -73,17 +73,19 @@
             source = weight_ref.at[where, :] if axis == 0 else weight_ref.at[:, where]
             return pltpu.make_async_copy(source, piece_ref.at[at], piece_sem.at[at])
 
-        copies = []
-        for at, block in enumerate(blocks):
-            for array, start, length, into in block_rows(s, block):
+        copies, top = [], 0
+        for block in blocks:
+            for at, (array, start, length) in enumerate(block):
+                into = top if len(block) == 1 else top + (s[1] if at == 0 else 1 - s[1]) * length
                 source = next(ref for ref, other in zip(sources, arrays) if other is array)
                 copies.append(
                     pltpu.make_async_copy(
-                        source.at[pl.ds(pl.multiple_of(start, 16), length), :],
-                        block_ref.at[at, pl.ds(pl.multiple_of(into, 16), length), :],
+                        source.at[pl.ds(pl.multiple_of(start(s), 16), length), :],
+                        block_ref.at[pl.ds(pl.multiple_of(into, 16), length), :],
                         block_sem.at[len(copies)],
                     )
                 )
+            top += sum(part[2] for part in block)
         piece(0).start()
         for copy in copies:
             copy.start()
@@ -99,22 +101,12 @@
             def _():
                 piece(at + AHEAD).start()
 
-            for block in range(len(blocks)):
-                write(s, block, at, dot(block_ref[block], piece_ref[at], dims), outs)
+            write(s, at, dot(block_ref[...], piece_ref[at], dims), outs)
             return carry
 
         lax.fori_loop(0, count, step, 0)
 
-    def block_rows(s, block):
-        into = 0
-        for array, start, length in block:
-            yield array, start(s), length, (into if len(block) == 1 else start_of(s, into // length) * length)
-            into += length
-
-    def start_of(s, at):
-        return s[1] if at == 0 else 1 - s[1]
-
-    moved = 2 * (len(blocks) * rows * depth + shape[0] * shape[1] * count)
+    moved = 2 * (total * depth + shape[0] * shape[1] * count)
     anywhere = pl.BlockSpec(memory_space=pl.ANY)
     return call(
         kernel,
@@ -127,11 +119,12 @@
         [whole(out.shape) for out in out_shape],
         out_shape,
         scratch=[
-            pltpu.VMEM((len(blocks), rows, depth), BF16),
+            pltpu.VMEM((total, depth), BF16),
             pltpu.VMEM((count, *shape), BF16),
             pltpu.SemaphoreType.DMA((parts,)),
             pltpu.SemaphoreType.DMA((count,)),
         ],
+        vmem=vmem,
     )
 
 
@@ -139,13 +132,14 @@
     return pl.ds(pl.multiple_of(at * size, size), size)
 
 
-def partials(place, blocks, weight, transposed):
+def partials(place, blocks, weight, transposed, vmem):
     hidden = weight.shape[0 if transposed else 1]
     rows = sum(part[2] for part in blocks[0])
     width = hidden // UNITS
 
-    def write(s, block, at, product, outs):
-        outs[block][:, columns_of(at, width)] = product.astype(BF16)
+    def write(s, at, product, outs):
+        for block, out in enumerate(outs):
+            out[:, columns_of(at, width)] = product[block * rows : (block + 1) * rows].astype(BF16)
 
     return streamed(
         place,
@@ -156,6 +150,7 @@
         2 * len(blocks) * rows * weight.size,
         write,
         [jax.ShapeDtypeStruct((rows, hidden), BF16)] * len(blocks),
+        vmem,
     )
 
 
@@ -164,12 +159,15 @@
     tile = depth // UNITS
     half = rows // 2
 
-    def write(s, block, at, product, outs):
-        product = product.astype(BF16)
+    def write(s, at, product, outs):
         low = s[1] == 0
-        place_of = (slice(block * half, (block + 1) * half), columns_of(at, tile))
-        outs[0][place_of] = jnp.where(low, product[:half], product[half:])
-        outs[1][place_of] = jnp.where(low, product[half:], product[:half])
+        for block in range(len(keys)):
+            first_half, second_half = (
+                product[(2 * block + side) * half : (2 * block + side + 1) * half].astype(BF16) for side in range(2)
+            )
+            to = (slice(block * half, (block + 1) * half), columns_of(at, tile))
+            outs[0][to] = jnp.where(low, first_half, second_half)
+            outs[1][to] = jnp.where(low, second_half, first_half)
 
     return streamed(
         place,
@@ -339,7 +337,7 @@
         else:
             gathered = link(held[kind])
             blocks = [[(gathered, lambda s, key=key: (s[0] ^ key) * rows, rows)] for key in keys]
-        outs = partials(place, blocks, weight, kind == "act")
+        outs = partials(place, blocks, weight, kind == "act", 58 if keys == others[:1] else 48)
         chain.append(outs[0])
         for key, out in zip(keys, outs):
             own[kind, key] = out
@@ -377,7 +375,11 @@
     def tokens_of(keys, first, last):
         keep, give = token_grad(place, link(held["grads"]), weight_in, keys, rows, first, last)
         chain.append(keep)
-        return keys, keep, swap(give, 1)
+        return keys, keep, give
+
+    def exchange(parts):
+        keys, keep, give = parts
+        return keys, keep, swap(link(give), 1)
 
     def deliver(parts):
         keys, keep, given = parts
@@ -401,39 +403,41 @@
         if 3 <= slot + 1 < total:
             first_send(slot + 1)
         late = slot == 2
-        order = range(steps, 1, -1) if late else range(2, steps + 1)
         if late and slot >= steps - 1:
             finish(slot - steps + 1)
-        for step in order:
+        for step in range(steps, 1, -1) if late else range(2, steps + 1):
             if 0 <= slot - step + 2 < total:
                 forward(slot - step + 2, step)
+            if step == 2 and slot == len(others):
+                compute_own("act", others)
         if slot == 1:
-            compute_own("pre", others)
+            compute_own("pre", others[:1])
             first_send(2)
+            compute_own("pre", others[1:])
         if not late and slot >= steps - 1:
             finish(slot - steps + 1)
-        if slot == len(others):
-            compute_own("act", others)
         if slot == end - 4:
             out_columns(0, 4)
         if slot == end - 3:
-            early = tokens_of([0] + others[:-2], 0, UNITS)
+            out_columns(4, UNITS - 4)
         if slot == end - 2:
-            out_columns(4, UNITS - 4)
+            early = tokens_of([0] + others[:-1], 0, UNITS)
+    early = exchange(early)
+    front = UNITS // 2
+    parts = [exchange(tokens_of(others[-1:], 0, front)), exchange(tokens_of(others[-1:], front, UNITS))]
+    sums = link(functools.reduce(jnp.add, [sums[key] for key in sorted(sums)]).reshape(hidden))
+    levels = [1 << i for i in range(rows_of.bit_length() - 1)]
+    sums = sums + lax.ppermute(sums, "row", [(i, i ^ levels[0]) for i in range(rows_of)])
     arrived += deliver(early)
-    front = UNITS // 2
-    parts = [tokens_of(others[-2:], 0, front), tokens_of(others[-2:], front, UNITS)]
-    sides = [deliver(parts[0])]
-    in_rows(0, 2)
-    sides.append(deliver(parts[1]))
-    in_rows(2, UNITS - 2)
+    sides = [deliver(part) for part in parts]
+    in_rows(0, UNITS)
+    sums = link(sums)
+    for bit in levels[1:]:
+        sums = sums + lax.ppermute(sums, "row", [(i, i ^ bit) for i in range(rows_of)])
+    grad_bias = sums * (1.0 / rows_of)
     arrived += [jnp.concatenate(halves, axis=1) for halves in zip(*sides)]
     grad_tokens = functools.reduce(jnp.add, [part.astype(F32) for part in arrived]).astype(BF16)
 
-    sums = functools.reduce(jnp.add, [sums[key] for key in sorted(sums)]).reshape(hidden)
-    for bit in [1 << i for i in range(rows_of.bit_length() - 1)]:
-        sums = sums + lax.ppermute(sums, "row", [(i, i ^ bit) for i in range(rows_of)])
-    grad_bias = sums * (1.0 / rows_of)
     return (grad_tokens, held["in"], grad_bias, held["out"])
 
 

time: 302 us -> 281 us (0.930)
  waiting for transfers between devices: 88.7 us -> 69.7 us
  starting transfers between devices: 62.7 us -> 54.4 us
  local copies, waits for them, and re-layouts: 0.4 us -> 7.2 us
  Pallas kernels: 124 us -> 119 us
  other arithmetic: 10.6 us -> 14.4 us
    ppermute x24, waiting for transfers between devices: 75.4 us -> 53.2 us  [send(): return lax.ppermute(value, 'row', pairs)]
    ppermute x24, starting transfers between devices: 53.6 us -> 46.5 us  [send(): return lax.ppermute(value, 'row', pairs)]
    unnamed x42 -> x50, local copies, waits for them, and re-layouts: 0.4 us -> 7.19 us
    pallas_call x19, Pallas kernels: 124 us -> 119 us  [call(): pl.pallas_call(kernel, grid_spec=pltpu.PrefetchScalarGridSpec(num_scalar_...]
    convert_element_type x19, other arithmetic: 8.63 us -> 12.5 us  [add_bf16(): return (left.astype(F32) + right.astype(F32)).astype(BF16)]
    ppermute x10 -> x9, starting transfers between devices: 7.59 us -> 6.65 us  [swap(): return lax.ppermute(value, 'col', [(i, i ^ bits) for i in range(cols_of)])]
    ppermute x10 -> x9, waiting for transfers between devices: 8.9 us -> 9.33 us  [swap(): return lax.ppermute(value, 'col', [(i, i ^ bits) for i in range(cols_of)])]
  transfers between devices with their start and end apart: 38 -> 37, of which waited for: 13 -> 11; matrix products, arithmetic and copies ran while one was open for 3% -> 5% of each run, Pallas kernels for 39% -> 42%
where the time goes in v5:
time: 281 us; the launch traced here: 280 us
  Pallas kernels  119 us (42%)
  waiting for transfers between devices  69.7 us (25%)
  starting transfers between devices  54.4 us (19%)
  between operations  14.7 us (5%)
  other arithmetic  14.4 us (5%)
  local copies, waits for them, and re-layouts  7.2 us (3%)
    pallas_call x19, Pallas kernels, call(): pl.pallas_call(kernel, grid_spec=pltpu.PrefetchScalarGridSpec(num_scalar_...  119 us
    ppermute x24, waiting for transfers between devices, send(): return lax.ppermute(value, 'row', pairs)  53.2 us
    ppermute x24, starting transfers between devices, send(): return lax.ppermute(value, 'row', pairs)  46.5 us
    convert_element_type x19, other arithmetic, add_bf16(): return (left.astype(F32) + right.astype(F32)).astype(BF16)  12.5 us
    ppermute x9, waiting for transfers between devices, swap(): return lax.ppermute(value, 'col', [(i, i ^ bits) for i in range(cols_of)])  9.33 us
    unnamed x50, local copies, waits for them, and re-layouts  7.19 us
    ppermute x9, starting transfers between devices, swap(): return lax.ppermute(value, 'col', [(i, i ^ bits) for i in range(cols_of)])  6.65 us
  transfers between devices with their start and end apart: 37, of which 11 were waited for; matrix products, arithmetic and copies ran while one was open for 5% of the time, Pallas kernels for 42%

profile of v5, /device:TPU:0, one launch (start us, length us, event | category | flops | bytes accessed | tf_op | source)
XLA Modules:
  0.0 279.6 jit_solution(17275398246192908680)
XLA Ops:
  8.5 2.0 collective-permute-done.refs_1_
  11.0 6.3 %shard_map.84 = bf16[192,1792]{1,0:T(8,128)(2,1)S(1)} custom-call(s32[2]{0:T(128)S(1)} %pad_add_fusion.s, bf16[96,3584]{1,0:T(8,128)(2,1)S(1)} %copy-done.2, bf16[96,3584]{1,0:T(8,128)(2,1)S(1)} %collective-permute-done.refs_1_, bf16[3584,1792]{1,0:T(8,128)(2,1)} %refs_1_.11), custom_call_target="tpu_custom_call" | custom-call | flops 2466250752 | bytes 14221312 | tf_op jit(solution)/shard_map/pallas_call | solution.py:30
  17.3 4.7 %collective-permute-start.1 = (bf16[192,1792]{1,0:T(8,128)(2,1)S(1)}, bf16[192,1792]{1,0:T(8,128)(2,1)S(1)}, u32[]{:S(2)}, u32[]{:S(2)}) collective-permute-start(bf16[192,1792]{1,0:T(8,128)(2,1)S(1)} %shard_map.84), channel_id=1, source_target_pairs={{0,8},{24,16},{1,9},{25,17},{2,10},{26,18},{3,11},{27,19},{4,12},{... | collective-permute-start | bytes 2064392 | tf_op jit(solution)/shard_map/ppermute | solution.py:317
  23.9 7.3 %shard_map.85 = bf16[192,1792]{1,0:T(8,128)(2,1)S(1)} custom-call(s32[2]{0:T(128)S(1)} %pad_add_fusion.s, bf16[96,3584]{1,0:T(8,128)(2,1)S(1)} %copy-done.3, bf16[96,3584]{1,0:T(8,128)(2,1)S(1)} %copy-done.17, bf16[1792,3584]{1,0:T(8,128)(2,1)} %refs_1_.8), custom_call_target="tpu_custom_call" | custom-call | flops 2466250752 | bytes 14221312 | tf_op jit(solution)/shard_map/pallas_call | solution.py:30
  31.3 1.3 collective-permute-start.4
  32.6 5.1 %collective-permute-done.1 = bf16[192,1792]{1,0:T(8,128)(2,1)S(1)} collective-permute-done((bf16[192,1792]{1,0:T(8,128)(2,1)S(1)}, bf16[192,1792]{1,0:T(8,128)(2,1)S(1)}, u32[]{:S(2)}, u32[]{:S(2)}) %collective-permute-start.1) | collective-permute-done | bytes 688160 | tf_op jit(solution)/shard_map/ppermute | solution.py:317
  38.6 13.3 %collective-permute-done.4 = bf16[192,1792]{1,0:T(8,128)(2,1)S(1)} collective-permute-done((bf16[192,1792]{1,0:T(8,128)(2,1)S(1)}, bf16[192,1792]{1,0:T(8,128)(2,1)S(1)}, u32[]{:S(2)}, u32[]{:S(2)}) %collective-permute-start.4) | collective-permute-done | bytes 688160 | tf_op jit(solution)/shard_map/ppermute | solution.py:317
  52.9 1.6 collective-permute-start.7
  55.3 1.4 collective-permute-start.8
  56.8 8.8 %shard_map.86 = bf16[192,1792]{1,0:T(8,128)(2,1)} custom-call(s32[2]{0:T(128)} %copy-done.20, bf16[768,3584]{1,0:T(8,128)(2,1)} %all-gather.3.cloned.1.call-done.refs_0_.tok_ref, bf16[3584,1792]{1,0:T(8,128)(2,1)} %refs_1_.11), custom_call_target="tpu_custom_call" | custom-call | flops 2466250752 | bytes 14221312 | tf_op jit(solution)/shard_map/pallas_call | solution.py:30
  65.6 6.8 %collective-permute-start.6 = (bf16[192,1792]{1,0:T(8,128)(2,1)}, bf16[192,1792]{1,0:T(8,128)(2,1)S(1)}, u32[]{:S(2)}, u32[]{:S(2)}) collective-permute-start(bf16[192,1792]{1,0:T(8,128)(2,1)} %shard_map.86), channel_id=1, source_target_pairs={{0,8},{24,16},{1,9},{25,17},{2,10},{26,18},{3,11},{27,19},{4,12},{... | collective-permute-start | bytes 2064392 | tf_op jit(solution)/shard_map/ppermute | solution.py:317
  72.5 9.7 %shard_map.87 = (bf16[192,1792]{1,0:T(8,128)(2,1)S(1)}, bf16[192,1792]{1,0:T(8,128)(2,1)S(1)}) custom-call(s32[2]{0:T(128)S(1)} %copy-done.21, bf16[768,3584]{1,0:T(8,128)(2,1)} %all-gather.3.cloned.1.call-done.refs_0_.tok_ref, bf16[3584,1792]{1,0:T(8,128)(2,1)} %refs_1_.11), custom_call_target="tpu_custom_call" | custom-call | flops 4932501504 | bytes 15597568 | tf_op jit(solution)/shard_map/pallas_call | solution.py:30
  83.0 1.3 collective-permute-start.5
  86.3 1.8 shard_map.88
  88.1 2.6 add_convert_fusion.16
  93.1 1.5 collective-permute-start.10
  94.6 7.1 %collective-permute-done.5 = bf16[192,1792]{1,0:T(8,128)(2,1)S(1)} collective-permute-done((bf16[192,1792]{1,0:T(8,128)(2,1)S(1)}, bf16[192,1792]{1,0:T(8,128)(2,1)S(1)}, u32[]{:S(2)}, u32[]{:S(2)}) %collective-permute-start.5) | collective-permute-done | bytes 688160 | tf_op jit(solution)/shard_map/ppermute | solution.py:317
  101.9 1.5 collective-permute-start.14
  103.4 5.2 %collective-permute-start.9 = (bf16[192,1792]{1,0:T(8,128)(2,1)}, bf16[192,1792]{1,0:T(8,128)(2,1)S(1)}, u32[]{:S(2)}, u32[]{:S(2)}) collective-permute-start(bf16[192,1792]{1,0:T(8,128)(2,1)} %copy-done.8), channel_id=1, source_target_pairs={{0,8},{24,16},{1,9},{25,17},{2,10},{26,18},{3,11},{27,19},{4,12},{... | collective-permute-start | bytes 2064392 | tf_op jit(solution)/shard_map/ppermute | solution.py:317
  108.6 12.7 %shard_map.89 = (bf16[192,1792]{1,0:T(8,128)(2,1)S(1)}, bf16[192,1792]{1,0:T(8,128)(2,1)S(1)}, bf16[192,1792]{1,0:T(8,128)(2,1)S(1)}) custom-call(s32[2]{0:T(128)S(1)} %copy-done.21, bf16[768,3584]{1,0:T(8,128)(2,1)} %all-gather.5.cloned.1.call-done.refs_0_.grad_ref, bf16[1792,3584]{1,0:T(8,128)(2,1)} %refs_1_.8), custom_call_target="tpu_custom_call" | custom-call | flops 7398752256 | bytes 16973824 | tf_op jit(solution)/shard_map/pallas_call | solution.py:30
  121.4 1.4 add_convert_fusion.13
  122.9 2.5 shard_map.90
  125.4 1.4 collective-permute-start.15
  126.8 4.6 %collective-permute-start.13 = (bf16[192,1792]{1,0:T(8,128)(2,1)S(1)}, bf16[192,1792]{1,0:T(8,128)(2,1)S(1)}, u32[]{:S(2)}, u32[]{:S(2)}) collective-permute-start(bf16[192,1792]{1,0:T(8,128)(2,1)S(1)} %get-tuple-element.122), channel_id=1, source_target_pairs={{0,8},{24,16},{1,9},{25,17},{2,10},{26,18},{3,11},{27,19},{4,12},{... | collective-permute-start | bytes 2064392 | tf_op jit(solution)/shard_map/ppermute | solution.py:317
  133.7 1.3 collective-permute-start.16
  135.0 10.8 %collective-permute-done.15.refs_2_ = bf16[192,1792]{1,0:T(8,128)(2,1)S(1)} collective-permute-done((bf16[192,1792]{1,0:T(8,128)(2,1)S(1)}, bf16[192,1792]{1,0:T(8,128)(2,1)S(1)}, u32[]{:S(2)}, u32[]{:S(2)}) %collective-permute-start.15) | collective-permute-done | bytes 688160 | tf_op jit(solution)/shard_map/ppermute | solution.py:317
  145.8 3.1 %shard_map.91 = (bf16[768,1792]{1,0:T(8,128)(2,1)S(1)}, f32[192,1792]{1,0:T(8,128)S(1)}) custom-call(s32[2]{0:T(128)S(1)} %copy-done.21, f32[1,1792]{1,0:T(1,128)S(1)} %reshape.14.bias_ref, bf16[192,1792]{1,0:T(8,128)(2,1)} %add_convert_fusion.15.refs_0_, bf16[192,1792]{1,0:T(8,128)(2,1)} %collective-permute-done.10.refs_1_, ...), custom_call_target="tpu_custom_call", output_to_operand_aliasing={{0}: (5, {})} | custom-call | flops 10321920 | bytes 4128768 | tf_op jit(solution)/shard_map/pallas_call | solution.py:30
  148.9 1.5 collective-permute-start.17
  153.6 6.9 %collective-permute-done.16.refs_2_ = bf16[192,1792]{1,0:T(8,128)(2,1)S(1)} collective-permute-done((bf16[192,1792]{1,0:T(8,128)(2,1)S(1)}, bf16[192,1792]{1,0:T(8,128)(2,1)S(1)}, u32[]{:S(2)}, u32[]{:S(2)}) %collective-permute-start.16) | collective-permute-done | bytes 688160 | tf_op jit(solution)/shard_map/ppermute | solution.py:317
  160.6 2.9 %shard_map.92 = (bf16[768,1792]{1,0:T(8,128)(2,1)S(1)}, f32[192,1792]{1,0:T(8,128)S(1)}) custom-call(s32[2]{0:T(128)S(1)} %copy-done.21, f32[1,1792]{1,0:T(1,128)S(1)} %reshape.14.bias_ref, bf16[192,1792]{1,0:T(8,128)(2,1)S(1)} %add_convert_fusion.14.refs_0_, bf16[192,1792]{1,0:T(8,128)(2,1)} %collective-permute-done.14.refs_1_, ...), custom_call_target="tpu_custom_call", output_to_operand_aliasing={{0}: (5, {})} | custom-call | flops 10321920 | bytes 4128768 | tf_op jit(solution)/shard_map/pallas_call | solution.py:30
  163.4 2.3 collective-permute-start.18
  169.0 6.5 %collective-permute-done.20.refs_2_ = bf16[192,1792]{1,0:T(8,128)(2,1)} collective-permute-done((bf16[192,1792]{1,0:T(8,128)(2,1)}, bf16[192,1792]{1,0:T(8,128)(2,1)}, u32[]{:S(2)}, u32[]{:S(2)}) %collective-permute-start.20) | collective-permute-done | bytes 688160 | tf_op jit(solution)/shard_map/ppermute | solution.py:317
  175.4 2.9 %shard_map.93 = (bf16[768,1792]{1,0:T(8,128)(2,1)S(1)}, f32[192,1792]{1,0:T(8,128)S(1)}) custom-call(s32[2]{0:T(128)S(1)} %copy-done.21, f32[1,1792]{1,0:T(1,128)S(1)} %reshape.14.bias_ref, bf16[192,1792]{1,0:T(8,128)(2,1)S(1)} %add_convert_fusion.12.refs_0_, bf16[192,1792]{1,0:T(8,128)(2,1)S(1)} %collective-permute-done.12.refs_1_, ...), custom_call_target="tpu_custom_call", output_to_operand_aliasing={{0}: (5, {})} | custom-call | flops 10321920 | bytes 4128768 | tf_op jit(solution)/shard_map/pallas_call | solution.py:30
  178.3 11.0 %shard_map.94.refs_0_ = f32[1792,3584]{1,0:T(8,128)} custom-call(s32[2]{0:T(128)S(1)} %copy-done.21, bf16[768,1792]{1,0:T(8,128)(2,1)S(1)} %get-tuple-element.131.act_ref, bf16[768,3584]{1,0:T(8,128)(2,1)} %all-gather.5.cloned.1.call-done.refs_0_.grad_ref), custom_call_target="tpu_custom_call" | custom-call | flops 5637144576 | bytes 20578304 | tf_op jit(solution)/shard_map/pallas_call | solution.py:30
  193.8 9.3 %shard_map.96 = f32[1792,3584]{1,0:T(8,128)} custom-call(s32[2]{0:T(128)S(1)} %copy-done.21, bf16[768,1792]{1,0:T(8,128)(2,1)S(1)} %get-tuple-element.131.act_ref, bf16[768,3584]{1,0:T(8,128)(2,1)} %all-gather.5.cloned.1.call-done.refs_0_.grad_ref, f32[1792,3584]{1,0:T(8,128)} %shard_map.94.refs_0_), custom_call_target="tpu_custom_call", output_to_operand_aliasing={{}: (3, {})} | custom-call | flops 4227858432 | bytes 16121856 | tf_op jit(solution)/shard_map/pallas_call | solution.py:30
  203.2 1.3 collective-permute-start.25
  204.5 3.5 %collective-permute-done.24.refs_2_ = bf16[192,1792]{1,0:T(8,128)(2,1)S(1)} collective-permute-done((bf16[192,1792]{1,0:T(8,128)(2,1)S(1)}, bf16[192,1792]{1,0:T(8,128)(2,1)S(1)}, u32[]{:S(2)}, u32[]{:S(2)}) %collective-permute-start.24) | collective-permute-done | bytes 688160 | tf_op jit(solution)/shard_map/ppermute | solution.py:317
  209.0 1.5 copy-done
  210.5 12.4 %shard_map.98 = (bf16[288,3584]{1,0:T(8,128)(2,1)S(1)}, bf16[288,3584]{1,0:T(8,128)(2,1)S(1)}) custom-call(s32[2]{0:T(128)S(1)} %copy-done.21, bf16[768,1792]{1,0:T(8,128)(2,1)} %copy-done, bf16[3584,1792]{1,0:T(8,128)(2,1)} %refs_1_.11), custom_call_target="tpu_custom_call" | custom-call | flops 7398752256 | bytes 14909440 | tf_op jit(solution)/shard_map/pallas_call | solution.py:30
  224.0 4.3 %shard_map.100 = (bf16[96,1536]{1,0:T(8,128)(2,1)S(1)}, bf16[96,1536]{1,0:T(8,128)(2,1)S(1)}) custom-call(s32[2]{0:T(128)S(1)} %copy-done.21, bf16[768,1792]{1,0:T(8,128)(2,1)S(1)} %get-tuple-element.153.refs_0_.grad_ref, bf16[3584,1792]{1,0:T(8,128)(2,1)} %refs_1_.11), custom_call_target="tpu_custom_call" | custom-call | flops 1056964608 | bytes 6193152 | tf_op jit(solution)/shard_map/pallas_call | solution.py:30
  228.4 5.1 %shard_map.101 = (bf16[96,2048]{1,0:T(8,128)(2,1)S(1)}, bf16[96,2048]{1,0:T(8,128)(2,1)S(1)}) custom-call(s32[2]{0:T(128)S(1)} %copy-done.21, bf16[768,1792]{1,0:T(8,128)(2,1)S(1)} %get-tuple-element.153.refs_0_.grad_ref, bf16[3584,1792]{1,0:T(8,128)(2,1)} %refs_1_.11), custom_call_target="tpu_custom_call" | custom-call | flops 1409286144 | bytes 8028160 | tf_op jit(solution)/shard_map/pallas_call | solution.py:30
  234.2 3.0 %collective-permute-done.33 = f32[1792]{0:T(1024)S(1)} collective-permute-done((f32[1792]{0:T(1024)S(1)}, f32[1792]{0:T(1024)S(1)}, u32[]{:S(2)}, u32[]{:S(2)}) %collective-permute-start.33) | collective-permute-done | bytes 7200 | tf_op jit(solution)/shard_map/ppermute | solution.py:430
  237.6 1.4 collective-permute-start.30
  239.9 1.3 collective-permute-start.28
  241.2 1.5 collective-permute-start.27
  242.7 16.4 %shard_map.102 = f32[3584,1792]{1,0:T(8,128)} custom-call(s32[2]{0:T(128)S(1)} %copy-done.21, bf16[768,3584]{1,0:T(8,128)(2,1)} %all-gather.3.cloned.1.call-done.refs_0_.tok_ref, bf16[768,1792]{1,0:T(8,128)(2,1)S(1)} %get-tuple-element.153.refs_0_.grad_ref), custom_call_target="tpu_custom_call" | custom-call | flops 9865003008 | bytes 33947648 | tf_op jit(solution)/shard_map/pallas_call | solution.py:30
  260.1 3.5 %collective-permute-done.34 = f32[1792]{0:T(1024)S(1)} collective-permute-done((f32[1792]{0:T(1024)S(1)}, f32[1792]{0:T(1024)S(1)}, u32[]{:S(2)}, u32[]{:S(2)}) %collective-permute-start.34) | collective-permute-done | bytes 7200 | tf_op jit(solution)/shard_map/ppermute | solution.py:436
  264.2 7.3 %collective-permute-done.27 = bf16[96,3584]{1,0:T(8,128)(2,1)S(1)} collective-permute-done((bf16[96,3584]{1,0:T(8,128)(2,1)S(1)}, bf16[96,3584]{1,0:T(8,128)(2,1)S(1)}, u32[]{:S(2)}, u32[]{:S(2)}) %collective-permute-start.27) | collective-permute-done | bytes 688160 | tf_op jit(solution)/shard_map/ppermute | solution.py:320
  (122 shorter events, 32.1 us)
Async XLA Ops:
  7.2 49.6 %all-gather.3.cloned.1.call-start = ((), (), s32[]{:S(2)}) async-start(), calls=%async_computation | async-start | bytes 6193152 | tf_op jit(solution)/shard_map/all_gather | solution.py:395
  7.9 95.5 %all-gather.5.cloned.1.call-start = ((), (), s32[]{:S(2)}) async-start(), calls=%async_computation.1 | async-start | bytes 6193152 | tf_op jit(solution)/shard_map/all_gather | solution.py:396
  8.0 2.5 collective-permute-start
  10.5 11.5 %collective-permute-start.2 = (bf16[96,3584]{1,0:T(8,128)(2,1)S(1)}, bf16[96,3584]{1,0:T(8,128)(2,1)S(1)}, u32[]{:S(2)}, u32[]{:S(2)}) collective-permute-start(bf16[96,3584]{1,0:T(8,128)(2,1)S(1)} %copy-done.3), channel_id=1, source_target_pairs={{0,1},{1,0},{2,3},{3,2},{4,5},{5,4},{6,7},{7,6},{8,9},{9,8},{10,11... | collective-permute-start | bytes 2064392 | tf_op jit(solution)/shard_map/ppermute | solution.py:320
  11.0 11.0 %copy-start.20 = (s32[2]{0:T(128)}, s32[2]{0:T(128)S(1)}, u32[]{:S(2)}) copy-start(s32[2]{0:T(128)S(1)} %pad_add_fusion.s) | copy-start | bytes 28
  17.3 20.4 %collective-permute-start.1 = (bf16[192,1792]{1,0:T(8,128)(2,1)S(1)}, bf16[192,1792]{1,0:T(8,128)(2,1)S(1)}, u32[]{:S(2)}, u32[]{:S(2)}) collective-permute-start(bf16[192,1792]{1,0:T(8,128)(2,1)S(1)} %shard_map.84), channel_id=1, source_target_pairs={{0,8},{24,16},{1,9},{25,17},{2,10},{26,18},{3,11},{27,19},{4,12},{... | collective-permute-start | bytes 2064392 | tf_op jit(solution)/shard_map/ppermute | solution.py:317
  31.3 20.6 %collective-permute-start.4 = (bf16[192,1792]{1,0:T(8,128)(2,1)S(1)}, bf16[192,1792]{1,0:T(8,128)(2,1)S(1)}, u32[]{:S(2)}, u32[]{:S(2)}) collective-permute-start(bf16[192,1792]{1,0:T(8,128)(2,1)S(1)} %shard_map.85), channel_id=1, source_target_pairs={{0,8},{24,16},{1,9},{25,17},{2,10},{26,18},{3,11},{27,19},{4,12},{... | collective-permute-start | bytes 2064392 | tf_op jit(solution)/shard_map/ppermute | solution.py:317
  37.8 16.8 %copy-start.4 = (bf16[192,1792]{1,0:T(8,128)(2,1)}, bf16[192,1792]{1,0:T(8,128)(2,1)S(1)}, u32[]{:S(2)}) copy-start(bf16[192,1792]{1,0:T(8,128)(2,1)S(1)} %add_convert_fusion.19.refs_0_) | copy-start | bytes 2064388
  37.8 16.6 %collective-permute-start.3 = (bf16[192,1792]{1,0:T(8,128)(2,1)S(1)}, bf16[192,1792]{1,0:T(8,128)(2,1)S(1)}, u32[]{:S(2)}, u32[]{:S(2)}) collective-permute-start(bf16[192,1792]{1,0:T(8,128)(2,1)S(1)} %add_convert_fusion.19.refs_0_), channel_id=1, source_target_pairs={{8,16},{16,8},{9,17},{17,9},{10,18},{18,10},{11,19},{19,11},{12,20... | collective-permute-start | bytes 2064392 | tf_op jit(solution)/shard_map/ppermute | solution.py:317
  52.9 35.2 %collective-permute-start.7 = (bf16[192,1792]{1,0:T(8,128)(2,1)}, bf16[192,1792]{1,0:T(8,128)(2,1)}, u32[]{:S(2)}, u32[]{:S(2)}) collective-permute-start(bf16[192,1792]{1,0:T(8,128)(2,1)} %add_convert_fusion.18.refs_0_), channel_id=1, source_target_pairs={{8,16},{16,8},{9,17},{17,9},{10,18},{18,10},{11,19},{19,11},{12,20... | collective-permute-start | bytes 2064392 | tf_op jit(solution)/shard_map/ppermute | solution.py:317
  55.3 17.1 %copy-start.21 = (s32[2]{0:T(128)S(1)}, s32[2]{0:T(128)}, u32[]{:S(2)}) copy-start(s32[2]{0:T(128)} %copy-done.20) | copy-start | bytes 28
  55.3 29.0 %collective-permute-start.8 = (bf16[192,1792]{1,0:T(8,128)(2,1)S(1)}, bf16[192,1792]{1,0:T(8,128)(2,1)S(1)}, u32[]{:S(2)}, u32[]{:S(2)}) collective-permute-start(bf16[192,1792]{1,0:T(8,128)(2,1)S(1)} %add_convert_fusion.17), channel_id=1, source_target_pairs={{16,24},{8,0},{17,25},{9,1},{18,26},{10,2},{19,27},{11,3},{20,28},... | collective-permute-start | bytes 2064392 | tf_op jit(solution)/shard_map/ppermute | solution.py:317
  65.6 19.6 %copy-start.5 = (bf16[192,1792]{1,0:T(8,128)(2,1)S(1)}, bf16[192,1792]{1,0:T(8,128)(2,1)}, u32[]{:S(2)}) copy-start(bf16[192,1792]{1,0:T(8,128)(2,1)} %copy-done.4) | copy-start | bytes 2064388
  65.6 19.6 %copy-start.7 = (bf16[192,1792]{1,0:T(8,128)(2,1)S(1)}, bf16[192,1792]{1,0:T(8,128)(2,1)}, u32[]{:S(2)}) copy-start(bf16[192,1792]{1,0:T(8,128)(2,1)} %copy-done.6) | copy-start | bytes 2064388
  65.6 26.4 %collective-permute-start.6 = (bf16[192,1792]{1,0:T(8,128)(2,1)}, bf16[192,1792]{1,0:T(8,128)(2,1)S(1)}, u32[]{:S(2)}, u32[]{:S(2)}) collective-permute-start(bf16[192,1792]{1,0:T(8,128)(2,1)} %shard_map.86), channel_id=1, source_target_pairs={{0,8},{24,16},{1,9},{25,17},{2,10},{26,18},{3,11},{27,19},{4,12},{... | collective-permute-start | bytes 2064392 | tf_op jit(solution)/shard_map/ppermute | solution.py:317
  83.0 18.7 %copy-start.10 = (bf16[192,1792]{1,0:T(8,128)(2,1)}, bf16[192,1792]{1,0:T(8,128)(2,1)S(1)}, u32[]{:S(2)}) copy-start(bf16[192,1792]{1,0:T(8,128)(2,1)S(1)} %get-tuple-element.109) | copy-start | bytes 2064388
  83.0 18.7 %collective-permute-start.5 = (bf16[192,1792]{1,0:T(8,128)(2,1)S(1)}, bf16[192,1792]{1,0:T(8,128)(2,1)S(1)}, u32[]{:S(2)}, u32[]{:S(2)}) collective-permute-start(bf16[192,1792]{1,0:T(8,128)(2,1)S(1)} %get-tuple-element.109), channel_id=1, source_target_pairs={{0,8},{24,16},{1,9},{25,17},{2,10},{26,18},{3,11},{27,19},{4,12},{... | collective-permute-start | bytes 2064392 | tf_op jit(solution)/shard_map/ppermute | solution.py:317
  90.8 32.0 %collective-permute-start.11 = (bf16[192,1792]{1,0:T(8,128)(2,1)}, bf16[192,1792]{1,0:T(8,128)(2,1)}, u32[]{:S(2)}, u32[]{:S(2)}) collective-permute-start(bf16[192,1792]{1,0:T(8,128)(2,1)} %add_convert_fusion.16), channel_id=1, source_target_pairs={{16,24},{8,0},{17,25},{9,1},{18,26},{10,2},{19,27},{11,3},{20,28},... | collective-permute-start | bytes 2064392 | tf_op jit(solution)/shard_map/ppermute | solution.py:317
  93.1 28.3 %collective-permute-start.10 = (bf16[192,1792]{1,0:T(8,128)(2,1)}, bf16[192,1792]{1,0:T(8,128)(2,1)}, u32[]{:S(2)}, u32[]{:S(2)}) collective-permute-start(bf16[192,1792]{1,0:T(8,128)(2,1)} %add_convert_fusion.15.refs_0_), channel_id=1, source_target_pairs={{8,16},{16,8},{9,17},{17,9},{10,18},{18,10},{11,19},{19,11},{12,20... | collective-permute-start | bytes 2064392 | tf_op jit(solution)/shard_map/ppermute | solution.py:317
  101.9 30.5 %collective-permute-start.14 = (bf16[192,1792]{1,0:T(8,128)(2,1)S(1)}, bf16[192,1792]{1,0:T(8,128)(2,1)}, u32[]{:S(2)}, u32[]{:S(2)}) collective-permute-start(bf16[192,1792]{1,0:T(8,128)(2,1)S(1)} %add_convert_fusion.14.refs_0_), channel_id=1, source_target_pairs={{8,16},{16,8},{9,17},{17,9},{10,18},{18,10},{11,19},{19,11},{12,20... | collective-permute-start | bytes 2064392 | tf_op jit(solution)/shard_map/ppermute | solution.py:317
  103.4 18.0 %copy-start.23 = (bf16[192,1792]{1,0:T(8,128)(2,1)S(1)}, bf16[192,1792]{1,0:T(8,128)(2,1)}, u32[]{:S(2)}) copy-start(bf16[192,1792]{1,0:T(8,128)(2,1)} %shard_map.86) | copy-start | bytes 2064388
  103.4 28.1 %collective-permute-start.9 = (bf16[192,1792]{1,0:T(8,128)(2,1)}, bf16[192,1792]{1,0:T(8,128)(2,1)S(1)}, u32[]{:S(2)}, u32[]{:S(2)}) collective-permute-start(bf16[192,1792]{1,0:T(8,128)(2,1)} %copy-done.8), channel_id=1, source_target_pairs={{0,8},{24,16},{1,9},{25,17},{2,10},{26,18},{3,11},{27,19},{4,12},{... | collective-permute-start | bytes 2064392 | tf_op jit(solution)/shard_map/ppermute | solution.py:317
  122.9 8.6 %copy-start.9 = (bf16[192,1792]{1,0:T(8,128)(2,1)S(1)}, bf16[192,1792]{1,0:T(8,128)(2,1)}, u32[]{:S(2)}) copy-start(bf16[192,1792]{1,0:T(8,128)(2,1)} %copy-done.8) | copy-start | bytes 2064388
  125.4 20.4 %collective-permute-start.15 = (bf16[192,1792]{1,0:T(8,128)(2,1)S(1)}, bf16[192,1792]{1,0:T(8,128)(2,1)S(1)}, u32[]{:S(2)}, u32[]{:S(2)}) collective-permute-start(bf16[192,1792]{1,0:T(8,128)(2,1)S(1)} %add_convert_fusion.13), channel_id=1, source_target_pairs={{16,24},{8,0},{17,25},{9,1},{18,26},{10,2},{19,27},{11,3},{20,28},... | collective-permute-start | bytes 2064392 | tf_op jit(solution)/shard_map/ppermute | solution.py:317
  126.8 23.5 %collective-permute-start.13 = (bf16[192,1792]{1,0:T(8,128)(2,1)S(1)}, bf16[192,1792]{1,0:T(8,128)(2,1)S(1)}, u32[]{:S(2)}, u32[]{:S(2)}) collective-permute-start(bf16[192,1792]{1,0:T(8,128)(2,1)S(1)} %get-tuple-element.122), channel_id=1, source_target_pairs={{0,8},{24,16},{1,9},{25,17},{2,10},{26,18},{3,11},{27,19},{4,12},{... | collective-permute-start | bytes 2064392 | tf_op jit(solution)/shard_map/ppermute | solution.py:317
  131.7 19.6 %collective-permute-start.12 = (bf16[192,1792]{1,0:T(8,128)(2,1)S(1)}, bf16[192,1792]{1,0:T(8,128)(2,1)S(1)}, u32[]{:S(2)}, u32[]{:S(2)}) collective-permute-start(bf16[192,1792]{1,0:T(8,128)(2,1)S(1)} %add_convert_fusion.12.refs_0_), channel_id=1, source_target_pairs={{8,16},{16,8},{9,17},{17,9},{10,18},{18,10},{11,19},{19,11},{12,20... | collective-permute-start | bytes 2064392 | tf_op jit(solution)/shard_map/ppermute | solution.py:317
  133.7 26.9 %collective-permute-start.16 = (bf16[192,1792]{1,0:T(8,128)(2,1)S(1)}, bf16[192,1792]{1,0:T(8,128)(2,1)S(1)}, u32[]{:S(2)}, u32[]{:S(2)}) collective-permute-start(bf16[192,1792]{1,0:T(8,128)(2,1)S(1)} %add_convert_fusion.11), channel_id=1, source_target_pairs={{16,24},{8,0},{17,25},{9,1},{18,26},{10,2},{19,27},{11,3},{20,28},... | collective-permute-start | bytes 2064392 | tf_op jit(solution)/shard_map/ppermute | solution.py:317
  148.9 16.9 %collective-permute-start.17 = (bf16[192,1792]{1,0:T(8,128)(2,1)S(1)}, bf16[192,1792]{1,0:T(8,128)(2,1)S(1)}, u32[]{:S(2)}, u32[]{:S(2)}) collective-permute-start(bf16[192,1792]{1,0:T(8,128)(2,1)S(1)} %get-tuple-element.128), channel_id=1, source_target_pairs={{0,8},{24,16},{1,9},{25,17},{2,10},{26,18},{3,11},{27,19},{4,12},{... | collective-permute-start | bytes 2064392 | tf_op jit(solution)/shard_map/ppermute | solution.py:317
  150.6 15.3 %collective-permute-start.19 = (bf16[192,1792]{1,0:T(8,128)(2,1)S(1)}, bf16[192,1792]{1,0:T(8,128)(2,1)S(1)}, u32[]{:S(2)}, u32[]{:S(2)}) collective-permute-start(bf16[192,1792]{1,0:T(8,128)(2,1)S(1)} %add_convert_fusion.10.refs_0_), channel_id=1, source_target_pairs={{8,16},{16,8},{9,17},{17,9},{10,18},{18,10},{11,19},{19,11},{12,20... | collective-permute-start | bytes 2064392 | tf_op jit(solution)/shard_map/ppermute | solution.py:317
  152.3 23.1 %collective-permute-start.20 = (bf16[192,1792]{1,0:T(8,128)(2,1)}, bf16[192,1792]{1,0:T(8,128)(2,1)}, u32[]{:S(2)}, u32[]{:S(2)}) collective-permute-start(bf16[192,1792]{1,0:T(8,128)(2,1)} %add_convert_fusion.9), channel_id=1, source_target_pairs={{16,24},{8,0},{17,25},{9,1},{18,26},{10,2},{19,27},{11,3},{20,28},... | collective-permute-start | bytes 2064392 | tf_op jit(solution)/shard_map/ppermute | solution.py:317
  163.4 25.9 %collective-permute-start.18 = (bf16[192,1792]{1,0:T(8,128)(2,1)S(1)}, bf16[192,1792]{1,0:T(8,128)(2,1)}, u32[]{:S(2)}, u32[]{:S(2)}) collective-permute-start(bf16[192,1792]{1,0:T(8,128)(2,1)S(1)} %get-tuple-element.132), channel_id=1, source_target_pairs={{0,8},{24,16},{1,9},{25,17},{2,10},{26,18},{3,11},{27,19},{4,12},{... | collective-permute-start | bytes 2064392 | tf_op jit(solution)/shard_map/ppermute | solution.py:317
  167.0 25.8 %collective-permute-start.23 = (bf16[192,1792]{1,0:T(8,128)(2,1)}, bf16[192,1792]{1,0:T(8,128)(2,1)S(1)}, u32[]{:S(2)}, u32[]{:S(2)}) collective-permute-start(bf16[192,1792]{1,0:T(8,128)(2,1)} %add_convert_fusion.7), channel_id=1, source_target_pairs={{16,24},{8,0},{17,25},{9,1},{18,26},{10,2},{19,27},{11,3},{20,28},... | collective-permute-start | bytes 2064392 | tf_op jit(solution)/shard_map/ppermute | solution.py:317
  168.2 23.0 %collective-permute-start.22 = (bf16[192,1792]{1,0:T(8,128)(2,1)S(1)}, bf16[192,1792]{1,0:T(8,128)(2,1)S(1)}, u32[]{:S(2)}, u32[]{:S(2)}) collective-permute-start(bf16[192,1792]{1,0:T(8,128)(2,1)S(1)} %add_convert_fusion.8.refs_0_), channel_id=1, source_target_pairs={{8,16},{16,8},{9,17},{17,9},{10,18},{18,10},{11,19},{19,11},{12,20... | collective-permute-start | bytes 2064392 | tf_op jit(solution)/shard_map/ppermute | solution.py:317
  178.3 11.0 %copy-start.12 = (f32[192,1792]{1,0:T(8,128)}, f32[192,1792]{1,0:T(8,128)S(1)}, u32[]{:S(2)}) copy-start(f32[192,1792]{1,0:T(8,128)S(1)} %get-tuple-element.137.slope_ref) | copy-start | bytes 4128772
  190.6 12.5 %collective-permute-start.21 = (bf16[192,1792]{1,0:T(8,128)(2,1)S(1)}, bf16[192,1792]{1,0:T(8,128)(2,1)S(1)}, u32[]{:S(2)}, u32[]{:S(2)}) collective-permute-start(bf16[192,1792]{1,0:T(8,128)(2,1)S(1)} %add_convert_fusion.6.refs_0_), channel_id=1, source_target_pairs={{8,16},{16,8},{9,17},{17,9},{10,18},{18,10},{11,19},{19,11},{12,20... | collective-permute-start | bytes 2064392 | tf_op jit(solution)/shard_map/ppermute | solution.py:317
  191.5 16.5 %collective-permute-start.24 = (bf16[192,1792]{1,0:T(8,128)(2,1)S(1)}, bf16[192,1792]{1,0:T(8,128)(2,1)S(1)}, u32[]{:S(2)}, u32[]{:S(2)}) collective-permute-start(bf16[192,1792]{1,0:T(8,128)(2,1)S(1)} %add_convert_fusion.5), channel_id=1, source_target_pairs={{16,24},{8,0},{17,25},{9,1},{18,26},{10,2},{19,27},{11,3},{20,28},... | collective-permute-start | bytes 2064392 | tf_op jit(solution)/shard_map/ppermute | solution.py:317
  203.2 19.7 %collective-permute-start.25 = (bf16[192,1792]{1,0:T(8,128)(2,1)S(1)}, bf16[192,1792]{1,0:T(8,128)(2,1)S(1)}, u32[]{:S(2)}, u32[]{:S(2)}) collective-permute-start(bf16[192,1792]{1,0:T(8,128)(2,1)S(1)} %add_convert_fusion.4), channel_id=1, source_target_pairs={{16,24},{8,0},{17,25},{9,1},{18,26},{10,2},{19,27},{11,3},{20,28},... | collective-permute-start | bytes 2064392 | tf_op jit(solution)/shard_map/ppermute | solution.py:317
  210.5 12.4 %copy-start.1 = (bf16[768,1792]{1,0:T(8,128)(2,1)S(1)}, bf16[768,1792]{1,0:T(8,128)(2,1)}, u32[]{:S(2)}) copy-start(bf16[768,1792]{1,0:T(8,128)(2,1)} %copy-done) | copy-start | bytes 8257540
  210.5 12.4 %copy-start.13 = (f32[192,1792]{1,0:T(8,128)S(1)}, f32[192,1792]{1,0:T(8,128)}, u32[]{:S(2)}) copy-start(f32[192,1792]{1,0:T(8,128)} %copy-done.12) | copy-start | bytes 4128772
  223.9 13.3 %collective-permute-start.26 = (bf16[288,3584]{1,0:T(8,128)(2,1)S(1)}, bf16[288,3584]{1,0:T(8,128)(2,1)S(1)}, u32[]{:S(2)}, u32[]{:S(2)}) collective-permute-start(bf16[288,3584]{1,0:T(8,128)(2,1)S(1)} %get-tuple-element.146), channel_id=1, source_target_pairs={{0,1},{1,0},{2,3},{3,2},{4,5},{5,4},{6,7},{7,6},{8,9},{9,8},{10,11... | collective-permute-start | bytes 6193160 | tf_op jit(solution)/shard_map/ppermute | solution.py:320
  233.5 3.7 %collective-permute-start.33 = (f32[1792]{0:T(1024)S(1)}, f32[1792]{0:T(1024)S(1)}, u32[]{:S(2)}, u32[]{:S(2)}) collective-permute-start(f32[1792]{0:T(1024)S(1)} %add_reduce_fusion), channel_id=1, source_target_pairs={{0,8},{8,0},{16,24},{24,16},{1,9},{9,1},{17,25},{25,17},{2,10},{10... | collective-permute-start | bytes 21512 | tf_op jit(solution)/shard_map/ppermute | solution.py:430
  233.5 4.0 %collective-permute-start.29 = (bf16[96,1536]{1,0:T(8,128)(2,1)S(1)}, bf16[96,1536]{1,0:T(8,128)(2,1)S(1)}, u32[]{:S(2)}, u32[]{:S(2)}) collective-permute-start(bf16[96,1536]{1,0:T(8,128)(2,1)S(1)} %get-tuple-element.149), channel_id=1, source_target_pairs={{0,1},{1,0},{2,3},{3,2},{4,5},{5,4},{6,7},{7,6},{8,9},{9,8},{10,11... | collective-permute-start | bytes 884744 | tf_op jit(solution)/shard_map/ppermute | solution.py:320
  234.1 4.9 %collective-permute-start.31 = (bf16[96,2048]{1,0:T(8,128)(2,1)S(1)}, bf16[96,2048]{1,0:T(8,128)(2,1)S(1)}, u32[]{:S(2)}, u32[]{:S(2)}) collective-permute-start(bf16[96,2048]{1,0:T(8,128)(2,1)S(1)} %get-tuple-element.152), channel_id=1, source_target_pairs={{0,1},{1,0},{2,3},{3,2},{4,5},{5,4},{6,7},{7,6},{8,9},{9,8},{10,11... | collective-permute-start | bytes 1179656 | tf_op jit(solution)/shard_map/ppermute | solution.py:320
  237.6 26.6 %collective-permute-start.30 = (bf16[96,1536]{1,0:T(8,128)(2,1)S(1)}, bf16[96,1536]{1,0:T(8,128)(2,1)S(1)}, u32[]{:S(2)}, u32[]{:S(2)}) collective-permute-start(bf16[96,1536]{1,0:T(8,128)(2,1)S(1)} %add_convert_fusion.21), channel_id=1, source_target_pairs={{0,4},{1,5},{2,6},{3,7},{4,0},{5,1},{6,2},{7,3},{8,12},{9,13},{10,... | collective-permute-start | bytes 884744 | tf_op jit(solution)/shard_map/ppermute | solution.py:320
  239.1 25.1 %collective-permute-start.32 = (bf16[96,2048]{1,0:T(8,128)(2,1)S(1)}, bf16[96,2048]{1,0:T(8,128)(2,1)S(1)}, u32[]{:S(2)}, u32[]{:S(2)}) collective-permute-start(bf16[96,2048]{1,0:T(8,128)(2,1)S(1)} %add_convert_fusion.20), channel_id=1, source_target_pairs={{0,4},{1,5},{2,6},{3,7},{4,0},{5,1},{6,2},{7,3},{8,12},{9,13},{10,... | collective-permute-start | bytes 1179656 | tf_op jit(solution)/shard_map/ppermute | solution.py:320
  239.9 31.7 %collective-permute-start.28 = (bf16[96,3584]{1,0:T(8,128)(2,1)S(1)}, bf16[96,3584]{1,0:T(8,128)(2,1)S(1)}, u32[]{:S(2)}, u32[]{:S(2)}) collective-permute-start(bf16[96,3584]{1,0:T(8,128)(2,1)S(1)} %get-tuple-element.161), channel_id=1, source_target_pairs={{0,2},{1,3},{2,0},{3,1},{4,6},{5,7},{6,4},{7,5},{8,10},{9,11},{10,... | collective-permute-start | bytes 2064392 | tf_op jit(solution)/shard_map/ppermute | solution.py:320
  241.2 30.3 %collective-permute-start.27 = (bf16[96,3584]{1,0:T(8,128)(2,1)S(1)}, bf16[96,3584]{1,0:T(8,128)(2,1)S(1)}, u32[]{:S(2)}, u32[]{:S(2)}) collective-permute-start(bf16[96,3584]{1,0:T(8,128)(2,1)S(1)} %get-tuple-element.160), channel_id=1, source_target_pairs={{0,6},{1,7},{2,4},{3,5},{4,2},{5,3},{6,0},{7,1},{8,14},{9,15},{10,... | collective-permute-start | bytes 2064392 | tf_op jit(solution)/shard_map/ppermute | solution.py:320
  259.0 4.5 %collective-permute-start.34 = (f32[1792]{0:T(1024)S(1)}, f32[1792]{0:T(1024)S(1)}, u32[]{:S(2)}, u32[]{:S(2)}) collective-permute-start(f32[1792]{0:T(1024)S(1)} %add.120), channel_id=1, source_target_pairs={{0,16},{8,24},{16,0},{24,8},{1,17},{9,25},{17,1},{25,9},{2,18},{10... | collective-permute-start | bytes 21512 | tf_op jit(solution)/shard_map/ppermute | solution.py:436
  (14 other events, 39.2 us)
Sparse Core Ops, SparseCore 0:
  9.9 44.9 all-gather.2
  56.7 42.3 all-gather.4

commit v6 on v5

--- a/solution.py
+++ b/solution.py
@@ -10,7 +10,7 @@
 GELU_SCALE = 0.7978845608
 GELU_CUBIC = 0.044715
 F32, BF16 = jnp.float32, jnp.bfloat16
-MIB = 1024 * 1024
+VMEM_LIMIT = 48 * 1024 * 1024
 UNITS, AHEAD = 7, 3
 
 
@@ -18,7 +18,7 @@
     return lax.dot_general(left, right, ((dims[:1], dims[1:]), ((), ())), preferred_element_type=F32)
 
 
-def call(kernel, flops, moved, place, operands, grid, in_specs, out_specs, out_shape, into=(), outs=(), scratch=(), vmem=48):
+def call(kernel, flops, moved, place, operands, grid, in_specs, out_specs, out_shape, into=(), outs=(), scratch=()):
     scalars = 1
     aliases = {}
     in_specs, operands = list(in_specs), list(operands)
@@ -38,7 +38,7 @@
         ),
         out_shape=out_shape,
         input_output_aliases=aliases,
-        compiler_params=pltpu.CompilerParams(vmem_limit_bytes=vmem * MIB),
+        compiler_params=pltpu.CompilerParams(vmem_limit_bytes=VMEM_LIMIT),
         cost_estimate=pl.CostEstimate(flops=flops, bytes_accessed=moved, transcendentals=0),
     )(place, *operands)
 
@@ -51,13 +51,13 @@
     return pl.BlockSpec((rows, columns), lambda i, s: (s[0] ^ key, 0))
 
 
-def streamed(place, blocks, weight, pieces, dims, flops, write, out_shape, vmem=48):
+def streamed(place, blocks, weight, pieces, dims, flops, write, out_shape):
     axis, first, last = pieces
     size = weight.shape[axis] // UNITS
     count = last - first
     arrays = []
     for block in blocks:
-        for array, _, _ in block:
+        for array, _, _, _ in block:
             if not any(array is other for other in arrays):
                 arrays.append(array)
     total, depth = sum(part[2] for block in blocks for part in block), blocks[0][0][0].shape[1]
@@ -75,13 +75,12 @@
 
         copies, top = [], 0
         for block in blocks:
-            for at, (array, start, length) in enumerate(block):
-                into = top if len(block) == 1 else top + (s[1] if at == 0 else 1 - s[1]) * length
+            for array, start, length, into in block:
                 source = next(ref for ref, other in zip(sources, arrays) if other is array)
                 copies.append(
                     pltpu.make_async_copy(
                         source.at[pl.ds(pl.multiple_of(start(s), 16), length), :],
-                        block_ref.at[pl.ds(pl.multiple_of(into, 16), length), :],
+                        block_ref.at[pl.ds(pl.multiple_of(top + into(s), 16), length), :],
                         block_sem.at[len(copies)],
                     )
                 )
@@ -124,15 +123,18 @@
             pltpu.SemaphoreType.DMA((parts,)),
             pltpu.SemaphoreType.DMA((count,)),
         ],
-        vmem=vmem,
-    )
+    )
+
+
+def zero(s):
+    return 0
 
 
 def columns_of(at, size):
     return pl.ds(pl.multiple_of(at * size, size), size)
 
 
-def partials(place, blocks, weight, transposed, vmem):
+def partials(place, blocks, weight, transposed):
     hidden = weight.shape[0 if transposed else 1]
     rows = sum(part[2] for part in blocks[0])
     width = hidden // UNITS
@@ -150,7 +152,6 @@
         2 * len(blocks) * rows * weight.size,
         write,
         [jax.ShapeDtypeStruct((rows, hidden), BF16)] * len(blocks),
-        vmem,
     )
 
 
@@ -171,7 +172,7 @@
 
     return streamed(
         place,
-        [[(grad, lambda s, key=key: (s[0] ^ key) * rows, rows)] for key in keys],
+        [[(grad, lambda s, key=key: (s[0] ^ key) * rows, rows, zero)] for key in keys],
         weight_in,
         (0, first, last),
         (1, 1),
@@ -283,8 +284,8 @@
 
     return call(
         kernel,
-        2 * tokens * tile * count * hidden,
-        2 * tokens * (tile * count + hidden) + 4 * tile * count * hidden,
+        2 * tokens * tile * count * hidden // 16,
+        (2 * tokens * (tile * count + hidden) + 4 * tile * count * hidden) // 16,
         place,
         [tok, grad],
         (count,),
@@ -293,6 +294,23 @@
         jax.ShapeDtypeStruct((depth, hidden), F32),
         [into],
         [0],
+    )
+
+
+def add_early(place, left, right):
+    def kernel(s, left_ref, right_ref, out):
+        out[...] = left_ref[...].astype(F32) + right_ref[...].astype(F32)
+
+    return call(
+        kernel,
+        left.size,
+        8 * left.size,
+        place,
+        [left, right],
+        (1,),
+        [whole(left.shape)] * 2,
+        whole(left.shape),
+        jax.ShapeDtypeStruct(left.shape, F32),
     )
 
 
@@ -308,7 +326,8 @@
     steps = rows_of - 1
     me = lax.axis_index("col")
     place = jnp.stack([me // 2, me % 2]).astype(jnp.int32)
-    others = sorted(range(1, cols_of // 2), key=lambda key: (-key.bit_count(), key))
+    lead = 1
+    others = [lead] + sorted(range(2, cols_of // 2), key=lambda key: (-key.bit_count(), key))
     chunks = [("pre", 0), ("act", 0)] + [(kind, key) for kind in ("pre", "act") for key in others]
     total = len(chunks)
 
@@ -330,14 +349,18 @@
     slopes, sums, arrived = {}, {}, []
 
     def compute_own(kind, keys):
-        source, weight = (tokens, weight_in) if kind == "pre" else (out_grad, weight_out)
-        if keys == [0]:
-            first = lambda s: 0
-            blocks = [[(link(source), first, mine), (held["pair", kind], first, mine)]]
-        else:
-            gathered = link(held[kind])
-            blocks = [[(gathered, lambda s, key=key: (s[0] ^ key) * rows, rows)] for key in keys]
-        outs = partials(place, blocks, weight, kind == "act", 58 if keys == others[:1] else 48)
+        weight = weight_in if kind == "pre" else weight_out
+        blocks = []
+        for key in keys:
+            if (kind, key) in held:
+                near, far = link(held[kind, key]), held[kind, key, "far"]
+                blocks.append([(near, zero, mine, lambda s: s[1] * mine), (far, zero, mine, lambda s: (1 - s[1]) * mine)])
+            else:
+                blocks.append([(held[kind, "all"], lambda s, key=key: (s[0] ^ key) * rows, rows, zero)])
+        if keys[0] not in (0, lead):
+            held[kind, "all"] = link(held[kind, "all"])
+            blocks = [[(held[kind, "all"], *part[1:]) for part in block] for block in blocks]
+        outs = partials(place, blocks, weight, kind == "act")
         chain.append(outs[0])
         for key, out in zip(keys, outs):
             own[kind, key] = out
@@ -364,12 +387,12 @@
 
     def out_columns(first, count):
         held["out"] = weight_out_grad(
-            place, link(held["activations"]), held["act"], held.get("out"), first, count
+            place, link(held["activations"]), held["cotangents"], held.get("out"), first, count
         )
         chain.append(held["out"])
 
     def in_rows(first, count):
-        held["in"] = weight_in_grad(place, held["pre"], link(held["grads"]), held.get("in"), first, count)
+        held["in"] = weight_in_grad(place, held["tokens"], link(held["grads"]), held.get("in"), first, count)
         chain.append(held["in"])
 
     def tokens_of(keys, first, last):
@@ -391,53 +414,60 @@
         chain.append(pair)
         return results
 
-    held["pair", "pre"], held["pair", "act"] = swap(tokens, 1), swap(out_grad, 1)
-    held["pre"] = lax.all_gather(tokens, "col", axis=0, tiled=True)
-    held["act"] = lax.all_gather(after(out_grad, held["pair", "pre"]), "col", axis=0, tiled=True)
+    held["pre", 0], held["act", 0] = tokens, out_grad
+    held["pre", 0, "far"], held["act", 0, "far"] = swap(tokens, 1), swap(out_grad, 1)
+    held["pre", "all"] = lax.all_gather(tokens, "col", axis=0, tiled=True)
+    held["act", "all"] = lax.all_gather(after(out_grad, held["pre", 0, "far"]), "col", axis=0, tiled=True)
+    held["tokens"], held["cotangents"] = held["pre", "all"], held["act", "all"]
     compute_own("pre", [0])
     first_send(0)
+    held["pre", lead] = swap(link(tokens), 2 * lead)
     compute_own("act", [0])
     first_send(1)
+    held["act", lead] = swap(link(out_grad), 2 * lead)
     end = total + steps - 1
     for slot in range(end):
-        if 3 <= slot + 1 < total:
+        if slot and slot + 1 < total:
             first_send(slot + 1)
-        late = slot == 2
-        if late and slot >= steps - 1:
-            finish(slot - steps + 1)
-        for step in range(steps, 1, -1) if late else range(2, steps + 1):
+        for step in range(2, steps + 1):
             if 0 <= slot - step + 2 < total:
                 forward(slot - step + 2, step)
-            if step == 2 and slot == len(others):
-                compute_own("act", others)
+        if slot == 0:
+            held["pre", lead, "far"] = swap(link(held["pre", lead]), 1)
+            compute_own("pre", [lead])
         if slot == 1:
-            compute_own("pre", others[:1])
-            first_send(2)
             compute_own("pre", others[1:])
-        if not late and slot >= steps - 1:
+            held["act", lead, "far"] = swap(link(held["act", lead]), 1)
+        if slot >= steps - 1:
             finish(slot - steps + 1)
+        if slot == 2:
+            compute_own("act", [lead])
+        if slot == len(others) + 1:
+            compute_own("act", others[1:])
         if slot == end - 4:
-            out_columns(0, 4)
+            out_columns(0, 3)
         if slot == end - 3:
-            out_columns(4, UNITS - 4)
+            first = tokens_of([0] + others[:-2], 0, UNITS)
         if slot == end - 2:
-            early = tokens_of([0] + others[:-1], 0, UNITS)
-    early = exchange(early)
-    front = UNITS // 2
-    parts = [exchange(tokens_of(others[-1:], 0, front)), exchange(tokens_of(others[-1:], front, UNITS))]
+            first = exchange(first)
+            second = tokens_of(others[-2:-1], 0, UNITS)
+            arrived += deliver(first)
+            second = exchange(second)
+            out_columns(3, UNITS - 3)
+    arrived += deliver(second)
+    head = add_early(place, link(arrived[0]), arrived[1])
+    chain.append(head)
+    third = exchange(tokens_of(others[-1:], 0, UNITS))
     sums = link(functools.reduce(jnp.add, [sums[key] for key in sorted(sums)]).reshape(hidden))
     levels = [1 << i for i in range(rows_of.bit_length() - 1)]
     sums = sums + lax.ppermute(sums, "row", [(i, i ^ levels[0]) for i in range(rows_of)])
-    arrived += deliver(early)
-    sides = [deliver(part) for part in parts]
+    arrived += deliver(third)
     in_rows(0, UNITS)
     sums = link(sums)
     for bit in levels[1:]:
         sums = sums + lax.ppermute(sums, "row", [(i, i ^ bit) for i in range(rows_of)])
     grad_bias = sums * (1.0 / rows_of)
-    arrived += [jnp.concatenate(halves, axis=1) for halves in zip(*sides)]
-    grad_tokens = functools.reduce(jnp.add, [part.astype(F32) for part in arrived]).astype(BF16)
-
+    grad_tokens = functools.reduce(jnp.add, [part.astype(F32) for part in arrived[2:]], head).astype(BF16)
     return (grad_tokens, held["in"], grad_bias, held["out"])
 
 

time: 281 us -> 287 us (1.021)
  starting transfers between devices: 54.4 us -> 74 us
  waiting for transfers between devices: 69.7 us -> 55.5 us
  Pallas kernels: 119 us -> 124 us
  local copies, waits for them, and re-layouts: 7.2 us -> 3.93 us
    ppermute x24, waiting for transfers between devices: 53.2 us -> 31.7 us  [send(): return lax.ppermute(value, 'row', pairs)]
    ppermute x24, starting transfers between devices: 46.5 us -> 60.7 us  [send(): return lax.ppermute(value, 'row', pairs)]
    ppermute x9 -> x12, waiting for transfers between devices: 9.33 us -> 19.8 us  [swap(): return lax.ppermute(value, 'col', [(i, i ^ bits) for i in range(cols_of)])]
    pallas_call x19 -> x21, Pallas kernels: 119 us -> 124 us  [call(): pl.pallas_call(kernel, grid_spec=pltpu.PrefetchScalarGridSpec(num_scalar_...]
    unnamed x50 -> x38, local copies, waits for them, and re-layouts: 7.19 us -> 3.92 us
    ppermute x9 -> x12, starting transfers between devices: 6.65 us -> 7.27 us  [swap(): return lax.ppermute(value, 'col', [(i, i ^ bits) for i in range(cols_of)])]
  transfers between devices with their start and end apart: 37 -> 40, of which waited for: 11 -> 15; matrix products, arithmetic and copies ran while one was open for 5% -> 5% of each run, Pallas kernels for 42% -> 40%
where the time goes in v6:
time: 287 us; the launch traced here: 286 us
  Pallas kernels  124 us (43%)
  starting transfers between devices  74 us (26%)
  waiting for transfers between devices  55.5 us (19%)
  between operations  14.7 us (5%)
  other arithmetic  14 us (5%)
  local copies, waits for them, and re-layouts  3.93 us (1%)
    pallas_call x21, Pallas kernels, call(): pl.pallas_call(kernel, grid_spec=pltpu.PrefetchScalarGridSpec(num_scalar_...  124 us
    ppermute x24, starting transfers between devices, send(): return lax.ppermute(value, 'row', pairs)  60.7 us
    ppermute x24, waiting for transfers between devices, send(): return lax.ppermute(value, 'row', pairs)  31.7 us
    ppermute x12, waiting for transfers between devices, swap(): return lax.ppermute(value, 'col', [(i, i ^ bits) for i in range(cols_of)])  19.8 us
    convert_element_type x19, other arithmetic, add_bf16(): return (left.astype(F32) + right.astype(F32)).astype(BF16)  12.2 us
    ppermute x12, starting transfers between devices, swap(): return lax.ppermute(value, 'col', [(i, i ^ bits) for i in range(cols_of)])  7.27 us
  transfers between devices with their start and end apart: 40, of which 15 were waited for; matrix products, arithmetic and copies ran while one was open for 5% of the time, Pallas kernels for 40%

profile of v6, /device:TPU:0, one launch (start us, length us, event | category | flops | bytes accessed | tf_op | source)
XLA Modules:
  0.0 285.9 jit_solution(8174890613986363296)
XLA Ops:
  8.5 2.0 collective-permute-done.refs_1_
  11.0 6.3 %shard_map.84 = bf16[192,1792]{1,0:T(8,128)(2,1)S(1)} custom-call(s32[2]{0:T(128)S(1)} %pad_add_fusion.s, bf16[96,3584]{1,0:T(8,128)(2,1)S(1)} %copy-done.2, bf16[96,3584]{1,0:T(8,128)(2,1)S(1)} %collective-permute-done.refs_1_, bf16[3584,1792]{1,0:T(8,128)(2,1)} %refs_1_.9), custom_call_target="tpu_custom_call" | custom-call | flops 2466250752 | bytes 14221312 | tf_op jit(solution)/shard_map/pallas_call | solution.py:30
  17.3 4.7 %collective-permute-start.2 = (bf16[192,1792]{1,0:T(8,128)(2,1)S(1)}, bf16[192,1792]{1,0:T(8,128)(2,1)S(1)}, u32[]{:S(2)}, u32[]{:S(2)}) collective-permute-start(bf16[192,1792]{1,0:T(8,128)(2,1)S(1)} %shard_map.84), channel_id=1, source_target_pairs={{0,8},{24,16},{1,9},{25,17},{2,10},{26,18},{3,11},{27,19},{4,12},{... | collective-permute-start | bytes 2064392 | tf_op jit(solution)/shard_map/ppermute | solution.py:336
  22.0 1.6 collective-permute-start.1
  23.5 7.3 %shard_map.85 = bf16[192,1792]{1,0:T(8,128)(2,1)S(1)} custom-call(s32[2]{0:T(128)S(1)} %pad_add_fusion.s, bf16[96,3584]{1,0:T(8,128)(2,1)S(1)} %copy-done.3, bf16[96,3584]{1,0:T(8,128)(2,1)S(1)} %collective-permute-done.3.refs_1_, bf16[1792,3584]{1,0:T(8,128)(2,1)} %refs_1_.6), custom_call_target="tpu_custom_call" | custom-call | flops 2466250752 | bytes 14221312 | tf_op jit(solution)/shard_map/pallas_call | solution.py:30
  30.8 6.3 %collective-permute-done.2 = bf16[192,1792]{1,0:T(8,128)(2,1)S(1)} collective-permute-done((bf16[192,1792]{1,0:T(8,128)(2,1)S(1)}, bf16[192,1792]{1,0:T(8,128)(2,1)S(1)}, u32[]{:S(2)}, u32[]{:S(2)}) %collective-permute-start.2) | collective-permute-done | bytes 688160 | tf_op jit(solution)/shard_map/ppermute | solution.py:336
  37.3 8.6 %collective-permute-done.1.refs_0_ = bf16[96,3584]{1,0:T(8,128)(2,1)S(1)} collective-permute-done((bf16[96,3584]{1,0:T(8,128)(2,1)S(1)}, bf16[96,3584]{1,0:T(8,128)(2,1)S(1)}, u32[]{:S(2)}, u32[]{:S(2)}) %collective-permute-start.1) | collective-permute-done | bytes 688160 | tf_op jit(solution)/shard_map/ppermute | solution.py:339
  45.9 2.9 %collective-permute-start.7 = (bf16[192,1792]{1,0:T(8,128)(2,1)S(1)}, bf16[192,1792]{1,0:T(8,128)(2,1)S(1)}, u32[]{:S(2)}, u32[]{:S(2)}) collective-permute-start(bf16[192,1792]{1,0:T(8,128)(2,1)S(1)} %shard_map.85), channel_id=1, source_target_pairs={{0,8},{24,16},{1,9},{25,17},{2,10},{26,18},{3,11},{27,19},{4,12},{... | collective-permute-start | bytes 2064392 | tf_op jit(solution)/shard_map/ppermute | solution.py:336
  50.4 6.3 %shard_map.86 = bf16[192,1792]{1,0:T(8,128)(2,1)S(1)} custom-call(s32[2]{0:T(128)S(1)} %pad_add_fusion.s, bf16[96,3584]{1,0:T(8,128)(2,1)S(1)} %collective-permute-done.1.refs_0_, bf16[96,3584]{1,0:T(8,128)(2,1)S(1)} %collective-permute-done.4.refs_1_, bf16[3584,1792]{1,0:T(8,128)(2,1)} %refs_1_.9), custom_call_target="tpu_custom_call" | custom-call | flops 2466250752 | bytes 14221312 | tf_op jit(solution)/shard_map/pallas_call | solution.py:30
  56.8 7.3 %collective-permute-done.7 = bf16[192,1792]{1,0:T(8,128)(2,1)S(1)} collective-permute-done((bf16[192,1792]{1,0:T(8,128)(2,1)S(1)}, bf16[192,1792]{1,0:T(8,128)(2,1)S(1)}, u32[]{:S(2)}, u32[]{:S(2)}) %collective-permute-start.7) | collective-permute-done | bytes 688160 | tf_op jit(solution)/shard_map/ppermute | solution.py:336
  65.1 1.5 collective-permute-start.10
  66.7 7.2 %collective-permute-start.5 = (bf16[192,1792]{1,0:T(8,128)(2,1)S(1)}, bf16[192,1792]{1,0:T(8,128)(2,1)}, u32[]{:S(2)}, u32[]{:S(2)}) collective-permute-start(bf16[192,1792]{1,0:T(8,128)(2,1)S(1)} %shard_map.86), channel_id=1, source_target_pairs={{0,8},{24,16},{1,9},{25,17},{2,10},{26,18},{3,11},{27,19},{4,12},{... | collective-permute-start | bytes 2064392 | tf_op jit(solution)/shard_map/ppermute | solution.py:336
  76.2 10.0 %shard_map.87 = (bf16[192,1792]{1,0:T(8,128)(2,1)S(1)}, bf16[192,1792]{1,0:T(8,128)(2,1)S(1)}) custom-call(s32[2]{0:T(128)S(1)} %pad_add_fusion.s, bf16[768,3584]{1,0:T(8,128)(2,1)} %all-gather.3.cloned.1.call-done.refs_0_.tok_ref, bf16[3584,1792]{1,0:T(8,128)(2,1)} %refs_1_.9), custom_call_target="tpu_custom_call" | custom-call | flops 4932501504 | bytes 15597568 | tf_op jit(solution)/shard_map/pallas_call | solution.py:30
  88.7 4.7 %collective-permute-start.8 = (bf16[192,1792]{1,0:T(8,128)(2,1)S(1)}, bf16[192,1792]{1,0:T(8,128)(2,1)S(1)}, u32[]{:S(2)}, u32[]{:S(2)}) collective-permute-start(bf16[192,1792]{1,0:T(8,128)(2,1)S(1)} %get-tuple-element.113), channel_id=1, source_target_pairs={{0,8},{24,16},{1,9},{25,17},{2,10},{26,18},{3,11},{27,19},{4,12},{... | collective-permute-start | bytes 2064392 | tf_op jit(solution)/shard_map/ppermute | solution.py:336
  96.7 2.9 %shard_map.88 = (bf16[768,1792]{1,0:T(8,128)(2,1)S(1)}, f32[192,1792]{1,0:T(8,128)S(1)}) custom-call(s32[2]{0:T(128)S(1)} %pad_add_fusion.s, f32[1,1792]{1,0:T(1,128)S(1)} %reshape.14.bias_ref, bf16[192,1792]{1,0:T(8,128)(2,1)S(1)} %add_convert_fusion.20.refs_0_, bf16[192,1792]{1,0:T(8,128)(2,1)S(1)} %collective-permute-done.6.refs_1_, ...), custom_call_target="tpu_custom_call" | custom-call | flops 10321920 | bytes 4128768 | tf_op jit(solution)/shard_map/pallas_call | solution.py:30
  99.6 7.5 %shard_map.89 = bf16[192,1792]{1,0:T(8,128)(2,1)S(1)} custom-call(s32[2]{0:T(128)S(1)} %pad_add_fusion.s, bf16[96,3584]{1,0:T(8,128)(2,1)} %collective-permute-done.9.refs_0_, bf16[96,3584]{1,0:T(8,128)(2,1)S(1)} %collective-permute-done.12.refs_1_, bf16[1792,3584]{1,0:T(8,128)(2,1)} %refs_1_.6), custom_call_target="tpu_custom_call" | custom-call | flops 2466250752 | bytes 14221312 | tf_op jit(solution)/shard_map/pallas_call | solution.py:30
  107.1 6.2 %collective-permute-start.14 = (bf16[192,1792]{1,0:T(8,128)(2,1)S(1)}, bf16[192,1792]{1,0:T(8,128)(2,1)S(1)}, u32[]{:S(2)}, u32[]{:S(2)}) collective-permute-start(bf16[192,1792]{1,0:T(8,128)(2,1)S(1)} %get-tuple-element.123), channel_id=1, source_target_pairs={{0,8},{24,16},{1,9},{25,17},{2,10},{26,18},{3,11},{27,19},{4,12},{... | collective-permute-start | bytes 2064392 | tf_op jit(solution)/shard_map/ppermute | solution.py:336
  114.4 2.3 shard_map.90
  118.0 7.1 %collective-permute-start.18 = (bf16[192,1792]{1,0:T(8,128)(2,1)S(1)}, bf16[192,1792]{1,0:T(8,128)(2,1)}, u32[]{:S(2)}, u32[]{:S(2)}) collective-permute-start(bf16[192,1792]{1,0:T(8,128)(2,1)S(1)} %shard_map.89), channel_id=1, source_target_pairs={{0,8},{24,16},{1,9},{25,17},{2,10},{26,18},{3,11},{27,19},{4,12},{... | collective-permute-start | bytes 2064392 | tf_op jit(solution)/shard_map/ppermute | solution.py:336
  125.1 4.1 %collective-permute-done.14 = bf16[192,1792]{1,0:T(8,128)(2,1)S(1)} collective-permute-done((bf16[192,1792]{1,0:T(8,128)(2,1)S(1)}, bf16[192,1792]{1,0:T(8,128)(2,1)S(1)}, u32[]{:S(2)}, u32[]{:S(2)}) %collective-permute-start.14) | collective-permute-done | bytes 688160 | tf_op jit(solution)/shard_map/ppermute | solution.py:336
  132.5 1.5 collective-permute-start.20
  134.0 2.5 collective-permute-done.17.refs_2_
  136.5 1.8 shard_map.91
  138.3 1.5 copy-done
  141.0 9.8 %shard_map.92 = (bf16[192,1792]{1,0:T(8,128)(2,1)S(1)}, bf16[192,1792]{1,0:T(8,128)(2,1)S(1)}) custom-call(s32[2]{0:T(128)S(1)} %pad_add_fusion.s, bf16[768,3584]{1,0:T(8,128)(2,1)} %all-gather.5.cloned.1.call-done.refs_0_.grad_ref, bf16[1792,3584]{1,0:T(8,128)(2,1)} %refs_1_.6), custom_call_target="tpu_custom_call" | custom-call | flops 4932501504 | bytes 15597568 | tf_op jit(solution)/shard_map/pallas_call | solution.py:30
  150.9 4.9 %collective-permute-start.19 = (bf16[192,1792]{1,0:T(8,128)(2,1)S(1)}, bf16[192,1792]{1,0:T(8,128)(2,1)S(1)}, u32[]{:S(2)}, u32[]{:S(2)}) collective-permute-start(bf16[192,1792]{1,0:T(8,128)(2,1)S(1)} %get-tuple-element.134), channel_id=1, source_target_pairs={{0,8},{24,16},{1,9},{25,17},{2,10},{26,18},{3,11},{27,19},{4,12},{... | collective-permute-start | bytes 2064392 | tf_op jit(solution)/shard_map/ppermute | solution.py:336
  155.8 1.4 add_convert_fusion.11.refs_0_
  159.4 1.5 collective-permute-start.25
  160.9 2.9 %shard_map.93 = (bf16[768,1792]{1,0:T(8,128)(2,1)S(1)}, f32[192,1792]{1,0:T(8,128)S(1)}) custom-call(s32[2]{0:T(128)S(1)} %pad_add_fusion.s, f32[1,1792]{1,0:T(1,128)S(1)} %reshape.14.bias_ref, bf16[192,1792]{1,0:T(8,128)(2,1)S(1)} %copy-done.5, bf16[192,1792]{1,0:T(8,128)(2,1)S(1)} %copy-done.7, ...), custom_call_target="tpu_custom_call", output_to_operand_aliasing={{0}: (5, {})} | custom-call | flops 10321920 | bytes 4128768 | tf_op jit(solution)/shard_map/pallas_call | solution.py:30
  163.8 4.6 %collective-permute-start.23 = (bf16[192,1792]{1,0:T(8,128)(2,1)S(1)}, bf16[192,1792]{1,0:T(8,128)(2,1)S(1)}, u32[]{:S(2)}, u32[]{:S(2)}) collective-permute-start(bf16[192,1792]{1,0:T(8,128)(2,1)S(1)} %get-tuple-element.140), channel_id=1, source_target_pairs={{0,8},{24,16},{1,9},{25,17},{2,10},{26,18},{3,11},{27,19},{4,12},{... | collective-permute-start | bytes 2064392 | tf_op jit(solution)/shard_map/ppermute | solution.py:336
  168.5 2.1 collective-permute-done.19
  173.0 5.8 %collective-permute-done.25.refs_2_ = bf16[192,1792]{1,0:T(8,128)(2,1)S(1)} collective-permute-done((bf16[192,1792]{1,0:T(8,128)(2,1)S(1)}, bf16[192,1792]{1,0:T(8,128)(2,1)S(1)}, u32[]{:S(2)}, u32[]{:S(2)}) %collective-permute-start.25) | collective-permute-done | bytes 688160 | tf_op jit(solution)/shard_map/ppermute | solution.py:336
  178.7 3.1 %shard_map.94 = (bf16[768,1792]{1,0:T(8,128)(2,1)S(1)}, f32[192,1792]{1,0:T(8,128)S(1)}) custom-call(s32[2]{0:T(128)S(1)} %pad_add_fusion.s, f32[1,1792]{1,0:T(1,128)S(1)} %reshape.14.bias_ref, bf16[192,1792]{1,0:T(8,128)(2,1)} %add_convert_fusion.13.refs_0_, bf16[192,1792]{1,0:T(8,128)(2,1)} %collective-permute-done.20.refs_1_, ...), custom_call_target="tpu_custom_call", output_to_operand_aliasing={{0}: (5, {})} | custom-call | flops 10321920 | bytes 4128768 | tf_op jit(solution)/shard_map/pallas_call | solution.py:30
  181.8 9.3 %shard_map.95.refs_0_ = f32[1792,3584]{1,0:T(8,128)} custom-call(s32[2]{0:T(128)S(1)} %pad_add_fusion.s, bf16[768,1792]{1,0:T(8,128)(2,1)S(1)} %get-tuple-element.149.act_ref, bf16[768,3584]{1,0:T(8,128)(2,1)} %all-gather.5.cloned.1.call-done.refs_0_.grad_ref), custom_call_target="tpu_custom_call" | custom-call | flops 4227858432 | bytes 16121856 | tf_op jit(solution)/shard_map/pallas_call | solution.py:30
  194.7 8.5 %shard_map.97 = (bf16[192,3584]{1,0:T(8,128)(2,1)S(1)}, bf16[192,3584]{1,0:T(8,128)(2,1)S(1)}) custom-call(s32[2]{0:T(128)S(1)} %pad_add_fusion.s, bf16[768,1792]{1,0:T(8,128)(2,1)S(1)} %get-tuple-element.137.refs_0_.refs_3_, bf16[3584,1792]{1,0:T(8,128)(2,1)} %refs_1_.9), custom_call_target="tpu_custom_call" | custom-call | flops 4932501504 | bytes 14221312 | tf_op jit(solution)/shard_map/pallas_call | solution.py:30
  205.3 2.5 collective-permute-done.28.refs_2_
  209.0 1.6 collective-permute-start.30
  210.6 7.4 %shard_map.99 = (bf16[96,3584]{1,0:T(8,128)(2,1)S(1)}, bf16[96,3584]{1,0:T(8,128)(2,1)S(1)}) custom-call(s32[2]{0:T(128)S(1)} %pad_add_fusion.s, bf16[768,1792]{1,0:T(8,128)(2,1)S(1)} %get-tuple-element.143.refs_0_.refs_3_, bf16[3584,1792]{1,0:T(8,128)(2,1)} %refs_1_.9), custom_call_target="tpu_custom_call" | custom-call | flops 2466250752 | bytes 13533184 | tf_op jit(solution)/shard_map/pallas_call | solution.py:30
  219.6 11.0 %shard_map.100 = f32[1792,3584]{1,0:T(8,128)} custom-call(s32[2]{0:T(128)S(1)} %pad_add_fusion.s, bf16[768,1792]{1,0:T(8,128)(2,1)S(1)} %get-tuple-element.149.act_ref, bf16[768,3584]{1,0:T(8,128)(2,1)} %all-gather.5.cloned.1.call-done.refs_0_.grad_ref, f32[1792,3584]{1,0:T(8,128)} %shard_map.95.refs_0_), custom_call_target="tpu_custom_call", output_to_operand_aliasing={{}: (3, {})} | custom-call | flops 5637144576 | bytes 20578304 | tf_op jit(solution)/shard_map/pallas_call | solution.py:30
  231.8 4.5 %collective-permute-done.32.right_ref = bf16[96,3584]{1,0:T(8,128)(2,1)S(1)} collective-permute-done((bf16[96,3584]{1,0:T(8,128)(2,1)S(1)}, bf16[96,3584]{1,0:T(8,128)(2,1)S(1)}, u32[]{:S(2)}, u32[]{:S(2)}) %collective-permute-start.32) | collective-permute-done | bytes 688160 | tf_op jit(solution)/shard_map/ppermute | solution.py:339
  237.0 7.4 %shard_map.103 = (bf16[96,3584]{1,0:T(8,128)(2,1)S(1)}, bf16[96,3584]{1,0:T(8,128)(2,1)S(1)}) custom-call(s32[2]{0:T(128)S(1)} %pad_add_fusion.s, bf16[768,1792]{1,0:T(8,128)(2,1)S(1)} %get-tuple-element.161.refs_0_.grad_ref, bf16[3584,1792]{1,0:T(8,128)(2,1)} %refs_1_.9), custom_call_target="tpu_custom_call" | custom-call | flops 2466250752 | bytes 13533184 | tf_op jit(solution)/shard_map/pallas_call | solution.py:30
  244.5 1.4 collective-permute-start.33
  247.8 2.8 collective-permute-start.36
  250.6 1.6 collective-permute-done.36
  252.2 16.4 %shard_map.104 = f32[3584,1792]{1,0:T(8,128)} custom-call(s32[2]{0:T(128)S(1)} %pad_add_fusion.s, bf16[768,3584]{1,0:T(8,128)(2,1)} %all-gather.3.cloned.1.call-done.refs_0_.tok_ref, bf16[768,1792]{1,0:T(8,128)(2,1)S(1)} %get-tuple-element.161.refs_0_.grad_ref), custom_call_target="tpu_custom_call" | custom-call | flops 616562688 | bytes 2121728 | tf_op jit(solution)/shard_map/pallas_call | solution.py:30
  268.6 3.2 %collective-permute-start.37 = (f32[1792]{0:T(1024)S(1)}, f32[1792]{0:T(1024)S(1)}, u32[]{:S(2)}, u32[]{:S(2)}) collective-permute-start(f32[1792]{0:T(1024)S(1)} %add.112), channel_id=1, source_target_pairs={{0,16},{8,24},{16,0},{24,8},{1,17},{9,25},{17,1},{25,9},{2,18},{10... | collective-permute-start | bytes 21512 | tf_op jit(solution)/shard_map/ppermute | solution.py:468
  271.8 1.6 collective-permute-done.37
  274.0 3.9 %collective-permute-done.35 = bf16[96,3584]{1,0:T(8,128)(2,1)S(1)} collective-permute-done((bf16[96,3584]{1,0:T(8,128)(2,1)S(1)}, bf16[96,3584]{1,0:T(8,128)(2,1)S(1)}, u32[]{:S(2)}, u32[]{:S(2)}) %collective-permute-start.35) | collective-permute-done | bytes 688160 | tf_op jit(solution)/shard_map/ppermute | solution.py:339
  (118 shorter events, 37.7 us)
Async XLA Ops:
  7.2 69.0 %all-gather.3.cloned.1.call-start = ((), (), s32[]{:S(2)}) async-start(), calls=%async_computation | async-start | bytes 6193152 | tf_op jit(solution)/shard_map/all_gather | solution.py:419
  7.9 133.1 %all-gather.5.cloned.1.call-start = ((), (), s32[]{:S(2)}) async-start(), calls=%async_computation.1 | async-start | bytes 6193152 | tf_op jit(solution)/shard_map/all_gather | solution.py:420
  8.0 2.5 collective-permute-start
  10.5 13.0 %collective-permute-start.3 = (bf16[96,3584]{1,0:T(8,128)(2,1)S(1)}, bf16[96,3584]{1,0:T(8,128)(2,1)S(1)}, u32[]{:S(2)}, u32[]{:S(2)}) collective-permute-start(bf16[96,3584]{1,0:T(8,128)(2,1)S(1)} %copy-done.3), channel_id=1, source_target_pairs={{0,1},{1,0},{2,3},{3,2},{4,5},{5,4},{6,7},{7,6},{8,9},{9,8},{10,11... | collective-permute-start | bytes 2064392 | tf_op jit(solution)/shard_map/ppermute | solution.py:339
  17.3 19.8 %collective-permute-start.2 = (bf16[192,1792]{1,0:T(8,128)(2,1)S(1)}, bf16[192,1792]{1,0:T(8,128)(2,1)S(1)}, u32[]{:S(2)}, u32[]{:S(2)}) collective-permute-start(bf16[192,1792]{1,0:T(8,128)(2,1)S(1)} %shard_map.84), channel_id=1, source_target_pairs={{0,8},{24,16},{1,9},{25,17},{2,10},{26,18},{3,11},{27,19},{4,12},{... | collective-permute-start | bytes 2064392 | tf_op jit(solution)/shard_map/ppermute | solution.py:336
  22.0 23.9 %collective-permute-start.1 = (bf16[96,3584]{1,0:T(8,128)(2,1)S(1)}, bf16[96,3584]{1,0:T(8,128)(2,1)S(1)}, u32[]{:S(2)}, u32[]{:S(2)}) collective-permute-start(bf16[96,3584]{1,0:T(8,128)(2,1)S(1)} %copy-done.2), channel_id=1, source_target_pairs={{0,2},{1,3},{2,0},{3,1},{4,6},{5,7},{6,4},{7,5},{8,10},{9,11},{10,... | collective-permute-start | bytes 2064392 | tf_op jit(solution)/shard_map/ppermute | solution.py:339
  30.8 18.0 %copy-start.18 = (f32[1792]{0:T(1024)S(1)}, f32[1792]{0:T(1024)}, u32[]{:S(2)}) copy-start(f32[1792]{0:T(1024)} %param.7) | copy-start | bytes 21508
  45.9 4.5 %collective-permute-start.4 = (bf16[96,3584]{1,0:T(8,128)(2,1)S(1)}, bf16[96,3584]{1,0:T(8,128)(2,1)S(1)}, u32[]{:S(2)}, u32[]{:S(2)}) collective-permute-start(bf16[96,3584]{1,0:T(8,128)(2,1)S(1)} %collective-permute-done.1.refs_0_), channel_id=1, source_target_pairs={{0,1},{1,0},{2,3},{3,2},{4,5},{5,4},{6,7},{7,6},{8,9},{9,8},{10,11... | collective-permute-start | bytes 2064392 | tf_op jit(solution)/shard_map/ppermute | solution.py:339
  45.9 18.2 %collective-permute-start.7 = (bf16[192,1792]{1,0:T(8,128)(2,1)S(1)}, bf16[192,1792]{1,0:T(8,128)(2,1)S(1)}, u32[]{:S(2)}, u32[]{:S(2)}) collective-permute-start(bf16[192,1792]{1,0:T(8,128)(2,1)S(1)} %shard_map.85), channel_id=1, source_target_pairs={{0,8},{24,16},{1,9},{25,17},{2,10},{26,18},{3,11},{27,19},{4,12},{... | collective-permute-start | bytes 2064392 | tf_op jit(solution)/shard_map/ppermute | solution.py:336
  48.8 37.5 %collective-permute-start.9 = (bf16[96,3584]{1,0:T(8,128)(2,1)S(1)}, bf16[96,3584]{1,0:T(8,128)(2,1)}, u32[]{:S(2)}, u32[]{:S(2)}) collective-permute-start(bf16[96,3584]{1,0:T(8,128)(2,1)S(1)} %copy-done.3), channel_id=1, source_target_pairs={{0,2},{1,3},{2,0},{3,1},{4,6},{5,7},{6,4},{7,5},{8,10},{9,11},{10,... | collective-permute-start | bytes 2064392 | tf_op jit(solution)/shard_map/ppermute | solution.py:339
  49.7 24.2 %collective-permute-start.6 = (bf16[192,1792]{1,0:T(8,128)(2,1)S(1)}, bf16[192,1792]{1,0:T(8,128)(2,1)S(1)}, u32[]{:S(2)}, u32[]{:S(2)}) collective-permute-start(bf16[192,1792]{1,0:T(8,128)(2,1)S(1)} %add_convert_fusion.20.refs_0_), channel_id=1, source_target_pairs={{8,16},{16,8},{9,17},{17,9},{10,18},{18,10},{11,19},{19,11},{12,20... | collective-permute-start | bytes 2064392 | tf_op jit(solution)/shard_map/ppermute | solution.py:336
  65.1 28.2 %collective-permute-start.10 = (bf16[192,1792]{1,0:T(8,128)(2,1)}, bf16[192,1792]{1,0:T(8,128)(2,1)}, u32[]{:S(2)}, u32[]{:S(2)}) collective-permute-start(bf16[192,1792]{1,0:T(8,128)(2,1)} %add_convert_fusion.19.refs_0_), channel_id=1, source_target_pairs={{8,16},{16,8},{9,17},{17,9},{10,18},{18,10},{11,19},{19,11},{12,20... | collective-permute-start | bytes 2064392 | tf_op jit(solution)/shard_map/ppermute | solution.py:336
  66.7 20.8 %collective-permute-start.5 = (bf16[192,1792]{1,0:T(8,128)(2,1)S(1)}, bf16[192,1792]{1,0:T(8,128)(2,1)}, u32[]{:S(2)}, u32[]{:S(2)}) collective-permute-start(bf16[192,1792]{1,0:T(8,128)(2,1)S(1)} %shard_map.86), channel_id=1, source_target_pairs={{0,8},{24,16},{1,9},{25,17},{2,10},{26,18},{3,11},{27,19},{4,12},{... | collective-permute-start | bytes 2064392 | tf_op jit(solution)/shard_map/ppermute | solution.py:336
  74.9 21.8 %collective-permute-start.11 = (bf16[192,1792]{1,0:T(8,128)(2,1)}, bf16[192,1792]{1,0:T(8,128)(2,1)}, u32[]{:S(2)}, u32[]{:S(2)}) collective-permute-start(bf16[192,1792]{1,0:T(8,128)(2,1)} %add_convert_fusion.18), channel_id=1, source_target_pairs={{16,24},{8,0},{17,25},{9,1},{18,26},{10,2},{19,27},{11,3},{20,28},... | collective-permute-start | bytes 2064392 | tf_op jit(solution)/shard_map/ppermute | solution.py:336
  86.3 42.8 %copy-start.8 = (bf16[192,1792]{1,0:T(8,128)(2,1)}, bf16[192,1792]{1,0:T(8,128)(2,1)S(1)}, u32[]{:S(2)}) copy-start(bf16[192,1792]{1,0:T(8,128)(2,1)S(1)} %get-tuple-element.123) | copy-start | bytes 2064388
  86.3 13.2 %collective-permute-start.12 = (bf16[96,3584]{1,0:T(8,128)(2,1)}, bf16[96,3584]{1,0:T(8,128)(2,1)S(1)}, u32[]{:S(2)}, u32[]{:S(2)}) collective-permute-start(bf16[96,3584]{1,0:T(8,128)(2,1)} %collective-permute-done.9.refs_0_), channel_id=1, source_target_pairs={{0,1},{1,0},{2,3},{3,2},{4,5},{5,4},{6,7},{7,6},{8,9},{9,8},{10,11... | collective-permute-start | bytes 2064392 | tf_op jit(solution)/shard_map/ppermute | solution.py:339
  88.7 24.6 %collective-permute-start.8 = (bf16[192,1792]{1,0:T(8,128)(2,1)S(1)}, bf16[192,1792]{1,0:T(8,128)(2,1)S(1)}, u32[]{:S(2)}, u32[]{:S(2)}) collective-permute-start(bf16[192,1792]{1,0:T(8,128)(2,1)S(1)} %get-tuple-element.113), channel_id=1, source_target_pairs={{0,8},{24,16},{1,9},{25,17},{2,10},{26,18},{3,11},{27,19},{4,12},{... | collective-permute-start | bytes 2064392 | tf_op jit(solution)/shard_map/ppermute | solution.py:336
  94.7 19.7 %collective-permute-start.16 = (bf16[192,1792]{1,0:T(8,128)(2,1)S(1)}, bf16[192,1792]{1,0:T(8,128)(2,1)S(1)}, u32[]{:S(2)}, u32[]{:S(2)}) collective-permute-start(bf16[192,1792]{1,0:T(8,128)(2,1)S(1)} %add_convert_fusion.16), channel_id=1, source_target_pairs={{16,24},{8,0},{17,25},{9,1},{18,26},{10,2},{19,27},{11,3},{20,28},... | collective-permute-start | bytes 2064392 | tf_op jit(solution)/shard_map/ppermute | solution.py:336
  96.0 18.2 %collective-permute-start.15 = (bf16[192,1792]{1,0:T(8,128)(2,1)S(1)}, bf16[192,1792]{1,0:T(8,128)(2,1)S(1)}, u32[]{:S(2)}, u32[]{:S(2)}) collective-permute-start(bf16[192,1792]{1,0:T(8,128)(2,1)S(1)} %add_convert_fusion.17.refs_0_), channel_id=1, source_target_pairs={{8,16},{16,8},{9,17},{17,9},{10,18},{18,10},{11,19},{19,11},{12,20... | collective-permute-start | bytes 2064392 | tf_op jit(solution)/shard_map/ppermute | solution.py:336
  107.1 22.1 %collective-permute-start.14 = (bf16[192,1792]{1,0:T(8,128)(2,1)S(1)}, bf16[192,1792]{1,0:T(8,128)(2,1)S(1)}, u32[]{:S(2)}, u32[]{:S(2)}) collective-permute-start(bf16[192,1792]{1,0:T(8,128)(2,1)S(1)} %get-tuple-element.123), channel_id=1, source_target_pairs={{0,8},{24,16},{1,9},{25,17},{2,10},{26,18},{3,11},{27,19},{4,12},{... | collective-permute-start | bytes 2064392 | tf_op jit(solution)/shard_map/ppermute | solution.py:336
  113.5 16.6 %collective-permute-start.13 = (bf16[192,1792]{1,0:T(8,128)(2,1)S(1)}, bf16[192,1792]{1,0:T(8,128)(2,1)S(1)}, u32[]{:S(2)}, u32[]{:S(2)}) collective-permute-start(bf16[192,1792]{1,0:T(8,128)(2,1)S(1)} %add_convert_fusion.15.refs_0_), channel_id=1, source_target_pairs={{8,16},{16,8},{9,17},{17,9},{10,18},{18,10},{11,19},{19,11},{12,20... | collective-permute-start | bytes 2064392 | tf_op jit(solution)/shard_map/ppermute | solution.py:336
  116.7 19.8 %collective-permute-start.17 = (bf16[192,1792]{1,0:T(8,128)(2,1)S(1)}, bf16[192,1792]{1,0:T(8,128)(2,1)S(1)}, u32[]{:S(2)}, u32[]{:S(2)}) collective-permute-start(bf16[192,1792]{1,0:T(8,128)(2,1)S(1)} %add_convert_fusion.14), channel_id=1, source_target_pairs={{16,24},{8,0},{17,25},{9,1},{18,26},{10,2},{19,27},{11,3},{20,28},... | collective-permute-start | bytes 2064392 | tf_op jit(solution)/shard_map/ppermute | solution.py:336
  118.0 37.8 %collective-permute-start.18 = (bf16[192,1792]{1,0:T(8,128)(2,1)S(1)}, bf16[192,1792]{1,0:T(8,128)(2,1)}, u32[]{:S(2)}, u32[]{:S(2)}) collective-permute-start(bf16[192,1792]{1,0:T(8,128)(2,1)S(1)} %shard_map.89), channel_id=1, source_target_pairs={{0,8},{24,16},{1,9},{25,17},{2,10},{26,18},{3,11},{27,19},{4,12},{... | collective-permute-start | bytes 2064392 | tf_op jit(solution)/shard_map/ppermute | solution.py:336
  131.2 29.7 %collective-permute-start.21 = (bf16[192,1792]{1,0:T(8,128)(2,1)}, bf16[192,1792]{1,0:T(8,128)(2,1)}, u32[]{:S(2)}, u32[]{:S(2)}) collective-permute-start(bf16[192,1792]{1,0:T(8,128)(2,1)} %add_convert_fusion.12), channel_id=1, source_target_pairs={{16,24},{8,0},{17,25},{9,1},{18,26},{10,2},{19,27},{11,3},{20,28},... | collective-permute-start | bytes 2064392 | tf_op jit(solution)/shard_map/ppermute | solution.py:336
  132.5 25.6 %collective-permute-start.20 = (bf16[192,1792]{1,0:T(8,128)(2,1)}, bf16[192,1792]{1,0:T(8,128)(2,1)}, u32[]{:S(2)}, u32[]{:S(2)}) collective-permute-start(bf16[192,1792]{1,0:T(8,128)(2,1)} %add_convert_fusion.13.refs_0_), channel_id=1, source_target_pairs={{8,16},{16,8},{9,17},{17,9},{10,18},{18,10},{11,19},{19,11},{12,20... | collective-permute-start | bytes 2064392 | tf_op jit(solution)/shard_map/ppermute | solution.py:336
  141.0 17.1 %copy-start.9 = (bf16[192,1792]{1,0:T(8,128)(2,1)S(1)}, bf16[192,1792]{1,0:T(8,128)(2,1)}, u32[]{:S(2)}) copy-start(bf16[192,1792]{1,0:T(8,128)(2,1)} %copy-done.8) | copy-start | bytes 2064388
  150.9 19.8 %collective-permute-start.19 = (bf16[192,1792]{1,0:T(8,128)(2,1)S(1)}, bf16[192,1792]{1,0:T(8,128)(2,1)S(1)}, u32[]{:S(2)}, u32[]{:S(2)}) collective-permute-start(bf16[192,1792]{1,0:T(8,128)(2,1)S(1)} %get-tuple-element.134), channel_id=1, source_target_pairs={{0,8},{24,16},{1,9},{25,17},{2,10},{26,18},{3,11},{27,19},{4,12},{... | collective-permute-start | bytes 2064392 | tf_op jit(solution)/shard_map/ppermute | solution.py:336
  155.8 5.1 %copy-start.1 = (bf16[768,1792]{1,0:T(8,128)(2,1)S(1)}, bf16[768,1792]{1,0:T(8,128)(2,1)}, u32[]{:S(2)}) copy-start(bf16[768,1792]{1,0:T(8,128)(2,1)} %copy-done) | copy-start | bytes 8257540
  157.3 13.5 %collective-permute-start.24 = (bf16[192,1792]{1,0:T(8,128)(2,1)S(1)}, bf16[192,1792]{1,0:T(8,128)(2,1)S(1)}, u32[]{:S(2)}, u32[]{:S(2)}) collective-permute-start(bf16[192,1792]{1,0:T(8,128)(2,1)S(1)} %add_convert_fusion.11.refs_0_), channel_id=1, source_target_pairs={{8,16},{16,8},{9,17},{17,9},{10,18},{18,10},{11,19},{19,11},{12,20... | collective-permute-start | bytes 2064392 | tf_op jit(solution)/shard_map/ppermute | solution.py:336
  159.4 19.3 %collective-permute-start.25 = (bf16[192,1792]{1,0:T(8,128)(2,1)S(1)}, bf16[192,1792]{1,0:T(8,128)(2,1)S(1)}, u32[]{:S(2)}, u32[]{:S(2)}) collective-permute-start(bf16[192,1792]{1,0:T(8,128)(2,1)S(1)} %add_convert_fusion.10), channel_id=1, source_target_pairs={{16,24},{8,0},{17,25},{9,1},{18,26},{10,2},{19,27},{11,3},{20,28},... | collective-permute-start | bytes 2064392 | tf_op jit(solution)/shard_map/ppermute | solution.py:336
  163.8 7.1 %copy-start.14 = (f32[192,1792]{1,0:T(8,128)}, f32[192,1792]{1,0:T(8,128)S(1)}, u32[]{:S(2)}) copy-start(f32[192,1792]{1,0:T(8,128)S(1)} %get-tuple-element.139.slope_ref) | copy-start | bytes 4128772
  163.8 27.3 %collective-permute-start.23 = (bf16[192,1792]{1,0:T(8,128)(2,1)S(1)}, bf16[192,1792]{1,0:T(8,128)(2,1)S(1)}, u32[]{:S(2)}, u32[]{:S(2)}) collective-permute-start(bf16[192,1792]{1,0:T(8,128)(2,1)S(1)} %get-tuple-element.140), channel_id=1, source_target_pairs={{0,8},{24,16},{1,9},{25,17},{2,10},{26,18},{3,11},{27,19},{4,12},{... | collective-permute-start | bytes 2064392 | tf_op jit(solution)/shard_map/ppermute | solution.py:336
  171.0 22.7 %collective-permute-start.26 = (bf16[192,1792]{1,0:T(8,128)(2,1)S(1)}, bf16[192,1792]{1,0:T(8,128)(2,1)S(1)}, u32[]{:S(2)}, u32[]{:S(2)}) collective-permute-start(bf16[192,1792]{1,0:T(8,128)(2,1)S(1)} %add_convert_fusion.8), channel_id=1, source_target_pairs={{16,24},{8,0},{17,25},{9,1},{18,26},{10,2},{19,27},{11,3},{20,28},... | collective-permute-start | bytes 2064392 | tf_op jit(solution)/shard_map/ppermute | solution.py:336
  172.3 19.9 %collective-permute-start.22 = (bf16[192,1792]{1,0:T(8,128)(2,1)S(1)}, bf16[192,1792]{1,0:T(8,128)(2,1)S(1)}, u32[]{:S(2)}, u32[]{:S(2)}) collective-permute-start(bf16[192,1792]{1,0:T(8,128)(2,1)S(1)} %add_convert_fusion.9.refs_0_), channel_id=1, source_target_pairs={{8,16},{16,8},{9,17},{17,9},{10,18},{18,10},{11,19},{19,11},{12,20... | collective-permute-start | bytes 2064392 | tf_op jit(solution)/shard_map/ppermute | solution.py:336
  181.8 9.3 %copy-start.12 = (f32[192,1792]{1,0:T(8,128)}, f32[192,1792]{1,0:T(8,128)S(1)}, u32[]{:S(2)}) copy-start(f32[192,1792]{1,0:T(8,128)S(1)} %get-tuple-element.148.slope_ref) | copy-start | bytes 4128772
  191.3 13.0 %collective-permute-start.27 = (bf16[192,1792]{1,0:T(8,128)(2,1)S(1)}, bf16[192,1792]{1,0:T(8,128)(2,1)S(1)}, u32[]{:S(2)}, u32[]{:S(2)}) collective-permute-start(bf16[192,1792]{1,0:T(8,128)(2,1)S(1)} %add_convert_fusion.7.refs_0_), channel_id=1, source_target_pairs={{8,16},{16,8},{9,17},{17,9},{10,18},{18,10},{11,19},{19,11},{12,20... | collective-permute-start | bytes 2064392 | tf_op jit(solution)/shard_map/ppermute | solution.py:336
  192.4 15.5 %collective-permute-start.28 = (bf16[192,1792]{1,0:T(8,128)(2,1)S(1)}, bf16[192,1792]{1,0:T(8,128)(2,1)S(1)}, u32[]{:S(2)}, u32[]{:S(2)}) collective-permute-start(bf16[192,1792]{1,0:T(8,128)(2,1)S(1)} %add_convert_fusion.6), channel_id=1, source_target_pairs={{16,24},{8,0},{17,25},{9,1},{18,26},{10,2},{19,27},{11,3},{20,28},... | collective-permute-start | bytes 2064392 | tf_op jit(solution)/shard_map/ppermute | solution.py:336
  208.9 9.1 %copy-start.17 = (bf16[192,3584]{1,0:T(8,128)(2,1)S(1)}, bf16[192,3584]{1,0:T(8,128)(2,1)}, u32[]{:S(2)}) copy-start(bf16[192,3584]{1,0:T(8,128)(2,1)} %copy-done.16) | copy-start | bytes 4128772
  208.9 9.1 %collective-permute-start.29 = (bf16[192,3584]{1,0:T(8,128)(2,1)S(1)}, bf16[192,3584]{1,0:T(8,128)(2,1)S(1)}, u32[]{:S(2)}, u32[]{:S(2)}) collective-permute-start(bf16[192,3584]{1,0:T(8,128)(2,1)S(1)} %get-tuple-element.147), channel_id=1, source_target_pairs={{0,1},{1,0},{2,3},{3,2},{4,5},{5,4},{6,7},{7,6},{8,9},{9,8},{10,11... | collective-permute-start | bytes 4128776 | tf_op jit(solution)/shard_map/ppermute | solution.py:339
  209.0 21.7 %collective-permute-start.30 = (bf16[192,1792]{1,0:T(8,128)(2,1)}, bf16[192,1792]{1,0:T(8,128)(2,1)S(1)}, u32[]{:S(2)}, u32[]{:S(2)}) collective-permute-start(bf16[192,1792]{1,0:T(8,128)(2,1)} %add_convert_fusion.5), channel_id=1, source_target_pairs={{16,24},{8,0},{17,25},{9,1},{18,26},{10,2},{19,27},{11,3},{20,28},... | collective-permute-start | bytes 2064392 | tf_op jit(solution)/shard_map/ppermute | solution.py:336
  218.4 12.2 %copy-start.13 = (f32[192,1792]{1,0:T(8,128)S(1)}, f32[192,1792]{1,0:T(8,128)}, u32[]{:S(2)}) copy-start(f32[192,1792]{1,0:T(8,128)} %copy-done.12) | copy-start | bytes 4128772
  218.4 13.2 %collective-permute-start.31 = (bf16[96,3584]{1,0:T(8,128)(2,1)S(1)}, bf16[96,3584]{1,0:T(8,128)(2,1)S(1)}, u32[]{:S(2)}, u32[]{:S(2)}) collective-permute-start(bf16[96,3584]{1,0:T(8,128)(2,1)S(1)} %get-tuple-element.154), channel_id=1, source_target_pairs={{0,1},{1,0},{2,3},{3,2},{4,5},{5,4},{6,7},{7,6},{8,9},{9,8},{10,11... | collective-permute-start | bytes 2064392 | tf_op jit(solution)/shard_map/ppermute | solution.py:339
  218.8 17.5 %collective-permute-start.32 = (bf16[96,3584]{1,0:T(8,128)(2,1)S(1)}, bf16[96,3584]{1,0:T(8,128)(2,1)S(1)}, u32[]{:S(2)}, u32[]{:S(2)}) collective-permute-start(bf16[96,3584]{1,0:T(8,128)(2,1)S(1)} %get-tuple-element.169), channel_id=1, source_target_pairs={{0,2},{1,3},{2,0},{3,1},{4,6},{5,7},{6,4},{7,5},{8,10},{9,11},{10,... | collective-permute-start | bytes 2064392 | tf_op jit(solution)/shard_map/ppermute | solution.py:339
  244.4 2.2 collective-permute-start.34
  244.5 29.6 %collective-permute-start.33 = (bf16[96,3584]{1,0:T(8,128)(2,1)S(1)}, bf16[96,3584]{1,0:T(8,128)(2,1)S(1)}, u32[]{:S(2)}, u32[]{:S(2)}) collective-permute-start(bf16[96,3584]{1,0:T(8,128)(2,1)S(1)} %add_convert_fusion.2), channel_id=1, source_target_pairs={{0,6},{1,7},{2,4},{3,5},{4,2},{5,3},{6,0},{7,1},{8,14},{9,15},{10,... | collective-permute-start | bytes 2064392 | tf_op jit(solution)/shard_map/ppermute | solution.py:339
  246.8 31.2 %collective-permute-start.35 = (bf16[96,3584]{1,0:T(8,128)(2,1)S(1)}, bf16[96,3584]{1,0:T(8,128)(2,1)S(1)}, u32[]{:S(2)}, u32[]{:S(2)}) collective-permute-start(bf16[96,3584]{1,0:T(8,128)(2,1)S(1)} %add_convert_fusion.1), channel_id=1, source_target_pairs={{0,4},{1,5},{2,6},{3,7},{4,0},{5,1},{6,2},{7,3},{8,12},{9,13},{10,... | collective-permute-start | bytes 2064392 | tf_op jit(solution)/shard_map/ppermute | solution.py:339
  247.8 4.4 %collective-permute-start.36 = (f32[1792]{0:T(1024)S(1)}, f32[1792]{0:T(1024)S(1)}, u32[]{:S(2)}, u32[]{:S(2)}) collective-permute-start(f32[1792]{0:T(1024)S(1)} %add_reduce_fusion), channel_id=1, source_target_pairs={{0,8},{8,0},{16,24},{24,16},{1,9},{9,1},{17,25},{25,17},{2,10},{10... | collective-permute-start | bytes 21512 | tf_op jit(solution)/shard_map/ppermute | solution.py:463
  268.6 4.8 %collective-permute-start.37 = (f32[1792]{0:T(1024)S(1)}, f32[1792]{0:T(1024)S(1)}, u32[]{:S(2)}, u32[]{:S(2)}) collective-permute-start(f32[1792]{0:T(1024)S(1)} %add.112), channel_id=1, source_target_pairs={{0,16},{8,24},{16,0},{24,8},{1,17},{9,25},{17,1},{25,9},{2,18},{10... | collective-permute-start | bytes 21512 | tf_op jit(solution)/shard_map/ppermute | solution.py:468
  (11 other events, 31.4 us)
Sparse Core Ops, SparseCore 0:
  9.9 59.4 all-gather.2
  71.3 42.9 all-gather.4

commit v7 on v6

--- a/solution.py
+++ b/solution.py
@@ -284,8 +284,8 @@
 
     return call(
         kernel,
-        2 * tokens * tile * count * hidden // 16,
-        (2 * tokens * (tile * count + hidden) + 4 * tile * count * hidden) // 16,
+        2 * tokens * tile * count * hidden,
+        2 * tokens * (tile * count + hidden) + 4 * tile * count * hidden,
         place,
         [tok, grad],
         (count,),
@@ -326,8 +326,7 @@
     steps = rows_of - 1
     me = lax.axis_index("col")
     place = jnp.stack([me // 2, me % 2]).astype(jnp.int32)
-    lead = 1
-    others = [lead] + sorted(range(2, cols_of // 2), key=lambda key: (-key.bit_count(), key))
+    others = sorted(range(1, cols_of // 2), key=lambda key: (-key.bit_count(), key))
     chunks = [("pre", 0), ("act", 0)] + [(kind, key) for kind in ("pre", "act") for key in others]
     total = len(chunks)
 
@@ -349,17 +348,13 @@
     slopes, sums, arrived = {}, {}, []
 
     def compute_own(kind, keys):
-        weight = weight_in if kind == "pre" else weight_out
-        blocks = []
-        for key in keys:
-            if (kind, key) in held:
-                near, far = link(held[kind, key]), held[kind, key, "far"]
-                blocks.append([(near, zero, mine, lambda s: s[1] * mine), (far, zero, mine, lambda s: (1 - s[1]) * mine)])
-            else:
-                blocks.append([(held[kind, "all"], lambda s, key=key: (s[0] ^ key) * rows, rows, zero)])
-        if keys[0] not in (0, lead):
-            held[kind, "all"] = link(held[kind, "all"])
-            blocks = [[(held[kind, "all"], *part[1:]) for part in block] for block in blocks]
+        source, weight = (tokens, weight_in) if kind == "pre" else (out_grad, weight_out)
+        if keys == [0]:
+            far = held[kind, "far"]
+            blocks = [[(link(source), zero, mine, lambda s: s[1] * mine), (far, zero, mine, lambda s: (1 - s[1]) * mine)]]
+        else:
+            gathered = link(held[kind])
+            blocks = [[(gathered, lambda s, key=key: (s[0] ^ key) * rows, rows, zero)] for key in keys]
         outs = partials(place, blocks, weight, kind == "act")
         chain.append(outs[0])
         for key, out in zip(keys, outs):
@@ -387,12 +382,12 @@
 
     def out_columns(first, count):
         held["out"] = weight_out_grad(
-            place, link(held["activations"]), held["cotangents"], held.get("out"), first, count
+            place, link(held["activations"]), held["act"], held.get("out"), first, count
         )
         chain.append(held["out"])
 
     def in_rows(first, count):
-        held["in"] = weight_in_grad(place, held["tokens"], link(held["grads"]), held.get("in"), first, count)
+        held["in"] = weight_in_grad(place, held["pre"], link(held["grads"]), held.get("in"), first, count)
         chain.append(held["in"])
 
     def tokens_of(keys, first, last):
@@ -414,58 +409,48 @@
         chain.append(pair)
         return results
 
-    held["pre", 0], held["act", 0] = tokens, out_grad
-    held["pre", 0, "far"], held["act", 0, "far"] = swap(tokens, 1), swap(out_grad, 1)
-    held["pre", "all"] = lax.all_gather(tokens, "col", axis=0, tiled=True)
-    held["act", "all"] = lax.all_gather(after(out_grad, held["pre", 0, "far"]), "col", axis=0, tiled=True)
-    held["tokens"], held["cotangents"] = held["pre", "all"], held["act", "all"]
+    held["pre", "far"], held["act", "far"] = swap(tokens, 1), swap(out_grad, 1)
+    held["pre"] = lax.all_gather(tokens, "col", axis=0, tiled=True)
+    held["act"] = lax.all_gather(after(out_grad, held["pre", "far"]), "col", axis=0, tiled=True)
     compute_own("pre", [0])
     first_send(0)
-    held["pre", lead] = swap(link(tokens), 2 * lead)
     compute_own("act", [0])
     first_send(1)
-    held["act", lead] = swap(link(out_grad), 2 * lead)
     end = total + steps - 1
     for slot in range(end):
-        if slot and slot + 1 < total:
+        if 3 <= slot + 1 < total:
             first_send(slot + 1)
-        for step in range(2, steps + 1):
+        late = slot == 2
+        if late and slot >= steps - 1:
+            finish(slot - steps + 1)
+        for step in range(steps, 1, -1) if late else range(2, steps + 1):
             if 0 <= slot - step + 2 < total:
                 forward(slot - step + 2, step)
-        if slot == 0:
-            held["pre", lead, "far"] = swap(link(held["pre", lead]), 1)
-            compute_own("pre", [lead])
+            if step == 2 and slot == len(others):
+                compute_own("act", others)
         if slot == 1:
-            compute_own("pre", others[1:])
-            held["act", lead, "far"] = swap(link(held["act", lead]), 1)
-        if slot >= steps - 1:
+            compute_own("pre", others)
+            first_send(2)
+        if not late and slot >= steps - 1:
             finish(slot - steps + 1)
-        if slot == 2:
-            compute_own("act", [lead])
-        if slot == len(others) + 1:
-            compute_own("act", others[1:])
         if slot == end - 4:
             out_columns(0, 3)
         if slot == end - 3:
             first = tokens_of([0] + others[:-2], 0, UNITS)
         if slot == end - 2:
-            first = exchange(first)
-            second = tokens_of(others[-2:-1], 0, UNITS)
-            arrived += deliver(first)
-            second = exchange(second)
+            arrived += deliver(exchange(first))
             out_columns(3, UNITS - 3)
-    arrived += deliver(second)
     head = add_early(place, link(arrived[0]), arrived[1])
     chain.append(head)
-    third = exchange(tokens_of(others[-1:], 0, UNITS))
+    levels = [1 << i for i in range(rows_of.bit_length() - 1)]
     sums = link(functools.reduce(jnp.add, [sums[key] for key in sorted(sums)]).reshape(hidden))
-    levels = [1 << i for i in range(rows_of.bit_length() - 1)]
     sums = sums + lax.ppermute(sums, "row", [(i, i ^ levels[0]) for i in range(rows_of)])
-    arrived += deliver(third)
-    in_rows(0, UNITS)
+    last = exchange(tokens_of(others[-2:], 0, UNITS))
     sums = link(sums)
     for bit in levels[1:]:
         sums = sums + lax.ppermute(sums, "row", [(i, i ^ bit) for i in range(rows_of)])
+    arrived += deliver(last)
+    in_rows(0, UNITS)
     grad_bias = sums * (1.0 / rows_of)
     grad_tokens = functools.reduce(jnp.add, [part.astype(F32) for part in arrived[2:]], head).astype(BF16)
     return (grad_tokens, held["in"], grad_bias, held["out"])

time: 287 us -> 278 us (0.969)
  Pallas kernels: 124 us -> 108 us
  starting transfers between devices: 74 us -> 58.8 us
  waiting for transfers between devices: 55.5 us -> 70.5 us
  local copies, waits for them, and re-layouts: 3.93 us -> 9.82 us
    ppermute x24, waiting for transfers between devices: 31.7 us -> 61.8 us  [send(): return lax.ppermute(value, 'row', pairs)]
    pallas_call x21 -> x18, Pallas kernels: 124 us -> 108 us  [call(): pl.pallas_call(kernel, grid_spec=pltpu.PrefetchScalarGridSpec(num_scalar_...]
    ppermute x12 -> x7, waiting for transfers between devices: 19.8 us -> 4.66 us  [swap(): return lax.ppermute(value, 'col', [(i, i ^ bits) for i in range(cols_of)])]
    ppermute x24, starting transfers between devices: 60.7 us -> 46.4 us  [send(): return lax.ppermute(value, 'row', pairs)]
    unnamed x38 -> x50, local copies, waits for them, and re-layouts: 3.92 us -> 9.81 us
    convert_element_type x19 -> x18, other arithmetic: 12.2 us -> 13.4 us  [add_bf16(): return (left.astype(F32) + right.astype(F32)).astype(BF16)]
    ppermute x12 -> x7, starting transfers between devices: 7.27 us -> 6.48 us  [swap(): return lax.ppermute(value, 'col', [(i, i ^ bits) for i in range(cols_of)])]
  transfers between devices with their start and end apart: 40 -> 35, of which waited for: 15 -> 14; matrix products, arithmetic and copies ran while one was open for 5% -> 5% of each run, Pallas kernels for 40% -> 35%
where the time goes in v7:
time: 278 us; the launch traced here: 277 us
  Pallas kernels  108 us (39%)
  waiting for transfers between devices  70.5 us (25%)
  starting transfers between devices  58.8 us (21%)
  other arithmetic  15.2 us (5%)
  between operations  14.7 us (5%)
  local copies, waits for them, and re-layouts  9.82 us (4%)
    pallas_call x18, Pallas kernels, call(): pl.pallas_call(kernel, grid_spec=pltpu.PrefetchScalarGridSpec(num_scalar_...  108 us
    ppermute x24, waiting for transfers between devices, send(): return lax.ppermute(value, 'row', pairs)  61.8 us
    ppermute x24, starting transfers between devices, send(): return lax.ppermute(value, 'row', pairs)  46.4 us
    convert_element_type x18, other arithmetic, add_bf16(): return (left.astype(F32) + right.astype(F32)).astype(BF16)  13.4 us
    unnamed x50, local copies, waits for them, and re-layouts  9.81 us
    ppermute x7, starting transfers between devices, swap(): return lax.ppermute(value, 'col', [(i, i ^ bits) for i in range(cols_of)])  6.48 us
  transfers between devices with their start and end apart: 35, of which 14 were waited for; matrix products, arithmetic and copies ran while one was open for 5% of the time, Pallas kernels for 35%

profile of v7, /device:TPU:0, one launch (start us, length us, event | category | flops | bytes accessed | tf_op | source)
XLA Modules:
  0.0 276.9 jit_solution(13014780067803948067)
XLA Ops:
  8.5 2.0 collective-permute-done.refs_1_
  11.0 6.3 %shard_map.84 = bf16[192,1792]{1,0:T(8,128)(2,1)S(1)} custom-call(s32[2]{0:T(128)S(1)} %pad_add_fusion.s, bf16[96,3584]{1,0:T(8,128)(2,1)S(1)} %copy-done, bf16[96,3584]{1,0:T(8,128)(2,1)S(1)} %collective-permute-done.refs_1_, bf16[3584,1792]{1,0:T(8,128)(2,1)} %refs_1_.7), custom_call_target="tpu_custom_call" | custom-call | flops 2466250752 | bytes 14221312 | tf_op jit(solution)/shard_map/pallas_call | solution.py:30
  17.3 4.7 %collective-permute-start.1 = (bf16[192,1792]{1,0:T(8,128)(2,1)S(1)}, bf16[192,1792]{1,0:T(8,128)(2,1)S(1)}, u32[]{:S(2)}, u32[]{:S(2)}) collective-permute-start(bf16[192,1792]{1,0:T(8,128)(2,1)S(1)} %shard_map.84), channel_id=1, source_target_pairs={{0,8},{24,16},{1,9},{25,17},{2,10},{26,18},{3,11},{27,19},{4,12},{... | collective-permute-start | bytes 2064392 | tf_op jit(solution)/shard_map/ppermute | solution.py:335
  23.9 7.3 %shard_map.85 = bf16[192,1792]{1,0:T(8,128)(2,1)S(1)} custom-call(s32[2]{0:T(128)S(1)} %pad_add_fusion.s, bf16[96,3584]{1,0:T(8,128)(2,1)S(1)} %copy-done.1, bf16[96,3584]{1,0:T(8,128)(2,1)S(1)} %copy-done.19, bf16[1792,3584]{1,0:T(8,128)(2,1)} %refs_1_.5), custom_call_target="tpu_custom_call" | custom-call | flops 2466250752 | bytes 14221312 | tf_op jit(solution)/shard_map/pallas_call | solution.py:30
  31.3 1.3 collective-permute-start.4
  32.6 5.1 %collective-permute-done.1 = bf16[192,1792]{1,0:T(8,128)(2,1)S(1)} collective-permute-done((bf16[192,1792]{1,0:T(8,128)(2,1)S(1)}, bf16[192,1792]{1,0:T(8,128)(2,1)S(1)}, u32[]{:S(2)}, u32[]{:S(2)}) %collective-permute-start.1) | collective-permute-done | bytes 688160 | tf_op jit(solution)/shard_map/ppermute | solution.py:335
  38.6 13.3 %collective-permute-done.4 = bf16[192,1792]{1,0:T(8,128)(2,1)S(1)} collective-permute-done((bf16[192,1792]{1,0:T(8,128)(2,1)S(1)}, bf16[192,1792]{1,0:T(8,128)(2,1)S(1)}, u32[]{:S(2)}, u32[]{:S(2)}) %collective-permute-start.4) | collective-permute-done | bytes 688160 | tf_op jit(solution)/shard_map/ppermute | solution.py:335
  52.9 1.6 collective-permute-start.6
  55.3 1.4 collective-permute-start.7
  56.8 12.6 %shard_map.86 = (bf16[192,1792]{1,0:T(8,128)(2,1)S(1)}, bf16[192,1792]{1,0:T(8,128)(2,1)S(1)}, bf16[192,1792]{1,0:T(8,128)(2,1)S(1)}) custom-call(s32[2]{0:T(128)S(1)} %pad_add_fusion.s, bf16[768,3584]{1,0:T(8,128)(2,1)} %all-gather.3.cloned.1.call-done.refs_0_.tok_ref, bf16[3584,1792]{1,0:T(8,128)(2,1)} %refs_1_.7), custom_call_target="tpu_custom_call" | custom-call | flops 7398752256 | bytes 16973824 | tf_op jit(solution)/shard_map/pallas_call | solution.py:30
  70.2 6.4 %collective-permute-start.5 = (bf16[192,1792]{1,0:T(8,128)(2,1)S(1)}, bf16[192,1792]{1,0:T(8,128)(2,1)S(1)}, u32[]{:S(2)}, u32[]{:S(2)}) collective-permute-start(bf16[192,1792]{1,0:T(8,128)(2,1)S(1)} %get-tuple-element.100), channel_id=1, source_target_pairs={{0,8},{24,16},{1,9},{25,17},{2,10},{26,18},{3,11},{27,19},{4,12},{... | collective-permute-start | bytes 2064392 | tf_op jit(solution)/shard_map/ppermute | solution.py:335
  76.6 1.3 collective-permute-start.8
  79.9 1.8 shard_map.87
  81.7 2.6 add_convert_fusion.17
  85.6 6.8 %collective-permute-done.5 = bf16[192,1792]{1,0:T(8,128)(2,1)S(1)} collective-permute-done((bf16[192,1792]{1,0:T(8,128)(2,1)S(1)}, bf16[192,1792]{1,0:T(8,128)(2,1)S(1)}, u32[]{:S(2)}, u32[]{:S(2)}) %collective-permute-start.5) | collective-permute-done | bytes 688160 | tf_op jit(solution)/shard_map/ppermute | solution.py:335
  93.5 1.5 collective-permute-start.11
  95.0 10.6 %collective-permute-done.8 = bf16[192,1792]{1,0:T(8,128)(2,1)S(1)} collective-permute-done((bf16[192,1792]{1,0:T(8,128)(2,1)S(1)}, bf16[192,1792]{1,0:T(8,128)(2,1)S(1)}, u32[]{:S(2)}, u32[]{:S(2)}) %collective-permute-start.8) | collective-permute-done | bytes 688160 | tf_op jit(solution)/shard_map/ppermute | solution.py:335
  105.7 1.5 collective-permute-start.9
  107.2 5.4 %collective-permute-start.10 = (bf16[192,1792]{1,0:T(8,128)(2,1)}, bf16[192,1792]{1,0:T(8,128)(2,1)S(1)}, u32[]{:S(2)}, u32[]{:S(2)}) collective-permute-start(bf16[192,1792]{1,0:T(8,128)(2,1)} %copy-done.6), channel_id=1, source_target_pairs={{0,8},{24,16},{1,9},{25,17},{2,10},{26,18},{3,11},{27,19},{4,12},{... | collective-permute-start | bytes 2064392 | tf_op jit(solution)/shard_map/ppermute | solution.py:335
  112.7 12.7 %shard_map.88 = (bf16[192,1792]{1,0:T(8,128)(2,1)S(1)}, bf16[192,1792]{1,0:T(8,128)(2,1)S(1)}, bf16[192,1792]{1,0:T(8,128)(2,1)S(1)}) custom-call(s32[2]{0:T(128)S(1)} %pad_add_fusion.s, bf16[768,3584]{1,0:T(8,128)(2,1)} %all-gather.5.cloned.1.call-done.refs_0_.grad_ref, bf16[1792,3584]{1,0:T(8,128)(2,1)} %refs_1_.5), custom_call_target="tpu_custom_call" | custom-call | flops 7398752256 | bytes 16973824 | tf_op jit(solution)/shard_map/pallas_call | solution.py:30
  125.4 1.4 add_convert_fusion.14
  127.0 2.5 shard_map.89
  129.4 1.4 collective-permute-start.13
  130.9 4.6 %collective-permute-start.14 = (bf16[192,1792]{1,0:T(8,128)(2,1)S(1)}, bf16[192,1792]{1,0:T(8,128)(2,1)S(1)}, u32[]{:S(2)}, u32[]{:S(2)}) collective-permute-start(bf16[192,1792]{1,0:T(8,128)(2,1)S(1)} %get-tuple-element.118), channel_id=1, source_target_pairs={{0,8},{24,16},{1,9},{25,17},{2,10},{26,18},{3,11},{27,19},{4,12},{... | collective-permute-start | bytes 2064392 | tf_op jit(solution)/shard_map/ppermute | solution.py:335
  137.7 1.3 collective-permute-start.17
  139.0 10.8 %collective-permute-done.13.refs_2_ = bf16[192,1792]{1,0:T(8,128)(2,1)S(1)} collective-permute-done((bf16[192,1792]{1,0:T(8,128)(2,1)S(1)}, bf16[192,1792]{1,0:T(8,128)(2,1)S(1)}, u32[]{:S(2)}, u32[]{:S(2)}) %collective-permute-start.13) | collective-permute-done | bytes 688160 | tf_op jit(solution)/shard_map/ppermute | solution.py:335
  149.8 3.1 %shard_map.90 = (bf16[768,1792]{1,0:T(8,128)(2,1)S(1)}, f32[192,1792]{1,0:T(8,128)S(1)}) custom-call(s32[2]{0:T(128)S(1)} %pad_add_fusion.s, f32[1,1792]{1,0:T(1,128)S(1)} %reshape.14.bias_ref, bf16[192,1792]{1,0:T(8,128)(2,1)} %add_convert_fusion.16.refs_0_, bf16[192,1792]{1,0:T(8,128)(2,1)} %collective-permute-done.11.refs_1_, ...), custom_call_target="tpu_custom_call", output_to_operand_aliasing={{0}: (5, {})} | custom-call | flops 10321920 | bytes 4128768 | tf_op jit(solution)/shard_map/pallas_call | solution.py:30
  152.9 2.3 collective-permute-start.15
  158.5 6.1 %collective-permute-done.17.refs_2_ = bf16[192,1792]{1,0:T(8,128)(2,1)S(1)} collective-permute-done((bf16[192,1792]{1,0:T(8,128)(2,1)S(1)}, bf16[192,1792]{1,0:T(8,128)(2,1)S(1)}, u32[]{:S(2)}, u32[]{:S(2)}) %collective-permute-start.17) | collective-permute-done | bytes 688160 | tf_op jit(solution)/shard_map/ppermute | solution.py:335
  164.6 2.9 %shard_map.91 = (bf16[768,1792]{1,0:T(8,128)(2,1)S(1)}, f32[192,1792]{1,0:T(8,128)S(1)}) custom-call(s32[2]{0:T(128)S(1)} %pad_add_fusion.s, f32[1,1792]{1,0:T(1,128)S(1)} %reshape.14.bias_ref, bf16[192,1792]{1,0:T(8,128)(2,1)S(1)} %add_convert_fusion.15.refs_0_, bf16[192,1792]{1,0:T(8,128)(2,1)} %collective-permute-done.9.refs_1_, ...), custom_call_target="tpu_custom_call", output_to_operand_aliasing={{0}: (5, {})} | custom-call | flops 10321920 | bytes 4128768 | tf_op jit(solution)/shard_map/pallas_call | solution.py:30
  168.5 1.7 collective-permute-start.19
  174.5 4.8 %collective-permute-done.21.refs_2_ = bf16[192,1792]{1,0:T(8,128)(2,1)S(1)} collective-permute-done((bf16[192,1792]{1,0:T(8,128)(2,1)}, bf16[192,1792]{1,0:T(8,128)(2,1)S(1)}, u32[]{:S(2)}, u32[]{:S(2)}) %collective-permute-start.21) | collective-permute-done | bytes 688160 | tf_op jit(solution)/shard_map/ppermute | solution.py:335
  181.3 1.8 shard_map.92
  183.0 9.3 %shard_map.93.refs_0_ = f32[1792,3584]{1,0:T(8,128)} custom-call(s32[2]{0:T(128)S(1)} %pad_add_fusion.s, bf16[768,1792]{1,0:T(8,128)(2,1)S(1)} %get-tuple-element.136.act_ref, bf16[768,3584]{1,0:T(8,128)(2,1)} %all-gather.5.cloned.1.call-done.refs_0_.grad_ref), custom_call_target="tpu_custom_call" | custom-call | flops 4227858432 | bytes 16121856 | tf_op jit(solution)/shard_map/pallas_call | solution.py:30
  196.5 8.5 %shard_map.95 = (bf16[192,3584]{1,0:T(8,128)(2,1)S(1)}, bf16[192,3584]{1,0:T(8,128)(2,1)S(1)}) custom-call(s32[2]{0:T(128)S(1)} %pad_add_fusion.s, bf16[768,1792]{1,0:T(8,128)(2,1)S(1)} %get-tuple-element.126.refs_0_.refs_3_, bf16[3584,1792]{1,0:T(8,128)(2,1)} %refs_1_.7), custom_call_target="tpu_custom_call" | custom-call | flops 4932501504 | bytes 14221312 | tf_op jit(solution)/shard_map/pallas_call | solution.py:30
  208.6 1.3 collective-permute-start.26
  209.9 1.8 collective-permute-done.25
  212.0 2.4 collective-permute-start.27
  214.4 11.0 %shard_map.97 = f32[1792,3584]{1,0:T(8,128)} custom-call(s32[2]{0:T(128)S(1)} %pad_add_fusion.s, bf16[768,1792]{1,0:T(8,128)(2,1)S(1)} %get-tuple-element.136.act_ref, bf16[768,3584]{1,0:T(8,128)(2,1)} %all-gather.5.cloned.1.call-done.refs_0_.grad_ref, f32[1792,3584]{1,0:T(8,128)} %shard_map.93.refs_0_), custom_call_target="tpu_custom_call", output_to_operand_aliasing={{}: (3, {})} | custom-call | flops 5637144576 | bytes 20578304 | tf_op jit(solution)/shard_map/pallas_call | solution.py:30
  225.4 3.2 %collective-permute-done.26.refs_2_ = bf16[192,1792]{1,0:T(8,128)(2,1)S(1)} collective-permute-done((bf16[192,1792]{1,0:T(8,128)(2,1)S(1)}, bf16[192,1792]{1,0:T(8,128)(2,1)S(1)}, u32[]{:S(2)}, u32[]{:S(2)}) %collective-permute-start.26) | collective-permute-done | bytes 688160 | tf_op jit(solution)/shard_map/ppermute | solution.py:335
  231.1 8.5 %shard_map.100 = (bf16[192,3584]{1,0:T(8,128)(2,1)S(1)}, bf16[192,3584]{1,0:T(8,128)(2,1)S(1)}) custom-call(s32[2]{0:T(128)S(1)} %pad_add_fusion.s, bf16[768,1792]{1,0:T(8,128)(2,1)S(1)} %get-tuple-element.145.refs_0_.grad_ref, bf16[3584,1792]{1,0:T(8,128)(2,1)} %refs_1_.7), custom_call_target="tpu_custom_call" | custom-call | flops 4932501504 | bytes 14221312 | tf_op jit(solution)/shard_map/pallas_call | solution.py:30
  239.7 2.7 collective-permute-start.31
  242.5 1.6 collective-permute-done.31
  244.1 3.0 %collective-permute-start.32 = (f32[1792]{0:T(1024)S(1)}, f32[1792]{0:T(1024)S(1)}, u32[]{:S(2)}, u32[]{:S(2)}) collective-permute-start(f32[1792]{0:T(1024)S(1)} %add.112), channel_id=1, source_target_pairs={{0,16},{8,24},{16,0},{24,8},{1,17},{9,25},{17,1},{25,9},{2,18},{10... | collective-permute-start | bytes 21512 | tf_op jit(solution)/shard_map/ppermute | solution.py:451
  247.1 1.6 collective-permute-done.32
  249.7 1.6 collective-permute-start.30
  251.3 1.4 collective-permute-start.29
  252.7 16.4 %shard_map.101 = f32[3584,1792]{1,0:T(8,128)} custom-call(s32[2]{0:T(128)S(1)} %pad_add_fusion.s, bf16[768,3584]{1,0:T(8,128)(2,1)} %all-gather.3.cloned.1.call-done.refs_0_.tok_ref, bf16[768,1792]{1,0:T(8,128)(2,1)S(1)} %get-tuple-element.145.refs_0_.grad_ref), custom_call_target="tpu_custom_call" | custom-call | flops 9865003008 | bytes 33947648 | tf_op jit(solution)/shard_map/pallas_call | solution.py:30
  (116 shorter events, 37.2 us)
Async XLA Ops:
  7.2 3.9 %copy-start = (bf16[96,3584]{1,0:T(8,128)(2,1)S(1)}, bf16[96,3584]{1,0:T(8,128)(2,1)}, u32[]{:S(2)}) copy-start(bf16[96,3584]{1,0:T(8,128)(2,1)} %refs_0_.1) | copy-start | bytes 2064388
  7.2 3.3 %copy-start.1 = (bf16[96,3584]{1,0:T(8,128)(2,1)S(1)}, bf16[96,3584]{1,0:T(8,128)(2,1)}, u32[]{:S(2)}) copy-start(bf16[96,3584]{1,0:T(8,128)(2,1)} %refs_0_.2) | copy-start | bytes 2064388
  7.2 49.6 %all-gather.3.cloned.1.call-start = ((), (), s32[]{:S(2)}) async-start(), calls=%async_computation | async-start | bytes 6193152 | tf_op jit(solution)/shard_map/all_gather | solution.py:413
  7.9 99.3 %all-gather.5.cloned.1.call-start = ((), (), s32[]{:S(2)}) async-start(), calls=%async_computation.1 | async-start | bytes 6193152 | tf_op jit(solution)/shard_map/all_gather | solution.py:414
  8.0 2.5 collective-permute-start
  10.5 11.5 %collective-permute-start.2 = (bf16[96,3584]{1,0:T(8,128)(2,1)S(1)}, bf16[96,3584]{1,0:T(8,128)(2,1)S(1)}, u32[]{:S(2)}, u32[]{:S(2)}) collective-permute-start(bf16[96,3584]{1,0:T(8,128)(2,1)S(1)} %copy-done.1), channel_id=1, source_target_pairs={{0,1},{1,0},{2,3},{3,2},{4,5},{5,4},{6,7},{7,6},{8,9},{9,8},{10,11... | collective-permute-start | bytes 2064392 | tf_op jit(solution)/shard_map/ppermute | solution.py:338
  17.3 20.4 %collective-permute-start.1 = (bf16[192,1792]{1,0:T(8,128)(2,1)S(1)}, bf16[192,1792]{1,0:T(8,128)(2,1)S(1)}, u32[]{:S(2)}, u32[]{:S(2)}) collective-permute-start(bf16[192,1792]{1,0:T(8,128)(2,1)S(1)} %shard_map.84), channel_id=1, source_target_pairs={{0,8},{24,16},{1,9},{25,17},{2,10},{26,18},{3,11},{27,19},{4,12},{... | collective-permute-start | bytes 2064392 | tf_op jit(solution)/shard_map/ppermute | solution.py:335
  31.3 20.6 %collective-permute-start.4 = (bf16[192,1792]{1,0:T(8,128)(2,1)S(1)}, bf16[192,1792]{1,0:T(8,128)(2,1)S(1)}, u32[]{:S(2)}, u32[]{:S(2)}) collective-permute-start(bf16[192,1792]{1,0:T(8,128)(2,1)S(1)} %shard_map.85), channel_id=1, source_target_pairs={{0,8},{24,16},{1,9},{25,17},{2,10},{26,18},{3,11},{27,19},{4,12},{... | collective-permute-start | bytes 2064392 | tf_op jit(solution)/shard_map/ppermute | solution.py:335
  37.8 16.8 %copy-start.2 = (bf16[192,1792]{1,0:T(8,128)(2,1)}, bf16[192,1792]{1,0:T(8,128)(2,1)S(1)}, u32[]{:S(2)}) copy-start(bf16[192,1792]{1,0:T(8,128)(2,1)S(1)} %add_convert_fusion.20.refs_0_) | copy-start | bytes 2064388
  37.8 16.6 %collective-permute-start.3 = (bf16[192,1792]{1,0:T(8,128)(2,1)S(1)}, bf16[192,1792]{1,0:T(8,128)(2,1)S(1)}, u32[]{:S(2)}, u32[]{:S(2)}) collective-permute-start(bf16[192,1792]{1,0:T(8,128)(2,1)S(1)} %add_convert_fusion.20.refs_0_), channel_id=1, source_target_pairs={{8,16},{16,8},{9,17},{17,9},{10,18},{18,10},{11,19},{19,11},{12,20... | collective-permute-start | bytes 2064392 | tf_op jit(solution)/shard_map/ppermute | solution.py:335
  52.9 28.8 %collective-permute-start.6 = (bf16[192,1792]{1,0:T(8,128)(2,1)}, bf16[192,1792]{1,0:T(8,128)(2,1)}, u32[]{:S(2)}, u32[]{:S(2)}) collective-permute-start(bf16[192,1792]{1,0:T(8,128)(2,1)} %add_convert_fusion.19.refs_0_), channel_id=1, source_target_pairs={{8,16},{16,8},{9,17},{17,9},{10,18},{18,10},{11,19},{19,11},{12,20... | collective-permute-start | bytes 2064392 | tf_op jit(solution)/shard_map/ppermute | solution.py:335
  55.3 21.3 %copy-start.24 = (f32[1792]{0:T(1024)S(1)}, f32[1792]{0:T(1024)}, u32[]{:S(2)}) copy-start(f32[1792]{0:T(1024)} %param.7) | copy-start | bytes 21508
  55.3 22.7 %collective-permute-start.7 = (bf16[192,1792]{1,0:T(8,128)(2,1)S(1)}, bf16[192,1792]{1,0:T(8,128)(2,1)S(1)}, u32[]{:S(2)}, u32[]{:S(2)}) collective-permute-start(bf16[192,1792]{1,0:T(8,128)(2,1)S(1)} %add_convert_fusion.18), channel_id=1, source_target_pairs={{16,24},{8,0},{17,25},{9,1},{18,26},{10,2},{19,27},{11,3},{20,28},... | collective-permute-start | bytes 2064392 | tf_op jit(solution)/shard_map/ppermute | solution.py:335
  56.8 22.1 %copy-start.3 = (bf16[192,1792]{1,0:T(8,128)(2,1)S(1)}, bf16[192,1792]{1,0:T(8,128)(2,1)}, u32[]{:S(2)}) copy-start(bf16[192,1792]{1,0:T(8,128)(2,1)} %copy-done.2) | copy-start | bytes 2064388
  56.8 22.1 %copy-start.5 = (bf16[192,1792]{1,0:T(8,128)(2,1)S(1)}, bf16[192,1792]{1,0:T(8,128)(2,1)}, u32[]{:S(2)}) copy-start(bf16[192,1792]{1,0:T(8,128)(2,1)} %copy-done.4) | copy-start | bytes 2064388
  70.2 22.2 %copy-start.10 = (bf16[192,1792]{1,0:T(8,128)(2,1)}, bf16[192,1792]{1,0:T(8,128)(2,1)S(1)}, u32[]{:S(2)}) copy-start(bf16[192,1792]{1,0:T(8,128)(2,1)S(1)} %get-tuple-element.100) | copy-start | bytes 2064388
  70.2 35.3 %copy-start.8 = (bf16[192,1792]{1,0:T(8,128)(2,1)}, bf16[192,1792]{1,0:T(8,128)(2,1)S(1)}, u32[]{:S(2)}) copy-start(bf16[192,1792]{1,0:T(8,128)(2,1)S(1)} %get-tuple-element.104) | copy-start | bytes 2064388
  70.2 22.2 %collective-permute-start.5 = (bf16[192,1792]{1,0:T(8,128)(2,1)S(1)}, bf16[192,1792]{1,0:T(8,128)(2,1)S(1)}, u32[]{:S(2)}, u32[]{:S(2)}) collective-permute-start(bf16[192,1792]{1,0:T(8,128)(2,1)S(1)} %get-tuple-element.100), channel_id=1, source_target_pairs={{0,8},{24,16},{1,9},{25,17},{2,10},{26,18},{3,11},{27,19},{4,12},{... | collective-permute-start | bytes 2064392 | tf_op jit(solution)/shard_map/ppermute | solution.py:335
  76.6 28.9 %collective-permute-start.8 = (bf16[192,1792]{1,0:T(8,128)(2,1)S(1)}, bf16[192,1792]{1,0:T(8,128)(2,1)S(1)}, u32[]{:S(2)}, u32[]{:S(2)}) collective-permute-start(bf16[192,1792]{1,0:T(8,128)(2,1)S(1)} %get-tuple-element.104), channel_id=1, source_target_pairs={{0,8},{24,16},{1,9},{25,17},{2,10},{26,18},{3,11},{27,19},{4,12},{... | collective-permute-start | bytes 2064392 | tf_op jit(solution)/shard_map/ppermute | solution.py:335
  81.7 11.7 %copy-start.14 = (f32[192,1792]{1,0:T(8,128)}, f32[192,1792]{1,0:T(8,128)S(1)}, u32[]{:S(2)}) copy-start(f32[192,1792]{1,0:T(8,128)S(1)} %get-tuple-element.96.slope_ref) | copy-start | bytes 4128772
  84.4 42.5 %collective-permute-start.12 = (bf16[192,1792]{1,0:T(8,128)(2,1)}, bf16[192,1792]{1,0:T(8,128)(2,1)}, u32[]{:S(2)}, u32[]{:S(2)}) collective-permute-start(bf16[192,1792]{1,0:T(8,128)(2,1)} %add_convert_fusion.17), channel_id=1, source_target_pairs={{16,24},{8,0},{17,25},{9,1},{18,26},{10,2},{19,27},{11,3},{20,28},... | collective-permute-start | bytes 2064392 | tf_op jit(solution)/shard_map/ppermute | solution.py:335
  93.5 32.0 %collective-permute-start.11 = (bf16[192,1792]{1,0:T(8,128)(2,1)}, bf16[192,1792]{1,0:T(8,128)(2,1)}, u32[]{:S(2)}, u32[]{:S(2)}) collective-permute-start(bf16[192,1792]{1,0:T(8,128)(2,1)} %add_convert_fusion.16.refs_0_), channel_id=1, source_target_pairs={{8,16},{16,8},{9,17},{17,9},{10,18},{18,10},{11,19},{19,11},{12,20... | collective-permute-start | bytes 2064392 | tf_op jit(solution)/shard_map/ppermute | solution.py:335
  105.7 30.7 %collective-permute-start.9 = (bf16[192,1792]{1,0:T(8,128)(2,1)S(1)}, bf16[192,1792]{1,0:T(8,128)(2,1)}, u32[]{:S(2)}, u32[]{:S(2)}) collective-permute-start(bf16[192,1792]{1,0:T(8,128)(2,1)S(1)} %add_convert_fusion.15.refs_0_), channel_id=1, source_target_pairs={{8,16},{16,8},{9,17},{17,9},{10,18},{18,10},{11,19},{19,11},{12,20... | collective-permute-start | bytes 2064392 | tf_op jit(solution)/shard_map/ppermute | solution.py:335
  107.2 18.2 %copy-start.11 = (bf16[192,1792]{1,0:T(8,128)(2,1)S(1)}, bf16[192,1792]{1,0:T(8,128)(2,1)}, u32[]{:S(2)}) copy-start(bf16[192,1792]{1,0:T(8,128)(2,1)} %copy-done.10) | copy-start | bytes 2064388
  107.2 28.3 %collective-permute-start.10 = (bf16[192,1792]{1,0:T(8,128)(2,1)}, bf16[192,1792]{1,0:T(8,128)(2,1)S(1)}, u32[]{:S(2)}, u32[]{:S(2)}) collective-permute-start(bf16[192,1792]{1,0:T(8,128)(2,1)} %copy-done.6), channel_id=1, source_target_pairs={{0,8},{24,16},{1,9},{25,17},{2,10},{26,18},{3,11},{27,19},{4,12},{... | collective-permute-start | bytes 2064392 | tf_op jit(solution)/shard_map/ppermute | solution.py:335
  127.0 8.6 %copy-start.7 = (bf16[192,1792]{1,0:T(8,128)(2,1)S(1)}, bf16[192,1792]{1,0:T(8,128)(2,1)}, u32[]{:S(2)}) copy-start(bf16[192,1792]{1,0:T(8,128)(2,1)} %copy-done.6) | copy-start | bytes 2064388
  129.4 7.0 %copy-start.9 = (bf16[192,1792]{1,0:T(8,128)(2,1)S(1)}, bf16[192,1792]{1,0:T(8,128)(2,1)}, u32[]{:S(2)}) copy-start(bf16[192,1792]{1,0:T(8,128)(2,1)} %copy-done.8) | copy-start | bytes 2064388
  129.4 20.4 %collective-permute-start.13 = (bf16[192,1792]{1,0:T(8,128)(2,1)S(1)}, bf16[192,1792]{1,0:T(8,128)(2,1)S(1)}, u32[]{:S(2)}, u32[]{:S(2)}) collective-permute-start(bf16[192,1792]{1,0:T(8,128)(2,1)S(1)} %add_convert_fusion.14), channel_id=1, source_target_pairs={{16,24},{8,0},{17,25},{9,1},{18,26},{10,2},{19,27},{11,3},{20,28},... | collective-permute-start | bytes 2064392 | tf_op jit(solution)/shard_map/ppermute | solution.py:335
  130.9 24.4 %collective-permute-start.14 = (bf16[192,1792]{1,0:T(8,128)(2,1)S(1)}, bf16[192,1792]{1,0:T(8,128)(2,1)S(1)}, u32[]{:S(2)}, u32[]{:S(2)}) collective-permute-start(bf16[192,1792]{1,0:T(8,128)(2,1)S(1)} %get-tuple-element.118), channel_id=1, source_target_pairs={{0,8},{24,16},{1,9},{25,17},{2,10},{26,18},{3,11},{27,19},{4,12},{... | collective-permute-start | bytes 2064392 | tf_op jit(solution)/shard_map/ppermute | solution.py:335
  135.7 20.4 %collective-permute-start.16 = (bf16[192,1792]{1,0:T(8,128)(2,1)S(1)}, bf16[192,1792]{1,0:T(8,128)(2,1)S(1)}, u32[]{:S(2)}, u32[]{:S(2)}) collective-permute-start(bf16[192,1792]{1,0:T(8,128)(2,1)S(1)} %add_convert_fusion.13.refs_0_), channel_id=1, source_target_pairs={{8,16},{16,8},{9,17},{17,9},{10,18},{18,10},{11,19},{19,11},{12,20... | collective-permute-start | bytes 2064392 | tf_op jit(solution)/shard_map/ppermute | solution.py:335
  137.7 26.9 %collective-permute-start.17 = (bf16[192,1792]{1,0:T(8,128)(2,1)S(1)}, bf16[192,1792]{1,0:T(8,128)(2,1)S(1)}, u32[]{:S(2)}, u32[]{:S(2)}) collective-permute-start(bf16[192,1792]{1,0:T(8,128)(2,1)S(1)} %add_convert_fusion.12), channel_id=1, source_target_pairs={{16,24},{8,0},{17,25},{9,1},{18,26},{10,2},{19,27},{11,3},{20,28},... | collective-permute-start | bytes 2064392 | tf_op jit(solution)/shard_map/ppermute | solution.py:335
  152.9 17.3 %collective-permute-start.15 = (bf16[192,1792]{1,0:T(8,128)(2,1)S(1)}, bf16[192,1792]{1,0:T(8,128)(2,1)}, u32[]{:S(2)}, u32[]{:S(2)}) collective-permute-start(bf16[192,1792]{1,0:T(8,128)(2,1)S(1)} %get-tuple-element.123), channel_id=1, source_target_pairs={{0,8},{24,16},{1,9},{25,17},{2,10},{26,18},{3,11},{27,19},{4,12},{... | collective-permute-start | bytes 2064392 | tf_op jit(solution)/shard_map/ppermute | solution.py:335
  155.4 16.0 %collective-permute-start.20 = (bf16[192,1792]{1,0:T(8,128)(2,1)S(1)}, bf16[192,1792]{1,0:T(8,128)(2,1)S(1)}, u32[]{:S(2)}, u32[]{:S(2)}) collective-permute-start(bf16[192,1792]{1,0:T(8,128)(2,1)S(1)} %add_convert_fusion.11.refs_0_), channel_id=1, source_target_pairs={{8,16},{16,8},{9,17},{17,9},{10,18},{18,10},{11,19},{19,11},{12,20... | collective-permute-start | bytes 2064392 | tf_op jit(solution)/shard_map/ppermute | solution.py:335
  157.2 22.1 %collective-permute-start.21 = (bf16[192,1792]{1,0:T(8,128)(2,1)}, bf16[192,1792]{1,0:T(8,128)(2,1)S(1)}, u32[]{:S(2)}, u32[]{:S(2)}) collective-permute-start(bf16[192,1792]{1,0:T(8,128)(2,1)} %add_convert_fusion.10), channel_id=1, source_target_pairs={{16,24},{8,0},{17,25},{9,1},{18,26},{10,2},{19,27},{11,3},{20,28},... | collective-permute-start | bytes 2064392 | tf_op jit(solution)/shard_map/ppermute | solution.py:335
  168.5 23.8 %collective-permute-start.19 = (bf16[192,1792]{1,0:T(8,128)(2,1)S(1)}, bf16[192,1792]{1,0:T(8,128)(2,1)S(1)}, u32[]{:S(2)}, u32[]{:S(2)}) collective-permute-start(bf16[192,1792]{1,0:T(8,128)(2,1)S(1)} %get-tuple-element.129), channel_id=1, source_target_pairs={{0,8},{24,16},{1,9},{25,17},{2,10},{26,18},{3,11},{27,19},{4,12},{... | collective-permute-start | bytes 2064392 | tf_op jit(solution)/shard_map/ppermute | solution.py:335
  172.5 23.0 %collective-permute-start.22 = (bf16[192,1792]{1,0:T(8,128)(2,1)}, bf16[192,1792]{1,0:T(8,128)(2,1)S(1)}, u32[]{:S(2)}, u32[]{:S(2)}) collective-permute-start(bf16[192,1792]{1,0:T(8,128)(2,1)} %add_convert_fusion.8), channel_id=1, source_target_pairs={{16,24},{8,0},{17,25},{9,1},{18,26},{10,2},{19,27},{11,3},{20,28},... | collective-permute-start | bytes 2064392 | tf_op jit(solution)/shard_map/ppermute | solution.py:335
  173.8 19.4 %collective-permute-start.18 = (bf16[192,1792]{1,0:T(8,128)(2,1)S(1)}, bf16[192,1792]{1,0:T(8,128)(2,1)S(1)}, u32[]{:S(2)}, u32[]{:S(2)}) collective-permute-start(bf16[192,1792]{1,0:T(8,128)(2,1)S(1)} %add_convert_fusion.9.refs_0_), channel_id=1, source_target_pairs={{8,16},{16,8},{9,17},{17,9},{10,18},{18,10},{11,19},{19,11},{12,20... | collective-permute-start | bytes 2064392 | tf_op jit(solution)/shard_map/ppermute | solution.py:335
  192.5 13.7 %collective-permute-start.23 = (bf16[192,1792]{1,0:T(8,128)(2,1)S(1)}, bf16[192,1792]{1,0:T(8,128)(2,1)S(1)}, u32[]{:S(2)}, u32[]{:S(2)}) collective-permute-start(bf16[192,1792]{1,0:T(8,128)(2,1)S(1)} %add_convert_fusion.7.refs_0_), channel_id=1, source_target_pairs={{8,16},{16,8},{9,17},{17,9},{10,18},{18,10},{11,19},{19,11},{12,20... | collective-permute-start | bytes 2064392 | tf_op jit(solution)/shard_map/ppermute | solution.py:335
  194.2 13.3 %collective-permute-start.24 = (bf16[192,1792]{1,0:T(8,128)(2,1)}, bf16[192,1792]{1,0:T(8,128)(2,1)S(1)}, u32[]{:S(2)}, u32[]{:S(2)}) collective-permute-start(bf16[192,1792]{1,0:T(8,128)(2,1)} %add_convert_fusion.6), channel_id=1, source_target_pairs={{16,24},{8,0},{17,25},{9,1},{18,26},{10,2},{19,27},{11,3},{20,28},... | collective-permute-start | bytes 2064392 | tf_op jit(solution)/shard_map/ppermute | solution.py:335
  207.5 4.2 %copy-start.17 = (bf16[192,3584]{1,0:T(8,128)(2,1)S(1)}, bf16[192,3584]{1,0:T(8,128)(2,1)}, u32[]{:S(2)}) copy-start(bf16[192,3584]{1,0:T(8,128)(2,1)} %copy-done.16) | copy-start | bytes 4128772
  208.5 3.2 %collective-permute-start.25 = (bf16[192,3584]{1,0:T(8,128)(2,1)S(1)}, bf16[192,3584]{1,0:T(8,128)(2,1)S(1)}, u32[]{:S(2)}, u32[]{:S(2)}) collective-permute-start(bf16[192,3584]{1,0:T(8,128)(2,1)S(1)} %get-tuple-element.134), channel_id=1, source_target_pairs={{0,1},{1,0},{2,3},{3,2},{4,5},{5,4},{6,7},{7,6},{8,9},{9,8},{10,11... | collective-permute-start | bytes 4128776 | tf_op jit(solution)/shard_map/ppermute | solution.py:338
  208.6 20.0 %collective-permute-start.26 = (bf16[192,1792]{1,0:T(8,128)(2,1)S(1)}, bf16[192,1792]{1,0:T(8,128)(2,1)S(1)}, u32[]{:S(2)}, u32[]{:S(2)}) collective-permute-start(bf16[192,1792]{1,0:T(8,128)(2,1)S(1)} %add_convert_fusion.5), channel_id=1, source_target_pairs={{16,24},{8,0},{17,25},{9,1},{18,26},{10,2},{19,27},{11,3},{20,28},... | collective-permute-start | bytes 2064392 | tf_op jit(solution)/shard_map/ppermute | solution.py:335
  212.0 18.4 %collective-permute-start.27 = (bf16[96,3584]{1,0:T(8,128)(2,1)S(1)}, bf16[96,3584]{1,0:T(8,128)(2,1)S(1)}, u32[]{:S(2)}, u32[]{:S(2)}) collective-permute-start(bf16[96,3584]{1,0:T(8,128)(2,1)S(1)} %get-tuple-element.155), channel_id=1, source_target_pairs={{0,6},{1,7},{2,4},{3,5},{4,2},{5,3},{6,0},{7,1},{8,14},{9,15},{10,... | collective-permute-start | bytes 2064392 | tf_op jit(solution)/shard_map/ppermute | solution.py:338
  239.6 9.8 %collective-permute-start.28 = (bf16[192,3584]{1,0:T(8,128)(2,1)S(1)}, bf16[192,3584]{1,0:T(8,128)(2,1)S(1)}, u32[]{:S(2)}, u32[]{:S(2)}) collective-permute-start(bf16[192,3584]{1,0:T(8,128)(2,1)S(1)} %get-tuple-element.144), channel_id=1, source_target_pairs={{0,1},{1,0},{2,3},{3,2},{4,5},{5,4},{6,7},{7,6},{8,9},{9,8},{10,11... | collective-permute-start | bytes 4128776 | tf_op jit(solution)/shard_map/ppermute | solution.py:338
  239.7 4.4 %collective-permute-start.31 = (f32[1792]{0:T(1024)S(1)}, f32[1792]{0:T(1024)S(1)}, u32[]{:S(2)}, u32[]{:S(2)}) collective-permute-start(f32[1792]{0:T(1024)S(1)} %add_reduce_fusion), channel_id=1, source_target_pairs={{0,8},{8,0},{16,24},{24,16},{1,9},{9,1},{17,25},{25,17},{2,10},{10... | collective-permute-start | bytes 21512 | tf_op jit(solution)/shard_map/ppermute | solution.py:447
  244.1 4.6 %collective-permute-start.32 = (f32[1792]{0:T(1024)S(1)}, f32[1792]{0:T(1024)S(1)}, u32[]{:S(2)}, u32[]{:S(2)}) collective-permute-start(f32[1792]{0:T(1024)S(1)} %add.112), channel_id=1, source_target_pairs={{0,16},{8,24},{16,0},{24,8},{1,17},{9,25},{17,1},{25,9},{2,18},{10... | collective-permute-start | bytes 21512 | tf_op jit(solution)/shard_map/ppermute | solution.py:451
  249.7 19.4 %collective-permute-start.30 = (bf16[96,3584]{1,0:T(8,128)(2,1)S(1)}, bf16[96,3584]{1,0:T(8,128)(2,1)S(1)}, u32[]{:S(2)}, u32[]{:S(2)}) collective-permute-start(bf16[96,3584]{1,0:T(8,128)(2,1)S(1)} %get-tuple-element.153), channel_id=1, source_target_pairs={{0,4},{1,5},{2,6},{3,7},{4,0},{5,1},{6,2},{7,3},{8,12},{9,13},{10,... | collective-permute-start | bytes 2064392 | tf_op jit(solution)/shard_map/ppermute | solution.py:338
  251.3 17.8 %collective-permute-start.29 = (bf16[96,3584]{1,0:T(8,128)(2,1)S(1)}, bf16[96,3584]{1,0:T(8,128)(2,1)S(1)}, u32[]{:S(2)}, u32[]{:S(2)}) collective-permute-start(bf16[96,3584]{1,0:T(8,128)(2,1)S(1)} %get-tuple-element.152), channel_id=1, source_target_pairs={{0,2},{1,3},{2,0},{3,1},{4,6},{5,7},{6,4},{7,5},{8,10},{9,11},{10,... | collective-permute-start | bytes 2064392 | tf_op jit(solution)/shard_map/ppermute | solution.py:338
  (12 other events, 12.7 us)
Sparse Core Ops, SparseCore 0:
  9.9 44.9 all-gather.2
  56.7 42.2 all-gather.4

commit v8 on v7

--- a/solution.py
+++ b/solution.py
@@ -51,7 +51,7 @@
     return pl.BlockSpec((rows, columns), lambda i, s: (s[0] ^ key, 0))
 
 
-def streamed(place, blocks, weight, pieces, dims, flops, write, out_shape):
+def streamed(place, blocks, weight, pieces, dims, flops, write, out_shape, shrink=1):
     axis, first, last = pieces
     size = weight.shape[axis] // UNITS
     count = last - first
@@ -109,8 +109,8 @@
     anywhere = pl.BlockSpec(memory_space=pl.ANY)
     return call(
         kernel,
-        flops,
-        moved,
+        flops // shrink,
+        moved // shrink,
         place,
         [*arrays, weight],
         (1,),
@@ -152,6 +152,7 @@
         2 * len(blocks) * rows * weight.size,
         write,
         [jax.ShapeDtypeStruct((rows, hidden), BF16)] * len(blocks),
+        64,
     )
 
 
@@ -297,18 +298,18 @@
     )
 
 
-def add_early(place, left, right):
-    def kernel(s, left_ref, right_ref, out):
-        out[...] = left_ref[...].astype(F32) + right_ref[...].astype(F32)
+def add_scaled(place, left, right, scale, *done):
+    def kernel(s, left_ref, right_ref, *refs):
+        refs[-1][...] = (left_ref[...].astype(F32) + right_ref[...].astype(F32)) * scale
 
     return call(
         kernel,
         left.size,
         8 * left.size,
         place,
-        [left, right],
+        [left, right, *done],
         (1,),
-        [whole(left.shape)] * 2,
+        [whole(left.shape)] * 2 + [pl.BlockSpec(memory_space=pl.ANY)] * len(done),
         whole(left.shape),
         jax.ShapeDtypeStruct(left.shape, F32),
     )
@@ -417,8 +418,9 @@
     compute_own("act", [0])
     first_send(1)
     end = total + steps - 1
+    gathered = len(others) + 2
     for slot in range(end):
-        if 3 <= slot + 1 < total:
+        if 2 < slot + 1 < total and slot + 1 != gathered - 1:
             first_send(slot + 1)
         late = slot == 2
         if late and slot >= steps - 1:
@@ -426,32 +428,32 @@
         for step in range(steps, 1, -1) if late else range(2, steps + 1):
             if 0 <= slot - step + 2 < total:
                 forward(slot - step + 2, step)
-            if step == 2 and slot == len(others):
-                compute_own("act", others)
         if slot == 1:
             compute_own("pre", others)
             first_send(2)
+        if slot == gathered - 3:
+            first_send(gathered - 1)
+            compute_own("act", others)
         if not late and slot >= steps - 1:
             finish(slot - steps + 1)
-        if slot == end - 4:
-            out_columns(0, 3)
         if slot == end - 3:
             first = tokens_of([0] + others[:-2], 0, UNITS)
         if slot == end - 2:
             arrived += deliver(exchange(first))
-            out_columns(3, UNITS - 3)
-    head = add_early(place, link(arrived[0]), arrived[1])
+            out_columns(0, UNITS)
+    levels = [1 << i for i in range(rows_of.bit_length() - 1)]
+    sums = link(functools.reduce(jnp.add, [sums[key] for key in sorted(sums)]))
+    for bit in levels[:-1]:
+        sums = sums + lax.ppermute(sums, "row", [(i, i ^ bit) for i in range(rows_of)])
+    head = add_scaled(place, link(arrived[0]), arrived[1], 1.0)
     chain.append(head)
-    levels = [1 << i for i in range(rows_of.bit_length() - 1)]
-    sums = link(functools.reduce(jnp.add, [sums[key] for key in sorted(sums)]).reshape(hidden))
-    sums = sums + lax.ppermute(sums, "row", [(i, i ^ levels[0]) for i in range(rows_of)])
+    sums = link(sums)
+    given = lax.ppermute(sums, "row", [(i, i ^ levels[-1]) for i in range(rows_of)])
+    chain.append(sums)
     last = exchange(tokens_of(others[-2:], 0, UNITS))
-    sums = link(sums)
-    for bit in levels[1:]:
-        sums = sums + lax.ppermute(sums, "row", [(i, i ^ bit) for i in range(rows_of)])
     arrived += deliver(last)
     in_rows(0, UNITS)
-    grad_bias = sums * (1.0 / rows_of)
+    grad_bias = add_scaled(place, sums, given, 1.0 / rows_of, held["in"]).reshape(hidden)
     grad_tokens = functools.reduce(jnp.add, [part.astype(F32) for part in arrived[2:]], head).astype(BF16)
     return (grad_tokens, held["in"], grad_bias, held["out"])
 

time: 278 us -> 272 us (0.978)
  starting transfers between devices: 58.8 us -> 63.3 us
  waiting for transfers between devices: 70.5 us -> 66.3 us
  local copies, waits for them, and re-layouts: 9.82 us -> 5.97 us
  Pallas kernels: 108 us -> 105 us
    ppermute x24, starting transfers between devices: 46.4 us -> 57.4 us  [send(): return lax.ppermute(value, 'row', pairs)]
    ppermute x24, waiting for transfers between devices: 61.8 us -> 56.1 us  [send(): return lax.ppermute(value, 'row', pairs)]
    unnamed x50 -> x46, local copies, waits for them, and re-layouts: 9.81 us -> 5.96 us
    pallas_call x18, Pallas kernels: 108 us -> 105 us  [call(): pl.pallas_call(kernel, grid_spec=pltpu.PrefetchScalarGridSpec(num_scalar_...]
where the time goes in v8:
time: 272 us; the launch traced here: 270 us
  Pallas kernels  105 us (39%)
  waiting for transfers between devices  66.3 us (24%)
  starting transfers between devices  63.3 us (23%)
  other arithmetic  15.1 us (6%)
  between operations  14.7 us (5%)
  local copies, waits for them, and re-layouts  5.97 us (2%)
    pallas_call x18, Pallas kernels, call(): pl.pallas_call(kernel, grid_spec=pltpu.PrefetchScalarGridSpec(num_scalar_...  105 us
    ppermute x24, starting transfers between devices, send(): return lax.ppermute(value, 'row', pairs)  57.4 us
    ppermute x24, waiting for transfers between devices, send(): return lax.ppermute(value, 'row', pairs)  56.1 us
    convert_element_type x18, other arithmetic, add_bf16(): return (left.astype(F32) + right.astype(F32)).astype(BF16)  13.3 us
    ppermute x7, waiting for transfers between devices, swap(): return lax.ppermute(value, 'col', [(i, i ^ bits) for i in range(cols_of)])  6.66 us
    unnamed x46, local copies, waits for them, and re-layouts  5.96 us
  transfers between devices with their start and end apart: 35, of which 14 were waited for; matrix products, arithmetic and copies ran while one was open for 5% of the time, Pallas kernels for 35%

profile of v8, /device:TPU:0, one launch (start us, length us, event | category | flops | bytes accessed | tf_op | source)
XLA Modules:
  0.0 270.4 jit_solution(17623727719268471939)
XLA Ops:
  8.5 2.0 collective-permute-done.refs_1_
  11.0 6.3 %shard_map.84 = bf16[192,1792]{1,0:T(8,128)(2,1)S(1)} custom-call(s32[2]{0:T(128)S(1)} %pad_add_fusion.s, bf16[96,3584]{1,0:T(8,128)(2,1)S(1)} %copy-done, bf16[96,3584]{1,0:T(8,128)(2,1)S(1)} %collective-permute-done.refs_1_, bf16[3584,1792]{1,0:T(8,128)(2,1)} %refs_1_.7), custom_call_target="tpu_custom_call" | custom-call | flops 38535168 | bytes 222208 | tf_op jit(solution)/shard_map/pallas_call | solution.py:30
  17.3 4.7 %collective-permute-start.1 = (bf16[192,1792]{1,0:T(8,128)(2,1)S(1)}, bf16[192,1792]{1,0:T(8,128)(2,1)S(1)}, u32[]{:S(2)}, u32[]{:S(2)}) collective-permute-start(bf16[192,1792]{1,0:T(8,128)(2,1)S(1)} %shard_map.84), channel_id=1, source_target_pairs={{0,8},{24,16},{1,9},{25,17},{2,10},{26,18},{3,11},{27,19},{4,12},{... | collective-permute-start | bytes 2064392 | tf_op jit(solution)/shard_map/ppermute | solution.py:336
  22.0 7.3 %shard_map.85 = bf16[192,1792]{1,0:T(8,128)(2,1)S(1)} custom-call(s32[2]{0:T(128)S(1)} %pad_add_fusion.s, bf16[96,3584]{1,0:T(8,128)(2,1)S(1)} %copy-done.1, bf16[96,3584]{1,0:T(8,128)(2,1)S(1)} %collective-permute-done.2.refs_1_, bf16[1792,3584]{1,0:T(8,128)(2,1)} %refs_1_.5), custom_call_target="tpu_custom_call" | custom-call | flops 38535168 | bytes 222208 | tf_op jit(solution)/shard_map/pallas_call | solution.py:30
  29.3 1.5 collective-permute-start.4
  30.8 6.9 %collective-permute-done.1 = bf16[192,1792]{1,0:T(8,128)(2,1)S(1)} collective-permute-done((bf16[192,1792]{1,0:T(8,128)(2,1)S(1)}, bf16[192,1792]{1,0:T(8,128)(2,1)S(1)}, u32[]{:S(2)}, u32[]{:S(2)}) %collective-permute-start.1) | collective-permute-done | bytes 688160 | tf_op jit(solution)/shard_map/ppermute | solution.py:336
  38.6 13.3 %collective-permute-done.4 = bf16[192,1792]{1,0:T(8,128)(2,1)S(1)} collective-permute-done((bf16[192,1792]{1,0:T(8,128)(2,1)S(1)}, bf16[192,1792]{1,0:T(8,128)(2,1)S(1)}, u32[]{:S(2)}, u32[]{:S(2)}) %collective-permute-start.4) | collective-permute-done | bytes 688160 | tf_op jit(solution)/shard_map/ppermute | solution.py:336
  53.1 1.4 collective-permute-start.7
  54.5 1.6 collective-permute-start.6
  56.1 13.4 %shard_map.86 = (bf16[192,1792]{1,0:T(8,128)(2,1)S(1)}, bf16[192,1792]{1,0:T(8,128)(2,1)}, bf16[192,1792]{1,0:T(8,128)(2,1)S(1)}) custom-call(s32[2]{0:T(128)S(1)} %pad_add_fusion.s, bf16[768,3584]{1,0:T(8,128)(2,1)} %all-gather.3.cloned.1.call-done.refs_0_.tok_ref, bf16[3584,1792]{1,0:T(8,128)(2,1)} %refs_1_.7), custom_call_target="tpu_custom_call" | custom-call | flops 115605504 | bytes 265216 | tf_op jit(solution)/shard_map/pallas_call | solution.py:30
  70.3 10.3 %collective-permute-start.5 = (bf16[192,1792]{1,0:T(8,128)(2,1)S(1)}, bf16[192,1792]{1,0:T(8,128)(2,1)S(1)}, u32[]{:S(2)}, u32[]{:S(2)}) collective-permute-start(bf16[192,1792]{1,0:T(8,128)(2,1)S(1)} %get-tuple-element.99), channel_id=1, source_target_pairs={{0,8},{24,16},{1,9},{25,17},{2,10},{26,18},{3,11},{27,19},{4,12},{... | collective-permute-start | bytes 2064392 | tf_op jit(solution)/shard_map/ppermute | solution.py:336
  82.6 1.8 shard_map.87
  84.4 2.2 collective-permute-start.8
  86.5 2.1 add_convert_fusion.17
  88.7 7.8 %collective-permute-done.5 = bf16[192,1792]{1,0:T(8,128)(2,1)S(1)} collective-permute-done((bf16[192,1792]{1,0:T(8,128)(2,1)S(1)}, bf16[192,1792]{1,0:T(8,128)(2,1)S(1)}, u32[]{:S(2)}, u32[]{:S(2)}) %collective-permute-start.5) | collective-permute-done | bytes 688160 | tf_op jit(solution)/shard_map/ppermute | solution.py:336
  96.6 1.5 collective-permute-start.11
  98.1 1.3 collective-permute-start.12
  99.4 12.7 %shard_map.88 = (bf16[192,1792]{1,0:T(8,128)(2,1)S(1)}, bf16[192,1792]{1,0:T(8,128)(2,1)S(1)}, bf16[192,1792]{1,0:T(8,128)(2,1)S(1)}) custom-call(s32[2]{0:T(128)S(1)} %pad_add_fusion.s, bf16[768,3584]{1,0:T(8,128)(2,1)} %all-gather.5.cloned.1.call-done.refs_0_.grad_ref, bf16[1792,3584]{1,0:T(8,128)(2,1)} %refs_1_.5), custom_call_target="tpu_custom_call" | custom-call | flops 115605504 | bytes 265216 | tf_op jit(solution)/shard_map/pallas_call | solution.py:30
  112.2 6.1 %collective-permute-start.10 = (bf16[192,1792]{1,0:T(8,128)(2,1)S(1)}, bf16[192,1792]{1,0:T(8,128)(2,1)S(1)}, u32[]{:S(2)}, u32[]{:S(2)}) collective-permute-start(bf16[192,1792]{1,0:T(8,128)(2,1)S(1)} %copy-done.7), channel_id=1, source_target_pairs={{0,8},{24,16},{1,9},{25,17},{2,10},{26,18},{3,11},{27,19},{4,12},{... | collective-permute-start | bytes 2064392 | tf_op jit(solution)/shard_map/ppermute | solution.py:336
  118.3 1.5 add_convert_fusion.15.refs_0_
  121.9 1.3 collective-permute-start.13
  123.2 2.5 shard_map.89
  125.7 4.6 %collective-permute-start.14 = (bf16[192,1792]{1,0:T(8,128)(2,1)S(1)}, bf16[192,1792]{1,0:T(8,128)(2,1)S(1)}, u32[]{:S(2)}, u32[]{:S(2)}) collective-permute-start(bf16[192,1792]{1,0:T(8,128)(2,1)S(1)} %get-tuple-element.117), channel_id=1, source_target_pairs={{0,8},{24,16},{1,9},{25,17},{2,10},{26,18},{3,11},{27,19},{4,12},{... | collective-permute-start | bytes 2064392 | tf_op jit(solution)/shard_map/ppermute | solution.py:336
  130.4 3.2 %collective-permute-done.10 = bf16[192,1792]{1,0:T(8,128)(2,1)S(1)} collective-permute-done((bf16[192,1792]{1,0:T(8,128)(2,1)S(1)}, bf16[192,1792]{1,0:T(8,128)(2,1)S(1)}, u32[]{:S(2)}, u32[]{:S(2)}) %collective-permute-start.10) | collective-permute-done | bytes 688160 | tf_op jit(solution)/shard_map/ppermute | solution.py:336
  134.4 2.1 add_convert_fusion.12
  137.8 1.7 collective-permute-done.13.refs_2_
  141.5 2.9 %shard_map.90 = (bf16[768,1792]{1,0:T(8,128)(2,1)S(1)}, f32[192,1792]{1,0:T(8,128)S(1)}) custom-call(s32[2]{0:T(128)S(1)} %pad_add_fusion.s, f32[1,1792]{1,0:T(1,128)S(1)} %reshape.14.bias_ref, bf16[192,1792]{1,0:T(8,128)(2,1)S(1)} %add_convert_fusion.16.refs_0_, bf16[192,1792]{1,0:T(8,128)(2,1)} %collective-permute-done.11.refs_1_, ...), custom_call_target="tpu_custom_call", output_to_operand_aliasing={{0}: (5, {})} | custom-call | flops 10321920 | bytes 4128768 | tf_op jit(solution)/shard_map/pallas_call | solution.py:30
  144.3 7.1 %collective-permute-start.15 = (bf16[192,1792]{1,0:T(8,128)(2,1)S(1)}, bf16[192,1792]{1,0:T(8,128)(2,1)}, u32[]{:S(2)}, u32[]{:S(2)}) collective-permute-start(bf16[192,1792]{1,0:T(8,128)(2,1)S(1)} %get-tuple-element.121), channel_id=1, source_target_pairs={{0,8},{24,16},{1,9},{25,17},{2,10},{26,18},{3,11},{27,19},{4,12},{... | collective-permute-start | bytes 2064392 | tf_op jit(solution)/shard_map/ppermute | solution.py:336
  152.5 1.3 collective-permute-start.21
  153.8 1.8 collective-permute-done.17.refs_2_
  155.7 2.9 %shard_map.91 = (bf16[768,1792]{1,0:T(8,128)(2,1)S(1)}, f32[192,1792]{1,0:T(8,128)S(1)}) custom-call(s32[2]{0:T(128)S(1)} %pad_add_fusion.s, f32[1,1792]{1,0:T(1,128)S(1)} %reshape.14.bias_ref, bf16[192,1792]{1,0:T(8,128)(2,1)S(1)} %add_convert_fusion.15.refs_0_, ...), custom_call_target="tpu_custom_call", output_to_operand_aliasing={{0}: (5, {})} | custom-call | flops 10321920 | bytes 4128768 | tf_op jit(solution)/shard_map/pallas_call | solution.py:30
  158.6 2.8 %collective-permute-start.19 = (bf16[192,1792]{1,0:T(8,128)(2,1)S(1)}, bf16[192,1792]{1,0:T(8,128)(2,1)S(1)}, u32[]{:S(2)}, u32[]{:S(2)}) collective-permute-start(bf16[192,1792]{1,0:T(8,128)(2,1)S(1)} %get-tuple-element.127), channel_id=1, source_target_pairs={{0,8},{24,16},{1,9},{25,17},{2,10},{26,18},{3,11},{27,19},{4,12},{... | collective-permute-start | bytes 2064392 | tf_op jit(solution)/shard_map/ppermute | solution.py:336
  161.4 4.0 %collective-permute-done.15 = bf16[192,1792]{1,0:T(8,128)(2,1)} collective-permute-done((bf16[192,1792]{1,0:T(8,128)(2,1)S(1)}, bf16[192,1792]{1,0:T(8,128)(2,1)}, u32[]{:S(2)}, u32[]{:S(2)}) %collective-permute-start.15) | collective-permute-done | bytes 688160 | tf_op jit(solution)/shard_map/ppermute | solution.py:336
  165.4 1.3 add_convert_fusion.9.refs_0_
  168.6 1.3 collective-permute-start.22
  170.4 1.8 shard_map.92
  172.1 2.5 collective-permute-done.19
  175.8 1.3 collective-permute-start.24
  177.1 14.4 %collective-permute-done.22.refs_2_ = bf16[192,1792]{1,0:T(8,128)(2,1)S(1)} collective-permute-done((bf16[192,1792]{1,0:T(8,128)(2,1)}, bf16[192,1792]{1,0:T(8,128)(2,1)S(1)}, u32[]{:S(2)}, u32[]{:S(2)}) %collective-permute-start.22) | collective-permute-done | bytes 688160 | tf_op jit(solution)/shard_map/ppermute | solution.py:336
  192.5 8.5 %shard_map.94 = (bf16[192,3584]{1,0:T(8,128)(2,1)S(1)}, bf16[192,3584]{1,0:T(8,128)(2,1)S(1)}) custom-call(s32[2]{0:T(128)S(1)} %pad_add_fusion.s, bf16[768,1792]{1,0:T(8,128)(2,1)S(1)} %get-tuple-element.124.refs_0_.refs_3_, bf16[3584,1792]{1,0:T(8,128)(2,1)} %refs_1_.7), custom_call_target="tpu_custom_call" | custom-call | flops 4932501504 | bytes 14221312 | tf_op jit(solution)/shard_map/pallas_call | solution.py:30
  203.4 1.3 collective-permute-start.26
  204.7 1.8 collective-permute-done.25
  206.9 1.8 collective-permute-start.27
  208.7 16.2 %shard_map.96 = f32[1792,3584]{1,0:T(8,128)} custom-call(s32[2]{0:T(128)S(1)} %pad_add_fusion.s, bf16[768,1792]{1,0:T(8,128)(2,1)S(1)} %get-tuple-element.134.act_ref, bf16[768,3584]{1,0:T(8,128)(2,1)} %all-gather.5.cloned.1.call-done.refs_0_.grad_ref), custom_call_target="tpu_custom_call" | custom-call | flops 9865003008 | bytes 33947648 | tf_op jit(solution)/shard_map/pallas_call | solution.py:30
  226.8 2.8 %collective-permute-done.28 = f32[1,1792]{1,0:T(1,128)S(1)} collective-permute-done((f32[1,1792]{1,0:T(1,128)S(1)}, f32[1,1792]{1,0:T(1,128)S(1)}, u32[]{:S(2)}, u32[]{:S(2)}) %collective-permute-start.28) | collective-permute-done | bytes 7200 | tf_op jit(solution)/shard_map/ppermute | solution.py:447
  230.3 8.5 %shard_map.99 = (bf16[192,3584]{1,0:T(8,128)(2,1)S(1)}, bf16[192,3584]{1,0:T(8,128)(2,1)S(1)}) custom-call(s32[2]{0:T(128)S(1)} %pad_add_fusion.s, bf16[768,1792]{1,0:T(8,128)(2,1)S(1)} %get-tuple-element.149.refs_0_.grad_ref, bf16[3584,1792]{1,0:T(8,128)(2,1)} %refs_1_.7), custom_call_target="tpu_custom_call" | custom-call | flops 4932501504 | bytes 14221312 | tf_op jit(solution)/shard_map/pallas_call | solution.py:30
  239.1 2.9 %collective-permute-done.29 = bf16[192,3584]{1,0:T(8,128)(2,1)S(1)} collective-permute-done((bf16[192,3584]{1,0:T(8,128)(2,1)S(1)}, bf16[192,3584]{1,0:T(8,128)(2,1)S(1)}, u32[]{:S(2)}, u32[]{:S(2)}) %collective-permute-start.29) | collective-permute-done | bytes 1376288 | tf_op jit(solution)/shard_map/ppermute | solution.py:339
  244.9 16.4 %shard_map.100.refs_0_ = f32[3584,1792]{1,0:T(8,128)} custom-call(s32[2]{0:T(128)S(1)} %pad_add_fusion.s, bf16[768,3584]{1,0:T(8,128)(2,1)} %all-gather.3.cloned.1.call-done.refs_0_.tok_ref, bf16[768,1792]{1,0:T(8,128)(2,1)S(1)} %get-tuple-element.149.refs_0_.grad_ref), custom_call_target="tpu_custom_call" | custom-call | flops 9865003008 | bytes 33947648 | tf_op jit(solution)/shard_map/pallas_call | solution.py:30
  (112 shorter events, 29.5 us)
Async XLA Ops:
  7.2 3.9 %copy-start = (bf16[96,3584]{1,0:T(8,128)(2,1)S(1)}, bf16[96,3584]{1,0:T(8,128)(2,1)}, u32[]{:S(2)}) copy-start(bf16[96,3584]{1,0:T(8,128)(2,1)} %refs_0_.1) | copy-start | bytes 2064388
  7.2 48.9 %all-gather.3.cloned.1.call-start = ((), (), s32[]{:S(2)}) async-start(), calls=%async_computation | async-start | bytes 6193152 | tf_op jit(solution)/shard_map/all_gather | solution.py:414
  7.9 91.5 %all-gather.5.cloned.1.call-start = ((), (), s32[]{:S(2)}) async-start(), calls=%async_computation.1 | async-start | bytes 6193152 | tf_op jit(solution)/shard_map/all_gather | solution.py:415
  8.0 2.5 collective-permute-start
  10.5 11.5 %collective-permute-start.2 = (bf16[96,3584]{1,0:T(8,128)(2,1)S(1)}, bf16[96,3584]{1,0:T(8,128)(2,1)S(1)}, u32[]{:S(2)}, u32[]{:S(2)}) collective-permute-start(bf16[96,3584]{1,0:T(8,128)(2,1)S(1)} %copy-done.1), channel_id=1, source_target_pairs={{0,1},{1,0},{2,3},{3,2},{4,5},{5,4},{6,7},{7,6},{8,9},{9,8},{10,11... | collective-permute-start | bytes 2064392 | tf_op jit(solution)/shard_map/ppermute | solution.py:339
  17.3 20.4 %collective-permute-start.1 = (bf16[192,1792]{1,0:T(8,128)(2,1)S(1)}, bf16[192,1792]{1,0:T(8,128)(2,1)S(1)}, u32[]{:S(2)}, u32[]{:S(2)}) collective-permute-start(bf16[192,1792]{1,0:T(8,128)(2,1)S(1)} %shard_map.84), channel_id=1, source_target_pairs={{0,8},{24,16},{1,9},{25,17},{2,10},{26,18},{3,11},{27,19},{4,12},{... | collective-permute-start | bytes 2064392 | tf_op jit(solution)/shard_map/ppermute | solution.py:336
  29.3 22.6 %collective-permute-start.4 = (bf16[192,1792]{1,0:T(8,128)(2,1)S(1)}, bf16[192,1792]{1,0:T(8,128)(2,1)S(1)}, u32[]{:S(2)}, u32[]{:S(2)}) collective-permute-start(bf16[192,1792]{1,0:T(8,128)(2,1)S(1)} %shard_map.85), channel_id=1, source_target_pairs={{0,8},{24,16},{1,9},{25,17},{2,10},{26,18},{3,11},{27,19},{4,12},{... | collective-permute-start | bytes 2064392 | tf_op jit(solution)/shard_map/ppermute | solution.py:336
  37.8 15.2 %copy-start.2 = (bf16[192,1792]{1,0:T(8,128)(2,1)}, bf16[192,1792]{1,0:T(8,128)(2,1)S(1)}, u32[]{:S(2)}) copy-start(bf16[192,1792]{1,0:T(8,128)(2,1)S(1)} %add_convert_fusion.20.refs_0_) | copy-start | bytes 2064388
  37.8 15.0 %collective-permute-start.3 = (bf16[192,1792]{1,0:T(8,128)(2,1)S(1)}, bf16[192,1792]{1,0:T(8,128)(2,1)S(1)}, u32[]{:S(2)}, u32[]{:S(2)}) collective-permute-start(bf16[192,1792]{1,0:T(8,128)(2,1)S(1)} %add_convert_fusion.20.refs_0_), channel_id=1, source_target_pairs={{8,16},{16,8},{9,17},{17,9},{10,18},{18,10},{11,19},{19,11},{12,20... | collective-permute-start | bytes 2064392 | tf_op jit(solution)/shard_map/ppermute | solution.py:336
  53.1 27.5 %copy-start.22 = (f32[1792]{0:T(1024)S(1)}, f32[1792]{0:T(1024)}, u32[]{:S(2)}) copy-start(f32[1792]{0:T(1024)} %param.7) | copy-start | bytes 21508
  53.1 27.5 %collective-permute-start.7 = (bf16[192,1792]{1,0:T(8,128)(2,1)S(1)}, bf16[192,1792]{1,0:T(8,128)(2,1)S(1)}, u32[]{:S(2)}, u32[]{:S(2)}) collective-permute-start(bf16[192,1792]{1,0:T(8,128)(2,1)S(1)} %add_convert_fusion.18), channel_id=1, source_target_pairs={{16,24},{8,0},{17,25},{9,1},{18,26},{10,2},{19,27},{11,3},{20,28},... | collective-permute-start | bytes 2064392 | tf_op jit(solution)/shard_map/ppermute | solution.py:336
  54.5 32.0 %collective-permute-start.6 = (bf16[192,1792]{1,0:T(8,128)(2,1)}, bf16[192,1792]{1,0:T(8,128)(2,1)}, u32[]{:S(2)}, u32[]{:S(2)}) collective-permute-start(bf16[192,1792]{1,0:T(8,128)(2,1)} %add_convert_fusion.19.refs_0_), channel_id=1, source_target_pairs={{8,16},{16,8},{9,17},{17,9},{10,18},{18,10},{11,19},{19,11},{12,20... | collective-permute-start | bytes 2064392 | tf_op jit(solution)/shard_map/ppermute | solution.py:336
  56.1 25.4 %copy-start.3 = (bf16[192,1792]{1,0:T(8,128)(2,1)S(1)}, bf16[192,1792]{1,0:T(8,128)(2,1)}, u32[]{:S(2)}) copy-start(bf16[192,1792]{1,0:T(8,128)(2,1)} %copy-done.2) | copy-start | bytes 2064388
  56.1 25.4 %copy-start.5 = (bf16[192,1792]{1,0:T(8,128)(2,1)S(1)}, bf16[192,1792]{1,0:T(8,128)(2,1)}, u32[]{:S(2)}) copy-start(bf16[192,1792]{1,0:T(8,128)(2,1)} %copy-done.4) | copy-start | bytes 2064388
  70.3 26.1 %copy-start.8 = (bf16[192,1792]{1,0:T(8,128)(2,1)}, bf16[192,1792]{1,0:T(8,128)(2,1)S(1)}, u32[]{:S(2)}) copy-start(bf16[192,1792]{1,0:T(8,128)(2,1)S(1)} %get-tuple-element.99) | copy-start | bytes 2064388
  70.3 26.1 %collective-permute-start.5 = (bf16[192,1792]{1,0:T(8,128)(2,1)S(1)}, bf16[192,1792]{1,0:T(8,128)(2,1)S(1)}, u32[]{:S(2)}, u32[]{:S(2)}) collective-permute-start(bf16[192,1792]{1,0:T(8,128)(2,1)S(1)} %get-tuple-element.99), channel_id=1, source_target_pairs={{0,8},{24,16},{1,9},{25,17},{2,10},{26,18},{3,11},{27,19},{4,12},{... | collective-permute-start | bytes 2064392 | tf_op jit(solution)/shard_map/ppermute | solution.py:336
  84.4 12.2 %copy-start.16 = (f32[192,1792]{1,0:T(8,128)}, f32[192,1792]{1,0:T(8,128)S(1)}, u32[]{:S(2)}) copy-start(f32[192,1792]{1,0:T(8,128)S(1)} %get-tuple-element.98.slope_ref) | copy-start | bytes 4128772
  84.4 33.9 %collective-permute-start.8 = (bf16[192,1792]{1,0:T(8,128)(2,1)}, bf16[192,1792]{1,0:T(8,128)(2,1)}, u32[]{:S(2)}, u32[]{:S(2)}) collective-permute-start(bf16[192,1792]{1,0:T(8,128)(2,1)} %get-tuple-element.103), channel_id=1, source_target_pairs={{0,8},{24,16},{1,9},{25,17},{2,10},{26,18},{3,11},{27,19},{4,12},{... | collective-permute-start | bytes 2064392 | tf_op jit(solution)/shard_map/ppermute | solution.py:336
  96.6 24.0 %collective-permute-start.11 = (bf16[192,1792]{1,0:T(8,128)(2,1)S(1)}, bf16[192,1792]{1,0:T(8,128)(2,1)}, u32[]{:S(2)}, u32[]{:S(2)}) collective-permute-start(bf16[192,1792]{1,0:T(8,128)(2,1)S(1)} %add_convert_fusion.16.refs_0_), channel_id=1, source_target_pairs={{8,16},{16,8},{9,17},{17,9},{10,18},{18,10},{11,19},{19,11},{12,20... | collective-permute-start | bytes 2064392 | tf_op jit(solution)/shard_map/ppermute | solution.py:336
  98.1 25.1 %collective-permute-start.12 = (bf16[192,1792]{1,0:T(8,128)(2,1)}, bf16[192,1792]{1,0:T(8,128)(2,1)}, u32[]{:S(2)}, u32[]{:S(2)}) collective-permute-start(bf16[192,1792]{1,0:T(8,128)(2,1)} %add_convert_fusion.17), channel_id=1, source_target_pairs={{16,24},{8,0},{17,25},{9,1},{18,26},{10,2},{19,27},{11,3},{20,28},... | collective-permute-start | bytes 2064392 | tf_op jit(solution)/shard_map/ppermute | solution.py:336
  99.4 12.8 %copy-start.7 = (bf16[192,1792]{1,0:T(8,128)(2,1)S(1)}, bf16[192,1792]{1,0:T(8,128)(2,1)}, u32[]{:S(2)}) copy-start(bf16[192,1792]{1,0:T(8,128)(2,1)} %copy-done.6) | copy-start | bytes 2064388
  112.2 8.5 %copy-start.9 = (bf16[192,1792]{1,0:T(8,128)(2,1)S(1)}, bf16[192,1792]{1,0:T(8,128)(2,1)}, u32[]{:S(2)}) copy-start(bf16[192,1792]{1,0:T(8,128)(2,1)} %copy-done.8) | copy-start | bytes 2064388
  112.2 21.4 %collective-permute-start.10 = (bf16[192,1792]{1,0:T(8,128)(2,1)S(1)}, bf16[192,1792]{1,0:T(8,128)(2,1)S(1)}, u32[]{:S(2)}, u32[]{:S(2)}) collective-permute-start(bf16[192,1792]{1,0:T(8,128)(2,1)S(1)} %copy-done.7), channel_id=1, source_target_pairs={{0,8},{24,16},{1,9},{25,17},{2,10},{26,18},{3,11},{27,19},{4,12},{... | collective-permute-start | bytes 2064392 | tf_op jit(solution)/shard_map/ppermute | solution.py:336
  119.8 14.7 %collective-permute-start.9 = (bf16[192,1792]{1,0:T(8,128)(2,1)S(1)}, bf16[192,1792]{1,0:T(8,128)(2,1)S(1)}, u32[]{:S(2)}, u32[]{:S(2)}) collective-permute-start(bf16[192,1792]{1,0:T(8,128)(2,1)S(1)} %add_convert_fusion.15.refs_0_), channel_id=1, source_target_pairs={{8,16},{16,8},{9,17},{17,9},{10,18},{18,10},{11,19},{19,11},{12,20... | collective-permute-start | bytes 2064392 | tf_op jit(solution)/shard_map/ppermute | solution.py:336
  121.9 17.6 %collective-permute-start.13 = (bf16[192,1792]{1,0:T(8,128)(2,1)S(1)}, bf16[192,1792]{1,0:T(8,128)(2,1)S(1)}, u32[]{:S(2)}, u32[]{:S(2)}) collective-permute-start(bf16[192,1792]{1,0:T(8,128)(2,1)S(1)} %add_convert_fusion.14), channel_id=1, source_target_pairs={{16,24},{8,0},{17,25},{9,1},{18,26},{10,2},{19,27},{11,3},{20,28},... | collective-permute-start | bytes 2064392 | tf_op jit(solution)/shard_map/ppermute | solution.py:336
  125.7 25.7 %collective-permute-start.14 = (bf16[192,1792]{1,0:T(8,128)(2,1)S(1)}, bf16[192,1792]{1,0:T(8,128)(2,1)S(1)}, u32[]{:S(2)}, u32[]{:S(2)}) collective-permute-start(bf16[192,1792]{1,0:T(8,128)(2,1)S(1)} %get-tuple-element.117), channel_id=1, source_target_pairs={{0,8},{24,16},{1,9},{25,17},{2,10},{26,18},{3,11},{27,19},{4,12},{... | collective-permute-start | bytes 2064392 | tf_op jit(solution)/shard_map/ppermute | solution.py:336
  133.7 18.6 %collective-permute-start.16 = (bf16[192,1792]{1,0:T(8,128)(2,1)S(1)}, bf16[192,1792]{1,0:T(8,128)(2,1)S(1)}, u32[]{:S(2)}, u32[]{:S(2)}) collective-permute-start(bf16[192,1792]{1,0:T(8,128)(2,1)S(1)} %add_convert_fusion.13.refs_0_), channel_id=1, source_target_pairs={{8,16},{16,8},{9,17},{17,9},{10,18},{18,10},{11,19},{19,11},{12,20... | collective-permute-start | bytes 2064392 | tf_op jit(solution)/shard_map/ppermute | solution.py:336
  136.6 19.1 %collective-permute-start.17 = (bf16[192,1792]{1,0:T(8,128)(2,1)}, bf16[192,1792]{1,0:T(8,128)(2,1)}, u32[]{:S(2)}, u32[]{:S(2)}) collective-permute-start(bf16[192,1792]{1,0:T(8,128)(2,1)} %add_convert_fusion.12), channel_id=1, source_target_pairs={{16,24},{8,0},{17,25},{9,1},{18,26},{10,2},{19,27},{11,3},{20,28},... | collective-permute-start | bytes 2064392 | tf_op jit(solution)/shard_map/ppermute | solution.py:336
  144.3 8.2 %copy-start.10 = (f32[192,1792]{1,0:T(8,128)}, f32[192,1792]{1,0:T(8,128)S(1)}, u32[]{:S(2)}) copy-start(f32[192,1792]{1,0:T(8,128)S(1)} %get-tuple-element.105.slope_ref) | copy-start | bytes 4128772
  144.3 21.1 %collective-permute-start.15 = (bf16[192,1792]{1,0:T(8,128)(2,1)S(1)}, bf16[192,1792]{1,0:T(8,128)(2,1)}, u32[]{:S(2)}, u32[]{:S(2)}) collective-permute-start(bf16[192,1792]{1,0:T(8,128)(2,1)S(1)} %get-tuple-element.121), channel_id=1, source_target_pairs={{0,8},{24,16},{1,9},{25,17},{2,10},{26,18},{3,11},{27,19},{4,12},{... | collective-permute-start | bytes 2064392 | tf_op jit(solution)/shard_map/ppermute | solution.py:336
  151.6 16.0 %collective-permute-start.20 = (bf16[192,1792]{1,0:T(8,128)(2,1)S(1)}, bf16[192,1792]{1,0:T(8,128)(2,1)S(1)}, u32[]{:S(2)}, u32[]{:S(2)}) collective-permute-start(bf16[192,1792]{1,0:T(8,128)(2,1)S(1)} %add_convert_fusion.11.refs_0_), channel_id=1, source_target_pairs={{8,16},{16,8},{9,17},{17,9},{10,18},{18,10},{11,19},{19,11},{12,20... | collective-permute-start | bytes 2064392 | tf_op jit(solution)/shard_map/ppermute | solution.py:336
  152.5 17.8 %collective-permute-start.21 = (bf16[192,1792]{1,0:T(8,128)(2,1)S(1)}, bf16[192,1792]{1,0:T(8,128)(2,1)S(1)}, u32[]{:S(2)}, u32[]{:S(2)}) collective-permute-start(bf16[192,1792]{1,0:T(8,128)(2,1)S(1)} %add_convert_fusion.10), channel_id=1, source_target_pairs={{16,24},{8,0},{17,25},{9,1},{18,26},{10,2},{19,27},{11,3},{20,28},... | collective-permute-start | bytes 2064392 | tf_op jit(solution)/shard_map/ppermute | solution.py:336
  158.5 10.1 %copy-start.14 = (f32[192,1792]{1,0:T(8,128)}, f32[192,1792]{1,0:T(8,128)S(1)}, u32[]{:S(2)}) copy-start(f32[192,1792]{1,0:T(8,128)S(1)} %get-tuple-element.126.slope_ref) | copy-start | bytes 4128772
  158.6 16.1 %collective-permute-start.19 = (bf16[192,1792]{1,0:T(8,128)(2,1)S(1)}, bf16[192,1792]{1,0:T(8,128)(2,1)S(1)}, u32[]{:S(2)}, u32[]{:S(2)}) collective-permute-start(bf16[192,1792]{1,0:T(8,128)(2,1)S(1)} %get-tuple-element.127), channel_id=1, source_target_pairs={{0,8},{24,16},{1,9},{25,17},{2,10},{26,18},{3,11},{27,19},{4,12},{... | collective-permute-start | bytes 2064392 | tf_op jit(solution)/shard_map/ppermute | solution.py:336
  166.7 8.9 %collective-permute-start.18 = (bf16[192,1792]{1,0:T(8,128)(2,1)S(1)}, bf16[192,1792]{1,0:T(8,128)(2,1)S(1)}, u32[]{:S(2)}, u32[]{:S(2)}) collective-permute-start(bf16[192,1792]{1,0:T(8,128)(2,1)S(1)} %add_convert_fusion.9.refs_0_), channel_id=1, source_target_pairs={{8,16},{16,8},{9,17},{17,9},{10,18},{18,10},{11,19},{19,11},{12,20... | collective-permute-start | bytes 2064392 | tf_op jit(solution)/shard_map/ppermute | solution.py:336
  168.6 22.9 %collective-permute-start.22 = (bf16[192,1792]{1,0:T(8,128)(2,1)}, bf16[192,1792]{1,0:T(8,128)(2,1)S(1)}, u32[]{:S(2)}, u32[]{:S(2)}) collective-permute-start(bf16[192,1792]{1,0:T(8,128)(2,1)} %add_convert_fusion.8), channel_id=1, source_target_pairs={{16,24},{8,0},{17,25},{9,1},{18,26},{10,2},{19,27},{11,3},{20,28},... | collective-permute-start | bytes 2064392 | tf_op jit(solution)/shard_map/ppermute | solution.py:336
  174.8 16.8 %copy-start.11 = (f32[192,1792]{1,0:T(8,128)S(1)}, f32[192,1792]{1,0:T(8,128)}, u32[]{:S(2)}) copy-start(f32[192,1792]{1,0:T(8,128)} %copy-done.10) | copy-start | bytes 4128772
  174.8 26.2 %collective-permute-start.23 = (bf16[192,1792]{1,0:T(8,128)(2,1)S(1)}, bf16[192,1792]{1,0:T(8,128)(2,1)S(1)}, u32[]{:S(2)}, u32[]{:S(2)}) collective-permute-start(bf16[192,1792]{1,0:T(8,128)(2,1)S(1)} %add_convert_fusion.7.refs_0_), channel_id=1, source_target_pairs={{8,16},{16,8},{9,17},{17,9},{10,18},{18,10},{11,19},{19,11},{12,20... | collective-permute-start | bytes 2064392 | tf_op jit(solution)/shard_map/ppermute | solution.py:336
  175.8 25.4 %collective-permute-start.24 = (bf16[192,1792]{1,0:T(8,128)(2,1)S(1)}, bf16[192,1792]{1,0:T(8,128)(2,1)S(1)}, u32[]{:S(2)}, u32[]{:S(2)}) collective-permute-start(bf16[192,1792]{1,0:T(8,128)(2,1)S(1)} %add_convert_fusion.6), channel_id=1, source_target_pairs={{16,24},{8,0},{17,25},{9,1},{18,26},{10,2},{19,27},{11,3},{20,28},... | collective-permute-start | bytes 2064392 | tf_op jit(solution)/shard_map/ppermute | solution.py:336
  203.3 3.2 %collective-permute-start.25 = (bf16[192,3584]{1,0:T(8,128)(2,1)S(1)}, bf16[192,3584]{1,0:T(8,128)(2,1)S(1)}, u32[]{:S(2)}, u32[]{:S(2)}) collective-permute-start(bf16[192,3584]{1,0:T(8,128)(2,1)S(1)} %get-tuple-element.132), channel_id=1, source_target_pairs={{0,1},{1,0},{2,3},{3,2},{4,5},{5,4},{6,7},{7,6},{8,9},{9,8},{10,11... | collective-permute-start | bytes 4128776 | tf_op jit(solution)/shard_map/ppermute | solution.py:339
  203.4 21.5 %collective-permute-start.26 = (bf16[192,1792]{1,0:T(8,128)(2,1)S(1)}, bf16[192,1792]{1,0:T(8,128)(2,1)S(1)}, u32[]{:S(2)}, u32[]{:S(2)}) collective-permute-start(bf16[192,1792]{1,0:T(8,128)(2,1)S(1)} %add_convert_fusion.5), channel_id=1, source_target_pairs={{16,24},{8,0},{17,25},{9,1},{18,26},{10,2},{19,27},{11,3},{20,28},... | collective-permute-start | bytes 2064392 | tf_op jit(solution)/shard_map/ppermute | solution.py:336
  206.9 18.0 %copy-start.13 = (f32[192,1792]{1,0:T(8,128)S(1)}, f32[192,1792]{1,0:T(8,128)}, u32[]{:S(2)}) copy-start(f32[192,1792]{1,0:T(8,128)} %copy-done.12) | copy-start | bytes 4128772
  206.9 22.7 %collective-permute-start.27 = (bf16[96,3584]{1,0:T(8,128)(2,1)S(1)}, bf16[96,3584]{1,0:T(8,128)(2,1)S(1)}, u32[]{:S(2)}, u32[]{:S(2)}) collective-permute-start(bf16[96,3584]{1,0:T(8,128)(2,1)S(1)} %get-tuple-element.153), channel_id=1, source_target_pairs={{0,6},{1,7},{2,4},{3,5},{4,2},{5,3},{6,0},{7,1},{8,14},{9,15},{10,... | collective-permute-start | bytes 2064392 | tf_op jit(solution)/shard_map/ppermute | solution.py:339
  225.9 3.7 %collective-permute-start.28 = (f32[1,1792]{1,0:T(1,128)S(1)}, f32[1,1792]{1,0:T(1,128)S(1)}, u32[]{:S(2)}, u32[]{:S(2)}) collective-permute-start(f32[1,1792]{1,0:T(1,128)S(1)} %add_add_fusion), channel_id=1, source_target_pairs={{0,8},{8,0},{16,24},{24,16},{1,9},{9,1},{17,25},{25,17},{2,10},{10... | collective-permute-start | bytes 21512 | tf_op jit(solution)/shard_map/ppermute | solution.py:447
  238.8 3.2 %collective-permute-start.29 = (bf16[192,3584]{1,0:T(8,128)(2,1)S(1)}, bf16[192,3584]{1,0:T(8,128)(2,1)S(1)}, u32[]{:S(2)}, u32[]{:S(2)}) collective-permute-start(bf16[192,3584]{1,0:T(8,128)(2,1)S(1)} %get-tuple-element.148), channel_id=1, source_target_pairs={{0,1},{1,0},{2,3},{3,2},{4,5},{5,4},{6,7},{7,6},{8,9},{9,8},{10,11... | collective-permute-start | bytes 4128776 | tf_op jit(solution)/shard_map/ppermute | solution.py:339
  238.9 22.4 %collective-permute-start.32 = (f32[1,1792]{1,0:T(1,128)S(1)}, f32[1,1792]{1,0:T(1,128)S(1)}, u32[]{:S(2)}, u32[]{:S(2)}) collective-permute-start(f32[1,1792]{1,0:T(1,128)S(1)} %add.105.left_ref), channel_id=1, source_target_pairs={{0,16},{8,24},{16,0},{24,8},{1,17},{9,25},{17,1},{25,9},{2,18},{10... | collective-permute-start | bytes 21512 | tf_op jit(solution)/shard_map/ppermute | solution.py:451
  243.2 19.3 %collective-permute-start.31 = (bf16[96,3584]{1,0:T(8,128)(2,1)}, bf16[96,3584]{1,0:T(8,128)(2,1)S(1)}, u32[]{:S(2)}, u32[]{:S(2)}) collective-permute-start(bf16[96,3584]{1,0:T(8,128)(2,1)} %get-tuple-element.151), channel_id=1, source_target_pairs={{0,4},{1,5},{2,6},{3,7},{4,0},{5,1},{6,2},{7,3},{8,12},{9,13},{10,... | collective-permute-start | bytes 2064392 | tf_op jit(solution)/shard_map/ppermute | solution.py:339
  244.3 18.1 %collective-permute-start.30 = (bf16[96,3584]{1,0:T(8,128)(2,1)S(1)}, bf16[96,3584]{1,0:T(8,128)(2,1)S(1)}, u32[]{:S(2)}, u32[]{:S(2)}) collective-permute-start(bf16[96,3584]{1,0:T(8,128)(2,1)S(1)} %get-tuple-element.150), channel_id=1, source_target_pairs={{0,2},{1,3},{2,0},{3,1},{4,6},{5,7},{6,4},{7,5},{8,10},{9,11},{10,... | collective-permute-start | bytes 2064392 | tf_op jit(solution)/shard_map/ppermute | solution.py:339
  (10 other events, 18.2 us)
Sparse Core Ops, SparseCore 0:
  9.9 44.9 all-gather.2
  56.7 42.2 all-gather.4

commit v9 on v8

--- a/solution.py
+++ b/solution.py
@@ -418,23 +418,20 @@
     compute_own("act", [0])
     first_send(1)
     end = total + steps - 1
-    gathered = len(others) + 2
     for slot in range(end):
-        if 2 < slot + 1 < total and slot + 1 != gathered - 1:
+        if slot > 1 and slot + 1 < total:
             first_send(slot + 1)
-        late = slot == 2
-        if late and slot >= steps - 1:
-            finish(slot - steps + 1)
-        for step in range(steps, 1, -1) if late else range(2, steps + 1):
+        if slot == 1:
+            compute_own("pre", others[:1])
+            first_send(2)
+        for step in range(2, steps + 1):
             if 0 <= slot - step + 2 < total:
                 forward(slot - step + 2, step)
+            if step == 2 and slot == len(others):
+                compute_own("act", others)
         if slot == 1:
-            compute_own("pre", others)
-            first_send(2)
-        if slot == gathered - 3:
-            first_send(gathered - 1)
-            compute_own("act", others)
-        if not late and slot >= steps - 1:
+            compute_own("pre", others[1:])
+        if slot >= steps - 1:
             finish(slot - steps + 1)
         if slot == end - 3:
             first = tokens_of([0] + others[:-2], 0, UNITS)
@@ -447,10 +444,9 @@
         sums = sums + lax.ppermute(sums, "row", [(i, i ^ bit) for i in range(rows_of)])
     head = add_scaled(place, link(arrived[0]), arrived[1], 1.0)
     chain.append(head)
+    last = exchange(tokens_of(others[-2:], 0, UNITS))
     sums = link(sums)
     given = lax.ppermute(sums, "row", [(i, i ^ levels[-1]) for i in range(rows_of)])
-    chain.append(sums)
-    last = exchange(tokens_of(others[-2:], 0, UNITS))
     arrived += deliver(last)
     in_rows(0, UNITS)
     grad_bias = add_scaled(place, sums, given, 1.0 / rows_of, held["in"]).reshape(hidden)

time: 272 us -> 266 us (0.978)
  starting transfers between devices: 63.3 us -> 56.1 us
  Pallas kernels: 105 us -> 109 us
  local copies, waits for them, and re-layouts: 5.97 us -> 2.76 us
    all_gather x1, waiting for transfers between devices: 0.01 us -> 16.3 us  [local(): held['pre'] = lax.all_gather(tokens, 'col', axis=0, tiled=True)]
    ppermute x24, waiting for transfers between devices: 56.1 us -> 41.4 us  [send(): return lax.ppermute(value, 'row', pairs)]
    ppermute x24, starting transfers between devices: 57.4 us -> 49.5 us  [send(): return lax.ppermute(value, 'row', pairs)]
    pallas_call x18 -> x19, Pallas kernels: 105 us -> 109 us  [call(): pl.pallas_call(kernel, grid_spec=pltpu.PrefetchScalarGridSpec(num_scalar_...]
    unnamed x46 -> x44, local copies, waits for them, and re-layouts: 5.96 us -> 2.75 us
    ppermute x7, waiting for transfers between devices: 6.66 us -> 3.81 us  [swap(): return lax.ppermute(value, 'col', [(i, i ^ bits) for i in range(cols_of)])]
  transfers between devices with their start and end apart: 35 -> 35, of which waited for: 14 -> 11; matrix products, arithmetic and copies ran while one was open for 5% -> 6% of each run, Pallas kernels for 35% -> 37%
where the time goes in v9:
time: 266 us; the launch traced here: 264 us
  Pallas kernels  109 us (41%)
  waiting for transfers between devices  65 us (24%)
  starting transfers between devices  56.1 us (21%)
  other arithmetic  17.2 us (6%)
  between operations  14.8 us (6%)
  local copies, waits for them, and re-layouts  2.76 us (1%)
    pallas_call x19, Pallas kernels, call(): pl.pallas_call(kernel, grid_spec=pltpu.PrefetchScalarGridSpec(num_scalar_...  109 us
    ppermute x24, starting transfers between devices, send(): return lax.ppermute(value, 'row', pairs)  49.5 us
    ppermute x24, waiting for transfers between devices, send(): return lax.ppermute(value, 'row', pairs)  41.4 us
    all_gather x1, waiting for transfers between devices, local(): held['pre'] = lax.all_gather(tokens, 'col', axis=0, tiled=True)  16.3 us
    convert_element_type x18, other arithmetic, add_bf16(): return (left.astype(F32) + right.astype(F32)).astype(BF16)  15.4 us
  transfers between devices with their start and end apart: 35, of which 11 were waited for; matrix products, arithmetic and copies ran while one was open for 6% of the time, Pallas kernels for 37%

profile of v9, /device:TPU:0, one launch (start us, length us, event | category | flops | bytes accessed | tf_op | source)
XLA Modules:
  0.0 264.3 jit_solution(1833589462887814706)
XLA Ops:
  8.5 2.0 collective-permute-done.refs_1_
  11.0 6.3 %shard_map.84 = bf16[192,1792]{1,0:T(8,128)(2,1)S(1)} custom-call(s32[2]{0:T(128)S(1)} %pad_add_fusion.s, bf16[96,3584]{1,0:T(8,128)(2,1)S(1)} %copy-done.1, bf16[96,3584]{1,0:T(8,128)(2,1)S(1)} %collective-permute-done.refs_1_, bf16[3584,1792]{1,0:T(8,128)(2,1)} %refs_1_.9), custom_call_target="tpu_custom_call" | custom-call | flops 38535168 | bytes 222208 | tf_op jit(solution)/shard_map/pallas_call | solution.py:30
  17.3 4.7 %collective-permute-start.1 = (bf16[192,1792]{1,0:T(8,128)(2,1)S(1)}, bf16[192,1792]{1,0:T(8,128)(2,1)S(1)}, u32[]{:S(2)}, u32[]{:S(2)}) collective-permute-start(bf16[192,1792]{1,0:T(8,128)(2,1)S(1)} %shard_map.84), channel_id=1, source_target_pairs={{0,8},{24,16},{1,9},{25,17},{2,10},{26,18},{3,11},{27,19},{4,12},{... | collective-permute-start | bytes 2064392 | tf_op jit(solution)/shard_map/ppermute | solution.py:336
  22.0 7.3 %shard_map.85 = bf16[192,1792]{1,0:T(8,128)(2,1)S(1)} custom-call(s32[2]{0:T(128)S(1)} %pad_add_fusion.s, bf16[96,3584]{1,0:T(8,128)(2,1)S(1)} %copy-done.2, bf16[96,3584]{1,0:T(8,128)(2,1)S(1)} %collective-permute-done.2.refs_1_, bf16[1792,3584]{1,0:T(8,128)(2,1)} %refs_1_.7), custom_call_target="tpu_custom_call" | custom-call | flops 38535168 | bytes 222208 | tf_op jit(solution)/shard_map/pallas_call | solution.py:30
  29.3 2.3 collective-permute-start.5
  31.6 6.1 %collective-permute-done.1 = bf16[192,1792]{1,0:T(8,128)(2,1)S(1)} collective-permute-done((bf16[192,1792]{1,0:T(8,128)(2,1)S(1)}, bf16[192,1792]{1,0:T(8,128)(2,1)S(1)}, u32[]{:S(2)}, u32[]{:S(2)}) %collective-permute-start.1) | collective-permute-done | bytes 688160 | tf_op jit(solution)/shard_map/ppermute | solution.py:336
  38.6 16.3 %all-gather.3.cloned.1.call-done.refs_0_.tok_ref = bf16[768,3584]{1,0:T(8,128)(2,1)} async-done(((bf16[96,3584]{1,0:T(8,128)(2,1)}), bf16[768,3584]{1,0:T(8,128)(2,1)}) %all-gather.3.cloned.1.call-update) | async-done | bytes 5505040 | tf_op jit(solution)/shard_map/all_gather | solution.py:414
  54.9 2.6 copy-done
  57.4 6.3 %shard_map.86 = bf16[192,1792]{1,0:T(8,128)(2,1)S(1)} custom-call(s32[2]{0:T(128)S(1)} %pad_add_fusion.s, bf16[768,3584]{1,0:T(8,128)(2,1)S(1)} %copy-done, bf16[3584,1792]{1,0:T(8,128)(2,1)} %refs_1_.9), custom_call_target="tpu_custom_call" | custom-call | flops 38535168 | bytes 222208 | tf_op jit(solution)/shard_map/pallas_call | solution.py:30
  63.7 3.4 %collective-permute-start.3 = (bf16[192,1792]{1,0:T(8,128)(2,1)S(1)}, bf16[192,1792]{1,0:T(8,128)(2,1)S(1)}, u32[]{:S(2)}, u32[]{:S(2)}) collective-permute-start(bf16[192,1792]{1,0:T(8,128)(2,1)S(1)} %shard_map.86), channel_id=1, source_target_pairs={{0,8},{24,16},{1,9},{25,17},{2,10},{26,18},{3,11},{27,19},{4,12},{... | collective-permute-start | bytes 2064392 | tf_op jit(solution)/shard_map/ppermute | solution.py:336
  69.3 1.3 collective-permute-start.8
  70.6 10.5 %shard_map.87 = (bf16[192,1792]{1,0:T(8,128)(2,1)S(1)}, bf16[192,1792]{1,0:T(8,128)(2,1)}) custom-call(s32[2]{0:T(128)S(1)} %pad_add_fusion.s, bf16[768,3584]{1,0:T(8,128)(2,1)} %all-gather.3.cloned.1.call-done.refs_0_.tok_ref, bf16[3584,1792]{1,0:T(8,128)(2,1)} %refs_1_.9), custom_call_target="tpu_custom_call" | custom-call | flops 77070336 | bytes 243712 | tf_op jit(solution)/shard_map/pallas_call | solution.py:30
  81.2 4.6 %collective-permute-start.6 = (bf16[192,1792]{1,0:T(8,128)(2,1)S(1)}, bf16[192,1792]{1,0:T(8,128)(2,1)S(1)}, u32[]{:S(2)}, u32[]{:S(2)}) collective-permute-start(bf16[192,1792]{1,0:T(8,128)(2,1)S(1)} %get-tuple-element.103), channel_id=1, source_target_pairs={{0,8},{24,16},{1,9},{25,17},{2,10},{26,18},{3,11},{27,19},{4,12},{... | collective-permute-start | bytes 2064392 | tf_op jit(solution)/shard_map/ppermute | solution.py:336
  86.9 1.6 collective-permute-start.11
  91.0 1.8 shard_map.88
  92.8 6.2 %collective-permute-start.10 = (bf16[192,1792]{1,0:T(8,128)(2,1)}, bf16[192,1792]{1,0:T(8,128)(2,1)}, u32[]{:S(2)}, u32[]{:S(2)}) collective-permute-start(bf16[192,1792]{1,0:T(8,128)(2,1)} %get-tuple-element.111), channel_id=1, source_target_pairs={{0,8},{24,16},{1,9},{25,17},{2,10},{26,18},{3,11},{27,19},{4,12},{... | collective-permute-start | bytes 2064392 | tf_op jit(solution)/shard_map/ppermute | solution.py:336
  99.0 2.6 collective-permute-done.6
  102.6 1.5 collective-permute-start.9
  104.2 12.7 %shard_map.89 = (bf16[192,1792]{1,0:T(8,128)(2,1)S(1)}, bf16[192,1792]{1,0:T(8,128)(2,1)S(1)}, bf16[192,1792]{1,0:T(8,128)(2,1)S(1)}) custom-call(s32[2]{0:T(128)S(1)} %pad_add_fusion.s, bf16[768,3584]{1,0:T(8,128)(2,1)} %all-gather.5.cloned.1.call-done.refs_0_.grad_ref, bf16[1792,3584]{1,0:T(8,128)(2,1)} %refs_1_.7), custom_call_target="tpu_custom_call" | custom-call | flops 115605504 | bytes 265216 | tf_op jit(solution)/shard_map/pallas_call | solution.py:30
  116.9 1.4 add_convert_fusion.14
  118.4 2.1 shard_map.90
  120.5 1.4 collective-permute-start.13
  121.9 6.4 %collective-permute-start.14 = (bf16[192,1792]{1,0:T(8,128)(2,1)S(1)}, bf16[192,1792]{1,0:T(8,128)(2,1)S(1)}, u32[]{:S(2)}, u32[]{:S(2)}) collective-permute-start(bf16[192,1792]{1,0:T(8,128)(2,1)S(1)} %get-tuple-element.117), channel_id=1, source_target_pairs={{0,8},{24,16},{1,9},{25,17},{2,10},{26,18},{3,11},{27,19},{4,12},{... | collective-permute-start | bytes 2064392 | tf_op jit(solution)/shard_map/ppermute | solution.py:336
  128.3 1.5 add_convert_fusion.13.refs_0_
  130.5 2.1 add_convert_fusion.12
  134.0 8.7 %collective-permute-done.13.refs_2_ = bf16[192,1792]{1,0:T(8,128)(2,1)S(1)} collective-permute-done((bf16[192,1792]{1,0:T(8,128)(2,1)S(1)}, bf16[192,1792]{1,0:T(8,128)(2,1)S(1)}, u32[]{:S(2)}, u32[]{:S(2)}) %collective-permute-start.13) | collective-permute-done | bytes 688160 | tf_op jit(solution)/shard_map/ppermute | solution.py:336
  142.7 3.1 %shard_map.91 = (bf16[768,1792]{1,0:T(8,128)(2,1)S(1)}, f32[192,1792]{1,0:T(8,128)S(1)}) custom-call(s32[2]{0:T(128)S(1)} %pad_add_fusion.s, f32[1,1792]{1,0:T(1,128)S(1)} %reshape.14.bias_ref, bf16[192,1792]{1,0:T(8,128)(2,1)} %add_convert_fusion.17.refs_0_, bf16[192,1792]{1,0:T(8,128)(2,1)} %collective-permute-done.11.refs_1_, ...), custom_call_target="tpu_custom_call", output_to_operand_aliasing={{0}: (5, {})} | custom-call | flops 10321920 | bytes 4128768 | tf_op jit(solution)/shard_map/pallas_call | solution.py:30
  145.7 1.5 collective-permute-start.15
  148.1 1.3 add_convert_fusion.10
  149.5 1.3 collective-permute-start.21
  150.8 6.6 %collective-permute-done.17.refs_2_ = bf16[192,1792]{1,0:T(8,128)(2,1)S(1)} collective-permute-done((bf16[192,1792]{1,0:T(8,128)(2,1)}, bf16[192,1792]{1,0:T(8,128)(2,1)S(1)}, u32[]{:S(2)}, u32[]{:S(2)}) %collective-permute-start.17) | collective-permute-done | bytes 688160 | tf_op jit(solution)/shard_map/ppermute | solution.py:336
  157.4 3.1 %shard_map.92 = (bf16[768,1792]{1,0:T(8,128)(2,1)S(1)}, f32[192,1792]{1,0:T(8,128)S(1)}) custom-call(s32[2]{0:T(128)S(1)} %pad_add_fusion.s, f32[1,1792]{1,0:T(1,128)S(1)} %reshape.14.bias_ref, bf16[192,1792]{1,0:T(8,128)(2,1)} %add_convert_fusion.15.refs_0_, bf16[192,1792]{1,0:T(8,128)(2,1)} %collective-permute-done.9.refs_1_, ...), custom_call_target="tpu_custom_call", output_to_operand_aliasing={{0}: (5, {})} | custom-call | flops 10321920 | bytes 4128768 | tf_op jit(solution)/shard_map/pallas_call | solution.py:30
  160.5 2.4 collective-permute-start.19
  165.3 6.9 %collective-permute-done.21.refs_2_ = bf16[192,1792]{1,0:T(8,128)(2,1)S(1)} collective-permute-done((bf16[192,1792]{1,0:T(8,128)(2,1)S(1)}, bf16[192,1792]{1,0:T(8,128)(2,1)S(1)}, u32[]{:S(2)}, u32[]{:S(2)}) %collective-permute-start.21) | collective-permute-done | bytes 688160 | tf_op jit(solution)/shard_map/ppermute | solution.py:336
  172.2 1.8 shard_map.93
  173.9 1.8 add_convert_fusion.7.refs_0_
  176.8 1.3 collective-permute-start.24
  178.1 8.8 %collective-permute-done.22.refs_2_ = bf16[192,1792]{1,0:T(8,128)(2,1)S(1)} collective-permute-done((bf16[192,1792]{1,0:T(8,128)(2,1)S(1)}, bf16[192,1792]{1,0:T(8,128)(2,1)S(1)}, u32[]{:S(2)}, u32[]{:S(2)}) %collective-permute-start.22) | collective-permute-done | bytes 688160 | tf_op jit(solution)/shard_map/ppermute | solution.py:336
  187.9 8.5 %shard_map.95 = (bf16[192,3584]{1,0:T(8,128)(2,1)S(1)}, bf16[192,3584]{1,0:T(8,128)(2,1)S(1)}) custom-call(s32[2]{0:T(128)S(1)} %pad_add_fusion.s, bf16[768,1792]{1,0:T(8,128)(2,1)S(1)} %get-tuple-element.124.refs_0_.refs_3_, bf16[3584,1792]{1,0:T(8,128)(2,1)} %refs_1_.9), custom_call_target="tpu_custom_call" | custom-call | flops 4932501504 | bytes 14221312 | tf_op jit(solution)/shard_map/pallas_call | solution.py:30
  196.6 1.7 collective-permute-done.24.refs_2_
  200.6 1.8 collective-permute-done.25
  202.8 1.6 collective-permute-start.27
  204.3 16.2 %shard_map.97 = f32[1792,3584]{1,0:T(8,128)} custom-call(s32[2]{0:T(128)S(1)} %pad_add_fusion.s, bf16[768,1792]{1,0:T(8,128)(2,1)S(1)} %get-tuple-element.134.act_ref, bf16[768,3584]{1,0:T(8,128)(2,1)} %all-gather.5.cloned.1.call-done.refs_0_.grad_ref), custom_call_target="tpu_custom_call" | custom-call | flops 9865003008 | bytes 33947648 | tf_op jit(solution)/shard_map/pallas_call | solution.py:30
  222.2 8.5 %shard_map.100 = (bf16[192,3584]{1,0:T(8,128)(2,1)S(1)}, bf16[192,3584]{1,0:T(8,128)(2,1)S(1)}) custom-call(s32[2]{0:T(128)S(1)} %pad_add_fusion.s, bf16[768,1792]{1,0:T(8,128)(2,1)S(1)} %get-tuple-element.143.refs_0_.grad_ref, bf16[3584,1792]{1,0:T(8,128)(2,1)} %refs_1_.9), custom_call_target="tpu_custom_call" | custom-call | flops 4932501504 | bytes 14221312 | tf_op jit(solution)/shard_map/pallas_call | solution.py:30
  231.7 2.8 %collective-permute-done.31 = f32[1,1792]{1,0:T(1,128)S(1)} collective-permute-done((f32[1,1792]{1,0:T(1,128)S(1)}, f32[1,1792]{1,0:T(1,128)S(1)}, u32[]{:S(2)}, u32[]{:S(2)}) %collective-permute-start.31) | collective-permute-done | bytes 7200 | tf_op jit(solution)/shard_map/ppermute | solution.py:444
  235.4 1.4 add_convert_fusion.2
  236.8 1.5 collective-permute-start.30
  238.9 16.4 %shard_map.101.refs_0_ = f32[3584,1792]{1,0:T(8,128)} custom-call(s32[2]{0:T(128)S(1)} %pad_add_fusion.s, bf16[768,3584]{1,0:T(8,128)(2,1)} %all-gather.3.cloned.1.call-done.refs_0_.tok_ref, bf16[768,1792]{1,0:T(8,128)(2,1)S(1)} %get-tuple-element.143.refs_0_.grad_ref), custom_call_target="tpu_custom_call" | custom-call | flops 9865003008 | bytes 33947648 | tf_op jit(solution)/shard_map/pallas_call | solution.py:30
  (111 shorter events, 25.9 us)
Async XLA Ops:
  7.2 47.7 %all-gather.3.cloned.1.call-start = ((), (), s32[]{:S(2)}) async-start(), calls=%async_computation | async-start | bytes 6193152 | tf_op jit(solution)/shard_map/all_gather | solution.py:414
  7.9 96.2 %all-gather.5.cloned.1.call-start = ((), (), s32[]{:S(2)}) async-start(), calls=%async_computation.1 | async-start | bytes 6193152 | tf_op jit(solution)/shard_map/all_gather | solution.py:415
  8.0 2.5 collective-permute-start
  10.5 11.5 %collective-permute-start.2 = (bf16[96,3584]{1,0:T(8,128)(2,1)S(1)}, bf16[96,3584]{1,0:T(8,128)(2,1)S(1)}, u32[]{:S(2)}, u32[]{:S(2)}) collective-permute-start(bf16[96,3584]{1,0:T(8,128)(2,1)S(1)} %copy-done.2), channel_id=1, source_target_pairs={{0,1},{1,0},{2,3},{3,2},{4,5},{5,4},{6,7},{7,6},{8,9},{9,8},{10,11... | collective-permute-start | bytes 2064392 | tf_op jit(solution)/shard_map/ppermute | solution.py:339
  17.3 20.4 %collective-permute-start.1 = (bf16[192,1792]{1,0:T(8,128)(2,1)S(1)}, bf16[192,1792]{1,0:T(8,128)(2,1)S(1)}, u32[]{:S(2)}, u32[]{:S(2)}) collective-permute-start(bf16[192,1792]{1,0:T(8,128)(2,1)S(1)} %shard_map.84), channel_id=1, source_target_pairs={{0,8},{24,16},{1,9},{25,17},{2,10},{26,18},{3,11},{27,19},{4,12},{... | collective-permute-start | bytes 2064392 | tf_op jit(solution)/shard_map/ppermute | solution.py:336
  29.3 9.3 %copy-start.21 = (f32[1792]{0:T(1024)S(1)}, f32[1792]{0:T(1024)}, u32[]{:S(2)}) copy-start(f32[1792]{0:T(1024)} %param.7) | copy-start | bytes 21508
  29.3 37.9 %collective-permute-start.5 = (bf16[192,1792]{1,0:T(8,128)(2,1)S(1)}, bf16[192,1792]{1,0:T(8,128)(2,1)}, u32[]{:S(2)}, u32[]{:S(2)}) collective-permute-start(bf16[192,1792]{1,0:T(8,128)(2,1)S(1)} %shard_map.85), channel_id=1, source_target_pairs={{0,8},{24,16},{1,9},{25,17},{2,10},{26,18},{3,11},{27,19},{4,12},{... | collective-permute-start | bytes 2064392 | tf_op jit(solution)/shard_map/ppermute | solution.py:336
  37.8 25.9 %copy-start.3 = (bf16[192,1792]{1,0:T(8,128)(2,1)}, bf16[192,1792]{1,0:T(8,128)(2,1)S(1)}, u32[]{:S(2)}) copy-start(bf16[192,1792]{1,0:T(8,128)(2,1)S(1)} %add_convert_fusion.20.refs_0_) | copy-start | bytes 2064388
  37.8 31.3 %collective-permute-start.4 = (bf16[192,1792]{1,0:T(8,128)(2,1)S(1)}, bf16[192,1792]{1,0:T(8,128)(2,1)S(1)}, u32[]{:S(2)}, u32[]{:S(2)}) collective-permute-start(bf16[192,1792]{1,0:T(8,128)(2,1)S(1)} %add_convert_fusion.20.refs_0_), channel_id=1, source_target_pairs={{8,16},{16,8},{9,17},{17,9},{10,18},{18,10},{11,19},{19,11},{12,20... | collective-permute-start | bytes 2064392 | tf_op jit(solution)/shard_map/ppermute | solution.py:336
  63.7 22.1 %collective-permute-start.3 = (bf16[192,1792]{1,0:T(8,128)(2,1)S(1)}, bf16[192,1792]{1,0:T(8,128)(2,1)S(1)}, u32[]{:S(2)}, u32[]{:S(2)}) collective-permute-start(bf16[192,1792]{1,0:T(8,128)(2,1)S(1)} %shard_map.86), channel_id=1, source_target_pairs={{0,8},{24,16},{1,9},{25,17},{2,10},{26,18},{3,11},{27,19},{4,12},{... | collective-permute-start | bytes 2064392 | tf_op jit(solution)/shard_map/ppermute | solution.py:336
  68.4 12.7 %copy-start.9 = (bf16[192,1792]{1,0:T(8,128)(2,1)}, bf16[192,1792]{1,0:T(8,128)(2,1)S(1)}, u32[]{:S(2)}) copy-start(bf16[192,1792]{1,0:T(8,128)(2,1)S(1)} %add_convert_fusion.19.refs_0_) | copy-start | bytes 2064388
  68.4 20.1 %collective-permute-start.7 = (bf16[192,1792]{1,0:T(8,128)(2,1)S(1)}, bf16[192,1792]{1,0:T(8,128)(2,1)S(1)}, u32[]{:S(2)}, u32[]{:S(2)}) collective-permute-start(bf16[192,1792]{1,0:T(8,128)(2,1)S(1)} %add_convert_fusion.19.refs_0_), channel_id=1, source_target_pairs={{8,16},{16,8},{9,17},{17,9},{10,18},{18,10},{11,19},{19,11},{12,20... | collective-permute-start | bytes 2064392 | tf_op jit(solution)/shard_map/ppermute | solution.py:336
  69.2 12.0 %copy-start.5 = (bf16[192,1792]{1,0:T(8,128)(2,1)}, bf16[192,1792]{1,0:T(8,128)(2,1)S(1)}, u32[]{:S(2)}) copy-start(bf16[192,1792]{1,0:T(8,128)(2,1)S(1)} %collective-permute-done.4.refs_1_) | copy-start | bytes 2064388
  69.3 21.6 %collective-permute-start.8 = (bf16[192,1792]{1,0:T(8,128)(2,1)S(1)}, bf16[192,1792]{1,0:T(8,128)(2,1)S(1)}, u32[]{:S(2)}, u32[]{:S(2)}) collective-permute-start(bf16[192,1792]{1,0:T(8,128)(2,1)S(1)} %add_convert_fusion.18), channel_id=1, source_target_pairs={{16,24},{8,0},{17,25},{9,1},{18,26},{10,2},{19,27},{11,3},{20,28},... | collective-permute-start | bytes 2064392 | tf_op jit(solution)/shard_map/ppermute | solution.py:336
  81.2 20.5 %copy-start.7 = (bf16[192,1792]{1,0:T(8,128)(2,1)}, bf16[192,1792]{1,0:T(8,128)(2,1)S(1)}, u32[]{:S(2)}) copy-start(bf16[192,1792]{1,0:T(8,128)(2,1)S(1)} %get-tuple-element.103) | copy-start | bytes 2064388
  81.2 20.4 %collective-permute-start.6 = (bf16[192,1792]{1,0:T(8,128)(2,1)S(1)}, bf16[192,1792]{1,0:T(8,128)(2,1)S(1)}, u32[]{:S(2)}, u32[]{:S(2)}) collective-permute-start(bf16[192,1792]{1,0:T(8,128)(2,1)S(1)} %get-tuple-element.103), channel_id=1, source_target_pairs={{0,8},{24,16},{1,9},{25,17},{2,10},{26,18},{3,11},{27,19},{4,12},{... | collective-permute-start | bytes 2064392 | tf_op jit(solution)/shard_map/ppermute | solution.py:336
  86.9 4.0 %copy-start.4 = (bf16[192,1792]{1,0:T(8,128)(2,1)S(1)}, bf16[192,1792]{1,0:T(8,128)(2,1)}, u32[]{:S(2)}) copy-start(bf16[192,1792]{1,0:T(8,128)(2,1)} %copy-done.3) | copy-start | bytes 2064388
  86.9 4.0 %copy-start.6 = (bf16[192,1792]{1,0:T(8,128)(2,1)S(1)}, bf16[192,1792]{1,0:T(8,128)(2,1)}, u32[]{:S(2)}) copy-start(bf16[192,1792]{1,0:T(8,128)(2,1)} %copy-done.5) | copy-start | bytes 2064388
  86.9 30.0 %collective-permute-start.11 = (bf16[192,1792]{1,0:T(8,128)(2,1)}, bf16[192,1792]{1,0:T(8,128)(2,1)}, u32[]{:S(2)}, u32[]{:S(2)}) collective-permute-start(bf16[192,1792]{1,0:T(8,128)(2,1)} %add_convert_fusion.17.refs_0_), channel_id=1, source_target_pairs={{8,16},{16,8},{9,17},{17,9},{10,18},{18,10},{11,19},{19,11},{12,20... | collective-permute-start | bytes 2064392 | tf_op jit(solution)/shard_map/ppermute | solution.py:336
  88.6 4.2 %copy-start.11 = (bf16[192,1792]{1,0:T(8,128)(2,1)}, bf16[192,1792]{1,0:T(8,128)(2,1)S(1)}, u32[]{:S(2)}) copy-start(bf16[192,1792]{1,0:T(8,128)(2,1)S(1)} %collective-permute-done.7.refs_1_) | copy-start | bytes 2064388
  89.7 28.6 %collective-permute-start.12 = (bf16[192,1792]{1,0:T(8,128)(2,1)}, bf16[192,1792]{1,0:T(8,128)(2,1)}, u32[]{:S(2)}, u32[]{:S(2)}) collective-permute-start(bf16[192,1792]{1,0:T(8,128)(2,1)} %add_convert_fusion.16), channel_id=1, source_target_pairs={{16,24},{8,0},{17,25},{9,1},{18,26},{10,2},{19,27},{11,3},{20,28},... | collective-permute-start | bytes 2064392 | tf_op jit(solution)/shard_map/ppermute | solution.py:336
  92.8 9.9 %copy-start.19 = (f32[192,1792]{1,0:T(8,128)}, f32[192,1792]{1,0:T(8,128)S(1)}, u32[]{:S(2)}) copy-start(f32[192,1792]{1,0:T(8,128)S(1)} %get-tuple-element.95.slope_ref) | copy-start | bytes 4128772
  92.8 35.6 %collective-permute-start.10 = (bf16[192,1792]{1,0:T(8,128)(2,1)}, bf16[192,1792]{1,0:T(8,128)(2,1)}, u32[]{:S(2)}, u32[]{:S(2)}) collective-permute-start(bf16[192,1792]{1,0:T(8,128)(2,1)} %get-tuple-element.111), channel_id=1, source_target_pairs={{0,8},{24,16},{1,9},{25,17},{2,10},{26,18},{3,11},{27,19},{4,12},{... | collective-permute-start | bytes 2064392 | tf_op jit(solution)/shard_map/ppermute | solution.py:336
  102.6 27.9 %collective-permute-start.9 = (bf16[192,1792]{1,0:T(8,128)(2,1)}, bf16[192,1792]{1,0:T(8,128)(2,1)}, u32[]{:S(2)}, u32[]{:S(2)}) collective-permute-start(bf16[192,1792]{1,0:T(8,128)(2,1)} %add_convert_fusion.15.refs_0_), channel_id=1, source_target_pairs={{8,16},{16,8},{9,17},{17,9},{10,18},{18,10},{11,19},{19,11},{12,20... | collective-permute-start | bytes 2064392 | tf_op jit(solution)/shard_map/ppermute | solution.py:336
  104.2 14.1 %copy-start.20 = (f32[192,1792]{1,0:T(8,128)S(1)}, f32[192,1792]{1,0:T(8,128)}, u32[]{:S(2)}) copy-start(f32[192,1792]{1,0:T(8,128)} %copy-done.19) | copy-start | bytes 4128772
  120.5 10.0 %copy-start.8 = (bf16[192,1792]{1,0:T(8,128)(2,1)S(1)}, bf16[192,1792]{1,0:T(8,128)(2,1)}, u32[]{:S(2)}) copy-start(bf16[192,1792]{1,0:T(8,128)(2,1)} %copy-done.7) | copy-start | bytes 2064388
  120.5 22.2 %collective-permute-start.13 = (bf16[192,1792]{1,0:T(8,128)(2,1)S(1)}, bf16[192,1792]{1,0:T(8,128)(2,1)S(1)}, u32[]{:S(2)}, u32[]{:S(2)}) collective-permute-start(bf16[192,1792]{1,0:T(8,128)(2,1)S(1)} %add_convert_fusion.14), channel_id=1, source_target_pairs={{16,24},{8,0},{17,25},{9,1},{18,26},{10,2},{19,27},{11,3},{20,28},... | collective-permute-start | bytes 2064392 | tf_op jit(solution)/shard_map/ppermute | solution.py:336
  121.9 25.3 %collective-permute-start.14 = (bf16[192,1792]{1,0:T(8,128)(2,1)S(1)}, bf16[192,1792]{1,0:T(8,128)(2,1)S(1)}, u32[]{:S(2)}, u32[]{:S(2)}) collective-permute-start(bf16[192,1792]{1,0:T(8,128)(2,1)S(1)} %get-tuple-element.117), channel_id=1, source_target_pairs={{0,8},{24,16},{1,9},{25,17},{2,10},{26,18},{3,11},{27,19},{4,12},{... | collective-permute-start | bytes 2064392 | tf_op jit(solution)/shard_map/ppermute | solution.py:336
  129.8 18.3 %collective-permute-start.16 = (bf16[192,1792]{1,0:T(8,128)(2,1)S(1)}, bf16[192,1792]{1,0:T(8,128)(2,1)S(1)}, u32[]{:S(2)}, u32[]{:S(2)}) collective-permute-start(bf16[192,1792]{1,0:T(8,128)(2,1)S(1)} %add_convert_fusion.13.refs_0_), channel_id=1, source_target_pairs={{8,16},{16,8},{9,17},{17,9},{10,18},{18,10},{11,19},{19,11},{12,20... | collective-permute-start | bytes 2064392 | tf_op jit(solution)/shard_map/ppermute | solution.py:336
  132.7 24.7 %collective-permute-start.17 = (bf16[192,1792]{1,0:T(8,128)(2,1)}, bf16[192,1792]{1,0:T(8,128)(2,1)S(1)}, u32[]{:S(2)}, u32[]{:S(2)}) collective-permute-start(bf16[192,1792]{1,0:T(8,128)(2,1)} %add_convert_fusion.12), channel_id=1, source_target_pairs={{16,24},{8,0},{17,25},{9,1},{18,26},{10,2},{19,27},{11,3},{20,28},... | collective-permute-start | bytes 2064392 | tf_op jit(solution)/shard_map/ppermute | solution.py:336
  145.7 17.2 %collective-permute-start.15 = (bf16[192,1792]{1,0:T(8,128)(2,1)S(1)}, bf16[192,1792]{1,0:T(8,128)(2,1)S(1)}, u32[]{:S(2)}, u32[]{:S(2)}) collective-permute-start(bf16[192,1792]{1,0:T(8,128)(2,1)S(1)} %get-tuple-element.121), channel_id=1, source_target_pairs={{0,8},{24,16},{1,9},{25,17},{2,10},{26,18},{3,11},{27,19},{4,12},{... | collective-permute-start | bytes 2064392 | tf_op jit(solution)/shard_map/ppermute | solution.py:336
  147.4 16.4 %collective-permute-start.20 = (bf16[192,1792]{1,0:T(8,128)(2,1)S(1)}, bf16[192,1792]{1,0:T(8,128)(2,1)S(1)}, u32[]{:S(2)}, u32[]{:S(2)}) collective-permute-start(bf16[192,1792]{1,0:T(8,128)(2,1)S(1)} %add_convert_fusion.11.refs_0_), channel_id=1, source_target_pairs={{8,16},{16,8},{9,17},{17,9},{10,18},{18,10},{11,19},{19,11},{12,20... | collective-permute-start | bytes 2064392 | tf_op jit(solution)/shard_map/ppermute | solution.py:336
  149.5 22.7 %collective-permute-start.21 = (bf16[192,1792]{1,0:T(8,128)(2,1)S(1)}, bf16[192,1792]{1,0:T(8,128)(2,1)S(1)}, u32[]{:S(2)}, u32[]{:S(2)}) collective-permute-start(bf16[192,1792]{1,0:T(8,128)(2,1)S(1)} %add_convert_fusion.10), channel_id=1, source_target_pairs={{16,24},{8,0},{17,25},{9,1},{18,26},{10,2},{19,27},{11,3},{20,28},... | collective-permute-start | bytes 2064392 | tf_op jit(solution)/shard_map/ppermute | solution.py:336
  160.5 13.4 %collective-permute-start.19 = (bf16[192,1792]{1,0:T(8,128)(2,1)S(1)}, bf16[192,1792]{1,0:T(8,128)(2,1)}, u32[]{:S(2)}, u32[]{:S(2)}) collective-permute-start(bf16[192,1792]{1,0:T(8,128)(2,1)S(1)} %get-tuple-element.127), channel_id=1, source_target_pairs={{0,8},{24,16},{1,9},{25,17},{2,10},{26,18},{3,11},{27,19},{4,12},{... | collective-permute-start | bytes 2064392 | tf_op jit(solution)/shard_map/ppermute | solution.py:336
  163.1 13.5 %collective-permute-start.18 = (bf16[192,1792]{1,0:T(8,128)(2,1)S(1)}, bf16[192,1792]{1,0:T(8,128)(2,1)S(1)}, u32[]{:S(2)}, u32[]{:S(2)}) collective-permute-start(bf16[192,1792]{1,0:T(8,128)(2,1)S(1)} %add_convert_fusion.9.refs_0_), channel_id=1, source_target_pairs={{8,16},{16,8},{9,17},{17,9},{10,18},{18,10},{11,19},{19,11},{12,20... | collective-permute-start | bytes 2064392 | tf_op jit(solution)/shard_map/ppermute | solution.py:336
  164.0 22.9 %collective-permute-start.22 = (bf16[192,1792]{1,0:T(8,128)(2,1)S(1)}, bf16[192,1792]{1,0:T(8,128)(2,1)S(1)}, u32[]{:S(2)}, u32[]{:S(2)}) collective-permute-start(bf16[192,1792]{1,0:T(8,128)(2,1)S(1)} %add_convert_fusion.8), channel_id=1, source_target_pairs={{16,24},{8,0},{17,25},{9,1},{18,26},{10,2},{19,27},{11,3},{20,28},... | collective-permute-start | bytes 2064392 | tf_op jit(solution)/shard_map/ppermute | solution.py:336
  175.7 11.2 %copy-start.14 = (f32[192,1792]{1,0:T(8,128)S(1)}, f32[192,1792]{1,0:T(8,128)}, u32[]{:S(2)}) copy-start(f32[192,1792]{1,0:T(8,128)} %copy-done.13) | copy-start | bytes 4128772
  175.8 20.6 %collective-permute-start.23 = (bf16[192,1792]{1,0:T(8,128)(2,1)S(1)}, bf16[192,1792]{1,0:T(8,128)(2,1)S(1)}, u32[]{:S(2)}, u32[]{:S(2)}) collective-permute-start(bf16[192,1792]{1,0:T(8,128)(2,1)S(1)} %add_convert_fusion.7.refs_0_), channel_id=1, source_target_pairs={{8,16},{16,8},{9,17},{17,9},{10,18},{18,10},{11,19},{19,11},{12,20... | collective-permute-start | bytes 2064392 | tf_op jit(solution)/shard_map/ppermute | solution.py:336
  176.8 21.4 %collective-permute-start.24 = (bf16[192,1792]{1,0:T(8,128)(2,1)S(1)}, bf16[192,1792]{1,0:T(8,128)(2,1)S(1)}, u32[]{:S(2)}, u32[]{:S(2)}) collective-permute-start(bf16[192,1792]{1,0:T(8,128)(2,1)S(1)} %add_convert_fusion.6), channel_id=1, source_target_pairs={{16,24},{8,0},{17,25},{9,1},{18,26},{10,2},{19,27},{11,3},{20,28},... | collective-permute-start | bytes 2064392 | tf_op jit(solution)/shard_map/ppermute | solution.py:336
  199.2 3.2 %collective-permute-start.25 = (bf16[192,3584]{1,0:T(8,128)(2,1)S(1)}, bf16[192,3584]{1,0:T(8,128)(2,1)S(1)}, u32[]{:S(2)}, u32[]{:S(2)}) collective-permute-start(bf16[192,3584]{1,0:T(8,128)(2,1)S(1)} %get-tuple-element.132), channel_id=1, source_target_pairs={{0,1},{1,0},{2,3},{3,2},{4,5},{5,4},{6,7},{7,6},{8,9},{9,8},{10,11... | collective-permute-start | bytes 4128776 | tf_op jit(solution)/shard_map/ppermute | solution.py:339
  199.3 21.2 %collective-permute-start.26 = (bf16[192,1792]{1,0:T(8,128)(2,1)S(1)}, bf16[192,1792]{1,0:T(8,128)(2,1)S(1)}, u32[]{:S(2)}, u32[]{:S(2)}) collective-permute-start(bf16[192,1792]{1,0:T(8,128)(2,1)S(1)} %add_convert_fusion.5), channel_id=1, source_target_pairs={{16,24},{8,0},{17,25},{9,1},{18,26},{10,2},{19,27},{11,3},{20,28},... | collective-permute-start | bytes 2064392 | tf_op jit(solution)/shard_map/ppermute | solution.py:336
  202.8 17.7 %copy-start.16 = (f32[192,1792]{1,0:T(8,128)S(1)}, f32[192,1792]{1,0:T(8,128)}, u32[]{:S(2)}) copy-start(f32[192,1792]{1,0:T(8,128)} %copy-done.15) | copy-start | bytes 4128772
  202.8 18.7 %collective-permute-start.27 = (bf16[96,3584]{1,0:T(8,128)(2,1)S(1)}, bf16[96,3584]{1,0:T(8,128)(2,1)S(1)}, u32[]{:S(2)}, u32[]{:S(2)}) collective-permute-start(bf16[96,3584]{1,0:T(8,128)(2,1)S(1)} %get-tuple-element.153), channel_id=1, source_target_pairs={{0,6},{1,7},{2,4},{3,5},{4,2},{5,3},{6,0},{7,1},{8,14},{9,15},{10,... | collective-permute-start | bytes 2064392 | tf_op jit(solution)/shard_map/ppermute | solution.py:339
  230.7 4.7 %collective-permute-start.28 = (bf16[192,3584]{1,0:T(8,128)(2,1)S(1)}, bf16[192,3584]{1,0:T(8,128)(2,1)S(1)}, u32[]{:S(2)}, u32[]{:S(2)}) collective-permute-start(bf16[192,3584]{1,0:T(8,128)(2,1)S(1)} %get-tuple-element.142), channel_id=1, source_target_pairs={{0,1},{1,0},{2,3},{3,2},{4,5},{5,4},{6,7},{7,6},{8,9},{9,8},{10,11... | collective-permute-start | bytes 4128776 | tf_op jit(solution)/shard_map/ppermute | solution.py:339
  230.8 3.7 %collective-permute-start.31 = (f32[1,1792]{1,0:T(1,128)S(1)}, f32[1,1792]{1,0:T(1,128)S(1)}, u32[]{:S(2)}, u32[]{:S(2)}) collective-permute-start(f32[1,1792]{1,0:T(1,128)S(1)} %add_add_fusion), channel_id=1, source_target_pairs={{0,8},{8,0},{16,24},{24,16},{1,9},{9,1},{17,25},{25,17},{2,10},{10... | collective-permute-start | bytes 21512 | tf_op jit(solution)/shard_map/ppermute | solution.py:444
  234.5 20.7 %collective-permute-start.32 = (f32[1,1792]{1,0:T(1,128)S(1)}, f32[1,1792]{1,0:T(1,128)S(1)}, u32[]{:S(2)}, u32[]{:S(2)}) collective-permute-start(f32[1,1792]{1,0:T(1,128)S(1)} %add.109.left_ref), channel_id=1, source_target_pairs={{0,16},{8,24},{16,0},{24,8},{1,17},{9,25},{17,1},{25,9},{2,18},{10... | collective-permute-start | bytes 21512 | tf_op jit(solution)/shard_map/ppermute | solution.py:449
  236.8 19.6 %collective-permute-start.30 = (bf16[96,3584]{1,0:T(8,128)(2,1)}, bf16[96,3584]{1,0:T(8,128)(2,1)S(1)}, u32[]{:S(2)}, u32[]{:S(2)}) collective-permute-start(bf16[96,3584]{1,0:T(8,128)(2,1)} %get-tuple-element.151), channel_id=1, source_target_pairs={{0,4},{1,5},{2,6},{3,7},{4,0},{5,1},{6,2},{7,3},{8,12},{9,13},{10,... | collective-permute-start | bytes 2064392 | tf_op jit(solution)/shard_map/ppermute | solution.py:339
  238.3 18.1 %collective-permute-start.29 = (bf16[96,3584]{1,0:T(8,128)(2,1)}, bf16[96,3584]{1,0:T(8,128)(2,1)S(1)}, u32[]{:S(2)}, u32[]{:S(2)}) collective-permute-start(bf16[96,3584]{1,0:T(8,128)(2,1)} %get-tuple-element.150), channel_id=1, source_target_pairs={{0,2},{1,3},{2,0},{3,1},{4,6},{5,7},{6,4},{7,5},{8,10},{9,11},{10,... | collective-permute-start | bytes 2064392 | tf_op jit(solution)/shard_map/ppermute | solution.py:339
  (9 other events, 24.6 us)
Sparse Core Ops, SparseCore 0:
  9.9 44.9 all-gather.2
  56.7 42.2 all-gather.4

commit v10 on v9

--- a/solution.py
+++ b/solution.py
@@ -11,7 +11,7 @@
 GELU_CUBIC = 0.044715
 F32, BF16 = jnp.float32, jnp.bfloat16
 VMEM_LIMIT = 48 * 1024 * 1024
-UNITS, AHEAD = 7, 3
+UNITS, AHEAD, SUBLANES = 7, 3, 8
 
 
 def dot(left, right, dims):
@@ -219,7 +219,7 @@
         grad = functools.reduce(jnp.add, [ref[...].astype(F32) for ref in ins]) * slope_ref[...]
         grad = grad.astype(BF16)
         grad_ref[...] = grad
-        sum_ref[...] = jnp.sum(grad.astype(F32), axis=0, keepdims=True)
+        sum_ref[...] = jnp.broadcast_to(jnp.sum(grad.astype(F32), axis=0, keepdims=True), sum_ref.shape)
 
     block = pl.BlockSpec((rows, hidden), lambda i, s: (0, 0))
     return call(
@@ -230,8 +230,8 @@
         [slope, *terms],
         (1,),
         [block] * (1 + len(terms)),
-        [chip_block(rows, hidden, key), pl.BlockSpec((1, hidden), lambda i, s: (0, 0))],
-        [jax.ShapeDtypeStruct((tokens, hidden), BF16), jax.ShapeDtypeStruct((1, hidden), F32)],
+        [chip_block(rows, hidden, key), pl.BlockSpec((SUBLANES, hidden), lambda i, s: (0, 0))],
+        [jax.ShapeDtypeStruct((tokens, hidden), BF16), jax.ShapeDtypeStruct((SUBLANES, hidden), F32)],
         [into],
         [0],
     )
@@ -298,20 +298,40 @@
     )
 
 
-def add_scaled(place, left, right, scale, *done):
-    def kernel(s, left_ref, right_ref, *refs):
-        refs[-1][...] = (left_ref[...].astype(F32) + right_ref[...].astype(F32)) * scale
+def add_early(place, left, right):
+    def kernel(s, left_ref, right_ref, out):
+        out[...] = left_ref[...].astype(F32) + right_ref[...].astype(F32)
 
     return call(
         kernel,
         left.size,
         8 * left.size,
         place,
-        [left, right, *done],
+        [left, right],
         (1,),
-        [whole(left.shape)] * 2 + [pl.BlockSpec(memory_space=pl.ANY)] * len(done),
+        [whole(left.shape)] * 2,
         whole(left.shape),
         jax.ShapeDtypeStruct(left.shape, F32),
+    )
+
+
+def mean_of(place, values, done):
+    count = values.shape[0] // SUBLANES
+
+    def kernel(s, values_ref, done_ref, out):
+        total = functools.reduce(jnp.add, [values_ref[at * SUBLANES : at * SUBLANES + 1, :] for at in range(count)])
+        out[...] = total * (1.0 / count)
+
+    return call(
+        kernel,
+        values.size,
+        4 * values.size,
+        place,
+        [values, done],
+        (1,),
+        [whole(values.shape), pl.BlockSpec(memory_space=pl.ANY)],
+        whole((1, values.shape[1])),
+        jax.ShapeDtypeStruct((1, values.shape[1]), F32),
     )
 
 
@@ -418,17 +438,32 @@
     compute_own("act", [0])
     first_send(1)
     end = total + steps - 1
+    begun = set()
+
+    def begin(at):
+        if at < total and at not in begun:
+            begun.add(at)
+            first_send(at)
+
+    def second(at):
+        if 0 <= at < total and ("second", at) not in begun:
+            begun.add(("second", at))
+            forward(at, 2)
+
     for slot in range(end):
-        if slot > 1 and slot + 1 < total:
-            first_send(slot + 1)
+        if slot > 1:
+            begin(slot + 1)
         if slot == 1:
             compute_own("pre", others[:1])
-            first_send(2)
-        for step in range(2, steps + 1):
+            begin(2)
+        second(slot)
+        if slot == len(others):
+            compute_own("act", others)
+            begin(slot + 2)
+            second(slot + 1)
+        for step in range(3, steps + 1):
             if 0 <= slot - step + 2 < total:
                 forward(slot - step + 2, step)
-            if step == 2 and slot == len(others):
-                compute_own("act", others)
         if slot == 1:
             compute_own("pre", others[1:])
         if slot >= steps - 1:
@@ -438,18 +473,14 @@
         if slot == end - 2:
             arrived += deliver(exchange(first))
             out_columns(0, UNITS)
-    levels = [1 << i for i in range(rows_of.bit_length() - 1)]
     sums = link(functools.reduce(jnp.add, [sums[key] for key in sorted(sums)]))
-    for bit in levels[:-1]:
-        sums = sums + lax.ppermute(sums, "row", [(i, i ^ bit) for i in range(rows_of)])
-    head = add_scaled(place, link(arrived[0]), arrived[1], 1.0)
+    sums = lax.all_gather(sums, "row", axis=0, tiled=True)
+    head = add_early(place, link(arrived[0]), arrived[1])
     chain.append(head)
     last = exchange(tokens_of(others[-2:], 0, UNITS))
-    sums = link(sums)
-    given = lax.ppermute(sums, "row", [(i, i ^ levels[-1]) for i in range(rows_of)])
     arrived += deliver(last)
     in_rows(0, UNITS)
-    grad_bias = add_scaled(place, sums, given, 1.0 / rows_of, held["in"]).reshape(hidden)
+    grad_bias = mean_of(place, sums, held["in"]).reshape(hidden)
     grad_tokens = functools.reduce(jnp.add, [part.astype(F32) for part in arrived[2:]], head).astype(BF16)
     return (grad_tokens, held["in"], grad_bias, held["out"])
 

time: 266 us -> 279 us (1.049)
  blocking collectives: 0 us -> 13.8 us
  starting transfers between devices: 56.1 us -> 49.4 us
  local copies, waits for them, and re-layouts: 2.76 us -> 7.38 us
  Pallas kernels: 109 us -> 112 us
    all_gather x0 -> x1, blocking collectives: none -> 13.8 us  [local(): sums = lax.all_gather(sums, 'row', axis=0, tiled=True)]
    ppermute x24, starting transfers between devices: 49.5 us -> 44.7 us  [send(): return lax.ppermute(value, 'row', pairs)]
    unnamed x44, local copies, waits for them, and re-layouts: 2.75 us -> 7.37 us
    pallas_call x19, Pallas kernels: 109 us -> 112 us  [call(): pl.pallas_call(kernel, grid_spec=pltpu.PrefetchScalarGridSpec(num_scalar_...]
    ppermute x24, waiting for transfers between devices: 41.4 us -> 44.3 us  [send(): return lax.ppermute(value, 'row', pairs)]
  transfers between devices with their start and end apart: 35 -> 33, of which waited for: 11 -> 10; matrix products, arithmetic and copies ran while one was open for 6% -> 5% of each run, Pallas kernels for 37% -> 36%
where the time goes in v10:
time: 279 us; the launch traced here: 278 us
  Pallas kernels  112 us (40%)
  waiting for transfers between devices  65.1 us (23%)
  starting transfers between devices  49.4 us (18%)
  other arithmetic  15.4 us (6%)
  between operations  14.7 us (5%)
  blocking collectives  13.8 us (5%)
  local copies, waits for them, and re-layouts  7.38 us (3%)
    pallas_call x19, Pallas kernels, call(): pl.pallas_call(kernel, grid_spec=pltpu.PrefetchScalarGridSpec(num_scalar_...  112 us
    ppermute x24, starting transfers between devices, send(): return lax.ppermute(value, 'row', pairs)  44.7 us
    ppermute x24, waiting for transfers between devices, send(): return lax.ppermute(value, 'row', pairs)  44.3 us
    all_gather x1, waiting for transfers between devices, local(): held['pre'] = lax.all_gather(tokens, 'col', axis=0, tiled=True)  16.3 us
    all_gather x1, blocking collectives, local(): sums = lax.all_gather(sums, 'row', axis=0, tiled=True)  13.8 us
    convert_element_type x18, other arithmetic, add_bf16(): return (left.astype(F32) + right.astype(F32)).astype(BF16)  13.6 us
    unnamed x44, local copies, waits for them, and re-layouts  7.37 us
  transfers between devices with their start and end apart: 33, of which 10 were waited for; matrix products, arithmetic and copies ran while one was open for 5% of the time, Pallas kernels for 36%

profile of v10, /device:TPU:0, one launch (start us, length us, event | category | flops | bytes accessed | tf_op | source)
XLA Modules:
  0.0 277.6 jit_solution(3455362012504407901)
XLA Ops:
  8.5 2.0 collective-permute-done.refs_1_
  11.0 6.3 %shard_map.84 = bf16[192,1792]{1,0:T(8,128)(2,1)S(1)} custom-call(s32[2]{0:T(128)S(1)} %pad_add_fusion.s, bf16[96,3584]{1,0:T(8,128)(2,1)S(1)} %copy-done.3, bf16[96,3584]{1,0:T(8,128)(2,1)S(1)} %collective-permute-done.refs_1_, bf16[3584,1792]{1,0:T(8,128)(2,1)} %refs_1_.9), custom_call_target="tpu_custom_call" | custom-call | flops 38535168 | bytes 222208 | tf_op jit(solution)/shard_map/pallas_call | solution.py:30
  17.3 4.7 %collective-permute-start.1 = (bf16[192,1792]{1,0:T(8,128)(2,1)S(1)}, bf16[192,1792]{1,0:T(8,128)(2,1)S(1)}, u32[]{:S(2)}, u32[]{:S(2)}) collective-permute-start(bf16[192,1792]{1,0:T(8,128)(2,1)S(1)} %shard_map.84), channel_id=1, source_target_pairs={{0,8},{24,16},{1,9},{25,17},{2,10},{26,18},{3,11},{27,19},{4,12},{... | collective-permute-start | bytes 2064392 | tf_op jit(solution)/shard_map/ppermute | solution.py:356
  22.0 7.3 %shard_map.85 = bf16[192,1792]{1,0:T(8,128)(2,1)S(1)} custom-call(s32[2]{0:T(128)S(1)} %pad_add_fusion.s, bf16[96,3584]{1,0:T(8,128)(2,1)S(1)} %copy-done.4, bf16[96,3584]{1,0:T(8,128)(2,1)S(1)} %collective-permute-done.2.refs_1_, bf16[1792,3584]{1,0:T(8,128)(2,1)} %refs_1_.7), custom_call_target="tpu_custom_call" | custom-call | flops 38535168 | bytes 222208 | tf_op jit(solution)/shard_map/pallas_call | solution.py:30
  29.3 2.3 collective-permute-start.5
  31.6 6.1 %collective-permute-done.1 = bf16[192,1792]{1,0:T(8,128)(2,1)S(1)} collective-permute-done((bf16[192,1792]{1,0:T(8,128)(2,1)S(1)}, bf16[192,1792]{1,0:T(8,128)(2,1)S(1)}, u32[]{:S(2)}, u32[]{:S(2)}) %collective-permute-start.1) | collective-permute-done | bytes 688160 | tf_op jit(solution)/shard_map/ppermute | solution.py:356
  38.6 16.3 %all-gather.3.cloned.1.call-done.refs_0_.tok_ref = bf16[768,3584]{1,0:T(8,128)(2,1)} async-done(((bf16[96,3584]{1,0:T(8,128)(2,1)}), bf16[768,3584]{1,0:T(8,128)(2,1)}) %all-gather.3.cloned.1.call-update) | async-done | bytes 5505040 | tf_op jit(solution)/shard_map/all_gather | solution.py:434
  54.9 2.6 copy-done.2
  57.4 6.3 %shard_map.86 = bf16[192,1792]{1,0:T(8,128)(2,1)S(1)} custom-call(s32[2]{0:T(128)S(1)} %pad_add_fusion.s, bf16[768,3584]{1,0:T(8,128)(2,1)S(1)} %copy-done.2, bf16[3584,1792]{1,0:T(8,128)(2,1)} %refs_1_.9), custom_call_target="tpu_custom_call" | custom-call | flops 38535168 | bytes 222208 | tf_op jit(solution)/shard_map/pallas_call | solution.py:30
  63.7 3.4 %collective-permute-start.3 = (bf16[192,1792]{1,0:T(8,128)(2,1)S(1)}, bf16[192,1792]{1,0:T(8,128)(2,1)S(1)}, u32[]{:S(2)}, u32[]{:S(2)}) collective-permute-start(bf16[192,1792]{1,0:T(8,128)(2,1)S(1)} %shard_map.86), channel_id=1, source_target_pairs={{0,8},{24,16},{1,9},{25,17},{2,10},{26,18},{3,11},{27,19},{4,12},{... | collective-permute-start | bytes 2064392 | tf_op jit(solution)/shard_map/ppermute | solution.py:356
  69.3 1.3 collective-permute-start.8
  70.6 10.5 %shard_map.87 = (bf16[192,1792]{1,0:T(8,128)(2,1)S(1)}, bf16[192,1792]{1,0:T(8,128)(2,1)}) custom-call(s32[2]{0:T(128)S(1)} %pad_add_fusion.s, bf16[768,3584]{1,0:T(8,128)(2,1)} %all-gather.3.cloned.1.call-done.refs_0_.tok_ref, bf16[3584,1792]{1,0:T(8,128)(2,1)} %refs_1_.9), custom_call_target="tpu_custom_call" | custom-call | flops 77070336 | bytes 243712 | tf_op jit(solution)/shard_map/pallas_call | solution.py:30
  81.2 4.6 %collective-permute-start.6 = (bf16[192,1792]{1,0:T(8,128)(2,1)S(1)}, bf16[192,1792]{1,0:T(8,128)(2,1)S(1)}, u32[]{:S(2)}, u32[]{:S(2)}) collective-permute-start(bf16[192,1792]{1,0:T(8,128)(2,1)S(1)} %get-tuple-element.102), channel_id=1, source_target_pairs={{0,8},{24,16},{1,9},{25,17},{2,10},{26,18},{3,11},{27,19},{4,12},{... | collective-permute-start | bytes 2064392 | tf_op jit(solution)/shard_map/ppermute | solution.py:356
  88.7 1.8 shard_map.88
  90.5 2.5 collective-permute-start.11
  94.3 1.5 collective-permute-start.10
  95.9 5.8 %collective-permute-done.6 = bf16[192,1792]{1,0:T(8,128)(2,1)S(1)} collective-permute-done((bf16[192,1792]{1,0:T(8,128)(2,1)S(1)}, bf16[192,1792]{1,0:T(8,128)(2,1)S(1)}, u32[]{:S(2)}, u32[]{:S(2)}) %collective-permute-start.6) | collective-permute-done | bytes 688160 | tf_op jit(solution)/shard_map/ppermute | solution.py:356
  102.6 1.5 collective-permute-start.9
  104.2 12.7 %shard_map.89 = (bf16[192,1792]{1,0:T(8,128)(2,1)S(1)}, bf16[192,1792]{1,0:T(8,128)(2,1)S(1)}, bf16[192,1792]{1,0:T(8,128)(2,1)S(1)}) custom-call(s32[2]{0:T(128)S(1)} %pad_add_fusion.s, bf16[768,3584]{1,0:T(8,128)(2,1)} %all-gather.5.cloned.1.call-done.refs_0_.grad_ref, bf16[1792,3584]{1,0:T(8,128)(2,1)} %refs_1_.7), custom_call_target="tpu_custom_call" | custom-call | flops 115605504 | bytes 265216 | tf_op jit(solution)/shard_map/pallas_call | solution.py:30
  116.9 1.6 add_convert_fusion.14.refs_0_
  118.5 1.4 add_convert_fusion.13
  119.9 1.3 collective-permute-start.13
  121.2 6.4 %collective-permute-start.14 = (bf16[192,1792]{1,0:T(8,128)(2,1)S(1)}, bf16[192,1792]{1,0:T(8,128)(2,1)S(1)}, u32[]{:S(2)}, u32[]{:S(2)}) collective-permute-start(bf16[192,1792]{1,0:T(8,128)(2,1)S(1)} %get-tuple-element.116), channel_id=1, source_target_pairs={{0,8},{24,16},{1,9},{25,17},{2,10},{26,18},{3,11},{27,19},{4,12},{... | collective-permute-start | bytes 2064392 | tf_op jit(solution)/shard_map/ppermute | solution.py:356
  128.3 2.9 %shard_map.90 = (bf16[768,1792]{1,0:T(8,128)(2,1)}, f32[8,1792]{1,0:T(8,128)S(1)}) custom-call(s32[2]{0:T(128)S(1)} %pad_add_fusion.s, f32[192,1792]{1,0:T(8,128)S(1)} %copy-done.20, bf16[192,1792]{1,0:T(8,128)(2,1)S(1)} %copy-done.10, bf16[192,1792]{1,0:T(8,128)(2,1)S(1)} %copy-done.12, bf16[192,1792]{1,0:T(8,128)(2,1)} %collective-permute-done.12.refs_2_), custom_call_target="tpu_custom_call" | custom-call | flops 2752512 | bytes 4128768 | tf_op jit(solution)/shard_map/pallas_call | solution.py:30
  131.2 1.3 add_convert_fusion.12
  132.5 1.3 collective-permute-start.17
  133.8 8.1 %collective-permute-done.13.refs_2_ = bf16[192,1792]{1,0:T(8,128)(2,1)S(1)} collective-permute-done((bf16[192,1792]{1,0:T(8,128)(2,1)S(1)}, bf16[192,1792]{1,0:T(8,128)(2,1)S(1)}, u32[]{:S(2)}, u32[]{:S(2)}) %collective-permute-start.13) | collective-permute-done | bytes 688160 | tf_op jit(solution)/shard_map/ppermute | solution.py:356
  141.9 3.1 %shard_map.91 = (bf16[768,1792]{1,0:T(8,128)(2,1)S(1)}, f32[192,1792]{1,0:T(8,128)S(1)}) custom-call(s32[2]{0:T(128)S(1)} %pad_add_fusion.s, f32[1,1792]{1,0:T(1,128)S(1)} %reshape.14.bias_ref, bf16[192,1792]{1,0:T(8,128)(2,1)} %add_convert_fusion.17.refs_0_, bf16[192,1792]{1,0:T(8,128)(2,1)} %collective-permute-done.10.refs_1_, ...), custom_call_target="tpu_custom_call", output_to_operand_aliasing={{0}: (5, {})} | custom-call | flops 10321920 | bytes 4128768 | tf_op jit(solution)/shard_map/pallas_call | solution.py:30
  145.0 1.5 collective-permute-start.15
  148.6 1.3 collective-permute-start.21
  149.9 6.7 %collective-permute-done.17.refs_2_ = bf16[192,1792]{1,0:T(8,128)(2,1)S(1)} collective-permute-done((bf16[192,1792]{1,0:T(8,128)(2,1)S(1)}, bf16[192,1792]{1,0:T(8,128)(2,1)S(1)}, u32[]{:S(2)}, u32[]{:S(2)}) %collective-permute-start.17) | collective-permute-done | bytes 688160 | tf_op jit(solution)/shard_map/ppermute | solution.py:356
  156.6 3.1 %shard_map.92 = (bf16[768,1792]{1,0:T(8,128)(2,1)S(1)}, f32[192,1792]{1,0:T(8,128)S(1)}) custom-call(s32[2]{0:T(128)S(1)} %pad_add_fusion.s, f32[1,1792]{1,0:T(1,128)S(1)} %reshape.14.bias_ref, bf16[192,1792]{1,0:T(8,128)(2,1)} %add_convert_fusion.15.refs_0_, bf16[192,1792]{1,0:T(8,128)(2,1)} %collective-permute-done.9.refs_1_, ...), custom_call_target="tpu_custom_call", output_to_operand_aliasing={{0}: (5, {})} | custom-call | flops 10321920 | bytes 4128768 | tf_op jit(solution)/shard_map/pallas_call | solution.py:30
  159.7 1.7 collective-permute-start.19
  163.8 7.6 %collective-permute-done.21.refs_2_ = bf16[192,1792]{1,0:T(8,128)(2,1)S(1)} collective-permute-done((bf16[192,1792]{1,0:T(8,128)(2,1)S(1)}, bf16[192,1792]{1,0:T(8,128)(2,1)S(1)}, u32[]{:S(2)}, u32[]{:S(2)}) %collective-permute-start.21) | collective-permute-done | bytes 688160 | tf_op jit(solution)/shard_map/ppermute | solution.py:356
  171.4 1.8 shard_map.93
  176.7 9.4 %collective-permute-done.22.refs_2_ = bf16[192,1792]{1,0:T(8,128)(2,1)S(1)} collective-permute-done((bf16[192,1792]{1,0:T(8,128)(2,1)S(1)}, bf16[192,1792]{1,0:T(8,128)(2,1)S(1)}, u32[]{:S(2)}, u32[]{:S(2)}) %collective-permute-start.22) | collective-permute-done | bytes 688160 | tf_op jit(solution)/shard_map/ppermute | solution.py:356
  186.1 1.8 shard_map.94
  187.9 1.8 copy-done
  189.7 8.5 %shard_map.95 = (bf16[192,3584]{1,0:T(8,128)(2,1)S(1)}, bf16[192,3584]{1,0:T(8,128)(2,1)S(1)}) custom-call(s32[2]{0:T(128)S(1)} %pad_add_fusion.s, bf16[768,1792]{1,0:T(8,128)(2,1)S(1)} %copy-done, bf16[3584,1792]{1,0:T(8,128)(2,1)} %refs_1_.9), custom_call_target="tpu_custom_call" | custom-call | flops 4932501504 | bytes 14221312 | tf_op jit(solution)/shard_map/pallas_call | solution.py:30
  199.8 1.8 shard_map.96
  202.9 1.8 collective-permute-done.25
  205.1 1.7 collective-permute-start.27
  206.8 16.1 %shard_map.97 = f32[1792,3584]{1,0:T(8,128)} custom-call(s32[2]{0:T(128)S(1)} %pad_add_fusion.s, bf16[768,1792]{1,0:T(8,128)(2,1)S(1)} %get-tuple-element.133.act_ref, bf16[768,3584]{1,0:T(8,128)(2,1)} %all-gather.5.cloned.1.call-done.refs_0_.grad_ref), custom_call_target="tpu_custom_call" | custom-call | flops 9865003008 | bytes 33947648 | tf_op jit(solution)/shard_map/pallas_call | solution.py:30
  222.9 1.8 shard_map.98
  226.5 8.5 %shard_map.100 = (bf16[192,3584]{1,0:T(8,128)(2,1)S(1)}, bf16[192,3584]{1,0:T(8,128)(2,1)S(1)}) custom-call(s32[2]{0:T(128)S(1)} %pad_add_fusion.s, bf16[768,1792]{1,0:T(8,128)(2,1)S(1)} %copy-done.1, bf16[3584,1792]{1,0:T(8,128)(2,1)} %refs_1_.9), custom_call_target="tpu_custom_call" | custom-call | flops 4932501504 | bytes 14221312 | tf_op jit(solution)/shard_map/pallas_call | solution.py:30
  235.1 13.8 %all_gather.11.values_ref = f32[32,1792]{1,0:T(8,128)S(1)} all-gather(f32[8,1792]{1,0:T(8,128)S(1)} %add_add_fusion), channel_id=1, replica_groups=mesh['row'=4,'col'=8] {'row'}, dimensions={0}, use_global_device_ids=true | all-gather | bytes 286720 | tf_op jit(solution)/shard_map/all_gather | solution.py:477
  250.1 1.4 collective-permute-start.30
  252.1 16.4 %shard_map.101.done_ref = f32[3584,1792]{1,0:T(8,128)} custom-call(s32[2]{0:T(128)S(1)} %pad_add_fusion.s, bf16[768,3584]{1,0:T(8,128)(2,1)} %all-gather.3.cloned.1.call-done.refs_0_.tok_ref, bf16[768,1792]{1,0:T(8,128)(2,1)S(1)} %copy-done.1), custom_call_target="tpu_custom_call" | custom-call | flops 9865003008 | bytes 33947648 | tf_op jit(solution)/shard_map/pallas_call | solution.py:30
  (107 shorter events, 27.8 us)
Async XLA Ops:
  7.2 3.9 %copy-start.3 = (bf16[96,3584]{1,0:T(8,128)(2,1)S(1)}, bf16[96,3584]{1,0:T(8,128)(2,1)}, u32[]{:S(2)}) copy-start(bf16[96,3584]{1,0:T(8,128)(2,1)} %refs_0_.1) | copy-start | bytes 2064388
  7.2 3.3 %copy-start.4 = (bf16[96,3584]{1,0:T(8,128)(2,1)S(1)}, bf16[96,3584]{1,0:T(8,128)(2,1)}, u32[]{:S(2)}) copy-start(bf16[96,3584]{1,0:T(8,128)(2,1)} %refs_0_.2) | copy-start | bytes 2064388
  7.2 47.7 %all-gather.3.cloned.1.call-start = ((), (), s32[]{:S(2)}) async-start(), calls=%async_computation | async-start | bytes 6193152 | tf_op jit(solution)/shard_map/all_gather | solution.py:434
  7.9 96.2 %all-gather.5.cloned.1.call-start = ((), (), s32[]{:S(2)}) async-start(), calls=%async_computation.1 | async-start | bytes 6193152 | tf_op jit(solution)/shard_map/all_gather | solution.py:435
  8.0 2.5 collective-permute-start
  10.5 11.5 %collective-permute-start.2 = (bf16[96,3584]{1,0:T(8,128)(2,1)S(1)}, bf16[96,3584]{1,0:T(8,128)(2,1)S(1)}, u32[]{:S(2)}, u32[]{:S(2)}) collective-permute-start(bf16[96,3584]{1,0:T(8,128)(2,1)S(1)} %copy-done.4), channel_id=1, source_target_pairs={{0,1},{1,0},{2,3},{3,2},{4,5},{5,4},{6,7},{7,6},{8,9},{9,8},{10,11... | collective-permute-start | bytes 2064392 | tf_op jit(solution)/shard_map/ppermute | solution.py:359
  17.3 20.4 %collective-permute-start.1 = (bf16[192,1792]{1,0:T(8,128)(2,1)S(1)}, bf16[192,1792]{1,0:T(8,128)(2,1)S(1)}, u32[]{:S(2)}, u32[]{:S(2)}) collective-permute-start(bf16[192,1792]{1,0:T(8,128)(2,1)S(1)} %shard_map.84), channel_id=1, source_target_pairs={{0,8},{24,16},{1,9},{25,17},{2,10},{26,18},{3,11},{27,19},{4,12},{... | collective-permute-start | bytes 2064392 | tf_op jit(solution)/shard_map/ppermute | solution.py:356
  29.3 9.3 %copy-start.21 = (f32[1792]{0:T(1024)S(1)}, f32[1792]{0:T(1024)}, u32[]{:S(2)}) copy-start(f32[1792]{0:T(1024)} %param.7) | copy-start | bytes 21508
  29.3 37.9 %collective-permute-start.5 = (bf16[192,1792]{1,0:T(8,128)(2,1)S(1)}, bf16[192,1792]{1,0:T(8,128)(2,1)}, u32[]{:S(2)}, u32[]{:S(2)}) collective-permute-start(bf16[192,1792]{1,0:T(8,128)(2,1)S(1)} %shard_map.85), channel_id=1, source_target_pairs={{0,8},{24,16},{1,9},{25,17},{2,10},{26,18},{3,11},{27,19},{4,12},{... | collective-permute-start | bytes 2064392 | tf_op jit(solution)/shard_map/ppermute | solution.py:356
  37.8 25.9 %copy-start.5 = (bf16[192,1792]{1,0:T(8,128)(2,1)}, bf16[192,1792]{1,0:T(8,128)(2,1)S(1)}, u32[]{:S(2)}) copy-start(bf16[192,1792]{1,0:T(8,128)(2,1)S(1)} %add_convert_fusion.20.refs_0_) | copy-start | bytes 2064388
  37.8 31.3 %collective-permute-start.4 = (bf16[192,1792]{1,0:T(8,128)(2,1)S(1)}, bf16[192,1792]{1,0:T(8,128)(2,1)S(1)}, u32[]{:S(2)}, u32[]{:S(2)}) collective-permute-start(bf16[192,1792]{1,0:T(8,128)(2,1)S(1)} %add_convert_fusion.20.refs_0_), channel_id=1, source_target_pairs={{8,16},{16,8},{9,17},{17,9},{10,18},{18,10},{11,19},{19,11},{12,20... | collective-permute-start | bytes 2064392 | tf_op jit(solution)/shard_map/ppermute | solution.py:356
  63.7 22.1 %collective-permute-start.3 = (bf16[192,1792]{1,0:T(8,128)(2,1)S(1)}, bf16[192,1792]{1,0:T(8,128)(2,1)S(1)}, u32[]{:S(2)}, u32[]{:S(2)}) collective-permute-start(bf16[192,1792]{1,0:T(8,128)(2,1)S(1)} %shard_map.86), channel_id=1, source_target_pairs={{0,8},{24,16},{1,9},{25,17},{2,10},{26,18},{3,11},{27,19},{4,12},{... | collective-permute-start | bytes 2064392 | tf_op jit(solution)/shard_map/ppermute | solution.py:356
  68.4 12.7 %copy-start.9 = (bf16[192,1792]{1,0:T(8,128)(2,1)}, bf16[192,1792]{1,0:T(8,128)(2,1)S(1)}, u32[]{:S(2)}) copy-start(bf16[192,1792]{1,0:T(8,128)(2,1)S(1)} %add_convert_fusion.19.refs_0_) | copy-start | bytes 2064388
  68.4 18.5 %collective-permute-start.7 = (bf16[192,1792]{1,0:T(8,128)(2,1)S(1)}, bf16[192,1792]{1,0:T(8,128)(2,1)S(1)}, u32[]{:S(2)}, u32[]{:S(2)}) collective-permute-start(bf16[192,1792]{1,0:T(8,128)(2,1)S(1)} %add_convert_fusion.19.refs_0_), channel_id=1, source_target_pairs={{8,16},{16,8},{9,17},{17,9},{10,18},{18,10},{11,19},{19,11},{12,20... | collective-permute-start | bytes 2064392 | tf_op jit(solution)/shard_map/ppermute | solution.py:356
  69.2 12.0 %copy-start.7 = (bf16[192,1792]{1,0:T(8,128)(2,1)}, bf16[192,1792]{1,0:T(8,128)(2,1)S(1)}, u32[]{:S(2)}) copy-start(bf16[192,1792]{1,0:T(8,128)(2,1)S(1)} %collective-permute-done.4.refs_1_) | copy-start | bytes 2064388
  69.3 19.2 %collective-permute-start.8 = (bf16[192,1792]{1,0:T(8,128)(2,1)S(1)}, bf16[192,1792]{1,0:T(8,128)(2,1)S(1)}, u32[]{:S(2)}, u32[]{:S(2)}) collective-permute-start(bf16[192,1792]{1,0:T(8,128)(2,1)S(1)} %add_convert_fusion.18), channel_id=1, source_target_pairs={{16,24},{8,0},{17,25},{9,1},{18,26},{10,2},{19,27},{11,3},{20,28},... | collective-permute-start | bytes 2064392 | tf_op jit(solution)/shard_map/ppermute | solution.py:356
  81.2 20.5 %copy-start.13 = (bf16[192,1792]{1,0:T(8,128)(2,1)}, bf16[192,1792]{1,0:T(8,128)(2,1)S(1)}, u32[]{:S(2)}) copy-start(bf16[192,1792]{1,0:T(8,128)(2,1)S(1)} %get-tuple-element.102) | copy-start | bytes 2064388
  81.2 20.4 %collective-permute-start.6 = (bf16[192,1792]{1,0:T(8,128)(2,1)S(1)}, bf16[192,1792]{1,0:T(8,128)(2,1)S(1)}, u32[]{:S(2)}, u32[]{:S(2)}) collective-permute-start(bf16[192,1792]{1,0:T(8,128)(2,1)S(1)} %get-tuple-element.102), channel_id=1, source_target_pairs={{0,8},{24,16},{1,9},{25,17},{2,10},{26,18},{3,11},{27,19},{4,12},{... | collective-permute-start | bytes 2064392 | tf_op jit(solution)/shard_map/ppermute | solution.py:356
  86.9 3.6 %copy-start.11 = (bf16[192,1792]{1,0:T(8,128)(2,1)}, bf16[192,1792]{1,0:T(8,128)(2,1)S(1)}, u32[]{:S(2)}) copy-start(bf16[192,1792]{1,0:T(8,128)(2,1)S(1)} %collective-permute-done.7.refs_1_) | copy-start | bytes 2064388
  90.5 12.1 %copy-start.19 = (f32[192,1792]{1,0:T(8,128)}, f32[192,1792]{1,0:T(8,128)S(1)}, u32[]{:S(2)}) copy-start(f32[192,1792]{1,0:T(8,128)S(1)} %get-tuple-element.92.slope_ref) | copy-start | bytes 4128772
  90.5 26.4 %collective-permute-start.11 = (bf16[192,1792]{1,0:T(8,128)(2,1)}, bf16[192,1792]{1,0:T(8,128)(2,1)}, u32[]{:S(2)}, u32[]{:S(2)}) collective-permute-start(bf16[192,1792]{1,0:T(8,128)(2,1)} %get-tuple-element.110), channel_id=1, source_target_pairs={{0,8},{24,16},{1,9},{25,17},{2,10},{26,18},{3,11},{27,19},{4,12},{... | collective-permute-start | bytes 2064392 | tf_op jit(solution)/shard_map/ppermute | solution.py:356
  93.1 35.2 %collective-permute-start.12 = (bf16[192,1792]{1,0:T(8,128)(2,1)}, bf16[192,1792]{1,0:T(8,128)(2,1)}, u32[]{:S(2)}, u32[]{:S(2)}) collective-permute-start(bf16[192,1792]{1,0:T(8,128)(2,1)} %add_convert_fusion.16), channel_id=1, source_target_pairs={{16,24},{8,0},{17,25},{9,1},{18,26},{10,2},{19,27},{11,3},{20,28},... | collective-permute-start | bytes 2064392 | tf_op jit(solution)/shard_map/ppermute | solution.py:356
  94.3 24.2 %collective-permute-start.10 = (bf16[192,1792]{1,0:T(8,128)(2,1)}, bf16[192,1792]{1,0:T(8,128)(2,1)}, u32[]{:S(2)}, u32[]{:S(2)}) collective-permute-start(bf16[192,1792]{1,0:T(8,128)(2,1)} %add_convert_fusion.17.refs_0_), channel_id=1, source_target_pairs={{8,16},{16,8},{9,17},{17,9},{10,18},{18,10},{11,19},{19,11},{12,20... | collective-permute-start | bytes 2064392 | tf_op jit(solution)/shard_map/ppermute | solution.py:356
  102.6 28.6 %collective-permute-start.9 = (bf16[192,1792]{1,0:T(8,128)(2,1)}, bf16[192,1792]{1,0:T(8,128)(2,1)}, u32[]{:S(2)}, u32[]{:S(2)}) collective-permute-start(bf16[192,1792]{1,0:T(8,128)(2,1)} %add_convert_fusion.15.refs_0_), channel_id=1, source_target_pairs={{8,16},{16,8},{9,17},{17,9},{10,18},{18,10},{11,19},{19,11},{12,20... | collective-permute-start | bytes 2064392 | tf_op jit(solution)/shard_map/ppermute | solution.py:356
  116.9 11.4 %copy-start.20 = (f32[192,1792]{1,0:T(8,128)S(1)}, f32[192,1792]{1,0:T(8,128)}, u32[]{:S(2)}) copy-start(f32[192,1792]{1,0:T(8,128)} %copy-done.19) | copy-start | bytes 4128772
  118.5 9.8 %copy-start.10 = (bf16[192,1792]{1,0:T(8,128)(2,1)S(1)}, bf16[192,1792]{1,0:T(8,128)(2,1)}, u32[]{:S(2)}) copy-start(bf16[192,1792]{1,0:T(8,128)(2,1)} %copy-done.9) | copy-start | bytes 2064388
  118.5 9.8 %copy-start.12 = (bf16[192,1792]{1,0:T(8,128)(2,1)S(1)}, bf16[192,1792]{1,0:T(8,128)(2,1)}, u32[]{:S(2)}) copy-start(bf16[192,1792]{1,0:T(8,128)(2,1)} %copy-done.11) | copy-start | bytes 2064388
  119.9 22.0 %collective-permute-start.13 = (bf16[192,1792]{1,0:T(8,128)(2,1)S(1)}, bf16[192,1792]{1,0:T(8,128)(2,1)S(1)}, u32[]{:S(2)}, u32[]{:S(2)}) collective-permute-start(bf16[192,1792]{1,0:T(8,128)(2,1)S(1)} %add_convert_fusion.13), channel_id=1, source_target_pairs={{16,24},{8,0},{17,25},{9,1},{18,26},{10,2},{19,27},{11,3},{20,28},... | collective-permute-start | bytes 2064392 | tf_op jit(solution)/shard_map/ppermute | solution.py:356
  121.2 25.3 %collective-permute-start.14 = (bf16[192,1792]{1,0:T(8,128)(2,1)S(1)}, bf16[192,1792]{1,0:T(8,128)(2,1)S(1)}, u32[]{:S(2)}, u32[]{:S(2)}) collective-permute-start(bf16[192,1792]{1,0:T(8,128)(2,1)S(1)} %get-tuple-element.116), channel_id=1, source_target_pairs={{0,8},{24,16},{1,9},{25,17},{2,10},{26,18},{3,11},{27,19},{4,12},{... | collective-permute-start | bytes 2064392 | tf_op jit(solution)/shard_map/ppermute | solution.py:356
  127.6 19.8 %collective-permute-start.16 = (bf16[192,1792]{1,0:T(8,128)(2,1)S(1)}, bf16[192,1792]{1,0:T(8,128)(2,1)S(1)}, u32[]{:S(2)}, u32[]{:S(2)}) collective-permute-start(bf16[192,1792]{1,0:T(8,128)(2,1)S(1)} %add_convert_fusion.14.refs_0_), channel_id=1, source_target_pairs={{8,16},{16,8},{9,17},{17,9},{10,18},{18,10},{11,19},{19,11},{12,20... | collective-permute-start | bytes 2064392 | tf_op jit(solution)/shard_map/ppermute | solution.py:356
  128.3 2.9 %copy-start.14 = (bf16[192,1792]{1,0:T(8,128)(2,1)S(1)}, bf16[192,1792]{1,0:T(8,128)(2,1)}, u32[]{:S(2)}) copy-start(bf16[192,1792]{1,0:T(8,128)(2,1)} %copy-done.13) | copy-start | bytes 2064388
  132.5 24.1 %collective-permute-start.17 = (bf16[192,1792]{1,0:T(8,128)(2,1)S(1)}, bf16[192,1792]{1,0:T(8,128)(2,1)S(1)}, u32[]{:S(2)}, u32[]{:S(2)}) collective-permute-start(bf16[192,1792]{1,0:T(8,128)(2,1)S(1)} %add_convert_fusion.12), channel_id=1, source_target_pairs={{16,24},{8,0},{17,25},{9,1},{18,26},{10,2},{19,27},{11,3},{20,28},... | collective-permute-start | bytes 2064392 | tf_op jit(solution)/shard_map/ppermute | solution.py:356
  145.0 16.4 %collective-permute-start.15 = (bf16[192,1792]{1,0:T(8,128)(2,1)S(1)}, bf16[192,1792]{1,0:T(8,128)(2,1)S(1)}, u32[]{:S(2)}, u32[]{:S(2)}) collective-permute-start(bf16[192,1792]{1,0:T(8,128)(2,1)S(1)} %get-tuple-element.120), channel_id=1, source_target_pairs={{0,8},{24,16},{1,9},{25,17},{2,10},{26,18},{3,11},{27,19},{4,12},{... | collective-permute-start | bytes 2064392 | tf_op jit(solution)/shard_map/ppermute | solution.py:356
  146.6 15.7 %collective-permute-start.20 = (bf16[192,1792]{1,0:T(8,128)(2,1)S(1)}, bf16[192,1792]{1,0:T(8,128)(2,1)S(1)}, u32[]{:S(2)}, u32[]{:S(2)}) collective-permute-start(bf16[192,1792]{1,0:T(8,128)(2,1)S(1)} %add_convert_fusion.11.refs_0_), channel_id=1, source_target_pairs={{8,16},{16,8},{9,17},{17,9},{10,18},{18,10},{11,19},{19,11},{12,20... | collective-permute-start | bytes 2064392 | tf_op jit(solution)/shard_map/ppermute | solution.py:356
  148.6 22.8 %collective-permute-start.21 = (bf16[192,1792]{1,0:T(8,128)(2,1)S(1)}, bf16[192,1792]{1,0:T(8,128)(2,1)S(1)}, u32[]{:S(2)}, u32[]{:S(2)}) collective-permute-start(bf16[192,1792]{1,0:T(8,128)(2,1)S(1)} %add_convert_fusion.10), channel_id=1, source_target_pairs={{16,24},{8,0},{17,25},{9,1},{18,26},{10,2},{19,27},{11,3},{20,28},... | collective-permute-start | bytes 2064392 | tf_op jit(solution)/shard_map/ppermute | solution.py:356
  159.7 2.8 copy-start.17
  159.7 14.6 %collective-permute-start.19 = (bf16[192,1792]{1,0:T(8,128)(2,1)S(1)}, bf16[192,1792]{1,0:T(8,128)(2,1)S(1)}, u32[]{:S(2)}, u32[]{:S(2)}) collective-permute-start(bf16[192,1792]{1,0:T(8,128)(2,1)S(1)} %get-tuple-element.126), channel_id=1, source_target_pairs={{0,8},{24,16},{1,9},{25,17},{2,10},{26,18},{3,11},{27,19},{4,12},{... | collective-permute-start | bytes 2064392 | tf_op jit(solution)/shard_map/ppermute | solution.py:356
  161.6 13.6 %collective-permute-start.18 = (bf16[192,1792]{1,0:T(8,128)(2,1)S(1)}, bf16[192,1792]{1,0:T(8,128)(2,1)S(1)}, u32[]{:S(2)}, u32[]{:S(2)}) collective-permute-start(bf16[192,1792]{1,0:T(8,128)(2,1)S(1)} %add_convert_fusion.9.refs_0_), channel_id=1, source_target_pairs={{8,16},{16,8},{9,17},{17,9},{10,18},{18,10},{11,19},{19,11},{12,20... | collective-permute-start | bytes 2064392 | tf_op jit(solution)/shard_map/ppermute | solution.py:356
  162.5 23.6 %collective-permute-start.22 = (bf16[192,1792]{1,0:T(8,128)(2,1)S(1)}, bf16[192,1792]{1,0:T(8,128)(2,1)S(1)}, u32[]{:S(2)}, u32[]{:S(2)}) collective-permute-start(bf16[192,1792]{1,0:T(8,128)(2,1)S(1)} %add_convert_fusion.8), channel_id=1, source_target_pairs={{16,24},{8,0},{17,25},{9,1},{18,26},{10,2},{19,27},{11,3},{20,28},... | collective-permute-start | bytes 2064392 | tf_op jit(solution)/shard_map/ppermute | solution.py:356
  174.5 23.7 %collective-permute-start.23 = (bf16[192,1792]{1,0:T(8,128)(2,1)S(1)}, bf16[192,1792]{1,0:T(8,128)(2,1)S(1)}, u32[]{:S(2)}, u32[]{:S(2)}) collective-permute-start(bf16[192,1792]{1,0:T(8,128)(2,1)S(1)} %add_convert_fusion.7.refs_0_), channel_id=1, source_target_pairs={{8,16},{16,8},{9,17},{17,9},{10,18},{18,10},{11,19},{19,11},{12,20... | collective-permute-start | bytes 2064392 | tf_op jit(solution)/shard_map/ppermute | solution.py:356
  175.4 23.8 %collective-permute-start.24 = (bf16[192,1792]{1,0:T(8,128)(2,1)S(1)}, bf16[192,1792]{1,0:T(8,128)(2,1)S(1)}, u32[]{:S(2)}, u32[]{:S(2)}) collective-permute-start(bf16[192,1792]{1,0:T(8,128)(2,1)S(1)} %add_convert_fusion.6), channel_id=1, source_target_pairs={{16,24},{8,0},{17,25},{9,1},{18,26},{10,2},{19,27},{11,3},{20,28},... | collective-permute-start | bytes 2064392 | tf_op jit(solution)/shard_map/ppermute | solution.py:356
  201.6 3.1 %collective-permute-start.25 = (bf16[192,3584]{1,0:T(8,128)(2,1)S(1)}, bf16[192,3584]{1,0:T(8,128)(2,1)S(1)}, u32[]{:S(2)}, u32[]{:S(2)}) collective-permute-start(bf16[192,3584]{1,0:T(8,128)(2,1)S(1)} %get-tuple-element.131), channel_id=1, source_target_pairs={{0,1},{1,0},{2,3},{3,2},{4,5},{5,4},{6,7},{7,6},{8,9},{9,8},{10,11... | collective-permute-start | bytes 4128776 | tf_op jit(solution)/shard_map/ppermute | solution.py:359
  201.6 21.3 %collective-permute-start.26 = (bf16[192,1792]{1,0:T(8,128)(2,1)}, bf16[192,1792]{1,0:T(8,128)(2,1)S(1)}, u32[]{:S(2)}, u32[]{:S(2)}) collective-permute-start(bf16[192,1792]{1,0:T(8,128)(2,1)} %add_convert_fusion.5), channel_id=1, source_target_pairs={{16,24},{8,0},{17,25},{9,1},{18,26},{10,2},{19,27},{11,3},{20,28},... | collective-permute-start | bytes 2064392 | tf_op jit(solution)/shard_map/ppermute | solution.py:356
  205.1 17.8 %copy-start.16 = (f32[192,1792]{1,0:T(8,128)S(1)}, f32[192,1792]{1,0:T(8,128)}, u32[]{:S(2)}) copy-start(f32[192,1792]{1,0:T(8,128)} %copy-done.15) | copy-start | bytes 4128772
  205.1 19.6 %collective-permute-start.27 = (bf16[96,3584]{1,0:T(8,128)(2,1)S(1)}, bf16[96,3584]{1,0:T(8,128)(2,1)S(1)}, u32[]{:S(2)}, u32[]{:S(2)}) collective-permute-start(bf16[96,3584]{1,0:T(8,128)(2,1)S(1)} %get-tuple-element.151), channel_id=1, source_target_pairs={{0,6},{1,7},{2,4},{3,5},{4,2},{5,3},{6,0},{7,1},{8,14},{9,15},{10,... | collective-permute-start | bytes 2064392 | tf_op jit(solution)/shard_map/ppermute | solution.py:359
  235.0 13.9 %collective-permute-start.28 = (bf16[192,3584]{1,0:T(8,128)(2,1)S(1)}, bf16[192,3584]{1,0:T(8,128)(2,1)S(1)}, u32[]{:S(2)}, u32[]{:S(2)}) collective-permute-start(bf16[192,3584]{1,0:T(8,128)(2,1)S(1)} %get-tuple-element.141), channel_id=1, source_target_pairs={{0,1},{1,0},{2,3},{3,2},{4,5},{5,4},{6,7},{7,6},{8,9},{9,8},{10,11... | collective-permute-start | bytes 4128776 | tf_op jit(solution)/shard_map/ppermute | solution.py:359
  250.1 19.5 %collective-permute-start.30 = (bf16[96,3584]{1,0:T(8,128)(2,1)S(1)}, bf16[96,3584]{1,0:T(8,128)(2,1)S(1)}, u32[]{:S(2)}, u32[]{:S(2)}) collective-permute-start(bf16[96,3584]{1,0:T(8,128)(2,1)S(1)} %get-tuple-element.149), channel_id=1, source_target_pairs={{0,4},{1,5},{2,6},{3,7},{4,0},{5,1},{6,2},{7,3},{8,12},{9,13},{10,... | collective-permute-start | bytes 2064392 | tf_op jit(solution)/shard_map/ppermute | solution.py:359
  251.5 18.1 %collective-permute-start.29 = (bf16[96,3584]{1,0:T(8,128)(2,1)}, bf16[96,3584]{1,0:T(8,128)(2,1)S(1)}, u32[]{:S(2)}, u32[]{:S(2)}) collective-permute-start(bf16[96,3584]{1,0:T(8,128)(2,1)} %get-tuple-element.148), channel_id=1, source_target_pairs={{0,2},{1,3},{2,0},{3,1},{4,6},{5,7},{6,4},{7,5},{8,10},{9,11},{10,... | collective-permute-start | bytes 2064392 | tf_op jit(solution)/shard_map/ppermute | solution.py:359
  (7 other events, 12.3 us)
Sparse Core Ops, SparseCore 0:
  9.9 44.9 all-gather.2
  56.7 42.2 all-gather.4

commit v11 on v9

--- a/solution.py
+++ b/solution.py
@@ -10,7 +10,7 @@
 GELU_SCALE = 0.7978845608
 GELU_CUBIC = 0.044715
 F32, BF16 = jnp.float32, jnp.bfloat16
-VMEM_LIMIT = 48 * 1024 * 1024
+VMEM_LIMIT = 40 * 1024 * 1024
 UNITS, AHEAD = 7, 3
 
 

time: 266 us -> 264 us (level)
  Pallas kernels: 109 us -> 104 us
  waiting for transfers between devices: 65 us -> 68.8 us
  other arithmetic: 17.2 us -> 14.5 us
    pallas_call x19, Pallas kernels: 109 us -> 104 us  [call(): pl.pallas_call(kernel, grid_spec=pltpu.PrefetchScalarGridSpec(num_scalar_...]
    ppermute x24, waiting for transfers between devices: 41.4 us -> 44.7 us  [send(): return lax.ppermute(value, 'row', pairs)]
    convert_element_type x18, other arithmetic: 15.4 us -> 12.7 us  [add_bf16(): return (left.astype(F32) + right.astype(F32)).astype(BF16)]
    unnamed x44 -> x50, local copies, waits for them, and re-layouts: 2.75 us -> 5.32 us
  transfers between devices with their start and end apart: 35 -> 35, of which waited for: 11 -> 12; matrix products, arithmetic and copies ran while one was open for 6% -> 5% of each run, Pallas kernels for 37% -> 36%
where the time goes in v11:
time: 264 us; the launch traced here: 263 us
  Pallas kernels  104 us (39%)
  waiting for transfers between devices  68.8 us (26%)
  starting transfers between devices  55.4 us (21%)
  between operations  14.8 us (6%)
  other arithmetic  14.5 us (5%)
  local copies, waits for them, and re-layouts  5.33 us (2%)
    pallas_call x19, Pallas kernels, call(): pl.pallas_call(kernel, grid_spec=pltpu.PrefetchScalarGridSpec(num_scalar_...  104 us
    ppermute x24, starting transfers between devices, send(): return lax.ppermute(value, 'row', pairs)  48.7 us
    ppermute x24, waiting for transfers between devices, send(): return lax.ppermute(value, 'row', pairs)  44.7 us
    all_gather x1, waiting for transfers between devices, local(): held['pre'] = lax.all_gather(tokens, 'col', axis=0, tiled=True)  16.3 us
    convert_element_type x18, other arithmetic, add_bf16(): return (left.astype(F32) + right.astype(F32)).astype(BF16)  12.7 us
    unnamed x50, local copies, waits for them, and re-layouts  5.32 us
  transfers between devices with their start and end apart: 35, of which 12 were waited for; matrix products, arithmetic and copies ran while one was open for 5% of the time, Pallas kernels for 36%

profile of v11, /device:TPU:0, one launch (start us, length us, event | category | flops | bytes accessed | tf_op | source)
XLA Modules:
  0.0 262.9 jit_solution(12948882659400706603)
XLA Ops:
  8.5 2.0 collective-permute-done.refs_1_
  11.0 6.3 %shard_map.84 = bf16[192,1792]{1,0:T(8,128)(2,1)S(1)} custom-call(s32[2]{0:T(128)S(1)} %pad_add_fusion.s, bf16[96,3584]{1,0:T(8,128)(2,1)S(1)} %copy-done.2, bf16[96,3584]{1,0:T(8,128)(2,1)S(1)} %collective-permute-done.refs_1_, bf16[3584,1792]{1,0:T(8,128)(2,1)} %refs_1_.9), custom_call_target="tpu_custom_call" | custom-call | flops 38535168 | bytes 222208 | tf_op jit(solution)/shard_map/pallas_call | solution.py:30
  17.3 4.7 %collective-permute-start.1 = (bf16[192,1792]{1,0:T(8,128)(2,1)S(1)}, bf16[192,1792]{1,0:T(8,128)(2,1)S(1)}, u32[]{:S(2)}, u32[]{:S(2)}) collective-permute-start(bf16[192,1792]{1,0:T(8,128)(2,1)S(1)} %shard_map.84), channel_id=1, source_target_pairs={{0,8},{24,16},{1,9},{25,17},{2,10},{26,18},{3,11},{27,19},{4,12},{... | collective-permute-start | bytes 2064392 | tf_op jit(solution)/shard_map/ppermute | solution.py:336
  22.0 7.3 %shard_map.85 = bf16[192,1792]{1,0:T(8,128)(2,1)S(1)} custom-call(s32[2]{0:T(128)S(1)} %pad_add_fusion.s, bf16[96,3584]{1,0:T(8,128)(2,1)S(1)} %copy-done.3, bf16[96,3584]{1,0:T(8,128)(2,1)S(1)} %collective-permute-done.2.refs_1_, bf16[1792,3584]{1,0:T(8,128)(2,1)} %refs_1_.7), custom_call_target="tpu_custom_call" | custom-call | flops 38535168 | bytes 222208 | tf_op jit(solution)/shard_map/pallas_call | solution.py:30
  29.3 2.3 collective-permute-start.5
  31.6 6.1 %collective-permute-done.1 = bf16[192,1792]{1,0:T(8,128)(2,1)S(1)} collective-permute-done((bf16[192,1792]{1,0:T(8,128)(2,1)S(1)}, bf16[192,1792]{1,0:T(8,128)(2,1)S(1)}, u32[]{:S(2)}, u32[]{:S(2)}) %collective-permute-start.1) | collective-permute-done | bytes 688160 | tf_op jit(solution)/shard_map/ppermute | solution.py:336
  38.6 16.3 %all-gather.3.cloned.1.call-done.refs_0_.tok_ref = bf16[768,3584]{1,0:T(8,128)(2,1)} async-done(((bf16[96,3584]{1,0:T(8,128)(2,1)}), bf16[768,3584]{1,0:T(8,128)(2,1)}) %all-gather.3.cloned.1.call-update) | async-done | bytes 5505040 | tf_op jit(solution)/shard_map/all_gather | solution.py:414
  54.9 2.6 copy-done
  57.4 6.3 %shard_map.86 = bf16[192,1792]{1,0:T(8,128)(2,1)S(1)} custom-call(s32[2]{0:T(128)S(1)} %pad_add_fusion.s, bf16[768,3584]{1,0:T(8,128)(2,1)S(1)} %copy-done, bf16[3584,1792]{1,0:T(8,128)(2,1)} %refs_1_.9), custom_call_target="tpu_custom_call" | custom-call | flops 38535168 | bytes 222208 | tf_op jit(solution)/shard_map/pallas_call | solution.py:30
  63.7 3.4 %collective-permute-start.3 = (bf16[192,1792]{1,0:T(8,128)(2,1)S(1)}, bf16[192,1792]{1,0:T(8,128)(2,1)S(1)}, u32[]{:S(2)}, u32[]{:S(2)}) collective-permute-start(bf16[192,1792]{1,0:T(8,128)(2,1)S(1)} %shard_map.86), channel_id=1, source_target_pairs={{0,8},{24,16},{1,9},{25,17},{2,10},{26,18},{3,11},{27,19},{4,12},{... | collective-permute-start | bytes 2064392 | tf_op jit(solution)/shard_map/ppermute | solution.py:336
  69.3 1.3 collective-permute-start.8
  70.6 9.1 %shard_map.87 = (bf16[192,1792]{1,0:T(8,128)(2,1)S(1)}, bf16[192,1792]{1,0:T(8,128)(2,1)}) custom-call(s32[2]{0:T(128)S(1)} %pad_add_fusion.s, bf16[768,3584]{1,0:T(8,128)(2,1)S(1)} %copy-done, bf16[3584,1792]{1,0:T(8,128)(2,1)} %refs_1_.9), custom_call_target="tpu_custom_call" | custom-call | flops 77070336 | bytes 243712 | tf_op jit(solution)/shard_map/pallas_call | solution.py:30
  79.8 4.6 %collective-permute-start.6 = (bf16[192,1792]{1,0:T(8,128)(2,1)S(1)}, bf16[192,1792]{1,0:T(8,128)(2,1)S(1)}, u32[]{:S(2)}, u32[]{:S(2)}) collective-permute-start(bf16[192,1792]{1,0:T(8,128)(2,1)S(1)} %get-tuple-element.103), channel_id=1, source_target_pairs={{0,8},{24,16},{1,9},{25,17},{2,10},{26,18},{3,11},{27,19},{4,12},{... | collective-permute-start | bytes 2064392 | tf_op jit(solution)/shard_map/ppermute | solution.py:336
  85.6 1.7 collective-permute-start.11
  89.6 1.8 shard_map.88
  91.4 6.3 %collective-permute-start.10 = (bf16[192,1792]{1,0:T(8,128)(2,1)}, bf16[192,1792]{1,0:T(8,128)(2,1)}, u32[]{:S(2)}, u32[]{:S(2)}) collective-permute-start(bf16[192,1792]{1,0:T(8,128)(2,1)} %get-tuple-element.111), channel_id=1, source_target_pairs={{0,8},{24,16},{1,9},{25,17},{2,10},{26,18},{3,11},{27,19},{4,12},{... | collective-permute-start | bytes 2064392 | tf_op jit(solution)/shard_map/ppermute | solution.py:336
  97.7 2.6 collective-permute-done.6
  101.3 1.5 collective-permute-start.9
  102.8 2.6 copy-done.1
  105.4 11.0 %shard_map.89 = (bf16[192,1792]{1,0:T(8,128)(2,1)S(1)}, bf16[192,1792]{1,0:T(8,128)(2,1)S(1)}, bf16[192,1792]{1,0:T(8,128)(2,1)S(1)}) custom-call(s32[2]{0:T(128)S(1)} %pad_add_fusion.s, bf16[768,3584]{1,0:T(8,128)(2,1)S(1)} %copy-done.1, bf16[1792,3584]{1,0:T(8,128)(2,1)} %refs_1_.7), custom_call_target="tpu_custom_call" | custom-call | flops 115605504 | bytes 265216 | tf_op jit(solution)/shard_map/pallas_call | solution.py:30
  116.4 1.4 add_convert_fusion.14
  117.9 2.1 shard_map.90
  120.0 1.4 collective-permute-start.13
  121.4 6.4 %collective-permute-start.14 = (bf16[192,1792]{1,0:T(8,128)(2,1)S(1)}, bf16[192,1792]{1,0:T(8,128)(2,1)S(1)}, u32[]{:S(2)}, u32[]{:S(2)}) collective-permute-start(bf16[192,1792]{1,0:T(8,128)(2,1)S(1)} %get-tuple-element.117), channel_id=1, source_target_pairs={{0,8},{24,16},{1,9},{25,17},{2,10},{26,18},{3,11},{27,19},{4,12},{... | collective-permute-start | bytes 2064392 | tf_op jit(solution)/shard_map/ppermute | solution.py:336
  127.8 1.5 add_convert_fusion.13.refs_0_
  130.0 1.3 add_convert_fusion.12
  131.3 1.3 collective-permute-start.17
  132.6 9.5 %collective-permute-done.13.refs_2_ = bf16[192,1792]{1,0:T(8,128)(2,1)S(1)} collective-permute-done((bf16[192,1792]{1,0:T(8,128)(2,1)S(1)}, bf16[192,1792]{1,0:T(8,128)(2,1)S(1)}, u32[]{:S(2)}, u32[]{:S(2)}) %collective-permute-start.13) | collective-permute-done | bytes 688160 | tf_op jit(solution)/shard_map/ppermute | solution.py:336
  142.1 3.1 %shard_map.91 = (bf16[768,1792]{1,0:T(8,128)(2,1)S(1)}, f32[192,1792]{1,0:T(8,128)S(1)}) custom-call(s32[2]{0:T(128)S(1)} %pad_add_fusion.s, f32[1,1792]{1,0:T(1,128)S(1)} %reshape.14.bias_ref, bf16[192,1792]{1,0:T(8,128)(2,1)} %add_convert_fusion.17.refs_0_, bf16[192,1792]{1,0:T(8,128)(2,1)} %collective-permute-done.11.refs_1_, ...), custom_call_target="tpu_custom_call", output_to_operand_aliasing={{0}: (5, {})} | custom-call | flops 10321920 | bytes 4128768 | tf_op jit(solution)/shard_map/pallas_call | solution.py:30
  145.2 1.5 collective-permute-start.15
  148.8 1.3 collective-permute-start.21
  150.1 6.7 %collective-permute-done.17.refs_2_ = bf16[192,1792]{1,0:T(8,128)(2,1)S(1)} collective-permute-done((bf16[192,1792]{1,0:T(8,128)(2,1)S(1)}, bf16[192,1792]{1,0:T(8,128)(2,1)S(1)}, u32[]{:S(2)}, u32[]{:S(2)}) %collective-permute-start.17) | collective-permute-done | bytes 688160 | tf_op jit(solution)/shard_map/ppermute | solution.py:336
  156.8 3.1 %shard_map.92 = (bf16[768,1792]{1,0:T(8,128)(2,1)S(1)}, f32[192,1792]{1,0:T(8,128)S(1)}) custom-call(s32[2]{0:T(128)S(1)} %pad_add_fusion.s, f32[1,1792]{1,0:T(1,128)S(1)} %reshape.14.bias_ref, bf16[192,1792]{1,0:T(8,128)(2,1)} %add_convert_fusion.15.refs_0_, bf16[192,1792]{1,0:T(8,128)(2,1)} %collective-permute-done.9.refs_1_, ...), custom_call_target="tpu_custom_call", output_to_operand_aliasing={{0}: (5, {})} | custom-call | flops 10321920 | bytes 4128768 | tf_op jit(solution)/shard_map/pallas_call | solution.py:30
  159.9 1.7 collective-permute-start.19
  162.7 1.3 collective-permute-start.22
  164.0 7.6 %collective-permute-done.21.refs_2_ = bf16[192,1792]{1,0:T(8,128)(2,1)S(1)} collective-permute-done((bf16[192,1792]{1,0:T(8,128)(2,1)S(1)}, bf16[192,1792]{1,0:T(8,128)(2,1)S(1)}, u32[]{:S(2)}, u32[]{:S(2)}) %collective-permute-start.21) | collective-permute-done | bytes 688160 | tf_op jit(solution)/shard_map/ppermute | solution.py:336
  171.6 1.8 shard_map.93
  174.4 1.3 collective-permute-start.24
  175.7 10.6 %collective-permute-done.22.refs_2_ = bf16[192,1792]{1,0:T(8,128)(2,1)S(1)} collective-permute-done((bf16[192,1792]{1,0:T(8,128)(2,1)S(1)}, bf16[192,1792]{1,0:T(8,128)(2,1)S(1)}, u32[]{:S(2)}, u32[]{:S(2)}) %collective-permute-start.22) | collective-permute-done | bytes 688160 | tf_op jit(solution)/shard_map/ppermute | solution.py:336
  187.3 8.5 %shard_map.95 = (bf16[192,3584]{1,0:T(8,128)(2,1)S(1)}, bf16[192,3584]{1,0:T(8,128)(2,1)S(1)}) custom-call(s32[2]{0:T(128)S(1)} %pad_add_fusion.s, bf16[768,1792]{1,0:T(8,128)(2,1)S(1)} %get-tuple-element.124.refs_0_.refs_3_, bf16[3584,1792]{1,0:T(8,128)(2,1)} %refs_1_.9), custom_call_target="tpu_custom_call" | custom-call | flops 4932501504 | bytes 14221312 | tf_op jit(solution)/shard_map/pallas_call | solution.py:30
  196.0 1.7 collective-permute-done.24.refs_2_
  198.7 1.3 collective-permute-start.26
  200.0 1.8 collective-permute-done.25
  202.2 1.6 collective-permute-start.27
  203.7 15.2 %shard_map.97 = f32[1792,3584]{1,0:T(8,128)} custom-call(s32[2]{0:T(128)S(1)} %pad_add_fusion.s, bf16[768,1792]{1,0:T(8,128)(2,1)S(1)} %get-tuple-element.134.act_ref, bf16[768,3584]{1,0:T(8,128)(2,1)S(1)} %bitcast.5), custom_call_target="tpu_custom_call" | custom-call | flops 9865003008 | bytes 33947648 | tf_op jit(solution)/shard_map/pallas_call | solution.py:30
  221.3 8.9 %shard_map.100 = (bf16[192,3584]{1,0:T(8,128)(2,1)S(1)}, bf16[192,3584]{1,0:T(8,128)(2,1)S(1)}) custom-call(s32[2]{0:T(128)S(1)} %pad_add_fusion.s, bf16[768,1792]{1,0:T(8,128)(2,1)S(1)} %get-tuple-element.143.refs_0_.grad_ref, bf16[3584,1792]{1,0:T(8,128)(2,1)} %refs_1_.9), custom_call_target="tpu_custom_call" | custom-call | flops 4932501504 | bytes 14221312 | tf_op jit(solution)/shard_map/pallas_call | solution.py:30
  231.3 2.7 %collective-permute-done.31 = f32[1,1792]{1,0:T(1,128)S(1)} collective-permute-done((f32[1,1792]{1,0:T(1,128)S(1)}, f32[1,1792]{1,0:T(1,128)S(1)}, u32[]{:S(2)}, u32[]{:S(2)}) %collective-permute-start.31) | collective-permute-done | bytes 7200 | tf_op jit(solution)/shard_map/ppermute | solution.py:444
  238.2 15.6 %shard_map.101.refs_0_ = f32[3584,1792]{1,0:T(8,128)} custom-call(s32[2]{0:T(128)S(1)} %pad_add_fusion.s, bf16[768,3584]{1,0:T(8,128)(2,1)S(1)} %bitcast.3, bf16[768,1792]{1,0:T(8,128)(2,1)S(1)} %get-tuple-element.143.refs_0_.grad_ref), custom_call_target="tpu_custom_call" | custom-call | flops 9865003008 | bytes 33947648 | tf_op jit(solution)/shard_map/pallas_call | solution.py:30
  (119 shorter events, 26.8 us)
Async XLA Ops:
  7.2 47.7 %all-gather.3.cloned.1.call-start = ((), (), s32[]{:S(2)}) async-start(), calls=%async_computation | async-start | bytes 6193152 | tf_op jit(solution)/shard_map/all_gather | solution.py:414
  7.9 94.9 %all-gather.5.cloned.1.call-start = ((), (), s32[]{:S(2)}) async-start(), calls=%async_computation.1 | async-start | bytes 6193152 | tf_op jit(solution)/shard_map/all_gather | solution.py:415
  8.0 2.5 collective-permute-start
  10.5 11.5 %collective-permute-start.2 = (bf16[96,3584]{1,0:T(8,128)(2,1)S(1)}, bf16[96,3584]{1,0:T(8,128)(2,1)S(1)}, u32[]{:S(2)}, u32[]{:S(2)}) collective-permute-start(bf16[96,3584]{1,0:T(8,128)(2,1)S(1)} %copy-done.3), channel_id=1, source_target_pairs={{0,1},{1,0},{2,3},{3,2},{4,5},{5,4},{6,7},{7,6},{8,9},{9,8},{10,11... | collective-permute-start | bytes 2064392 | tf_op jit(solution)/shard_map/ppermute | solution.py:339
  17.3 20.4 %collective-permute-start.1 = (bf16[192,1792]{1,0:T(8,128)(2,1)S(1)}, bf16[192,1792]{1,0:T(8,128)(2,1)S(1)}, u32[]{:S(2)}, u32[]{:S(2)}) collective-permute-start(bf16[192,1792]{1,0:T(8,128)(2,1)S(1)} %shard_map.84), channel_id=1, source_target_pairs={{0,8},{24,16},{1,9},{25,17},{2,10},{26,18},{3,11},{27,19},{4,12},{... | collective-permute-start | bytes 2064392 | tf_op jit(solution)/shard_map/ppermute | solution.py:336
  29.3 9.3 %copy-start.20 = (f32[1792]{0:T(1024)S(1)}, f32[1792]{0:T(1024)}, u32[]{:S(2)}) copy-start(f32[1792]{0:T(1024)} %param.7) | copy-start | bytes 21508
  29.3 37.9 %collective-permute-start.5 = (bf16[192,1792]{1,0:T(8,128)(2,1)S(1)}, bf16[192,1792]{1,0:T(8,128)(2,1)}, u32[]{:S(2)}, u32[]{:S(2)}) collective-permute-start(bf16[192,1792]{1,0:T(8,128)(2,1)S(1)} %shard_map.85), channel_id=1, source_target_pairs={{0,8},{24,16},{1,9},{25,17},{2,10},{26,18},{3,11},{27,19},{4,12},{... | collective-permute-start | bytes 2064392 | tf_op jit(solution)/shard_map/ppermute | solution.py:336
  37.8 25.9 %copy-start.4 = (bf16[192,1792]{1,0:T(8,128)(2,1)}, bf16[192,1792]{1,0:T(8,128)(2,1)S(1)}, u32[]{:S(2)}) copy-start(bf16[192,1792]{1,0:T(8,128)(2,1)S(1)} %add_convert_fusion.20.refs_0_) | copy-start | bytes 2064388
  37.8 31.3 %collective-permute-start.4 = (bf16[192,1792]{1,0:T(8,128)(2,1)S(1)}, bf16[192,1792]{1,0:T(8,128)(2,1)S(1)}, u32[]{:S(2)}, u32[]{:S(2)}) collective-permute-start(bf16[192,1792]{1,0:T(8,128)(2,1)S(1)} %add_convert_fusion.20.refs_0_), channel_id=1, source_target_pairs={{8,16},{16,8},{9,17},{17,9},{10,18},{18,10},{11,19},{19,11},{12,20... | collective-permute-start | bytes 2064392 | tf_op jit(solution)/shard_map/ppermute | solution.py:336
  63.7 20.7 %collective-permute-start.3 = (bf16[192,1792]{1,0:T(8,128)(2,1)S(1)}, bf16[192,1792]{1,0:T(8,128)(2,1)S(1)}, u32[]{:S(2)}, u32[]{:S(2)}) collective-permute-start(bf16[192,1792]{1,0:T(8,128)(2,1)S(1)} %shard_map.86), channel_id=1, source_target_pairs={{0,8},{24,16},{1,9},{25,17},{2,10},{26,18},{3,11},{27,19},{4,12},{... | collective-permute-start | bytes 2064392 | tf_op jit(solution)/shard_map/ppermute | solution.py:336
  68.4 11.4 %copy-start.10 = (bf16[192,1792]{1,0:T(8,128)(2,1)}, bf16[192,1792]{1,0:T(8,128)(2,1)S(1)}, u32[]{:S(2)}) copy-start(bf16[192,1792]{1,0:T(8,128)(2,1)S(1)} %add_convert_fusion.19.refs_0_) | copy-start | bytes 2064388
  68.4 18.8 %collective-permute-start.7 = (bf16[192,1792]{1,0:T(8,128)(2,1)S(1)}, bf16[192,1792]{1,0:T(8,128)(2,1)S(1)}, u32[]{:S(2)}, u32[]{:S(2)}) collective-permute-start(bf16[192,1792]{1,0:T(8,128)(2,1)S(1)} %add_convert_fusion.19.refs_0_), channel_id=1, source_target_pairs={{8,16},{16,8},{9,17},{17,9},{10,18},{18,10},{11,19},{19,11},{12,20... | collective-permute-start | bytes 2064392 | tf_op jit(solution)/shard_map/ppermute | solution.py:336
  69.2 10.6 %copy-start.6 = (bf16[192,1792]{1,0:T(8,128)(2,1)}, bf16[192,1792]{1,0:T(8,128)(2,1)S(1)}, u32[]{:S(2)}) copy-start(bf16[192,1792]{1,0:T(8,128)(2,1)S(1)} %collective-permute-done.4.refs_1_) | copy-start | bytes 2064388
  69.3 20.3 %collective-permute-start.8 = (bf16[192,1792]{1,0:T(8,128)(2,1)S(1)}, bf16[192,1792]{1,0:T(8,128)(2,1)S(1)}, u32[]{:S(2)}, u32[]{:S(2)}) collective-permute-start(bf16[192,1792]{1,0:T(8,128)(2,1)S(1)} %add_convert_fusion.18), channel_id=1, source_target_pairs={{16,24},{8,0},{17,25},{9,1},{18,26},{10,2},{19,27},{11,3},{20,28},... | collective-permute-start | bytes 2064392 | tf_op jit(solution)/shard_map/ppermute | solution.py:336
  79.8 20.4 %copy-start.8 = (bf16[192,1792]{1,0:T(8,128)(2,1)}, bf16[192,1792]{1,0:T(8,128)(2,1)S(1)}, u32[]{:S(2)}) copy-start(bf16[192,1792]{1,0:T(8,128)(2,1)S(1)} %get-tuple-element.103) | copy-start | bytes 2064388
  79.8 20.4 %collective-permute-start.6 = (bf16[192,1792]{1,0:T(8,128)(2,1)S(1)}, bf16[192,1792]{1,0:T(8,128)(2,1)S(1)}, u32[]{:S(2)}, u32[]{:S(2)}) collective-permute-start(bf16[192,1792]{1,0:T(8,128)(2,1)S(1)} %get-tuple-element.103), channel_id=1, source_target_pairs={{0,8},{24,16},{1,9},{25,17},{2,10},{26,18},{3,11},{27,19},{4,12},{... | collective-permute-start | bytes 2064392 | tf_op jit(solution)/shard_map/ppermute | solution.py:336
  85.6 30.8 %collective-permute-start.11 = (bf16[192,1792]{1,0:T(8,128)(2,1)}, bf16[192,1792]{1,0:T(8,128)(2,1)}, u32[]{:S(2)}, u32[]{:S(2)}) collective-permute-start(bf16[192,1792]{1,0:T(8,128)(2,1)} %add_convert_fusion.17.refs_0_), channel_id=1, source_target_pairs={{8,16},{16,8},{9,17},{17,9},{10,18},{18,10},{11,19},{19,11},{12,20... | collective-permute-start | bytes 2064392 | tf_op jit(solution)/shard_map/ppermute | solution.py:336
  88.3 29.4 %collective-permute-start.12 = (bf16[192,1792]{1,0:T(8,128)(2,1)}, bf16[192,1792]{1,0:T(8,128)(2,1)}, u32[]{:S(2)}, u32[]{:S(2)}) collective-permute-start(bf16[192,1792]{1,0:T(8,128)(2,1)} %add_convert_fusion.16), channel_id=1, source_target_pairs={{16,24},{8,0},{17,25},{9,1},{18,26},{10,2},{19,27},{11,3},{20,28},... | collective-permute-start | bytes 2064392 | tf_op jit(solution)/shard_map/ppermute | solution.py:336
  91.4 9.9 %copy-start.18 = (f32[192,1792]{1,0:T(8,128)}, f32[192,1792]{1,0:T(8,128)S(1)}, u32[]{:S(2)}) copy-start(f32[192,1792]{1,0:T(8,128)S(1)} %get-tuple-element.95.slope_ref) | copy-start | bytes 4128772
  91.4 36.3 %collective-permute-start.10 = (bf16[192,1792]{1,0:T(8,128)(2,1)}, bf16[192,1792]{1,0:T(8,128)(2,1)}, u32[]{:S(2)}, u32[]{:S(2)}) collective-permute-start(bf16[192,1792]{1,0:T(8,128)(2,1)} %get-tuple-element.111), channel_id=1, source_target_pairs={{0,8},{24,16},{1,9},{25,17},{2,10},{26,18},{3,11},{27,19},{4,12},{... | collective-permute-start | bytes 2064392 | tf_op jit(solution)/shard_map/ppermute | solution.py:336
  101.3 28.7 %collective-permute-start.9 = (bf16[192,1792]{1,0:T(8,128)(2,1)}, bf16[192,1792]{1,0:T(8,128)(2,1)}, u32[]{:S(2)}, u32[]{:S(2)}) collective-permute-start(bf16[192,1792]{1,0:T(8,128)(2,1)} %add_convert_fusion.15.refs_0_), channel_id=1, source_target_pairs={{8,16},{16,8},{9,17},{17,9},{10,18},{18,10},{11,19},{19,11},{12,20... | collective-permute-start | bytes 2064392 | tf_op jit(solution)/shard_map/ppermute | solution.py:336
  105.4 12.4 %copy-start.19 = (f32[192,1792]{1,0:T(8,128)S(1)}, f32[192,1792]{1,0:T(8,128)}, u32[]{:S(2)}) copy-start(f32[192,1792]{1,0:T(8,128)} %copy-done.18) | copy-start | bytes 4128772
  119.9 10.0 %copy-start.9 = (bf16[192,1792]{1,0:T(8,128)(2,1)S(1)}, bf16[192,1792]{1,0:T(8,128)(2,1)}, u32[]{:S(2)}) copy-start(bf16[192,1792]{1,0:T(8,128)(2,1)} %copy-done.8) | copy-start | bytes 2064388
  120.0 22.1 %collective-permute-start.13 = (bf16[192,1792]{1,0:T(8,128)(2,1)S(1)}, bf16[192,1792]{1,0:T(8,128)(2,1)S(1)}, u32[]{:S(2)}, u32[]{:S(2)}) collective-permute-start(bf16[192,1792]{1,0:T(8,128)(2,1)S(1)} %add_convert_fusion.14), channel_id=1, source_target_pairs={{16,24},{8,0},{17,25},{9,1},{18,26},{10,2},{19,27},{11,3},{20,28},... | collective-permute-start | bytes 2064392 | tf_op jit(solution)/shard_map/ppermute | solution.py:336
  121.4 25.3 %collective-permute-start.14 = (bf16[192,1792]{1,0:T(8,128)(2,1)S(1)}, bf16[192,1792]{1,0:T(8,128)(2,1)S(1)}, u32[]{:S(2)}, u32[]{:S(2)}) collective-permute-start(bf16[192,1792]{1,0:T(8,128)(2,1)S(1)} %get-tuple-element.117), channel_id=1, source_target_pairs={{0,8},{24,16},{1,9},{25,17},{2,10},{26,18},{3,11},{27,19},{4,12},{... | collective-permute-start | bytes 2064392 | tf_op jit(solution)/shard_map/ppermute | solution.py:336
  129.2 18.3 %collective-permute-start.16 = (bf16[192,1792]{1,0:T(8,128)(2,1)S(1)}, bf16[192,1792]{1,0:T(8,128)(2,1)S(1)}, u32[]{:S(2)}, u32[]{:S(2)}) collective-permute-start(bf16[192,1792]{1,0:T(8,128)(2,1)S(1)} %add_convert_fusion.13.refs_0_), channel_id=1, source_target_pairs={{8,16},{16,8},{9,17},{17,9},{10,18},{18,10},{11,19},{19,11},{12,20... | collective-permute-start | bytes 2064392 | tf_op jit(solution)/shard_map/ppermute | solution.py:336
  131.3 25.6 %collective-permute-start.17 = (bf16[192,1792]{1,0:T(8,128)(2,1)S(1)}, bf16[192,1792]{1,0:T(8,128)(2,1)S(1)}, u32[]{:S(2)}, u32[]{:S(2)}) collective-permute-start(bf16[192,1792]{1,0:T(8,128)(2,1)S(1)} %add_convert_fusion.12), channel_id=1, source_target_pairs={{16,24},{8,0},{17,25},{9,1},{18,26},{10,2},{19,27},{11,3},{20,28},... | collective-permute-start | bytes 2064392 | tf_op jit(solution)/shard_map/ppermute | solution.py:336
  145.2 16.4 %collective-permute-start.15 = (bf16[192,1792]{1,0:T(8,128)(2,1)S(1)}, bf16[192,1792]{1,0:T(8,128)(2,1)S(1)}, u32[]{:S(2)}, u32[]{:S(2)}) collective-permute-start(bf16[192,1792]{1,0:T(8,128)(2,1)S(1)} %get-tuple-element.121), channel_id=1, source_target_pairs={{0,8},{24,16},{1,9},{25,17},{2,10},{26,18},{3,11},{27,19},{4,12},{... | collective-permute-start | bytes 2064392 | tf_op jit(solution)/shard_map/ppermute | solution.py:336
  146.8 15.7 %collective-permute-start.20 = (bf16[192,1792]{1,0:T(8,128)(2,1)S(1)}, bf16[192,1792]{1,0:T(8,128)(2,1)S(1)}, u32[]{:S(2)}, u32[]{:S(2)}) collective-permute-start(bf16[192,1792]{1,0:T(8,128)(2,1)S(1)} %add_convert_fusion.11.refs_0_), channel_id=1, source_target_pairs={{8,16},{16,8},{9,17},{17,9},{10,18},{18,10},{11,19},{19,11},{12,20... | collective-permute-start | bytes 2064392 | tf_op jit(solution)/shard_map/ppermute | solution.py:336
  148.8 22.7 %collective-permute-start.21 = (bf16[192,1792]{1,0:T(8,128)(2,1)S(1)}, bf16[192,1792]{1,0:T(8,128)(2,1)S(1)}, u32[]{:S(2)}, u32[]{:S(2)}) collective-permute-start(bf16[192,1792]{1,0:T(8,128)(2,1)S(1)} %add_convert_fusion.10), channel_id=1, source_target_pairs={{16,24},{8,0},{17,25},{9,1},{18,26},{10,2},{19,27},{11,3},{20,28},... | collective-permute-start | bytes 2064392 | tf_op jit(solution)/shard_map/ppermute | solution.py:336
  159.9 13.4 %collective-permute-start.19 = (bf16[192,1792]{1,0:T(8,128)(2,1)S(1)}, bf16[192,1792]{1,0:T(8,128)(2,1)S(1)}, u32[]{:S(2)}, u32[]{:S(2)}) collective-permute-start(bf16[192,1792]{1,0:T(8,128)(2,1)S(1)} %get-tuple-element.127), channel_id=1, source_target_pairs={{0,8},{24,16},{1,9},{25,17},{2,10},{26,18},{3,11},{27,19},{4,12},{... | collective-permute-start | bytes 2064392 | tf_op jit(solution)/shard_map/ppermute | solution.py:336
  161.8 12.5 %collective-permute-start.18 = (bf16[192,1792]{1,0:T(8,128)(2,1)S(1)}, bf16[192,1792]{1,0:T(8,128)(2,1)S(1)}, u32[]{:S(2)}, u32[]{:S(2)}) collective-permute-start(bf16[192,1792]{1,0:T(8,128)(2,1)S(1)} %add_convert_fusion.9.refs_0_), channel_id=1, source_target_pairs={{8,16},{16,8},{9,17},{17,9},{10,18},{18,10},{11,19},{19,11},{12,20... | collective-permute-start | bytes 2064392 | tf_op jit(solution)/shard_map/ppermute | solution.py:336
  162.7 23.6 %collective-permute-start.22 = (bf16[192,1792]{1,0:T(8,128)(2,1)S(1)}, bf16[192,1792]{1,0:T(8,128)(2,1)S(1)}, u32[]{:S(2)}, u32[]{:S(2)}) collective-permute-start(bf16[192,1792]{1,0:T(8,128)(2,1)S(1)} %add_convert_fusion.8), channel_id=1, source_target_pairs={{16,24},{8,0},{17,25},{9,1},{18,26},{10,2},{19,27},{11,3},{20,28},... | collective-permute-start | bytes 2064392 | tf_op jit(solution)/shard_map/ppermute | solution.py:336
  173.5 22.3 %collective-permute-start.23 = (bf16[192,1792]{1,0:T(8,128)(2,1)S(1)}, bf16[192,1792]{1,0:T(8,128)(2,1)S(1)}, u32[]{:S(2)}, u32[]{:S(2)}) collective-permute-start(bf16[192,1792]{1,0:T(8,128)(2,1)S(1)} %add_convert_fusion.7.refs_0_), channel_id=1, source_target_pairs={{8,16},{16,8},{9,17},{17,9},{10,18},{18,10},{11,19},{19,11},{12,20... | collective-permute-start | bytes 2064392 | tf_op jit(solution)/shard_map/ppermute | solution.py:336
  174.4 23.2 %collective-permute-start.24 = (bf16[192,1792]{1,0:T(8,128)(2,1)S(1)}, bf16[192,1792]{1,0:T(8,128)(2,1)S(1)}, u32[]{:S(2)}, u32[]{:S(2)}) collective-permute-start(bf16[192,1792]{1,0:T(8,128)(2,1)S(1)} %add_convert_fusion.6), channel_id=1, source_target_pairs={{16,24},{8,0},{17,25},{9,1},{18,26},{10,2},{19,27},{11,3},{20,28},... | collective-permute-start | bytes 2064392 | tf_op jit(solution)/shard_map/ppermute | solution.py:336
  195.8 7.9 %slice-start.2 = ((s8[5505024]{0:T(1024)(128)(4,1)}), s8[4194304]{0:T(1024)(128)(4,1)S(1)}, s32[]{:S(2)}) async-start(s8[5505024]{0:T(1024)(128)(4,1)} %bitcast.4), calls=%async_computation.4 | async-start | bytes 8388608
  197.7 6.1 %slice-start.3 = ((s8[5505024]{0:T(1024)(128)(4,1)}), s8[1310720]{0:T(1024)(128)(4,1)S(1)}, s32[]{:S(2)}) async-start(s8[5505024]{0:T(1024)(128)(4,1)} %bitcast.4), calls=%async_computation.5 | async-start | bytes 2621440
  198.6 3.2 %collective-permute-start.25 = (bf16[192,3584]{1,0:T(8,128)(2,1)S(1)}, bf16[192,3584]{1,0:T(8,128)(2,1)S(1)}, u32[]{:S(2)}, u32[]{:S(2)}) collective-permute-start(bf16[192,3584]{1,0:T(8,128)(2,1)S(1)} %get-tuple-element.132), channel_id=1, source_target_pairs={{0,1},{1,0},{2,3},{3,2},{4,5},{5,4},{6,7},{7,6},{8,9},{9,8},{10,11... | collective-permute-start | bytes 4128776 | tf_op jit(solution)/shard_map/ppermute | solution.py:339
  198.7 20.3 %collective-permute-start.26 = (bf16[192,1792]{1,0:T(8,128)(2,1)S(1)}, bf16[192,1792]{1,0:T(8,128)(2,1)S(1)}, u32[]{:S(2)}, u32[]{:S(2)}) collective-permute-start(bf16[192,1792]{1,0:T(8,128)(2,1)S(1)} %add_convert_fusion.5), channel_id=1, source_target_pairs={{16,24},{8,0},{17,25},{9,1},{18,26},{10,2},{19,27},{11,3},{20,28},... | collective-permute-start | bytes 2064392 | tf_op jit(solution)/shard_map/ppermute | solution.py:336
  202.1 16.8 %copy-start.15 = (f32[192,1792]{1,0:T(8,128)S(1)}, f32[192,1792]{1,0:T(8,128)}, u32[]{:S(2)}) copy-start(f32[192,1792]{1,0:T(8,128)} %copy-done.14) | copy-start | bytes 4128772
  202.2 18.4 %collective-permute-start.27 = (bf16[96,3584]{1,0:T(8,128)(2,1)S(1)}, bf16[96,3584]{1,0:T(8,128)(2,1)S(1)}, u32[]{:S(2)}, u32[]{:S(2)}) collective-permute-start(bf16[96,3584]{1,0:T(8,128)(2,1)S(1)} %get-tuple-element.153), channel_id=1, source_target_pairs={{0,6},{1,7},{2,4},{3,5},{4,2},{5,3},{6,0},{7,1},{8,14},{9,15},{10,... | collective-permute-start | bytes 2064392 | tf_op jit(solution)/shard_map/ppermute | solution.py:339
  220.6 17.6 %slice-start = ((s8[5505024]{0:T(1024)(128)(4,1)}), s8[4194304]{0:T(1024)(128)(4,1)S(1)}, s32[]{:S(2)}) async-start(s8[5505024]{0:T(1024)(128)(4,1)} %bitcast.2), calls=%async_computation.2 | async-start | bytes 8388608
  221.3 16.9 %slice-start.1 = ((s8[5505024]{0:T(1024)(128)(4,1)}), s8[1310720]{0:T(1024)(128)(4,1)S(1)}, s32[]{:S(2)}) async-start(s8[5505024]{0:T(1024)(128)(4,1)} %bitcast.2), calls=%async_computation.3 | async-start | bytes 2621440
  230.2 4.8 %collective-permute-start.28 = (bf16[192,3584]{1,0:T(8,128)(2,1)S(1)}, bf16[192,3584]{1,0:T(8,128)(2,1)S(1)}, u32[]{:S(2)}, u32[]{:S(2)}) collective-permute-start(bf16[192,3584]{1,0:T(8,128)(2,1)S(1)} %get-tuple-element.142), channel_id=1, source_target_pairs={{0,1},{1,0},{2,3},{3,2},{4,5},{5,4},{6,7},{7,6},{8,9},{9,8},{10,11... | collective-permute-start | bytes 4128776 | tf_op jit(solution)/shard_map/ppermute | solution.py:339
  230.3 3.7 %collective-permute-start.31 = (f32[1,1792]{1,0:T(1,128)S(1)}, f32[1,1792]{1,0:T(1,128)S(1)}, u32[]{:S(2)}, u32[]{:S(2)}) collective-permute-start(f32[1,1792]{1,0:T(1,128)S(1)} %add_add_fusion), channel_id=1, source_target_pairs={{0,8},{8,0},{16,24},{24,16},{1,9},{9,1},{17,25},{25,17},{2,10},{10... | collective-permute-start | bytes 21512 | tf_op jit(solution)/shard_map/ppermute | solution.py:444
  234.0 19.8 %collective-permute-start.32 = (f32[1,1792]{1,0:T(1,128)S(1)}, f32[1,1792]{1,0:T(1,128)S(1)}, u32[]{:S(2)}, u32[]{:S(2)}) collective-permute-start(f32[1,1792]{1,0:T(1,128)S(1)} %add.109.left_ref), channel_id=1, source_target_pairs={{0,16},{8,24},{16,0},{24,8},{1,17},{9,25},{17,1},{25,9},{2,18},{10... | collective-permute-start | bytes 21512 | tf_op jit(solution)/shard_map/ppermute | solution.py:449
  236.2 18.8 %collective-permute-start.30 = (bf16[96,3584]{1,0:T(8,128)(2,1)S(1)}, bf16[96,3584]{1,0:T(8,128)(2,1)S(1)}, u32[]{:S(2)}, u32[]{:S(2)}) collective-permute-start(bf16[96,3584]{1,0:T(8,128)(2,1)S(1)} %get-tuple-element.151), channel_id=1, source_target_pairs={{0,4},{1,5},{2,6},{3,7},{4,0},{5,1},{6,2},{7,3},{8,12},{9,13},{10,... | collective-permute-start | bytes 2064392 | tf_op jit(solution)/shard_map/ppermute | solution.py:339
  237.4 17.6 %collective-permute-start.29 = (bf16[96,3584]{1,0:T(8,128)(2,1)}, bf16[96,3584]{1,0:T(8,128)(2,1)S(1)}, u32[]{:S(2)}, u32[]{:S(2)}) collective-permute-start(bf16[96,3584]{1,0:T(8,128)(2,1)} %get-tuple-element.150), channel_id=1, source_target_pairs={{0,2},{1,3},{2,0},{3,1},{4,6},{5,7},{6,4},{7,5},{8,10},{9,11},{10,... | collective-permute-start | bytes 2064392 | tf_op jit(solution)/shard_map/ppermute | solution.py:339
  (12 other events, 33.2 us)
Sparse Core Ops, SparseCore 0:
  9.9 44.9 all-gather.2
  56.7 42.2 all-gather.4

commit v12 on v11

--- a/solution.py
+++ b/solution.py
@@ -418,26 +418,43 @@
     compute_own("act", [0])
     first_send(1)
     end = total + steps - 1
+    begun = set()
+
+    def begin(at):
+        if at < total and at not in begun:
+            begun.add(at)
+            first_send(at)
+
+    def second(at):
+        if 0 <= at < total and ("second", at) not in begun:
+            begun.add(("second", at))
+            forward(at, 2)
+
     for slot in range(end):
-        if slot > 1 and slot + 1 < total:
-            first_send(slot + 1)
+        if slot > 1:
+            begin(slot + 1)
         if slot == 1:
             compute_own("pre", others[:1])
-            first_send(2)
-        for step in range(2, steps + 1):
+            begin(2)
+        second(slot)
+        for step in range(3, steps + 1):
             if 0 <= slot - step + 2 < total:
                 forward(slot - step + 2, step)
-            if step == 2 and slot == len(others):
-                compute_own("act", others)
         if slot == 1:
             compute_own("pre", others[1:])
+        if slot == len(others):
+            compute_own("act", others)
+            second(slot + 1)
+            begin(slot + 2)
+        if slot == end - 3:
+            out_columns(0, 2)
         if slot >= steps - 1:
             finish(slot - steps + 1)
         if slot == end - 3:
             first = tokens_of([0] + others[:-2], 0, UNITS)
         if slot == end - 2:
             arrived += deliver(exchange(first))
-            out_columns(0, UNITS)
+            out_columns(2, UNITS - 2)
     levels = [1 << i for i in range(rows_of.bit_length() - 1)]
     sums = link(functools.reduce(jnp.add, [sums[key] for key in sorted(sums)]))
     for bit in levels[:-1]:

time: 264 us -> 258 us (0.977)
  waiting for transfers between devices: 68.8 us -> 57.7 us
  starting transfers between devices: 55.4 us -> 60.2 us
  Pallas kernels: 104 us -> 107 us
    ppermute x24, waiting for transfers between devices: 44.7 us -> 33.8 us  [send(): return lax.ppermute(value, 'row', pairs)]
    ppermute x24, starting transfers between devices: 48.7 us -> 52 us  [send(): return lax.ppermute(value, 'row', pairs)]
    pallas_call x19 -> x20, Pallas kernels: 104 us -> 107 us  [call(): pl.pallas_call(kernel, grid_spec=pltpu.PrefetchScalarGridSpec(num_scalar_...]
    unnamed x50 -> x54, local copies, waits for them, and re-layouts: 5.32 us -> 5.24 us
  transfers between devices with their start and end apart: 35 -> 35, of which waited for: 12 -> 16; matrix products, arithmetic and copies ran while one was open for 5% -> 4% of each run, Pallas kernels for 36% -> 37%
where the time goes in v12:
time: 258 us; the launch traced here: 257 us
  Pallas kernels  107 us (41%)
  starting transfers between devices  60.2 us (23%)
  waiting for transfers between devices  57.7 us (22%)
  between operations  14.8 us (6%)
  other arithmetic  12.3 us (5%)
  local copies, waits for them, and re-layouts  5.24 us (2%)
    pallas_call x20, Pallas kernels, call(): pl.pallas_call(kernel, grid_spec=pltpu.PrefetchScalarGridSpec(num_scalar_...  107 us
    ppermute x24, starting transfers between devices, send(): return lax.ppermute(value, 'row', pairs)  52 us
    ppermute x24, waiting for transfers between devices, send(): return lax.ppermute(value, 'row', pairs)  33.8 us
    all_gather x1, waiting for transfers between devices, local(): held['pre'] = lax.all_gather(tokens, 'col', axis=0, tiled=True)  16.3 us
    convert_element_type x18, other arithmetic, add_bf16(): return (left.astype(F32) + right.astype(F32)).astype(BF16)  10.5 us
    unnamed x54, local copies, waits for them, and re-layouts  5.24 us
  transfers between devices with their start and end apart: 35, of which 16 were waited for; matrix products, arithmetic and copies ran while one was open for 4% of the time, Pallas kernels for 37%

profile of v12, /device:TPU:0, one launch (start us, length us, event | category | flops | bytes accessed | tf_op | source)
XLA Modules:
  0.0 257.2 jit_solution(7519178635730316947)
XLA Ops:
  8.5 2.0 collective-permute-done.refs_1_
  11.0 6.3 %shard_map.84 = bf16[192,1792]{1,0:T(8,128)(2,1)S(1)} custom-call(s32[2]{0:T(128)S(1)} %pad_add_fusion.s, bf16[96,3584]{1,0:T(8,128)(2,1)S(1)} %copy-done.2, bf16[96,3584]{1,0:T(8,128)(2,1)S(1)} %collective-permute-done.refs_1_, bf16[3584,1792]{1,0:T(8,128)(2,1)} %refs_1_.9), custom_call_target="tpu_custom_call" | custom-call | flops 38535168 | bytes 222208 | tf_op jit(solution)/shard_map/pallas_call | solution.py:30
  17.3 4.7 %collective-permute-start.1 = (bf16[192,1792]{1,0:T(8,128)(2,1)S(1)}, bf16[192,1792]{1,0:T(8,128)(2,1)S(1)}, u32[]{:S(2)}, u32[]{:S(2)}) collective-permute-start(bf16[192,1792]{1,0:T(8,128)(2,1)S(1)} %shard_map.84), channel_id=1, source_target_pairs={{0,8},{24,16},{1,9},{25,17},{2,10},{26,18},{3,11},{27,19},{4,12},{... | collective-permute-start | bytes 2064392 | tf_op jit(solution)/shard_map/ppermute | solution.py:336
  22.0 7.3 %shard_map.85 = bf16[192,1792]{1,0:T(8,128)(2,1)S(1)} custom-call(s32[2]{0:T(128)S(1)} %pad_add_fusion.s, bf16[96,3584]{1,0:T(8,128)(2,1)S(1)} %copy-done.3, bf16[96,3584]{1,0:T(8,128)(2,1)S(1)} %collective-permute-done.2.refs_1_, bf16[1792,3584]{1,0:T(8,128)(2,1)} %refs_1_.7), custom_call_target="tpu_custom_call" | custom-call | flops 38535168 | bytes 222208 | tf_op jit(solution)/shard_map/pallas_call | solution.py:30
  29.3 1.5 collective-permute-start.5
  30.8 6.9 %collective-permute-done.1 = bf16[192,1792]{1,0:T(8,128)(2,1)S(1)} collective-permute-done((bf16[192,1792]{1,0:T(8,128)(2,1)S(1)}, bf16[192,1792]{1,0:T(8,128)(2,1)S(1)}, u32[]{:S(2)}, u32[]{:S(2)}) %collective-permute-start.1) | collective-permute-done | bytes 688160 | tf_op jit(solution)/shard_map/ppermute | solution.py:336
  38.6 16.3 %all-gather.3.cloned.1.call-done.refs_0_.tok_ref = bf16[768,3584]{1,0:T(8,128)(2,1)} async-done(((bf16[96,3584]{1,0:T(8,128)(2,1)}), bf16[768,3584]{1,0:T(8,128)(2,1)}) %all-gather.3.cloned.1.call-update) | async-done | bytes 5505040 | tf_op jit(solution)/shard_map/all_gather | solution.py:414
  54.9 2.6 copy-done.1
  57.4 6.3 %shard_map.86 = bf16[192,1792]{1,0:T(8,128)(2,1)S(1)} custom-call(s32[2]{0:T(128)S(1)} %pad_add_fusion.s, bf16[768,3584]{1,0:T(8,128)(2,1)S(1)} %copy-done.1, bf16[3584,1792]{1,0:T(8,128)(2,1)} %refs_1_.9), custom_call_target="tpu_custom_call" | custom-call | flops 38535168 | bytes 222208 | tf_op jit(solution)/shard_map/pallas_call | solution.py:30
  63.7 3.4 %collective-permute-start.3 = (bf16[192,1792]{1,0:T(8,128)(2,1)S(1)}, bf16[192,1792]{1,0:T(8,128)(2,1)S(1)}, u32[]{:S(2)}, u32[]{:S(2)}) collective-permute-start(bf16[192,1792]{1,0:T(8,128)(2,1)S(1)} %shard_map.86), channel_id=1, source_target_pairs={{0,8},{24,16},{1,9},{25,17},{2,10},{26,18},{3,11},{27,19},{4,12},{... | collective-permute-start | bytes 2064392 | tf_op jit(solution)/shard_map/ppermute | solution.py:336
  69.5 9.1 %shard_map.87 = (bf16[192,1792]{1,0:T(8,128)(2,1)S(1)}, bf16[192,1792]{1,0:T(8,128)(2,1)}) custom-call(s32[2]{0:T(128)S(1)} %pad_add_fusion.s, bf16[768,3584]{1,0:T(8,128)(2,1)S(1)} %copy-done.1, bf16[3584,1792]{1,0:T(8,128)(2,1)} %refs_1_.9), custom_call_target="tpu_custom_call" | custom-call | flops 77070336 | bytes 243712 | tf_op jit(solution)/shard_map/pallas_call | solution.py:30
  78.7 4.6 %collective-permute-start.6 = (bf16[192,1792]{1,0:T(8,128)(2,1)S(1)}, bf16[192,1792]{1,0:T(8,128)(2,1)S(1)}, u32[]{:S(2)}, u32[]{:S(2)}) collective-permute-start(bf16[192,1792]{1,0:T(8,128)(2,1)S(1)} %get-tuple-element.104), channel_id=1, source_target_pairs={{0,8},{24,16},{1,9},{25,17},{2,10},{26,18},{3,11},{27,19},{4,12},{... | collective-permute-start | bytes 2064392 | tf_op jit(solution)/shard_map/ppermute | solution.py:336
  87.5 1.8 shard_map.88
  89.3 7.0 %collective-permute-start.10 = (bf16[192,1792]{1,0:T(8,128)(2,1)}, bf16[192,1792]{1,0:T(8,128)(2,1)}, u32[]{:S(2)}, u32[]{:S(2)}) collective-permute-start(bf16[192,1792]{1,0:T(8,128)(2,1)} %get-tuple-element.112), channel_id=1, source_target_pairs={{0,8},{24,16},{1,9},{25,17},{2,10},{26,18},{3,11},{27,19},{4,12},{... | collective-permute-start | bytes 2064392 | tf_op jit(solution)/shard_map/ppermute | solution.py:336
  96.3 2.9 %collective-permute-done.6 = bf16[192,1792]{1,0:T(8,128)(2,1)S(1)} collective-permute-done((bf16[192,1792]{1,0:T(8,128)(2,1)S(1)}, bf16[192,1792]{1,0:T(8,128)(2,1)S(1)}, u32[]{:S(2)}, u32[]{:S(2)}) %collective-permute-start.6) | collective-permute-done | bytes 688160 | tf_op jit(solution)/shard_map/ppermute | solution.py:336
  100.2 1.6 collective-permute-start.9
  104.2 2.6 copy-done
  106.7 11.0 %shard_map.89 = (bf16[192,1792]{1,0:T(8,128)(2,1)S(1)}, bf16[192,1792]{1,0:T(8,128)(2,1)S(1)}, bf16[192,1792]{1,0:T(8,128)(2,1)S(1)}) custom-call(s32[2]{0:T(128)S(1)} %pad_add_fusion.s, bf16[768,3584]{1,0:T(8,128)(2,1)S(1)} %copy-done, bf16[1792,3584]{1,0:T(8,128)(2,1)} %refs_1_.7), custom_call_target="tpu_custom_call" | custom-call | flops 115605504 | bytes 265216 | tf_op jit(solution)/shard_map/pallas_call | solution.py:30
  117.7 1.6 add_convert_fusion.13.refs_0_
  119.3 7.1 %collective-permute-start.14 = (bf16[192,1792]{1,0:T(8,128)(2,1)S(1)}, bf16[192,1792]{1,0:T(8,128)(2,1)S(1)}, u32[]{:S(2)}, u32[]{:S(2)}) collective-permute-start(bf16[192,1792]{1,0:T(8,128)(2,1)S(1)} %get-tuple-element.116), channel_id=1, source_target_pairs={{0,8},{24,16},{1,9},{25,17},{2,10},{26,18},{3,11},{27,19},{4,12},{... | collective-permute-start | bytes 2064392 | tf_op jit(solution)/shard_map/ppermute | solution.py:336
  127.2 2.1 shard_map.90
  129.3 1.3 add_convert_fusion.12
  130.6 1.3 collective-permute-start.18
  131.9 2.9 %shard_map.91 = (bf16[768,1792]{1,0:T(8,128)(2,1)S(1)}, f32[192,1792]{1,0:T(8,128)S(1)}) custom-call(s32[2]{0:T(128)S(1)} %pad_add_fusion.s, f32[1,1792]{1,0:T(1,128)S(1)} %reshape.14.bias_ref, bf16[192,1792]{1,0:T(8,128)(2,1)S(1)} %add_convert_fusion.17.refs_0_, bf16[192,1792]{1,0:T(8,128)(2,1)S(1)} %copy-done.5, ...), custom_call_target="tpu_custom_call", output_to_operand_aliasing={{0}: (5, {})} | custom-call | flops 10321920 | bytes 4128768 | tf_op jit(solution)/shard_map/pallas_call | solution.py:30
  134.8 4.6 %collective-permute-start.16 = (bf16[192,1792]{1,0:T(8,128)(2,1)S(1)}, bf16[192,1792]{1,0:T(8,128)(2,1)S(1)}, u32[]{:S(2)}, u32[]{:S(2)}) collective-permute-start(bf16[192,1792]{1,0:T(8,128)(2,1)S(1)} %get-tuple-element.122), channel_id=1, source_target_pairs={{0,8},{24,16},{1,9},{25,17},{2,10},{26,18},{3,11},{27,19},{4,12},{... | collective-permute-start | bytes 2064392 | tf_op jit(solution)/shard_map/ppermute | solution.py:336
  142.8 1.5 collective-permute-start.19
  144.3 6.3 %collective-permute-done.18.refs_2_ = bf16[192,1792]{1,0:T(8,128)(2,1)S(1)} collective-permute-done((bf16[192,1792]{1,0:T(8,128)(2,1)S(1)}, bf16[192,1792]{1,0:T(8,128)(2,1)S(1)}, u32[]{:S(2)}, u32[]{:S(2)}) %collective-permute-start.18) | collective-permute-done | bytes 688160 | tf_op jit(solution)/shard_map/ppermute | solution.py:336
  150.5 3.1 %shard_map.92 = (bf16[768,1792]{1,0:T(8,128)(2,1)S(1)}, f32[192,1792]{1,0:T(8,128)S(1)}) custom-call(s32[2]{0:T(128)S(1)} %pad_add_fusion.s, f32[1,1792]{1,0:T(1,128)S(1)} %reshape.14.bias_ref, bf16[192,1792]{1,0:T(8,128)(2,1)} %add_convert_fusion.15.refs_0_, bf16[192,1792]{1,0:T(8,128)(2,1)} %collective-permute-done.9.refs_1_, ...), custom_call_target="tpu_custom_call", output_to_operand_aliasing={{0}: (5, {})} | custom-call | flops 10321920 | bytes 4128768 | tf_op jit(solution)/shard_map/pallas_call | solution.py:30
  153.6 1.5 collective-permute-start.21
  156.5 1.6 collective-permute-start.22
  158.0 6.5 %collective-permute-done.19.refs_2_ = bf16[192,1792]{1,0:T(8,128)(2,1)S(1)} collective-permute-done((bf16[192,1792]{1,0:T(8,128)(2,1)S(1)}, bf16[192,1792]{1,0:T(8,128)(2,1)S(1)}, u32[]{:S(2)}, u32[]{:S(2)}) %collective-permute-start.19) | collective-permute-done | bytes 688160 | tf_op jit(solution)/shard_map/ppermute | solution.py:336
  164.5 1.8 shard_map.93
  166.3 1.6 collective-permute-done.21
  170.3 6.5 %shard_map.94.refs_0_ = f32[1792,3584]{1,0:T(8,128)} custom-call(s32[2]{0:T(128)S(1)} %pad_add_fusion.s, bf16[768,1792]{1,0:T(8,128)(2,1)S(1)} %get-tuple-element.136.act_ref, bf16[768,3584]{1,0:T(8,128)(2,1)S(1)} %bitcast.3), custom_call_target="tpu_custom_call" | custom-call | flops 2818572288 | bytes 11665408 | tf_op jit(solution)/shard_map/pallas_call | solution.py:30
  176.8 2.5 collective-permute-done.22.refs_2_
  180.2 8.5 %shard_map.96 = (bf16[192,3584]{1,0:T(8,128)(2,1)S(1)}, bf16[192,3584]{1,0:T(8,128)(2,1)S(1)}) custom-call(s32[2]{0:T(128)S(1)} %pad_add_fusion.s, bf16[768,1792]{1,0:T(8,128)(2,1)S(1)} %get-tuple-element.126.refs_0_.refs_3_, bf16[3584,1792]{1,0:T(8,128)(2,1)} %refs_1_.9), custom_call_target="tpu_custom_call" | custom-call | flops 4932501504 | bytes 14221312 | tf_op jit(solution)/shard_map/pallas_call | solution.py:30
  188.9 2.1 collective-permute-done.24.refs_2_
  192.0 1.5 collective-permute-start.26
  193.6 1.6 collective-permute-done.25
  195.5 1.5 collective-permute-start.27
  197.0 11.8 %shard_map.98 = f32[1792,3584]{1,0:T(8,128)} custom-call(s32[2]{0:T(128)S(1)} %pad_add_fusion.s, bf16[768,1792]{1,0:T(8,128)(2,1)S(1)} %get-tuple-element.136.act_ref, bf16[768,3584]{1,0:T(8,128)(2,1)S(1)} %bitcast.3, f32[1792,3584]{1,0:T(8,128)} %shard_map.94.refs_0_), custom_call_target="tpu_custom_call", output_to_operand_aliasing={{}: (3, {})} | custom-call | flops 7046430720 | bytes 25034752 | tf_op jit(solution)/shard_map/pallas_call | solution.py:30
  208.8 3.0 %collective-permute-done.26.refs_2_ = bf16[192,1792]{1,0:T(8,128)(2,1)S(1)} collective-permute-done((bf16[192,1792]{1,0:T(8,128)(2,1)S(1)}, bf16[192,1792]{1,0:T(8,128)(2,1)S(1)}, u32[]{:S(2)}, u32[]{:S(2)}) %collective-permute-start.26) | collective-permute-done | bytes 688160 | tf_op jit(solution)/shard_map/ppermute | solution.py:336
  214.6 8.9 %shard_map.101 = (bf16[192,3584]{1,0:T(8,128)(2,1)S(1)}, bf16[192,3584]{1,0:T(8,128)(2,1)S(1)}) custom-call(s32[2]{0:T(128)S(1)} %pad_add_fusion.s, bf16[768,1792]{1,0:T(8,128)(2,1)S(1)} %get-tuple-element.145.refs_0_.grad_ref, bf16[3584,1792]{1,0:T(8,128)(2,1)} %refs_1_.9), custom_call_target="tpu_custom_call" | custom-call | flops 4932501504 | bytes 14221312 | tf_op jit(solution)/shard_map/pallas_call | solution.py:30
  223.6 1.6 collective-permute-start.31
  225.2 2.1 collective-permute-done.31
  227.4 1.8 collective-permute-start.32
  230.4 1.3 collective-permute-start.30
  232.4 15.6 %shard_map.102.refs_0_ = f32[3584,1792]{1,0:T(8,128)} custom-call(s32[2]{0:T(128)S(1)} %pad_add_fusion.s, bf16[768,3584]{1,0:T(8,128)(2,1)S(1)} %bitcast.5, bf16[768,1792]{1,0:T(8,128)(2,1)S(1)} %get-tuple-element.145.refs_0_.grad_ref), custom_call_target="tpu_custom_call" | custom-call | flops 9865003008 | bytes 33947648 | tf_op jit(solution)/shard_map/pallas_call | solution.py:30
  (124 shorter events, 29.8 us)
Async XLA Ops:
  7.2 47.7 %all-gather.3.cloned.1.call-start = ((), (), s32[]{:S(2)}) async-start(), calls=%async_computation | async-start | bytes 6193152 | tf_op jit(solution)/shard_map/all_gather | solution.py:414
  7.9 96.2 %all-gather.5.cloned.1.call-start = ((), (), s32[]{:S(2)}) async-start(), calls=%async_computation.1 | async-start | bytes 6193152 | tf_op jit(solution)/shard_map/all_gather | solution.py:415
  8.0 2.5 collective-permute-start
  10.5 11.5 %collective-permute-start.2 = (bf16[96,3584]{1,0:T(8,128)(2,1)S(1)}, bf16[96,3584]{1,0:T(8,128)(2,1)S(1)}, u32[]{:S(2)}, u32[]{:S(2)}) collective-permute-start(bf16[96,3584]{1,0:T(8,128)(2,1)S(1)} %copy-done.3), channel_id=1, source_target_pairs={{0,1},{1,0},{2,3},{3,2},{4,5},{5,4},{6,7},{7,6},{8,9},{9,8},{10,11... | collective-permute-start | bytes 2064392 | tf_op jit(solution)/shard_map/ppermute | solution.py:339
  17.3 20.4 %collective-permute-start.1 = (bf16[192,1792]{1,0:T(8,128)(2,1)S(1)}, bf16[192,1792]{1,0:T(8,128)(2,1)S(1)}, u32[]{:S(2)}, u32[]{:S(2)}) collective-permute-start(bf16[192,1792]{1,0:T(8,128)(2,1)S(1)} %shard_map.84), channel_id=1, source_target_pairs={{0,8},{24,16},{1,9},{25,17},{2,10},{26,18},{3,11},{27,19},{4,12},{... | collective-permute-start | bytes 2064392 | tf_op jit(solution)/shard_map/ppermute | solution.py:336
  29.3 37.9 %collective-permute-start.5 = (bf16[192,1792]{1,0:T(8,128)(2,1)S(1)}, bf16[192,1792]{1,0:T(8,128)(2,1)S(1)}, u32[]{:S(2)}, u32[]{:S(2)}) collective-permute-start(bf16[192,1792]{1,0:T(8,128)(2,1)S(1)} %shard_map.85), channel_id=1, source_target_pairs={{0,8},{24,16},{1,9},{25,17},{2,10},{26,18},{3,11},{27,19},{4,12},{... | collective-permute-start | bytes 2064392 | tf_op jit(solution)/shard_map/ppermute | solution.py:336
  37.8 25.9 %copy-start.6 = (bf16[192,1792]{1,0:T(8,128)(2,1)}, bf16[192,1792]{1,0:T(8,128)(2,1)S(1)}, u32[]{:S(2)}) copy-start(bf16[192,1792]{1,0:T(8,128)(2,1)S(1)} %add_convert_fusion.20.refs_0_) | copy-start | bytes 2064388
  37.8 30.2 %collective-permute-start.4 = (bf16[192,1792]{1,0:T(8,128)(2,1)S(1)}, bf16[192,1792]{1,0:T(8,128)(2,1)S(1)}, u32[]{:S(2)}, u32[]{:S(2)}) collective-permute-start(bf16[192,1792]{1,0:T(8,128)(2,1)S(1)} %add_convert_fusion.20.refs_0_), channel_id=1, source_target_pairs={{8,16},{16,8},{9,17},{17,9},{10,18},{18,10},{11,19},{19,11},{12,20... | collective-permute-start | bytes 2064392 | tf_op jit(solution)/shard_map/ppermute | solution.py:336
  63.7 19.6 %collective-permute-start.3 = (bf16[192,1792]{1,0:T(8,128)(2,1)S(1)}, bf16[192,1792]{1,0:T(8,128)(2,1)S(1)}, u32[]{:S(2)}, u32[]{:S(2)}) collective-permute-start(bf16[192,1792]{1,0:T(8,128)(2,1)S(1)} %shard_map.86), channel_id=1, source_target_pairs={{0,8},{24,16},{1,9},{25,17},{2,10},{26,18},{3,11},{27,19},{4,12},{... | collective-permute-start | bytes 2064392 | tf_op jit(solution)/shard_map/ppermute | solution.py:336
  67.3 11.4 %copy-start.10 = (bf16[192,1792]{1,0:T(8,128)(2,1)}, bf16[192,1792]{1,0:T(8,128)(2,1)S(1)}, u32[]{:S(2)}) copy-start(bf16[192,1792]{1,0:T(8,128)(2,1)S(1)} %add_convert_fusion.19.refs_0_) | copy-start | bytes 2064388
  67.3 17.1 %collective-permute-start.7 = (bf16[192,1792]{1,0:T(8,128)(2,1)S(1)}, bf16[192,1792]{1,0:T(8,128)(2,1)S(1)}, u32[]{:S(2)}, u32[]{:S(2)}) collective-permute-start(bf16[192,1792]{1,0:T(8,128)(2,1)S(1)} %add_convert_fusion.19.refs_0_), channel_id=1, source_target_pairs={{8,16},{16,8},{9,17},{17,9},{10,18},{18,10},{11,19},{19,11},{12,20... | collective-permute-start | bytes 2064392 | tf_op jit(solution)/shard_map/ppermute | solution.py:336
  68.1 10.6 %copy-start.8 = (bf16[192,1792]{1,0:T(8,128)(2,1)}, bf16[192,1792]{1,0:T(8,128)(2,1)S(1)}, u32[]{:S(2)}) copy-start(bf16[192,1792]{1,0:T(8,128)(2,1)S(1)} %collective-permute-done.4.refs_1_) | copy-start | bytes 2064388
  68.2 19.2 %collective-permute-start.8 = (bf16[192,1792]{1,0:T(8,128)(2,1)S(1)}, bf16[192,1792]{1,0:T(8,128)(2,1)S(1)}, u32[]{:S(2)}, u32[]{:S(2)}) collective-permute-start(bf16[192,1792]{1,0:T(8,128)(2,1)S(1)} %add_convert_fusion.18), channel_id=1, source_target_pairs={{16,24},{8,0},{17,25},{9,1},{18,26},{10,2},{19,27},{11,3},{20,28},... | collective-permute-start | bytes 2064392 | tf_op jit(solution)/shard_map/ppermute | solution.py:336
  78.7 20.5 %copy-start.14 = (bf16[192,1792]{1,0:T(8,128)(2,1)}, bf16[192,1792]{1,0:T(8,128)(2,1)S(1)}, u32[]{:S(2)}) copy-start(bf16[192,1792]{1,0:T(8,128)(2,1)S(1)} %get-tuple-element.104) | copy-start | bytes 2064388
  78.7 20.4 %collective-permute-start.6 = (bf16[192,1792]{1,0:T(8,128)(2,1)S(1)}, bf16[192,1792]{1,0:T(8,128)(2,1)S(1)}, u32[]{:S(2)}, u32[]{:S(2)}) collective-permute-start(bf16[192,1792]{1,0:T(8,128)(2,1)S(1)} %get-tuple-element.104), channel_id=1, source_target_pairs={{0,8},{24,16},{1,9},{25,17},{2,10},{26,18},{3,11},{27,19},{4,12},{... | collective-permute-start | bytes 2064392 | tf_op jit(solution)/shard_map/ppermute | solution.py:336
  83.5 18.2 %collective-permute-start.11 = (bf16[192,1792]{1,0:T(8,128)(2,1)S(1)}, bf16[192,1792]{1,0:T(8,128)(2,1)S(1)}, u32[]{:S(2)}, u32[]{:S(2)}) collective-permute-start(bf16[192,1792]{1,0:T(8,128)(2,1)S(1)} %add_convert_fusion.17.refs_0_), channel_id=1, source_target_pairs={{8,16},{16,8},{9,17},{17,9},{10,18},{18,10},{11,19},{19,11},{12,20... | collective-permute-start | bytes 2064392 | tf_op jit(solution)/shard_map/ppermute | solution.py:336
  85.5 41.6 %collective-permute-start.12 = (bf16[192,1792]{1,0:T(8,128)(2,1)}, bf16[192,1792]{1,0:T(8,128)(2,1)}, u32[]{:S(2)}, u32[]{:S(2)}) collective-permute-start(bf16[192,1792]{1,0:T(8,128)(2,1)} %add_convert_fusion.16), channel_id=1, source_target_pairs={{16,24},{8,0},{17,25},{9,1},{18,26},{10,2},{19,27},{11,3},{20,28},... | collective-permute-start | bytes 2064392 | tf_op jit(solution)/shard_map/ppermute | solution.py:336
  89.2 13.6 %copy-start.20 = (f32[192,1792]{1,0:T(8,128)}, f32[192,1792]{1,0:T(8,128)S(1)}, u32[]{:S(2)}) copy-start(f32[192,1792]{1,0:T(8,128)S(1)} %get-tuple-element.94.slope_ref) | copy-start | bytes 4128772
  89.3 28.5 %collective-permute-start.10 = (bf16[192,1792]{1,0:T(8,128)(2,1)}, bf16[192,1792]{1,0:T(8,128)(2,1)}, u32[]{:S(2)}, u32[]{:S(2)}) collective-permute-start(bf16[192,1792]{1,0:T(8,128)(2,1)} %get-tuple-element.112), channel_id=1, source_target_pairs={{0,8},{24,16},{1,9},{25,17},{2,10},{26,18},{3,11},{27,19},{4,12},{... | collective-permute-start | bytes 2064392 | tf_op jit(solution)/shard_map/ppermute | solution.py:336
  100.2 29.1 %collective-permute-start.9 = (bf16[192,1792]{1,0:T(8,128)(2,1)}, bf16[192,1792]{1,0:T(8,128)(2,1)}, u32[]{:S(2)}, u32[]{:S(2)}) collective-permute-start(bf16[192,1792]{1,0:T(8,128)(2,1)} %add_convert_fusion.15.refs_0_), channel_id=1, source_target_pairs={{8,16},{16,8},{9,17},{17,9},{10,18},{18,10},{11,19},{19,11},{12,20... | collective-permute-start | bytes 2064392 | tf_op jit(solution)/shard_map/ppermute | solution.py:336
  102.8 29.1 %collective-permute-start.13 = (bf16[192,1792]{1,0:T(8,128)(2,1)}, bf16[192,1792]{1,0:T(8,128)(2,1)}, u32[]{:S(2)}, u32[]{:S(2)}) collective-permute-start(bf16[192,1792]{1,0:T(8,128)(2,1)} %add_convert_fusion.14), channel_id=1, source_target_pairs={{16,24},{8,0},{17,25},{9,1},{18,26},{10,2},{19,27},{11,3},{20,28},... | collective-permute-start | bytes 2064392 | tf_op jit(solution)/shard_map/ppermute | solution.py:336
  106.7 20.4 %copy-start.21 = (f32[192,1792]{1,0:T(8,128)S(1)}, f32[192,1792]{1,0:T(8,128)}, u32[]{:S(2)}) copy-start(f32[192,1792]{1,0:T(8,128)} %copy-done.20) | copy-start | bytes 4128772
  117.7 9.4 %copy-start.11 = (bf16[192,1792]{1,0:T(8,128)(2,1)S(1)}, bf16[192,1792]{1,0:T(8,128)(2,1)}, u32[]{:S(2)}) copy-start(bf16[192,1792]{1,0:T(8,128)(2,1)} %copy-done.10) | copy-start | bytes 2064388
  117.7 9.4 %copy-start.13 = (bf16[192,1792]{1,0:T(8,128)(2,1)S(1)}, bf16[192,1792]{1,0:T(8,128)(2,1)}, u32[]{:S(2)}) copy-start(bf16[192,1792]{1,0:T(8,128)(2,1)} %copy-done.12) | copy-start | bytes 2064388
  119.3 21.3 %collective-permute-start.14 = (bf16[192,1792]{1,0:T(8,128)(2,1)S(1)}, bf16[192,1792]{1,0:T(8,128)(2,1)S(1)}, u32[]{:S(2)}, u32[]{:S(2)}) collective-permute-start(bf16[192,1792]{1,0:T(8,128)(2,1)S(1)} %get-tuple-element.116), channel_id=1, source_target_pairs={{0,8},{24,16},{1,9},{25,17},{2,10},{26,18},{3,11},{27,19},{4,12},{... | collective-permute-start | bytes 2064392 | tf_op jit(solution)/shard_map/ppermute | solution.py:336
  126.4 15.1 %collective-permute-start.17 = (bf16[192,1792]{1,0:T(8,128)(2,1)S(1)}, bf16[192,1792]{1,0:T(8,128)(2,1)S(1)}, u32[]{:S(2)}, u32[]{:S(2)}) collective-permute-start(bf16[192,1792]{1,0:T(8,128)(2,1)S(1)} %add_convert_fusion.13.refs_0_), channel_id=1, source_target_pairs={{8,16},{16,8},{9,17},{17,9},{10,18},{18,10},{11,19},{19,11},{12,20... | collective-permute-start | bytes 2064392 | tf_op jit(solution)/shard_map/ppermute | solution.py:336
  130.6 19.9 %collective-permute-start.18 = (bf16[192,1792]{1,0:T(8,128)(2,1)S(1)}, bf16[192,1792]{1,0:T(8,128)(2,1)S(1)}, u32[]{:S(2)}, u32[]{:S(2)}) collective-permute-start(bf16[192,1792]{1,0:T(8,128)(2,1)S(1)} %add_convert_fusion.12), channel_id=1, source_target_pairs={{16,24},{8,0},{17,25},{9,1},{18,26},{10,2},{19,27},{11,3},{20,28},... | collective-permute-start | bytes 2064392 | tf_op jit(solution)/shard_map/ppermute | solution.py:336
  134.8 20.6 %collective-permute-start.16 = (bf16[192,1792]{1,0:T(8,128)(2,1)S(1)}, bf16[192,1792]{1,0:T(8,128)(2,1)S(1)}, u32[]{:S(2)}, u32[]{:S(2)}) collective-permute-start(bf16[192,1792]{1,0:T(8,128)(2,1)S(1)} %get-tuple-element.122), channel_id=1, source_target_pairs={{0,8},{24,16},{1,9},{25,17},{2,10},{26,18},{3,11},{27,19},{4,12},{... | collective-permute-start | bytes 2064392 | tf_op jit(solution)/shard_map/ppermute | solution.py:336
  140.8 15.5 %collective-permute-start.15 = (bf16[192,1792]{1,0:T(8,128)(2,1)S(1)}, bf16[192,1792]{1,0:T(8,128)(2,1)S(1)}, u32[]{:S(2)}, u32[]{:S(2)}) collective-permute-start(bf16[192,1792]{1,0:T(8,128)(2,1)S(1)} %add_convert_fusion.11.refs_0_), channel_id=1, source_target_pairs={{8,16},{16,8},{9,17},{17,9},{10,18},{18,10},{11,19},{19,11},{12,20... | collective-permute-start | bytes 2064392 | tf_op jit(solution)/shard_map/ppermute | solution.py:336
  142.8 21.7 %collective-permute-start.19 = (bf16[192,1792]{1,0:T(8,128)(2,1)S(1)}, bf16[192,1792]{1,0:T(8,128)(2,1)S(1)}, u32[]{:S(2)}, u32[]{:S(2)}) collective-permute-start(bf16[192,1792]{1,0:T(8,128)(2,1)S(1)} %add_convert_fusion.10), channel_id=1, source_target_pairs={{16,24},{8,0},{17,25},{9,1},{18,26},{10,2},{19,27},{11,3},{20,28},... | collective-permute-start | bytes 2064392 | tf_op jit(solution)/shard_map/ppermute | solution.py:336
  153.6 14.3 %collective-permute-start.21 = (bf16[192,1792]{1,0:T(8,128)(2,1)S(1)}, bf16[192,1792]{1,0:T(8,128)(2,1)S(1)}, u32[]{:S(2)}, u32[]{:S(2)}) collective-permute-start(bf16[192,1792]{1,0:T(8,128)(2,1)S(1)} %get-tuple-element.129), channel_id=1, source_target_pairs={{0,8},{24,16},{1,9},{25,17},{2,10},{26,18},{3,11},{27,19},{4,12},{... | collective-permute-start | bytes 2064392 | tf_op jit(solution)/shard_map/ppermute | solution.py:336
  155.5 13.2 %collective-permute-start.20 = (bf16[192,1792]{1,0:T(8,128)(2,1)S(1)}, bf16[192,1792]{1,0:T(8,128)(2,1)S(1)}, u32[]{:S(2)}, u32[]{:S(2)}) collective-permute-start(bf16[192,1792]{1,0:T(8,128)(2,1)S(1)} %add_convert_fusion.9.refs_0_), channel_id=1, source_target_pairs={{8,16},{16,8},{9,17},{17,9},{10,18},{18,10},{11,19},{19,11},{12,20... | collective-permute-start | bytes 2064392 | tf_op jit(solution)/shard_map/ppermute | solution.py:336
  156.3 14.0 %slice-start = ((s8[5505024]{0:T(1024)(128)(4,1)}), s8[4194304]{0:T(1024)(128)(4,1)S(1)}, s32[]{:S(2)}) async-start(s8[5505024]{0:T(1024)(128)(4,1)} %bitcast.2), calls=%async_computation.2 | async-start | bytes 8388608
  156.4 13.8 %slice-start.1 = ((s8[5505024]{0:T(1024)(128)(4,1)}), s8[1310720]{0:T(1024)(128)(4,1)S(1)}, s32[]{:S(2)}) async-start(s8[5505024]{0:T(1024)(128)(4,1)} %bitcast.2), calls=%async_computation.3 | async-start | bytes 2621440
  156.5 22.8 %collective-permute-start.22 = (bf16[192,1792]{1,0:T(8,128)(2,1)S(1)}, bf16[192,1792]{1,0:T(8,128)(2,1)S(1)}, u32[]{:S(2)}, u32[]{:S(2)}) collective-permute-start(bf16[192,1792]{1,0:T(8,128)(2,1)S(1)} %add_convert_fusion.8), channel_id=1, source_target_pairs={{16,24},{8,0},{17,25},{9,1},{18,26},{10,2},{19,27},{11,3},{20,28},... | collective-permute-start | bytes 2064392 | tf_op jit(solution)/shard_map/ppermute | solution.py:336
  168.1 20.7 %collective-permute-start.23 = (bf16[192,1792]{1,0:T(8,128)(2,1)S(1)}, bf16[192,1792]{1,0:T(8,128)(2,1)S(1)}, u32[]{:S(2)}, u32[]{:S(2)}) collective-permute-start(bf16[192,1792]{1,0:T(8,128)(2,1)S(1)} %add_convert_fusion.7.refs_0_), channel_id=1, source_target_pairs={{8,16},{16,8},{9,17},{17,9},{10,18},{18,10},{11,19},{19,11},{12,20... | collective-permute-start | bytes 2064392 | tf_op jit(solution)/shard_map/ppermute | solution.py:336
  169.0 22.0 %collective-permute-start.24 = (bf16[192,1792]{1,0:T(8,128)(2,1)S(1)}, bf16[192,1792]{1,0:T(8,128)(2,1)S(1)}, u32[]{:S(2)}, u32[]{:S(2)}) collective-permute-start(bf16[192,1792]{1,0:T(8,128)(2,1)S(1)} %add_convert_fusion.6), channel_id=1, source_target_pairs={{16,24},{8,0},{17,25},{9,1},{18,26},{10,2},{19,27},{11,3},{20,28},... | collective-permute-start | bytes 2064392 | tf_op jit(solution)/shard_map/ppermute | solution.py:336
  192.0 3.2 %collective-permute-start.25 = (bf16[192,3584]{1,0:T(8,128)(2,1)S(1)}, bf16[192,3584]{1,0:T(8,128)(2,1)S(1)}, u32[]{:S(2)}, u32[]{:S(2)}) collective-permute-start(bf16[192,3584]{1,0:T(8,128)(2,1)S(1)} %get-tuple-element.134), channel_id=1, source_target_pairs={{0,1},{1,0},{2,3},{3,2},{4,5},{5,4},{6,7},{7,6},{8,9},{9,8},{10,11... | collective-permute-start | bytes 4128776 | tf_op jit(solution)/shard_map/ppermute | solution.py:339
  192.0 19.7 %collective-permute-start.26 = (bf16[192,1792]{1,0:T(8,128)(2,1)S(1)}, bf16[192,1792]{1,0:T(8,128)(2,1)S(1)}, u32[]{:S(2)}, u32[]{:S(2)}) collective-permute-start(bf16[192,1792]{1,0:T(8,128)(2,1)S(1)} %add_convert_fusion.5), channel_id=1, source_target_pairs={{16,24},{8,0},{17,25},{9,1},{18,26},{10,2},{19,27},{11,3},{20,28},... | collective-permute-start | bytes 2064392 | tf_op jit(solution)/shard_map/ppermute | solution.py:336
  195.5 16.3 %copy-start.17 = (f32[192,1792]{1,0:T(8,128)S(1)}, f32[192,1792]{1,0:T(8,128)}, u32[]{:S(2)}) copy-start(f32[192,1792]{1,0:T(8,128)} %copy-done.16) | copy-start | bytes 4128772
  195.5 18.4 %collective-permute-start.27 = (bf16[96,3584]{1,0:T(8,128)(2,1)S(1)}, bf16[96,3584]{1,0:T(8,128)(2,1)S(1)}, u32[]{:S(2)}, u32[]{:S(2)}) collective-permute-start(bf16[96,3584]{1,0:T(8,128)(2,1)S(1)} %get-tuple-element.155), channel_id=1, source_target_pairs={{0,6},{1,7},{2,4},{3,5},{4,2},{5,3},{6,0},{7,1},{8,14},{9,15},{10,... | collective-permute-start | bytes 2064392 | tf_op jit(solution)/shard_map/ppermute | solution.py:339
  213.9 18.5 %slice-start.2 = ((s8[5505024]{0:T(1024)(128)(4,1)}), s8[4194304]{0:T(1024)(128)(4,1)S(1)}, s32[]{:S(2)}) async-start(s8[5505024]{0:T(1024)(128)(4,1)} %bitcast.4), calls=%async_computation.4 | async-start | bytes 8388608
  214.6 17.8 %slice-start.3 = ((s8[5505024]{0:T(1024)(128)(4,1)}), s8[1310720]{0:T(1024)(128)(4,1)S(1)}, s32[]{:S(2)}) async-start(s8[5505024]{0:T(1024)(128)(4,1)} %bitcast.4), calls=%async_computation.5 | async-start | bytes 2621440
  223.5 5.7 %collective-permute-start.28 = (bf16[192,3584]{1,0:T(8,128)(2,1)S(1)}, bf16[192,3584]{1,0:T(8,128)(2,1)S(1)}, u32[]{:S(2)}, u32[]{:S(2)}) collective-permute-start(bf16[192,3584]{1,0:T(8,128)(2,1)S(1)} %get-tuple-element.144), channel_id=1, source_target_pairs={{0,1},{1,0},{2,3},{3,2},{4,5},{5,4},{6,7},{7,6},{8,9},{9,8},{10,11... | collective-permute-start | bytes 4128776 | tf_op jit(solution)/shard_map/ppermute | solution.py:339
  223.6 3.7 %collective-permute-start.31 = (f32[1,1792]{1,0:T(1,128)S(1)}, f32[1,1792]{1,0:T(1,128)S(1)}, u32[]{:S(2)}, u32[]{:S(2)}) collective-permute-start(f32[1,1792]{1,0:T(1,128)S(1)} %add_add_fusion), channel_id=1, source_target_pairs={{0,8},{8,0},{16,24},{24,16},{1,9},{9,1},{17,25},{25,17},{2,10},{10... | collective-permute-start | bytes 21512 | tf_op jit(solution)/shard_map/ppermute | solution.py:461
  227.4 20.7 %collective-permute-start.32 = (f32[1,1792]{1,0:T(1,128)S(1)}, f32[1,1792]{1,0:T(1,128)S(1)}, u32[]{:S(2)}, u32[]{:S(2)}) collective-permute-start(f32[1,1792]{1,0:T(1,128)S(1)} %add.109.left_ref), channel_id=1, source_target_pairs={{0,16},{8,24},{16,0},{24,8},{1,17},{9,25},{17,1},{25,9},{2,18},{10... | collective-permute-start | bytes 21512 | tf_op jit(solution)/shard_map/ppermute | solution.py:466
  230.4 18.9 %collective-permute-start.30 = (bf16[96,3584]{1,0:T(8,128)(2,1)S(1)}, bf16[96,3584]{1,0:T(8,128)(2,1)S(1)}, u32[]{:S(2)}, u32[]{:S(2)}) collective-permute-start(bf16[96,3584]{1,0:T(8,128)(2,1)S(1)} %get-tuple-element.153), channel_id=1, source_target_pairs={{0,4},{1,5},{2,6},{3,7},{4,0},{5,1},{6,2},{7,3},{8,12},{9,13},{10,... | collective-permute-start | bytes 2064392 | tf_op jit(solution)/shard_map/ppermute | solution.py:339
  231.7 17.5 %collective-permute-start.29 = (bf16[96,3584]{1,0:T(8,128)(2,1)}, bf16[96,3584]{1,0:T(8,128)(2,1)S(1)}, u32[]{:S(2)}, u32[]{:S(2)}) collective-permute-start(bf16[96,3584]{1,0:T(8,128)(2,1)} %get-tuple-element.152), channel_id=1, source_target_pairs={{0,2},{1,3},{2,0},{3,1},{4,6},{5,7},{6,4},{7,5},{8,10},{9,11},{10,... | collective-permute-start | bytes 2064392 | tf_op jit(solution)/shard_map/ppermute | solution.py:339
  (14 other events, 48.0 us)
Sparse Core Ops, SparseCore 0:
  9.9 44.9 all-gather.2
  56.7 42.2 all-gather.4

commit v13 on v12

--- a/solution.py
+++ b/solution.py
@@ -11,7 +11,7 @@
 GELU_CUBIC = 0.044715
 F32, BF16 = jnp.float32, jnp.bfloat16
 VMEM_LIMIT = 40 * 1024 * 1024
-UNITS, AHEAD = 7, 3
+UNITS, AHEAD = 7, 5
 
 
 def dot(left, right, dims):
@@ -461,8 +461,9 @@
         sums = sums + lax.ppermute(sums, "row", [(i, i ^ bit) for i in range(rows_of)])
     head = add_scaled(place, link(arrived[0]), arrived[1], 1.0)
     chain.append(head)
+    sums = link(sums)
+    chain.append(sums)
     last = exchange(tokens_of(others[-2:], 0, UNITS))
-    sums = link(sums)
     given = lax.ppermute(sums, "row", [(i, i ^ levels[-1]) for i in range(rows_of)])
     arrived += deliver(last)
     in_rows(0, UNITS)

time: 258 us -> 258 us (level)
  waiting for transfers between devices: 57.7 us -> 61.2 us
  starting transfers between devices: 60.2 us -> 56.9 us
where the time goes in v13:
time: 258 us; the launch traced here: 257 us
  Pallas kernels  107 us (41%)
  waiting for transfers between devices  61.2 us (24%)
  starting transfers between devices  56.9 us (22%)
  between operations  14.9 us (6%)
  other arithmetic  12.3 us (5%)
  local copies, waits for them, and re-layouts  5.24 us (2%)
    pallas_call x20, Pallas kernels, call(): pl.pallas_call(kernel, grid_spec=pltpu.PrefetchScalarGridSpec(num_scalar_...  107 us
    ppermute x24, starting transfers between devices, send(): return lax.ppermute(value, 'row', pairs)  52.1 us
    ppermute x24, waiting for transfers between devices, send(): return lax.ppermute(value, 'row', pairs)  33.9 us
    all_gather x1, waiting for transfers between devices, local(): held['pre'] = lax.all_gather(tokens, 'col', axis=0, tiled=True)  16.4 us
    convert_element_type x18, other arithmetic, add_bf16(): return (left.astype(F32) + right.astype(F32)).astype(BF16)  10.5 us
    ppermute x7, waiting for transfers between devices, swap(): return lax.ppermute(value, 'col', [(i, i ^ bits) for i in range(cols_of)])  6.62 us
    unnamed x54, local copies, waits for them, and re-layouts  5.24 us
  transfers between devices with their start and end apart: 35, of which 16 were waited for; matrix products, arithmetic and copies ran while one was open for 4% of the time, Pallas kernels for 37%

profile of v13, /device:TPU:0, one launch (start us, length us, event | category | flops | bytes accessed | tf_op | source)
XLA Modules:
  0.0 257.2 jit_solution(3415472341600586760)
XLA Ops:
  8.5 2.0 collective-permute-done.refs_1_
  11.0 6.2 %shard_map.84 = bf16[192,1792]{1,0:T(8,128)(2,1)S(1)} custom-call(s32[2]{0:T(128)S(1)} %pad_add_fusion.s, bf16[96,3584]{1,0:T(8,128)(2,1)S(1)} %copy-done.2, bf16[96,3584]{1,0:T(8,128)(2,1)S(1)} %collective-permute-done.refs_1_, bf16[3584,1792]{1,0:T(8,128)(2,1)} %refs_1_.9), custom_call_target="tpu_custom_call" | custom-call | flops 38535168 | bytes 222208 | tf_op jit(solution)/shard_map/pallas_call | solution.py:30
  17.2 4.7 %collective-permute-start.1 = (bf16[192,1792]{1,0:T(8,128)(2,1)S(1)}, bf16[192,1792]{1,0:T(8,128)(2,1)S(1)}, u32[]{:S(2)}, u32[]{:S(2)}) collective-permute-start(bf16[192,1792]{1,0:T(8,128)(2,1)S(1)} %shard_map.84), channel_id=1, source_target_pairs={{0,8},{24,16},{1,9},{25,17},{2,10},{26,18},{3,11},{27,19},{4,12},{... | collective-permute-start | bytes 2064392 | tf_op jit(solution)/shard_map/ppermute | solution.py:336
  21.9 7.3 %shard_map.85 = bf16[192,1792]{1,0:T(8,128)(2,1)S(1)} custom-call(s32[2]{0:T(128)S(1)} %pad_add_fusion.s, bf16[96,3584]{1,0:T(8,128)(2,1)S(1)} %copy-done.3, bf16[96,3584]{1,0:T(8,128)(2,1)S(1)} %collective-permute-done.2.refs_1_, bf16[1792,3584]{1,0:T(8,128)(2,1)} %refs_1_.7), custom_call_target="tpu_custom_call" | custom-call | flops 38535168 | bytes 222208 | tf_op jit(solution)/shard_map/pallas_call | solution.py:30
  29.2 1.5 collective-permute-start.5
  30.7 6.9 %collective-permute-done.1 = bf16[192,1792]{1,0:T(8,128)(2,1)S(1)} collective-permute-done((bf16[192,1792]{1,0:T(8,128)(2,1)S(1)}, bf16[192,1792]{1,0:T(8,128)(2,1)S(1)}, u32[]{:S(2)}, u32[]{:S(2)}) %collective-permute-start.1) | collective-permute-done | bytes 688160 | tf_op jit(solution)/shard_map/ppermute | solution.py:336
  38.5 16.4 %all-gather.3.cloned.1.call-done.refs_0_.tok_ref = bf16[768,3584]{1,0:T(8,128)(2,1)} async-done(((bf16[96,3584]{1,0:T(8,128)(2,1)}), bf16[768,3584]{1,0:T(8,128)(2,1)}) %all-gather.3.cloned.1.call-update) | async-done | bytes 5505040 | tf_op jit(solution)/shard_map/all_gather | solution.py:414
  54.9 2.6 copy-done.1
  57.4 6.2 %shard_map.86 = bf16[192,1792]{1,0:T(8,128)(2,1)S(1)} custom-call(s32[2]{0:T(128)S(1)} %pad_add_fusion.s, bf16[768,3584]{1,0:T(8,128)(2,1)S(1)} %copy-done.1, bf16[3584,1792]{1,0:T(8,128)(2,1)} %refs_1_.9), custom_call_target="tpu_custom_call" | custom-call | flops 38535168 | bytes 222208 | tf_op jit(solution)/shard_map/pallas_call | solution.py:30
  63.6 3.4 %collective-permute-start.3 = (bf16[192,1792]{1,0:T(8,128)(2,1)S(1)}, bf16[192,1792]{1,0:T(8,128)(2,1)S(1)}, u32[]{:S(2)}, u32[]{:S(2)}) collective-permute-start(bf16[192,1792]{1,0:T(8,128)(2,1)S(1)} %shard_map.86), channel_id=1, source_target_pairs={{0,8},{24,16},{1,9},{25,17},{2,10},{26,18},{3,11},{27,19},{4,12},{... | collective-permute-start | bytes 2064392 | tf_op jit(solution)/shard_map/ppermute | solution.py:336
  68.1 1.3 collective-permute-start.8
  69.4 9.1 %shard_map.87 = (bf16[192,1792]{1,0:T(8,128)(2,1)S(1)}, bf16[192,1792]{1,0:T(8,128)(2,1)}) custom-call(s32[2]{0:T(128)S(1)} %pad_add_fusion.s, bf16[768,3584]{1,0:T(8,128)(2,1)S(1)} %copy-done.1, bf16[3584,1792]{1,0:T(8,128)(2,1)} %refs_1_.9), custom_call_target="tpu_custom_call" | custom-call | flops 77070336 | bytes 243712 | tf_op jit(solution)/shard_map/pallas_call | solution.py:30
  78.6 4.6 %collective-permute-start.6 = (bf16[192,1792]{1,0:T(8,128)(2,1)S(1)}, bf16[192,1792]{1,0:T(8,128)(2,1)S(1)}, u32[]{:S(2)}, u32[]{:S(2)}) collective-permute-start(bf16[192,1792]{1,0:T(8,128)(2,1)S(1)} %get-tuple-element.104), channel_id=1, source_target_pairs={{0,8},{24,16},{1,9},{25,17},{2,10},{26,18},{3,11},{27,19},{4,12},{... | collective-permute-start | bytes 2064392 | tf_op jit(solution)/shard_map/ppermute | solution.py:336
  87.4 1.8 shard_map.88
  89.2 7.0 %collective-permute-start.10 = (bf16[192,1792]{1,0:T(8,128)(2,1)}, bf16[192,1792]{1,0:T(8,128)(2,1)}, u32[]{:S(2)}, u32[]{:S(2)}) collective-permute-start(bf16[192,1792]{1,0:T(8,128)(2,1)} %get-tuple-element.112), channel_id=1, source_target_pairs={{0,8},{24,16},{1,9},{25,17},{2,10},{26,18},{3,11},{27,19},{4,12},{... | collective-permute-start | bytes 2064392 | tf_op jit(solution)/shard_map/ppermute | solution.py:336
  96.2 2.9 %collective-permute-done.6 = bf16[192,1792]{1,0:T(8,128)(2,1)S(1)} collective-permute-done((bf16[192,1792]{1,0:T(8,128)(2,1)S(1)}, bf16[192,1792]{1,0:T(8,128)(2,1)S(1)}, u32[]{:S(2)}, u32[]{:S(2)}) %collective-permute-start.6) | collective-permute-done | bytes 688160 | tf_op jit(solution)/shard_map/ppermute | solution.py:336
  100.1 1.6 collective-permute-start.9
  104.1 2.6 copy-done
  106.6 11.0 %shard_map.89 = (bf16[192,1792]{1,0:T(8,128)(2,1)S(1)}, bf16[192,1792]{1,0:T(8,128)(2,1)S(1)}, bf16[192,1792]{1,0:T(8,128)(2,1)S(1)}) custom-call(s32[2]{0:T(128)S(1)} %pad_add_fusion.s, bf16[768,3584]{1,0:T(8,128)(2,1)S(1)} %copy-done, bf16[1792,3584]{1,0:T(8,128)(2,1)} %refs_1_.7), custom_call_target="tpu_custom_call" | custom-call | flops 115605504 | bytes 265216 | tf_op jit(solution)/shard_map/pallas_call | solution.py:30
  117.6 1.6 add_convert_fusion.13.refs_0_
  119.2 7.1 %collective-permute-start.14 = (bf16[192,1792]{1,0:T(8,128)(2,1)S(1)}, bf16[192,1792]{1,0:T(8,128)(2,1)S(1)}, u32[]{:S(2)}, u32[]{:S(2)}) collective-permute-start(bf16[192,1792]{1,0:T(8,128)(2,1)S(1)} %get-tuple-element.116), channel_id=1, source_target_pairs={{0,8},{24,16},{1,9},{25,17},{2,10},{26,18},{3,11},{27,19},{4,12},{... | collective-permute-start | bytes 2064392 | tf_op jit(solution)/shard_map/ppermute | solution.py:336
  127.1 2.1 shard_map.90
  129.2 1.3 add_convert_fusion.12
  130.5 1.3 collective-permute-start.18
  131.8 2.9 %shard_map.91 = (bf16[768,1792]{1,0:T(8,128)(2,1)S(1)}, f32[192,1792]{1,0:T(8,128)S(1)}) custom-call(s32[2]{0:T(128)S(1)} %pad_add_fusion.s, f32[1,1792]{1,0:T(1,128)S(1)} %reshape.14.bias_ref, bf16[192,1792]{1,0:T(8,128)(2,1)S(1)} %add_convert_fusion.17.refs_0_, bf16[192,1792]{1,0:T(8,128)(2,1)S(1)} %copy-done.5, ...), custom_call_target="tpu_custom_call", output_to_operand_aliasing={{0}: (5, {})} | custom-call | flops 10321920 | bytes 4128768 | tf_op jit(solution)/shard_map/pallas_call | solution.py:30
  134.7 4.6 %collective-permute-start.16 = (bf16[192,1792]{1,0:T(8,128)(2,1)S(1)}, bf16[192,1792]{1,0:T(8,128)(2,1)S(1)}, u32[]{:S(2)}, u32[]{:S(2)}) collective-permute-start(bf16[192,1792]{1,0:T(8,128)(2,1)S(1)} %get-tuple-element.122), channel_id=1, source_target_pairs={{0,8},{24,16},{1,9},{25,17},{2,10},{26,18},{3,11},{27,19},{4,12},{... | collective-permute-start | bytes 2064392 | tf_op jit(solution)/shard_map/ppermute | solution.py:336
  142.8 1.5 collective-permute-start.19
  144.2 6.2 %collective-permute-done.18.refs_2_ = bf16[192,1792]{1,0:T(8,128)(2,1)S(1)} collective-permute-done((bf16[192,1792]{1,0:T(8,128)(2,1)S(1)}, bf16[192,1792]{1,0:T(8,128)(2,1)S(1)}, u32[]{:S(2)}, u32[]{:S(2)}) %collective-permute-start.18) | collective-permute-done | bytes 688160 | tf_op jit(solution)/shard_map/ppermute | solution.py:336
  150.5 3.1 %shard_map.92 = (bf16[768,1792]{1,0:T(8,128)(2,1)S(1)}, f32[192,1792]{1,0:T(8,128)S(1)}) custom-call(s32[2]{0:T(128)S(1)} %pad_add_fusion.s, f32[1,1792]{1,0:T(1,128)S(1)} %reshape.14.bias_ref, bf16[192,1792]{1,0:T(8,128)(2,1)} %add_convert_fusion.15.refs_0_, bf16[192,1792]{1,0:T(8,128)(2,1)} %collective-permute-done.9.refs_1_, ...), custom_call_target="tpu_custom_call", output_to_operand_aliasing={{0}: (5, {})} | custom-call | flops 10321920 | bytes 4128768 | tf_op jit(solution)/shard_map/pallas_call | solution.py:30
  153.5 1.5 collective-permute-start.21
  156.4 1.6 collective-permute-start.22
  158.0 6.5 %collective-permute-done.19.refs_2_ = bf16[192,1792]{1,0:T(8,128)(2,1)S(1)} collective-permute-done((bf16[192,1792]{1,0:T(8,128)(2,1)S(1)}, bf16[192,1792]{1,0:T(8,128)(2,1)S(1)}, u32[]{:S(2)}, u32[]{:S(2)}) %collective-permute-start.19) | collective-permute-done | bytes 688160 | tf_op jit(solution)/shard_map/ppermute | solution.py:336
  164.5 1.8 shard_map.93
  166.2 1.6 collective-permute-done.21
  168.9 1.3 collective-permute-start.24
  170.3 6.5 %shard_map.94.refs_0_ = f32[1792,3584]{1,0:T(8,128)} custom-call(s32[2]{0:T(128)S(1)} %pad_add_fusion.s, bf16[768,1792]{1,0:T(8,128)(2,1)S(1)} %get-tuple-element.136.act_ref, bf16[768,3584]{1,0:T(8,128)(2,1)S(1)} %bitcast.3), custom_call_target="tpu_custom_call" | custom-call | flops 2818572288 | bytes 11665408 | tf_op jit(solution)/shard_map/pallas_call | solution.py:30
  176.7 2.5 collective-permute-done.22.refs_2_
  180.2 8.5 %shard_map.96 = (bf16[192,3584]{1,0:T(8,128)(2,1)S(1)}, bf16[192,3584]{1,0:T(8,128)(2,1)S(1)}) custom-call(s32[2]{0:T(128)S(1)} %pad_add_fusion.s, bf16[768,1792]{1,0:T(8,128)(2,1)S(1)} %get-tuple-element.126.refs_0_.refs_3_, bf16[3584,1792]{1,0:T(8,128)(2,1)} %refs_1_.9), custom_call_target="tpu_custom_call" | custom-call | flops 4932501504 | bytes 14221312 | tf_op jit(solution)/shard_map/pallas_call | solution.py:30
  188.9 2.1 collective-permute-done.24.refs_2_
  192.0 1.5 collective-permute-start.26
  193.5 1.6 collective-permute-done.25
  195.5 1.5 collective-permute-start.27
  197.0 11.8 %shard_map.98 = f32[1792,3584]{1,0:T(8,128)} custom-call(s32[2]{0:T(128)S(1)} %pad_add_fusion.s, bf16[768,1792]{1,0:T(8,128)(2,1)S(1)} %get-tuple-element.136.act_ref, bf16[768,3584]{1,0:T(8,128)(2,1)S(1)} %bitcast.3, f32[1792,3584]{1,0:T(8,128)} %shard_map.94.refs_0_), custom_call_target="tpu_custom_call", output_to_operand_aliasing={{}: (3, {})} | custom-call | flops 7046430720 | bytes 25034752 | tf_op jit(solution)/shard_map/pallas_call | solution.py:30
  208.8 3.0 %collective-permute-done.26.refs_2_ = bf16[192,1792]{1,0:T(8,128)(2,1)S(1)} collective-permute-done((bf16[192,1792]{1,0:T(8,128)(2,1)S(1)}, bf16[192,1792]{1,0:T(8,128)(2,1)S(1)}, u32[]{:S(2)}, u32[]{:S(2)}) %collective-permute-start.26) | collective-permute-done | bytes 688160 | tf_op jit(solution)/shard_map/ppermute | solution.py:336
  212.8 3.6 %collective-permute-done.28 = f32[1,1792]{1,0:T(1,128)S(1)} collective-permute-done((f32[1,1792]{1,0:T(1,128)S(1)}, f32[1,1792]{1,0:T(1,128)S(1)}, u32[]{:S(2)}, u32[]{:S(2)}) %collective-permute-start.28) | collective-permute-done | bytes 7200 | tf_op jit(solution)/shard_map/ppermute | solution.py:461
  217.2 8.9 %shard_map.101 = (bf16[192,3584]{1,0:T(8,128)(2,1)S(1)}, bf16[192,3584]{1,0:T(8,128)(2,1)S(1)}) custom-call(s32[2]{0:T(128)S(1)} %pad_add_fusion.s, bf16[768,1792]{1,0:T(8,128)(2,1)S(1)} %get-tuple-element.151.refs_0_.grad_ref, bf16[3584,1792]{1,0:T(8,128)(2,1)} %refs_1_.9), custom_call_target="tpu_custom_call" | custom-call | flops 4932501504 | bytes 14221312 | tf_op jit(solution)/shard_map/pallas_call | solution.py:30
  226.2 3.0 %collective-permute-done.29 = bf16[192,3584]{1,0:T(8,128)(2,1)S(1)} collective-permute-done((bf16[192,3584]{1,0:T(8,128)(2,1)S(1)}, bf16[192,3584]{1,0:T(8,128)(2,1)S(1)}, u32[]{:S(2)}, u32[]{:S(2)}) %collective-permute-start.29) | collective-permute-done | bytes 1376288 | tf_op jit(solution)/shard_map/ppermute | solution.py:339
  232.5 15.6 %shard_map.102.refs_0_ = f32[3584,1792]{1,0:T(8,128)} custom-call(s32[2]{0:T(128)S(1)} %pad_add_fusion.s, bf16[768,3584]{1,0:T(8,128)(2,1)S(1)} %bitcast.5, bf16[768,1792]{1,0:T(8,128)(2,1)S(1)} %get-tuple-element.151.refs_0_.grad_ref), custom_call_target="tpu_custom_call" | custom-call | flops 9865003008 | bytes 33947648 | tf_op jit(solution)/shard_map/pallas_call | solution.py:30
  (124 shorter events, 27.6 us)
Async XLA Ops:
  7.2 47.7 %all-gather.3.cloned.1.call-start = ((), (), s32[]{:S(2)}) async-start(), calls=%async_computation | async-start | bytes 6193152 | tf_op jit(solution)/shard_map/all_gather | solution.py:414
  7.9 96.1 %all-gather.5.cloned.1.call-start = ((), (), s32[]{:S(2)}) async-start(), calls=%async_computation.1 | async-start | bytes 6193152 | tf_op jit(solution)/shard_map/all_gather | solution.py:415
  8.0 2.5 collective-permute-start
  10.5 11.4 %collective-permute-start.2 = (bf16[96,3584]{1,0:T(8,128)(2,1)S(1)}, bf16[96,3584]{1,0:T(8,128)(2,1)S(1)}, u32[]{:S(2)}, u32[]{:S(2)}) collective-permute-start(bf16[96,3584]{1,0:T(8,128)(2,1)S(1)} %copy-done.3), channel_id=1, source_target_pairs={{0,1},{1,0},{2,3},{3,2},{4,5},{5,4},{6,7},{7,6},{8,9},{9,8},{10,11... | collective-permute-start | bytes 2064392 | tf_op jit(solution)/shard_map/ppermute | solution.py:339
  17.2 20.4 %collective-permute-start.1 = (bf16[192,1792]{1,0:T(8,128)(2,1)S(1)}, bf16[192,1792]{1,0:T(8,128)(2,1)S(1)}, u32[]{:S(2)}, u32[]{:S(2)}) collective-permute-start(bf16[192,1792]{1,0:T(8,128)(2,1)S(1)} %shard_map.84), channel_id=1, source_target_pairs={{0,8},{24,16},{1,9},{25,17},{2,10},{26,18},{3,11},{27,19},{4,12},{... | collective-permute-start | bytes 2064392 | tf_op jit(solution)/shard_map/ppermute | solution.py:336
  29.2 37.8 %collective-permute-start.5 = (bf16[192,1792]{1,0:T(8,128)(2,1)S(1)}, bf16[192,1792]{1,0:T(8,128)(2,1)S(1)}, u32[]{:S(2)}, u32[]{:S(2)}) collective-permute-start(bf16[192,1792]{1,0:T(8,128)(2,1)S(1)} %shard_map.85), channel_id=1, source_target_pairs={{0,8},{24,16},{1,9},{25,17},{2,10},{26,18},{3,11},{27,19},{4,12},{... | collective-permute-start | bytes 2064392 | tf_op jit(solution)/shard_map/ppermute | solution.py:336
  37.8 25.8 %copy-start.6 = (bf16[192,1792]{1,0:T(8,128)(2,1)}, bf16[192,1792]{1,0:T(8,128)(2,1)S(1)}, u32[]{:S(2)}) copy-start(bf16[192,1792]{1,0:T(8,128)(2,1)S(1)} %add_convert_fusion.20.refs_0_) | copy-start | bytes 2064388
  37.8 30.2 %collective-permute-start.4 = (bf16[192,1792]{1,0:T(8,128)(2,1)S(1)}, bf16[192,1792]{1,0:T(8,128)(2,1)S(1)}, u32[]{:S(2)}, u32[]{:S(2)}) collective-permute-start(bf16[192,1792]{1,0:T(8,128)(2,1)S(1)} %add_convert_fusion.20.refs_0_), channel_id=1, source_target_pairs={{8,16},{16,8},{9,17},{17,9},{10,18},{18,10},{11,19},{19,11},{12,20... | collective-permute-start | bytes 2064392 | tf_op jit(solution)/shard_map/ppermute | solution.py:336
  63.6 19.6 %collective-permute-start.3 = (bf16[192,1792]{1,0:T(8,128)(2,1)S(1)}, bf16[192,1792]{1,0:T(8,128)(2,1)S(1)}, u32[]{:S(2)}, u32[]{:S(2)}) collective-permute-start(bf16[192,1792]{1,0:T(8,128)(2,1)S(1)} %shard_map.86), channel_id=1, source_target_pairs={{0,8},{24,16},{1,9},{25,17},{2,10},{26,18},{3,11},{27,19},{4,12},{... | collective-permute-start | bytes 2064392 | tf_op jit(solution)/shard_map/ppermute | solution.py:336
  67.2 11.4 %copy-start.10 = (bf16[192,1792]{1,0:T(8,128)(2,1)}, bf16[192,1792]{1,0:T(8,128)(2,1)S(1)}, u32[]{:S(2)}) copy-start(bf16[192,1792]{1,0:T(8,128)(2,1)S(1)} %add_convert_fusion.19.refs_0_) | copy-start | bytes 2064388
  67.2 17.1 %collective-permute-start.7 = (bf16[192,1792]{1,0:T(8,128)(2,1)S(1)}, bf16[192,1792]{1,0:T(8,128)(2,1)S(1)}, u32[]{:S(2)}, u32[]{:S(2)}) collective-permute-start(bf16[192,1792]{1,0:T(8,128)(2,1)S(1)} %add_convert_fusion.19.refs_0_), channel_id=1, source_target_pairs={{8,16},{16,8},{9,17},{17,9},{10,18},{18,10},{11,19},{19,11},{12,20... | collective-permute-start | bytes 2064392 | tf_op jit(solution)/shard_map/ppermute | solution.py:336
  68.0 10.6 %copy-start.8 = (bf16[192,1792]{1,0:T(8,128)(2,1)}, bf16[192,1792]{1,0:T(8,128)(2,1)S(1)}, u32[]{:S(2)}) copy-start(bf16[192,1792]{1,0:T(8,128)(2,1)S(1)} %collective-permute-done.4.refs_1_) | copy-start | bytes 2064388
  68.1 19.2 %collective-permute-start.8 = (bf16[192,1792]{1,0:T(8,128)(2,1)S(1)}, bf16[192,1792]{1,0:T(8,128)(2,1)S(1)}, u32[]{:S(2)}, u32[]{:S(2)}) collective-permute-start(bf16[192,1792]{1,0:T(8,128)(2,1)S(1)} %add_convert_fusion.18), channel_id=1, source_target_pairs={{16,24},{8,0},{17,25},{9,1},{18,26},{10,2},{19,27},{11,3},{20,28},... | collective-permute-start | bytes 2064392 | tf_op jit(solution)/shard_map/ppermute | solution.py:336
  78.6 20.4 %copy-start.14 = (bf16[192,1792]{1,0:T(8,128)(2,1)}, bf16[192,1792]{1,0:T(8,128)(2,1)S(1)}, u32[]{:S(2)}) copy-start(bf16[192,1792]{1,0:T(8,128)(2,1)S(1)} %get-tuple-element.104) | copy-start | bytes 2064388
  78.6 20.4 %collective-permute-start.6 = (bf16[192,1792]{1,0:T(8,128)(2,1)S(1)}, bf16[192,1792]{1,0:T(8,128)(2,1)S(1)}, u32[]{:S(2)}, u32[]{:S(2)}) collective-permute-start(bf16[192,1792]{1,0:T(8,128)(2,1)S(1)} %get-tuple-element.104), channel_id=1, source_target_pairs={{0,8},{24,16},{1,9},{25,17},{2,10},{26,18},{3,11},{27,19},{4,12},{... | collective-permute-start | bytes 2064392 | tf_op jit(solution)/shard_map/ppermute | solution.py:336
  83.4 18.2 %collective-permute-start.11 = (bf16[192,1792]{1,0:T(8,128)(2,1)S(1)}, bf16[192,1792]{1,0:T(8,128)(2,1)S(1)}, u32[]{:S(2)}, u32[]{:S(2)}) collective-permute-start(bf16[192,1792]{1,0:T(8,128)(2,1)S(1)} %add_convert_fusion.17.refs_0_), channel_id=1, source_target_pairs={{8,16},{16,8},{9,17},{17,9},{10,18},{18,10},{11,19},{19,11},{12,20... | collective-permute-start | bytes 2064392 | tf_op jit(solution)/shard_map/ppermute | solution.py:336
  85.4 41.6 %collective-permute-start.12 = (bf16[192,1792]{1,0:T(8,128)(2,1)}, bf16[192,1792]{1,0:T(8,128)(2,1)}, u32[]{:S(2)}, u32[]{:S(2)}) collective-permute-start(bf16[192,1792]{1,0:T(8,128)(2,1)} %add_convert_fusion.16), channel_id=1, source_target_pairs={{16,24},{8,0},{17,25},{9,1},{18,26},{10,2},{19,27},{11,3},{20,28},... | collective-permute-start | bytes 2064392 | tf_op jit(solution)/shard_map/ppermute | solution.py:336
  89.1 13.6 %copy-start.20 = (f32[192,1792]{1,0:T(8,128)}, f32[192,1792]{1,0:T(8,128)S(1)}, u32[]{:S(2)}) copy-start(f32[192,1792]{1,0:T(8,128)S(1)} %get-tuple-element.94.slope_ref) | copy-start | bytes 4128772
  89.2 28.5 %collective-permute-start.10 = (bf16[192,1792]{1,0:T(8,128)(2,1)}, bf16[192,1792]{1,0:T(8,128)(2,1)}, u32[]{:S(2)}, u32[]{:S(2)}) collective-permute-start(bf16[192,1792]{1,0:T(8,128)(2,1)} %get-tuple-element.112), channel_id=1, source_target_pairs={{0,8},{24,16},{1,9},{25,17},{2,10},{26,18},{3,11},{27,19},{4,12},{... | collective-permute-start | bytes 2064392 | tf_op jit(solution)/shard_map/ppermute | solution.py:336
  100.1 29.1 %collective-permute-start.9 = (bf16[192,1792]{1,0:T(8,128)(2,1)}, bf16[192,1792]{1,0:T(8,128)(2,1)}, u32[]{:S(2)}, u32[]{:S(2)}) collective-permute-start(bf16[192,1792]{1,0:T(8,128)(2,1)} %add_convert_fusion.15.refs_0_), channel_id=1, source_target_pairs={{8,16},{16,8},{9,17},{17,9},{10,18},{18,10},{11,19},{19,11},{12,20... | collective-permute-start | bytes 2064392 | tf_op jit(solution)/shard_map/ppermute | solution.py:336
  102.7 29.1 %collective-permute-start.13 = (bf16[192,1792]{1,0:T(8,128)(2,1)}, bf16[192,1792]{1,0:T(8,128)(2,1)}, u32[]{:S(2)}, u32[]{:S(2)}) collective-permute-start(bf16[192,1792]{1,0:T(8,128)(2,1)} %add_convert_fusion.14), channel_id=1, source_target_pairs={{16,24},{8,0},{17,25},{9,1},{18,26},{10,2},{19,27},{11,3},{20,28},... | collective-permute-start | bytes 2064392 | tf_op jit(solution)/shard_map/ppermute | solution.py:336
  106.6 20.4 %copy-start.21 = (f32[192,1792]{1,0:T(8,128)S(1)}, f32[192,1792]{1,0:T(8,128)}, u32[]{:S(2)}) copy-start(f32[192,1792]{1,0:T(8,128)} %copy-done.20) | copy-start | bytes 4128772
  117.6 9.4 %copy-start.11 = (bf16[192,1792]{1,0:T(8,128)(2,1)S(1)}, bf16[192,1792]{1,0:T(8,128)(2,1)}, u32[]{:S(2)}) copy-start(bf16[192,1792]{1,0:T(8,128)(2,1)} %copy-done.10) | copy-start | bytes 2064388
  117.6 9.4 %copy-start.13 = (bf16[192,1792]{1,0:T(8,128)(2,1)S(1)}, bf16[192,1792]{1,0:T(8,128)(2,1)}, u32[]{:S(2)}) copy-start(bf16[192,1792]{1,0:T(8,128)(2,1)} %copy-done.12) | copy-start | bytes 2064388
  119.2 21.4 %collective-permute-start.14 = (bf16[192,1792]{1,0:T(8,128)(2,1)S(1)}, bf16[192,1792]{1,0:T(8,128)(2,1)S(1)}, u32[]{:S(2)}, u32[]{:S(2)}) collective-permute-start(bf16[192,1792]{1,0:T(8,128)(2,1)S(1)} %get-tuple-element.116), channel_id=1, source_target_pairs={{0,8},{24,16},{1,9},{25,17},{2,10},{26,18},{3,11},{27,19},{4,12},{... | collective-permute-start | bytes 2064392 | tf_op jit(solution)/shard_map/ppermute | solution.py:336
  126.3 15.2 %collective-permute-start.17 = (bf16[192,1792]{1,0:T(8,128)(2,1)S(1)}, bf16[192,1792]{1,0:T(8,128)(2,1)S(1)}, u32[]{:S(2)}, u32[]{:S(2)}) collective-permute-start(bf16[192,1792]{1,0:T(8,128)(2,1)S(1)} %add_convert_fusion.13.refs_0_), channel_id=1, source_target_pairs={{8,16},{16,8},{9,17},{17,9},{10,18},{18,10},{11,19},{19,11},{12,20... | collective-permute-start | bytes 2064392 | tf_op jit(solution)/shard_map/ppermute | solution.py:336
  130.5 19.9 %collective-permute-start.18 = (bf16[192,1792]{1,0:T(8,128)(2,1)S(1)}, bf16[192,1792]{1,0:T(8,128)(2,1)S(1)}, u32[]{:S(2)}, u32[]{:S(2)}) collective-permute-start(bf16[192,1792]{1,0:T(8,128)(2,1)S(1)} %add_convert_fusion.12), channel_id=1, source_target_pairs={{16,24},{8,0},{17,25},{9,1},{18,26},{10,2},{19,27},{11,3},{20,28},... | collective-permute-start | bytes 2064392 | tf_op jit(solution)/shard_map/ppermute | solution.py:336
  134.7 20.7 %collective-permute-start.16 = (bf16[192,1792]{1,0:T(8,128)(2,1)S(1)}, bf16[192,1792]{1,0:T(8,128)(2,1)S(1)}, u32[]{:S(2)}, u32[]{:S(2)}) collective-permute-start(bf16[192,1792]{1,0:T(8,128)(2,1)S(1)} %get-tuple-element.122), channel_id=1, source_target_pairs={{0,8},{24,16},{1,9},{25,17},{2,10},{26,18},{3,11},{27,19},{4,12},{... | collective-permute-start | bytes 2064392 | tf_op jit(solution)/shard_map/ppermute | solution.py:336
  140.8 15.5 %collective-permute-start.15 = (bf16[192,1792]{1,0:T(8,128)(2,1)S(1)}, bf16[192,1792]{1,0:T(8,128)(2,1)S(1)}, u32[]{:S(2)}, u32[]{:S(2)}) collective-permute-start(bf16[192,1792]{1,0:T(8,128)(2,1)S(1)} %add_convert_fusion.11.refs_0_), channel_id=1, source_target_pairs={{8,16},{16,8},{9,17},{17,9},{10,18},{18,10},{11,19},{19,11},{12,20... | collective-permute-start | bytes 2064392 | tf_op jit(solution)/shard_map/ppermute | solution.py:336
  142.8 21.7 %collective-permute-start.19 = (bf16[192,1792]{1,0:T(8,128)(2,1)S(1)}, bf16[192,1792]{1,0:T(8,128)(2,1)S(1)}, u32[]{:S(2)}, u32[]{:S(2)}) collective-permute-start(bf16[192,1792]{1,0:T(8,128)(2,1)S(1)} %add_convert_fusion.10), channel_id=1, source_target_pairs={{16,24},{8,0},{17,25},{9,1},{18,26},{10,2},{19,27},{11,3},{20,28},... | collective-permute-start | bytes 2064392 | tf_op jit(solution)/shard_map/ppermute | solution.py:336
  153.5 14.3 %collective-permute-start.21 = (bf16[192,1792]{1,0:T(8,128)(2,1)S(1)}, bf16[192,1792]{1,0:T(8,128)(2,1)S(1)}, u32[]{:S(2)}, u32[]{:S(2)}) collective-permute-start(bf16[192,1792]{1,0:T(8,128)(2,1)S(1)} %get-tuple-element.129), channel_id=1, source_target_pairs={{0,8},{24,16},{1,9},{25,17},{2,10},{26,18},{3,11},{27,19},{4,12},{... | collective-permute-start | bytes 2064392 | tf_op jit(solution)/shard_map/ppermute | solution.py:336
  155.5 13.2 %collective-permute-start.20 = (bf16[192,1792]{1,0:T(8,128)(2,1)S(1)}, bf16[192,1792]{1,0:T(8,128)(2,1)S(1)}, u32[]{:S(2)}, u32[]{:S(2)}) collective-permute-start(bf16[192,1792]{1,0:T(8,128)(2,1)S(1)} %add_convert_fusion.9.refs_0_), channel_id=1, source_target_pairs={{8,16},{16,8},{9,17},{17,9},{10,18},{18,10},{11,19},{19,11},{12,20... | collective-permute-start | bytes 2064392 | tf_op jit(solution)/shard_map/ppermute | solution.py:336
  156.2 14.0 %slice-start = ((s8[5505024]{0:T(1024)(128)(4,1)}), s8[4194304]{0:T(1024)(128)(4,1)S(1)}, s32[]{:S(2)}) async-start(s8[5505024]{0:T(1024)(128)(4,1)} %bitcast.2), calls=%async_computation.2 | async-start | bytes 8388608
  156.4 13.8 %slice-start.1 = ((s8[5505024]{0:T(1024)(128)(4,1)}), s8[1310720]{0:T(1024)(128)(4,1)S(1)}, s32[]{:S(2)}) async-start(s8[5505024]{0:T(1024)(128)(4,1)} %bitcast.2), calls=%async_computation.3 | async-start | bytes 2621440
  156.4 22.8 %collective-permute-start.22 = (bf16[192,1792]{1,0:T(8,128)(2,1)S(1)}, bf16[192,1792]{1,0:T(8,128)(2,1)S(1)}, u32[]{:S(2)}, u32[]{:S(2)}) collective-permute-start(bf16[192,1792]{1,0:T(8,128)(2,1)S(1)} %add_convert_fusion.8), channel_id=1, source_target_pairs={{16,24},{8,0},{17,25},{9,1},{18,26},{10,2},{19,27},{11,3},{20,28},... | collective-permute-start | bytes 2064392 | tf_op jit(solution)/shard_map/ppermute | solution.py:336
  168.0 20.7 %collective-permute-start.23 = (bf16[192,1792]{1,0:T(8,128)(2,1)S(1)}, bf16[192,1792]{1,0:T(8,128)(2,1)S(1)}, u32[]{:S(2)}, u32[]{:S(2)}) collective-permute-start(bf16[192,1792]{1,0:T(8,128)(2,1)S(1)} %add_convert_fusion.7.refs_0_), channel_id=1, source_target_pairs={{8,16},{16,8},{9,17},{17,9},{10,18},{18,10},{11,19},{19,11},{12,20... | collective-permute-start | bytes 2064392 | tf_op jit(solution)/shard_map/ppermute | solution.py:336
  168.9 22.0 %collective-permute-start.24 = (bf16[192,1792]{1,0:T(8,128)(2,1)S(1)}, bf16[192,1792]{1,0:T(8,128)(2,1)S(1)}, u32[]{:S(2)}, u32[]{:S(2)}) collective-permute-start(bf16[192,1792]{1,0:T(8,128)(2,1)S(1)} %add_convert_fusion.6), channel_id=1, source_target_pairs={{16,24},{8,0},{17,25},{9,1},{18,26},{10,2},{19,27},{11,3},{20,28},... | collective-permute-start | bytes 2064392 | tf_op jit(solution)/shard_map/ppermute | solution.py:336
  191.9 3.2 %collective-permute-start.25 = (bf16[192,3584]{1,0:T(8,128)(2,1)S(1)}, bf16[192,3584]{1,0:T(8,128)(2,1)S(1)}, u32[]{:S(2)}, u32[]{:S(2)}) collective-permute-start(bf16[192,3584]{1,0:T(8,128)(2,1)S(1)} %get-tuple-element.134), channel_id=1, source_target_pairs={{0,1},{1,0},{2,3},{3,2},{4,5},{5,4},{6,7},{7,6},{8,9},{9,8},{10,11... | collective-permute-start | bytes 4128776 | tf_op jit(solution)/shard_map/ppermute | solution.py:339
  192.0 19.7 %collective-permute-start.26 = (bf16[192,1792]{1,0:T(8,128)(2,1)S(1)}, bf16[192,1792]{1,0:T(8,128)(2,1)S(1)}, u32[]{:S(2)}, u32[]{:S(2)}) collective-permute-start(bf16[192,1792]{1,0:T(8,128)(2,1)S(1)} %add_convert_fusion.5), channel_id=1, source_target_pairs={{16,24},{8,0},{17,25},{9,1},{18,26},{10,2},{19,27},{11,3},{20,28},... | collective-permute-start | bytes 2064392 | tf_op jit(solution)/shard_map/ppermute | solution.py:336
  195.5 16.3 %copy-start.17 = (f32[192,1792]{1,0:T(8,128)S(1)}, f32[192,1792]{1,0:T(8,128)}, u32[]{:S(2)}) copy-start(f32[192,1792]{1,0:T(8,128)} %copy-done.16) | copy-start | bytes 4128772
  195.5 21.0 %collective-permute-start.27 = (bf16[96,3584]{1,0:T(8,128)(2,1)S(1)}, bf16[96,3584]{1,0:T(8,128)(2,1)S(1)}, u32[]{:S(2)}, u32[]{:S(2)}) collective-permute-start(bf16[96,3584]{1,0:T(8,128)(2,1)S(1)} %get-tuple-element.155), channel_id=1, source_target_pairs={{0,6},{1,7},{2,4},{3,5},{4,2},{5,3},{6,0},{7,1},{8,14},{9,15},{10,... | collective-permute-start | bytes 2064392 | tf_op jit(solution)/shard_map/ppermute | solution.py:339
  212.8 3.7 %collective-permute-start.28 = (f32[1,1792]{1,0:T(1,128)S(1)}, f32[1,1792]{1,0:T(1,128)S(1)}, u32[]{:S(2)}, u32[]{:S(2)}) collective-permute-start(f32[1,1792]{1,0:T(1,128)S(1)} %add_add_fusion), channel_id=1, source_target_pairs={{0,8},{8,0},{16,24},{24,16},{1,9},{9,1},{17,25},{25,17},{2,10},{10... | collective-permute-start | bytes 21512 | tf_op jit(solution)/shard_map/ppermute | solution.py:461
  216.5 16.0 %slice-start.2 = ((s8[5505024]{0:T(1024)(128)(4,1)}), s8[4194304]{0:T(1024)(128)(4,1)S(1)}, s32[]{:S(2)}) async-start(s8[5505024]{0:T(1024)(128)(4,1)} %bitcast.4), calls=%async_computation.4 | async-start | bytes 8388608
  217.2 15.3 %slice-start.3 = ((s8[5505024]{0:T(1024)(128)(4,1)}), s8[1310720]{0:T(1024)(128)(4,1)S(1)}, s32[]{:S(2)}) async-start(s8[5505024]{0:T(1024)(128)(4,1)} %bitcast.4), calls=%async_computation.5 | async-start | bytes 2621440
  226.1 3.2 %collective-permute-start.29 = (bf16[192,3584]{1,0:T(8,128)(2,1)S(1)}, bf16[192,3584]{1,0:T(8,128)(2,1)S(1)}, u32[]{:S(2)}, u32[]{:S(2)}) collective-permute-start(bf16[192,3584]{1,0:T(8,128)(2,1)S(1)} %get-tuple-element.150), channel_id=1, source_target_pairs={{0,1},{1,0},{2,3},{3,2},{4,5},{5,4},{6,7},{7,6},{8,9},{9,8},{10,11... | collective-permute-start | bytes 4128776 | tf_op jit(solution)/shard_map/ppermute | solution.py:339
  226.2 22.0 %collective-permute-start.32 = (f32[1,1792]{1,0:T(1,128)S(1)}, f32[1,1792]{1,0:T(1,128)S(1)}, u32[]{:S(2)}, u32[]{:S(2)}) collective-permute-start(f32[1,1792]{1,0:T(1,128)S(1)} %add.105.left_ref), channel_id=1, source_target_pairs={{0,16},{8,24},{16,0},{24,8},{1,17},{9,25},{17,1},{25,9},{2,18},{10... | collective-permute-start | bytes 21512 | tf_op jit(solution)/shard_map/ppermute | solution.py:467
  230.4 18.9 %collective-permute-start.31 = (bf16[96,3584]{1,0:T(8,128)(2,1)S(1)}, bf16[96,3584]{1,0:T(8,128)(2,1)S(1)}, u32[]{:S(2)}, u32[]{:S(2)}) collective-permute-start(bf16[96,3584]{1,0:T(8,128)(2,1)S(1)} %get-tuple-element.153), channel_id=1, source_target_pairs={{0,4},{1,5},{2,6},{3,7},{4,0},{5,1},{6,2},{7,3},{8,12},{9,13},{10,... | collective-permute-start | bytes 2064392 | tf_op jit(solution)/shard_map/ppermute | solution.py:339
  231.7 17.6 %collective-permute-start.30 = (bf16[96,3584]{1,0:T(8,128)(2,1)}, bf16[96,3584]{1,0:T(8,128)(2,1)S(1)}, u32[]{:S(2)}, u32[]{:S(2)}) collective-permute-start(bf16[96,3584]{1,0:T(8,128)(2,1)} %get-tuple-element.152), channel_id=1, source_target_pairs={{0,2},{1,3},{2,0},{3,1},{4,6},{5,7},{6,4},{7,5},{8,10},{9,11},{10,... | collective-permute-start | bytes 2064392 | tf_op jit(solution)/shard_map/ppermute | solution.py:339
  (14 other events, 48.0 us)
Sparse Core Ops, SparseCore 0:
  9.9 44.9 all-gather.2
  56.7 42.3 all-gather.4
